TPU v7x, 32 devices: a whole 2x2x4 slice. The times are simulated.
32 devices in a mesh: fsdp: 4 (over z), ctx: 4 (over y, x), tp: 2 (over core).
Axes of the slice: x: 2, y: 2, z: 4, core: 2. Of those that a mesh axis runs over, the one named last changes fastest.
Arguments:
- hidden_in: bfloat16 [4, 2048, 2048], P('fsdp', 'ctx'), may hold values from -6 to 6
- out_grad: bfloat16 [4, 2048, 2048], P('fsdp', 'ctx'), may hold values from -8 to 8
- ln_gain: bfloat16 [2048], replicated, may hold values from 0.5 to 1.5
- ln_bias: bfloat16 [2048], replicated, may hold values from -1.25 to 1.25
- w_qkv: bfloat16 [2048, 6144], P('fsdp', 'tp'), may hold values from -0.125 to 0.125
- b_qkv: bfloat16 [6144], P('tp'), may hold values from -1.75 to 1.75
- w_dense: bfloat16 [2048, 2048], P('fsdp', 'tp'), may hold values from -0.5 to 0.5
- b_dense: bfloat16 [2048], replicated, may hold values from -1.25 to 1.25
- w_fc1: bfloat16 [2048, 8192], P('fsdp', 'tp'), may hold values from -0.125 to 0.125
- b_fc1: bfloat16 [8192], P('tp'), may hold values from -1.75 to 1.75
- w_fc2: bfloat16 [2048, 8192], P('fsdp', 'tp'), may hold values from -0.125 to 0.125
- b_fc2: bfloat16 [2048], replicated, may hold values from -1.25 to 1.25
- lengths: int32 [4, 4], P('fsdp'), may hold values from 1 to 1024, 2048 in all within a row
- assignment: int32 [4, 2048], P('fsdp'), may hold values from 0 to 2047, each once within a row
Outputs:
- hidden_out: bfloat16 [4, 2048, 2048], P('fsdp', 'ctx')
- input_grad: float32 [4, 2048, 2048], P('fsdp', 'ctx')
- ln_gain_grad: float32 [2048], replicated
- ln_bias_grad: float32 [2048], replicated
- qkv_weight_grad: float32 [2048, 6144], P(('fsdp', 'ctx'), 'tp')
- qkv_bias_grad: float32 [6144], P('tp')
- dense_weight_grad: float32 [2048, 2048], P(('fsdp', 'ctx'), 'tp')
- dense_bias_grad: float32 [2048], replicated
- fc1_weight_grad: float32 [2048, 8192], P(('fsdp', 'ctx'), 'tp')
- fc1_bias_grad: float32 [8192], P('tp')
- fc2_weight_grad: float32 [2048, 8192], P(('fsdp', 'ctx'), 'tp')
- fc2_bias_grad: float32 [2048], replicated
Inputs may be any that keep to these rules, and one draw needn't show every extreme that they name: `lengths`: each row sums to 2048 and its largest entry is 1024. `assignment`: each row holds every number from 0 to 2047 once.
All inputs are finite; a program needn't handle non-finite values.
Results may differ from a plain program's by a relative error of at most 0.0074.
Values may be sent and summed in bfloat16 or wider, within the bound.
No kernel may reach another device: no remote copies, remote signals or barrier semaphores. Data moves between devices by JAX's collectives and lax.ppermute only.
A program may use at most 384 MiB of HBM per device.

v0:
```python
import math

import jax
import jax.numpy as jnp
from jax import lax
from jax.sharding import PartitionSpec as P

HEAD = 64
ROT = 32


MASKED = -1e30
EPSILON = 1e-05


def layer_norm(source, gain_vec, shift_vec):
    centred = source - jnp.mean(source, axis=-1, keepdims=True)
    spread = jnp.mean(centred * centred, axis=-1, keepdims=True)
    return centred * lax.rsqrt(spread + EPSILON) * gain_vec + shift_vec


def rotate(values, places):
    half_dim = ROT // 2
    frequency = jnp.power(10000.0, -(jnp.arange(half_dim, dtype=jnp.float32) * 2.0 / ROT))
    angles = places.astype(jnp.float32)[:, None] * frequency[None, :]
    cosine = jnp.cos(angles)[:, None, :]
    sine_part = jnp.sin(angles)[:, None, :]
    leading = values[..., :half_dim]
    trailing = values[..., half_dim:ROT]
    return jnp.concatenate(
        [
            leading * cosine - trailing * sine_part,
            trailing * cosine + leading * sine_part,
            values[..., ROT:],
        ],
        axis=-1,
    )


def positions(packed, lengths):
    seq_ends = jnp.cumsum(lengths)
    starts = seq_ends - lengths
    segment = jnp.sum((packed[:, None] >= seq_ends[None, :]).astype(jnp.int32), axis=1)
    owner_mask = segment[:, None] == jnp.arange(lengths.shape[0], dtype=jnp.int32)[None, :]
    return (segment, packed - jnp.sum(jnp.where(owner_mask, starts[None, :], 0), axis=1))


def gelu_tanh(values):
    return jax.nn.gelu(values, approximate=True)


def shards(
    hidden_in,
    out_grad,
    ln_gain,
    ln_bias,
    w_qkv,
    b_qkv,
    w_dense,
    b_dense,
    w_fc1,
    b_fc1,
    w_fc2,
    b_fc2,
    lengths,
    assignment,
):
    f32 = jnp.float32
    bf16 = jnp.bfloat16
    row_count = hidden_in.shape[1]
    ctx_count = lax.axis_size("ctx")
    group_rows = row_count * ctx_count
    local_heads = w_qkv.shape[1] // (3 * HEAD)
    head_share = local_heads // ctx_count
    block_rows = min(512, group_rows)
    block_count = group_rows // block_rows
    scaling = 1.0 / math.sqrt(HEAD)
    by_columns = (((1,), (1,)), ((), ()))
    by_rows = (((0,), (0,)), ((), ()))
    packed_all = assignment[0]
    segment_all, place_all = positions(packed_all, lengths[0])
    row_offset = lax.axis_index("ctx") * row_count
    my_place = lax.dynamic_slice_in_dim(place_all, row_offset, row_count)
    source = hidden_in[0].astype(f32)
    gain_vec = ln_gain.astype(f32)
    shift_vec = ln_bias.astype(f32)
    normed_low = layer_norm(source, gain_vec, shift_vec).astype(bf16)
    pieces = (
        lax.all_gather(w_qkv, "fsdp", axis=0, tiled=True),
        lax.all_gather(w_fc1, "fsdp", axis=0, tiled=True),
    )
    columns = normed_low
    qkv_mm = jnp.dot(columns, pieces[0], preferred_element_type=f32)
    up_mm = jnp.dot(columns, pieces[1], preferred_element_type=f32)
    qkv_pre = (qkv_mm + b_qkv.astype(f32)).reshape(row_count, local_heads, 3, HEAD)
    rotated = jnp.stack(
        [rotate(qkv_pre[:, :, 0], my_place), rotate(qkv_pre[:, :, 1], my_place), qkv_pre[:, :, 2]],
        axis=2,
    )
    qkv_low = rotated.astype(bf16).reshape(row_count, local_heads * 3 * HEAD)
    grouped = lax.all_to_all(qkv_low, "ctx", split_axis=1, concat_axis=0, tiled=True).reshape(
        group_rows, head_share, 3, HEAD
    )
    query_all = grouped[:, :, 0]
    key_all = grouped[:, :, 1]
    value_all = grouped[:, :, 2]

    def block_scores(row_start):
        query_blk = lax.dynamic_slice_in_dim(query_all, row_start, block_rows)
        seg_query = lax.dynamic_slice_in_dim(segment_all, row_start, block_rows)
        pos_query = lax.dynamic_slice_in_dim(packed_all, row_start, block_rows)
        keep_mask = (seg_query[:, None] == segment_all[None, :]) & (
            packed_all[None, :] <= pos_query[:, None]
        )
        scores = (
            jnp.einsum("qhd,khd->hqk", query_blk, key_all, preferred_element_type=f32) * scaling
        )
        return (query_blk, jnp.where(keep_mask[None], scores, MASKED))

    def attend(block_index):
        query_blk, scores = block_scores(block_index * block_rows)
        row_max = jnp.max(scores, axis=-1, keepdims=True)
        raised = jnp.exp(scores - row_max)
        row_sum = jnp.sum(raised, axis=-1, keepdims=True)
        weights = (raised / row_sum).astype(bf16)
        mixed_blk = jnp.einsum(
            "hqk,khd->qhd", weights, value_all, preferred_element_type=f32
        ).astype(bf16)
        return (mixed_blk, (row_max + jnp.log(row_sum))[..., 0])

    block_ids = jnp.arange(block_count, dtype=jnp.int32)
    mixed_blocks, lse_blocks = lax.map(attend, block_ids)
    attn_local = lax.all_to_all(
        mixed_blocks.reshape(group_rows, head_share * HEAD),
        "ctx",
        split_axis=0,
        concat_axis=1,
        tiled=True,
    )
    up_pre = up_mm + b_fc1.astype(f32)
    act_low = gelu_tanh(up_pre).astype(bf16)
    pieces = (
        lax.all_gather(w_dense, "fsdp", axis=0, tiled=True),
        lax.all_gather(w_fc2, "fsdp", axis=0, tiled=True),
    )
    part = lax.dot_general(
        attn_local, pieces[0], by_columns, preferred_element_type=f32
    ) + lax.dot_general(act_low, pieces[1], by_columns, preferred_element_type=f32)
    branch = part
    branch = lax.psum(branch, "tp")
    result = source + branch + b_dense.astype(f32) + b_fc2.astype(f32)
    grad_low = out_grad[0]
    grad_full = grad_low.astype(f32)
    pieces = (
        lax.all_gather(w_dense, "fsdp", axis=0, tiled=True),
        lax.all_gather(w_fc2, "fsdp", axis=0, tiled=True),
    )
    columns = grad_low
    attn_grad = jnp.dot(columns, pieces[0], preferred_element_type=f32)
    act_grad = jnp.dot(columns, pieces[1], preferred_element_type=f32)
    _, gelu_back = jax.vjp(gelu_tanh, up_pre)
    up_grad = gelu_back(act_grad)[0]
    up_grad_low = up_grad.astype(bf16)
    mixed_grad = lax.all_to_all(
        attn_grad.astype(bf16), "ctx", split_axis=1, concat_axis=0, tiled=True
    ).reshape(group_rows, head_share, HEAD)

    def attend_back(carried, inputs):
        key_grad, value_grad = carried
        block_index, lse_blk = inputs
        row_start = block_index * block_rows
        query_blk, scores = block_scores(row_start)
        probs = jnp.exp(scores - lse_blk[:, :, None])
        grad_blk = lax.dynamic_slice_in_dim(mixed_grad, row_start, block_rows)
        prob_grad = jnp.einsum("qhd,khd->hqk", grad_blk, value_all, preferred_element_type=f32)
        inner = jnp.sum(probs * prob_grad, axis=-1, keepdims=True)
        score_grad = (probs * (prob_grad - inner)).astype(bf16)
        query_grad = (
            jnp.einsum("hqk,khd->qhd", score_grad, key_all, preferred_element_type=f32) * scaling
        )
        key_grad = (
            key_grad
            + jnp.einsum("hqk,qhd->khd", score_grad, query_blk, preferred_element_type=f32)
            * scaling
        )
        value_grad = value_grad + jnp.einsum(
            "hqk,qhd->khd", probs.astype(bf16), grad_blk, preferred_element_type=f32
        )
        return ((key_grad, value_grad), query_grad)

    zero_keys = jnp.zeros((group_rows, head_share, HEAD), f32)
    (key_grads, value_grads), query_grads = lax.scan(
        attend_back, (zero_keys, zero_keys), (block_ids, lse_blocks)
    )
    query_grads = query_grads.reshape(group_rows, head_share, HEAD)
    qkv_grad_group = (
        jnp.stack([query_grads, key_grads, value_grads], axis=2)
        .astype(bf16)
        .reshape(group_rows, head_share * 3 * HEAD)
    )
    back_local = (
        lax.all_to_all(qkv_grad_group, "ctx", split_axis=0, concat_axis=1, tiled=True)
        .reshape(row_count, local_heads, 3, HEAD)
        .astype(f32)
    )
    back_place = -my_place
    pre_grad = jnp.stack(
        [
            rotate(back_local[:, :, 0], back_place),
            rotate(back_local[:, :, 1], back_place),
            back_local[:, :, 2],
        ],
        axis=2,
    )
    pre_grad = pre_grad.reshape(row_count, local_heads * 3 * HEAD)
    pre_grad_low = pre_grad.astype(bf16)
    pieces = (
        lax.all_gather(w_qkv, "fsdp", axis=0, tiled=True),
        lax.all_gather(w_fc1, "fsdp", axis=0, tiled=True),
    )
    part = lax.dot_general(
        pre_grad_low, pieces[0], by_columns, preferred_element_type=f32
    ) + lax.dot_general(up_grad_low, pieces[1], by_columns, preferred_element_type=f32)
    normed_grad = part
    normed_grad = lax.psum(normed_grad, "tp")
    _, norm_back = jax.vjp(layer_norm, source, gain_vec, shift_vec)
    source_grad, gain_grad, shift_grad = norm_back(normed_grad)
    input_grad = source_grad + grad_full
    out_bias_grad = jnp.sum(grad_full, axis=0)
    small_sums = lax.psum(
        (gain_grad, shift_grad, jnp.sum(pre_grad, axis=0), out_bias_grad, jnp.sum(up_grad, axis=0)),
        ("fsdp", "ctx"),
    )
    right_in = jnp.concatenate([pre_grad_low, up_grad_low], axis=1)
    right_out = jnp.concatenate([attn_local, act_low], axis=1)
    weight_sums = lax.psum_scatter(
        jnp.concatenate(
            [
                lax.dot_general(normed_low, right_in, by_rows, preferred_element_type=f32),
                lax.dot_general(grad_low, right_out, by_rows, preferred_element_type=f32),
            ],
            axis=1,
        ),
        ("fsdp", "ctx"),
        scatter_dimension=0,
        tiled=True,
    )
    qkv_cols = w_qkv.shape[1]
    up_cols = w_fc1.shape[1]
    dense_cols = w_dense.shape[1]
    qkv_part = weight_sums[:, :qkv_cols]
    up_part = weight_sums[:, qkv_cols : qkv_cols + up_cols]
    dense_part = weight_sums[:, qkv_cols + up_cols : qkv_cols + up_cols + dense_cols]
    down_part = weight_sums[:, qkv_cols + up_cols + dense_cols :]
    return (
        result.astype(bf16)[None],
        input_grad[None],
        small_sums[0],
        small_sums[1],
        qkv_part,
        small_sums[2],
        dense_part,
        small_sums[3],
        up_part,
        small_sums[4],
        down_part,
        small_sums[3],
    )


def solution(mesh):
    in_specs = (
        P("fsdp", "ctx", None),
        P("fsdp", "ctx", None),
        P(),
        P(),
        P("fsdp", "tp"),
        P("tp"),
        P("fsdp", "tp"),
        P(),
        P("fsdp", "tp"),
        P("tp"),
        P("fsdp", "tp"),
        P(),
        P("fsdp", None),
        P("fsdp", None),
    )
    out_specs = (
        P("fsdp", "ctx", None),
        P("fsdp", "ctx", None),
        P(),
        P(),
        P(("fsdp", "ctx"), "tp"),
        P("tp"),
        P(("fsdp", "ctx"), "tp"),
        P(),
        P(("fsdp", "ctx"), "tp"),
        P("tp"),
        P(("fsdp", "ctx"), "tp"),
        P(),
    )
    return jax.shard_map(shards, mesh=mesh, in_specs=in_specs, out_specs=out_specs, check_vma=False)
```

profile of v0, /device:TPU:0, one launch (start us, length us, event | category | flops | bytes accessed | tf_op | source)
XLA Modules:
  0.0 3613.9 jit_solution(11570743387819316277)
XLA Ops:
  12.1 81.1 %all-gather.7.cloned.1.call-done = bf16[2048,1024]{1,0:T(8,128)(2,1)} async-done(((bf16[512,1024]{1,0:T(8,128)(2,1)}), bf16[2048,1024]{1,0:T(8,128)(2,1)}) %all-gather.7.cloned.1.call-update) | async-done | bytes 4194320 | tf_op jit(solution)/shard_map/all_gather | solution.py:143
  93.1 5.2 fusion.77
  103.0 208.4 %all-gather.5.cloned.1.call-done = bf16[2048,3072]{1,0:T(8,128)(2,1)} async-done(((bf16[512,3072]{1,0:T(8,128)(2,1)}), bf16[2048,3072]{1,0:T(8,128)(2,1)}) %all-gather.5.cloned.1.call-update) | async-done | bytes 12582928 | tf_op jit(solution)/shard_map/all_gather | solution.py:89
  311.5 11.5 convolution_add_fusion
  323.0 7.0 copy.81
  348.0 30.7 all-to-all-done
  382.8 6.2 reshape.354
  391.1 71.4 %while.27 = (s32[]{:T(128)}, bf16[4,512,4,64]{1,3,2,0:T(8,128)(2,1)}, f32[4,4,512]{2,1,0:T(4,128)}, s32[4]{0:T(128)S(1)}, s32[2048]{0:T(1024)S(1)}, /*index=5*/s...) while((s32[]{:T(128)}, ...), condition=%wide.region_8.9_spmd, body=%wide.region_5.8_spmd.sunk | while | flops 1127348224 | bytes 57241816 | solution.py:132
  398.0 4.3 fusion.135
  402.4 5.9 fusion.136
  415.9 4.3 fusion.135
  420.2 5.9 fusion.136
  433.7 4.3 fusion.135
  438.1 5.9 fusion.136
  451.6 4.3 fusion.135
  455.9 5.9 fusion.136
  469.0 212.9 %while.28 = (s32[]{:T(128)}, f32[2048,4,64]{0,2,1:T(8,128)}, f32[2048,4,64]{0,2,1:T(8,128)}, bf16[4,512,4,64]{1,3,2,0:T(8,128)(2,1)}, s32[4]{0:T(128)S(1)}, /*in...) while((s32[]{:T(128)}, f32[2048,4,64]{0,2,1:T(8,128)}, ...), condition=%wide.region_12.13_spmd.clone, body=%wide.region_10.12_spmd.clone.sunk | while | flops 2753165312 | bytes 281727680 | solution.py:192
  479.1 12.7 multiply_reduce_fusion.2
  491.8 11.0 multiply_convert_fusion.3
  502.8 6.5 fusion.147
  509.4 8.6 fusion.148
  531.4 12.6 multiply_reduce_fusion.2
  544.0 10.9 multiply_convert_fusion.3
  554.9 7.1 fusion.147
  562.1 8.5 fusion.148
  584.0 12.6 multiply_reduce_fusion.2
  596.6 11.4 multiply_convert_fusion.3
  608.1 8.3 fusion.147
  616.4 8.7 fusion.148
  638.5 12.7 multiply_reduce_fusion.2
  651.2 10.9 multiply_convert_fusion.3
  662.2 7.2 fusion.147
  669.4 8.6 fusion.148
  703.0 6.6 fusion.93
  709.5 26.7 all-to-all-done.3
  746.8 12.3 fusion.94
  759.2 17.1 multiply_convert_fusion.1
  776.3 108.2 %all-gather.11.cloned.1.call-done = bf16[2048,4096]{1,0:T(8,128)(2,1)} async-done(((bf16[512,4096]{1,0:T(8,128)(2,1)}), bf16[2048,4096]{1,0:T(8,128)(2,1)}) %all-gather.11.cloned.1.call-update) | async-done | bytes 16777232 | tf_op jit(solution)/shard_map/all_gather | solution.py:144
  884.5 20.0 fusion.92
  904.5 17.1 convolution_add_fusion.2
  921.6 14.5 convolution_add_fusion.1
  936.2 31.6 fusion.43
  967.8 22.2 convolution_bitcast_fusion
  990.0 65.5 %pad_maximum_fusion = f32[2048,12288]{1,0:T(8,128)} fusion(f32[2048,5120]{1,0:T(8,128)} %convolution_bitcast_fusion, f32[2048,7168]{1,0:T(8,128)} %fusion.43), kind=kLoop, calls=%fused_computation.44 | loop fusion | flops 25165824 | bytes 201326592 | tf_op jit(solution)/shard_map/concatenate | solution.py:237
  1067.9 5.0 convert_reduce_fusion
  1072.9 79.4 %all-reduce.1 = (f32[2048]{0:T(1024)}, f32[2048]{0:T(1024)}, f32[3072]{0:T(1024)}, f32[2048]{0:T(1024)S(1)}, f32[4096]{0:T(1024)}) all-reduce(f32[2048]{0:T(1024)S(1)} %get-tuple-element.194, f32[2048]{0:T(1024)S(1)} %get-tuple-element.196, f32[3072]{0:T(1024)S(1)} %reduce_sum.152, ...), channel_id=1, replica_groups=mesh['fsdp'=4,'ctx'=4,'tp'=2] {'fsdp','ctx'}, use_global_device_ids=true, to_apply=%region_17.18 | all-reduce | flops 13312 | bytes 106496 | tf_op jit(solution)/shard_map/psum | solution.py:230
  1152.3 2443.7 %all-reduce.6.cloned.1.call-done = f32[2048,12288]{1,0:T(8,128)} async-done(((f32[2048,12288]{1,0:T(8,128)}), f32[2048,12288]{1,0:T(8,128)}) %all-reduce.6.cloned.1.call-update) | async-done | bytes 100663312
  3600.8 5.4 fusion.91
  (337 shorter events, 166.7 us)
Async XLA Ops:
  7.2 85.9 %all-gather.7.cloned.1.call-start = ((), (), s32[]{:S(2)}) async-start(), calls=%async_computation.5 | async-start | bytes 5242880 | tf_op jit(solution)/shard_map/all_gather | solution.py:143
  8.0 303.5 %all-gather.5.cloned.1.call-start = ((), (), s32[]{:S(2)}) async-start(), calls=%async_computation.4 | async-start | bytes 15728640 | tf_op jit(solution)/shard_map/all_gather | solution.py:89
  8.7 750.4 %all-gather.9.cloned.1.call-start = ((), (), s32[]{:S(2)}) async-start(), calls=%async_computation.6 | async-start | bytes 20971520 | tf_op jit(solution)/shard_map/all_gather | solution.py:90
  9.5 302.0 %copy-start.35 = (f32[2048]{0:T(1024)}, f32[2048]{0:T(1024)S(1)}, u32[]{:S(2)}) copy-start(f32[2048]{0:T(1024)S(1)} %convert_element_type.99) | copy-start | bytes 24580
  9.5 301.9 %copy-start.25 = (f32[2048]{0:T(1024)}, f32[2048]{0:T(1024)S(1)}, u32[]{:S(2)}) copy-start(f32[2048]{0:T(1024)S(1)} %convert_element_type.98) | copy-start | bytes 24580
  10.4 301.1 %copy-start.31 = (f32[512]{0:T(512)}, f32[512]{0:T(512)S(1)}, u32[]{:S(2)}) copy-start(f32[512]{0:T(512)S(1)} %broadcast_multiply_fusion) | copy-start | bytes 6148
  11.1 87.2 %copy-start.39 = (f32[512]{0:T(512)}, f32[512]{0:T(512)S(1)}, u32[]{:S(2)}) copy-start(f32[512]{0:T(512)S(1)} %fusion.63) | copy-start | bytes 6148
  11.1 300.4 %copy-start.33 = (f32[512]{0:T(512)}, f32[512]{0:T(512)S(1)}, u32[]{:S(2)}) copy-start(f32[512]{0:T(512)S(1)} %fusion.80) | copy-start | bytes 6148
  99.3 238.0 %all-to-all-start.2 = ((bf16[512,4,256]{2,0,1:T(8,128)(2,1)}), bf16[512,4,256]{2,0,1:T(8,128)(2,1)S(1)}, u32[]{:S(2)}, u32[]{:S(2)}) async-start(bf16[512,4,256]{2,0,1:T(8,128)(2,1)} %bitcast.230), calls=%async_computation.2 | async-start | bytes 2097152 | tf_op jit(solution)/shard_map/all_to_all | solution.py:164
  338.4 40.4 %all-to-all-start = ((bf16[512,4,768]{0,2,1:T(8,128)(2,1)}), bf16[512,4,768]{0,2,1:T(8,128)(2,1)S(1)}, u32[]{:S(2)}, u32[]{:S(2)}) async-start(bf16[512,4,768]{0,2,1:T(8,128)(2,1)} %bitcast.16), calls=%async_computation | async-start | bytes 6291456 | tf_op jit(solution)/shard_map/all_to_all | solution.py:101
  342.1 542.4 %all-gather.11.cloned.1.call-start = ((), (), s32[]{:S(2)}) async-start(), calls=%async_computation.7 | async-start | bytes 20971520 | tf_op jit(solution)/shard_map/all_gather | solution.py:144
  464.7 231.7 %all-to-all-start.1 = ((bf16[4,512,256]{2,1,0:T(8,128)(2,1)}), bf16[4,512,256]{2,1,0:T(8,128)(2,1)}, u32[]{:S(2)}, u32[]{:S(2)}) async-start(bf16[4,512,256]{2,1,0:T(8,128)(2,1)} %copy.85), calls=%async_computation.1 | async-start | bytes 2097152 | tf_op jit(solution)/shard_map/all_to_all | solution.py:133
  474.2 17.7 copy-start
  502.8 6.5 copy-start.1
  502.8 6.5 copy-start.19
  502.8 15.1 slice-start
  509.3 8.6 slice-start.1
  509.4 8.6 copy-start.27
  526.5 17.5 copy-start
  554.9 7.1 copy-start.1
  554.9 7.1 copy-start.19
  554.9 15.6 slice-start
  562.1 8.5 slice-start.1
  562.1 8.5 copy-start.27
  579.1 17.5 copy-start
  608.1 8.3 copy-start.1
  608.1 8.3 copy-start.19
  608.1 17.0 slice-start
  616.4 8.7 slice-start.1
  616.4 8.7 copy-start.27
  633.6 17.6 copy-start
  662.2 7.2 copy-start.1
  662.2 7.2 copy-start.19
  662.2 15.8 slice-start
  669.4 8.6 slice-start.1
  669.4 8.6 copy-start.27
  681.9 5.7 copy-start.2
  696.4 39.8 %all-to-all-start.3 = ((bf16[4,512,768]{1,2,0:T(8,128)(2,1)}), bf16[4,512,768]{1,2,0:T(8,128)(2,1)S(1)}, u32[]{:S(2)}, u32[]{:S(2)}) async-start(bf16[4,512,768]{1,2,0:T(8,128)(2,1)} %copy.91), calls=%async_computation.3 | async-start | bytes 6291456 | tf_op jit(solution)/shard_map/all_to_all | solution.py:202
  700.6 361.2 %all-reduce.8.cloned.1.call-start = ((), (), s32[]{:S(2)}) async-start(), calls=%async_computation.9 | async-start | bytes 16777216 | tf_op jit(solution)/shard_map/psum | solution.py:150
  746.8 12.3 copy-start.4
  746.8 12.3 copy-start.26
  746.8 12.3 copy-start.32
  746.8 12.3 copy-start.34
  746.8 12.3 copy-start.36
  904.5 17.1 copy-start.14
  936.1 31.7 copy-start.30
  936.1 2659.9 %all-reduce.6.cloned.1.call-start = ((), (), s32[]{:S(2)}) async-start(), calls=%async_computation.8 | async-start | bytes 201326592
  1152.3 2453.9 %copy-start.43 = (f32[2048]{0:T(1024)}, f32[2048]{0:T(1024)S(1)}, u32[]{:S(2)}) copy-start(f32[2048]{0:T(1024)S(1)} %get-tuple-element.559) | copy-start | bytes 24580
  (60 other events, 156.3 us)
Sparse Core Ops, SparseCore 0:
  9.6 83.4 all-gather.6
  94.7 216.7 all-gather.4
  313.1 284.9 all-gather.8
  599.5 284.9 all-gather.10
  936.3 37.0 all-reduce.7
  1055.7 2540.2 all-reduce.5
where the time goes:
time: 3620 us; the launch traced here: 3610 us
  waiting for transfers between devices  2900 us (80%)
  matrix products  333 us (9%)
  other arithmetic  173 us (5%)
  local copies, waits for them, and re-layouts  88.5 us (2%)
  blocking collectives  79.4 us (2%)
    unnamed x7, waiting for transfers between devices  2450 us
    all_gather x1, waiting for transfers between devices, shards(): lax.all_gather(w_qkv, 'fsdp', axis=0, tiled=True)  208 us
    all_gather x1, waiting for transfers between devices, shards(): lax.all_gather(w_fc2, 'fsdp', axis=0, tiled=True)  108 us
    all_gather x1, waiting for transfers between devices, shards(): lax.all_gather(w_dense, 'fsdp', axis=0, tiled=True)  81.1 us
    psum x1, blocking collectives, shards(): lax.psum((gain_grad, shift_grad, jnp.sum(pre_grad, axis=0), out_bias_grad...  79.4 us
  transfers between devices with their start and end apart: 10, of which 6 were waited for; matrix products, arithmetic and copies ran while one was open for 14% of the time, Pallas kernels for 0%

commit v1 on v0

v1 whole, which is shorter than its diff:
```python
import math

import jax
import jax.numpy as jnp
from jax import lax
from jax.sharding import PartitionSpec as P

HEAD = 64
ROT = 32
MASKED = -1e30
EPSILON = 1e-05
f32 = jnp.float32
bf16 = jnp.bfloat16


def positions(packed, lengths):
    seq_ends = jnp.cumsum(lengths)
    starts = seq_ends - lengths
    segment = jnp.sum((packed[:, None] >= seq_ends[None, :]).astype(jnp.int32), axis=1)
    owner_mask = segment[:, None] == jnp.arange(lengths.shape[0], dtype=jnp.int32)[None, :]
    return (segment, packed - jnp.sum(jnp.where(owner_mask, starts[None, :], 0), axis=1))


def gelu_tanh(values):
    return jax.nn.gelu(values, approximate=True)


def swap(x, axis, bit):
    size = lax.axis_size(axis)
    return lax.ppermute(x, axis, [(i, i ^ bit) for i in range(size)])


def line_gather(own):
    n = lax.axis_size("fsdp")
    z = lax.axis_index("fsdp")
    up = down = own
    ups, downs = [None], [None]
    for s in range(1, n):
        up = lax.ppermute(up, "fsdp", [(i, i + 1) for i in range(s - 1, n - 1)])
        down = lax.ppermute(down, "fsdp", [(i, i - 1) for i in range(1, n - s + 1)])
        ups.append(up)
        downs.append(down)
    return [own] + [jnp.where(s <= z, ups[s], downs[n - s]) for s in range(1, n)]


def line_scatter(parts):
    n = lax.axis_size("fsdp")
    up = down = None
    for s in range(1, n):
        send_up, send_down = parts[s], parts[n - s]
        if s > 1:
            send_up, send_down = add(send_up, up), add(send_down, down)
        up = lax.ppermute(send_up, "fsdp", [(i, i + 1) for i in range(0, min(s, n - 1))])
        down = lax.ppermute(send_down, "fsdp", [(i, i - 1) for i in range(max(n - s, 1), n)])
    return parts[0].astype(f32) + up.astype(f32) + down.astype(f32)


def add(a, b):
    return (a.astype(f32) + b.astype(f32)).astype(bf16)


def gather_rows(rows):
    m = lax.axis_size("ctx")
    half = rows.shape[0] // 2
    mine = rows[:half]
    if m == 4:
        quarter = half // 2
        first = swap(mine, "ctx", 1)
        second = swap(mine, "ctx", 2)
        third_a = swap(first[:quarter], "ctx", 2)
        third_b = swap(second[quarter:], "ctx", 1)
        got = [[first], [second], [third_a, third_b]]
    else:
        slots = [mine]
        bit = 1
        while bit < m:
            slots = slots + [swap(piece, "ctx", bit) for piece in slots]
            bit *= 2
        got = [[piece] for piece in slots[1:]]
    blocks = [rows]
    for pieces in got:
        blocks = blocks + pieces + [swap(piece, "tp", 1) for piece in pieces]
    return jnp.concatenate(blocks, axis=0)


def scatter_rows(part):
    m = lax.axis_size("ctx")
    half = part.shape[0] // (2 * m)
    blocks = part.reshape(m, 2, half, part.shape[1])
    slots = add(blocks[:, 0], swap(blocks[:, 1], "tp", 1))
    if m == 4:
        quarter = half // 2
        to_second = swap(slots[3, :quarter], "ctx", 2)
        to_first = swap(slots[3, quarter:], "ctx", 1)
        first = jnp.concatenate([add(slots[1, :quarter], to_second), slots[1, quarter:]], axis=0)
        second = jnp.concatenate([slots[2, :quarter], add(slots[2, quarter:], to_first)], axis=0)
        return (
            slots[0].astype(f32)
            + swap(first, "ctx", 1).astype(f32)
            + swap(second, "ctx", 2).astype(f32)
        )
    bit = m // 2
    while bit >= 1:
        slots = add(slots[:bit], swap(slots[bit : 2 * bit], "ctx", bit))
        bit //= 2
    return slots[0].astype(f32)


def spread_columns(block):
    m = lax.axis_size("ctx")
    c = lax.axis_index("ctx")
    rows, cols = block.shape[0] // m, block.shape[1]
    pieces = []
    for j in range(m):
        piece = lax.dynamic_slice_in_dim(block, (c ^ j) * rows, rows, axis=0)
        pieces.append(piece if j == 0 else swap(piece, "ctx", j))
    stacked = jnp.stack(pieces)
    ordered = [
        lax.dynamic_index_in_dim(stacked, c ^ k, axis=0, keepdims=False) for k in range(m)
    ]
    return jnp.concatenate(ordered, axis=1).astype(f32)


def column_order(heads):
    order = []
    for part in range(2):
        for start, width in ((0, ROT // 2), (ROT // 2, ROT // 2), (ROT, HEAD - ROT)):
            for head in range(heads):
                base = (head * 3 + part) * HEAD + start
                order += list(range(base, base + width))
    for head in range(heads):
        base = (head * 3 + 2) * HEAD
        order += list(range(base, base + HEAD))
    return order


def shards(
    hidden_in,
    out_grad,
    ln_gain,
    ln_bias,
    w_qkv,
    b_qkv,
    w_dense,
    b_dense,
    w_fc1,
    b_fc1,
    w_fc2,
    b_fc2,
    lengths,
    assignment,
):
    n = lax.axis_size("fsdp")
    m = lax.axis_size("ctx")
    z = lax.axis_index("fsdp")
    c = lax.axis_index("ctx")
    t = lax.axis_index("tp")
    rows, width = hidden_in.shape[1], hidden_in.shape[2]
    half = rows // 2
    group_rows = rows * m
    feat = width // n
    heads = w_qkv.shape[1] // (3 * HEAD) // m
    wide = heads * HEAD
    by_columns = (((1,), (1,)), ((), ()))
    by_rows = (((0,), (0,)), ((), ()))
    scaling = 1.0 / math.sqrt(HEAD)

    def turn(x):
        return jnp.concatenate(
            [lax.dynamic_slice_in_dim(x, lax.rem(z - s + n, n) * feat, feat, axis=1) for s in range(n)],
            axis=1,
        )

    def halves(x):
        return jnp.where(t == 0, x, jnp.concatenate([x[half:], x[:half]], axis=0))

    def mine(weight):
        share = weight.shape[-1] // m
        return lax.dynamic_slice_in_dim(weight, c * share, share, axis=weight.ndim - 1)

    order = jnp.array(column_order(heads), jnp.int32)
    place_of = (jnp.arange(3 * wide, dtype=jnp.int32)[:, None] == order[None, :]).astype(bf16)
    qkv_own = jnp.dot(mine(w_qkv), place_of, preferred_element_type=f32).astype(bf16)
    qkv_bias = jnp.dot(mine(b_qkv)[None], place_of, preferred_element_type=f32)
    up_bias = mine(b_fc1).astype(f32)

    up_slots = line_gather(mine(w_fc1))
    qkv_slots = line_gather(qkv_own)
    dense_slots = line_gather(mine(w_dense))
    down_slots = line_gather(mine(w_fc2))
    w_up = jnp.concatenate(up_slots, axis=0)
    w_in = jnp.concatenate(qkv_slots, axis=0)
    w_out = jnp.concatenate(dense_slots, axis=0)
    w_down = jnp.concatenate(down_slots, axis=0)

    source = halves(hidden_in[0]).astype(f32)
    gain_vec = ln_gain.astype(f32)
    shift_vec = ln_bias.astype(f32)
    centred = source - jnp.mean(source, axis=-1, keepdims=True)
    rstd = lax.rsqrt(jnp.mean(centred * centred, axis=-1, keepdims=True) + EPSILON)
    xhat = centred * rstd
    normed = gather_rows(turn((xhat * gain_vec + shift_vec).astype(bf16)))
    grad_own = halves(out_grad[0])
    grads = gather_rows(turn(grad_own))

    block_of = [((c ^ j) * 2 + (t ^ h)) * half for j in range(m) for h in range(2)]
    packed = jnp.concatenate(
        [lax.dynamic_slice_in_dim(assignment[0], at, half) for at in block_of]
    )
    segment, place = positions(packed, lengths[0])
    frequency = jnp.power(
        10000.0, -(jnp.arange(ROT // 2, dtype=f32) * 2.0 / ROT)
    )
    angles = place.astype(f32)[:, None] * jnp.tile(frequency, 2 * heads)[None, :]
    cosine = jnp.cos(angles)
    sine = jnp.sin(angles) * jnp.where(jnp.arange(ROT * heads) < ROT // 2 * heads, -1.0, 1.0)[None, :]
    split = ROT // 2 * heads

    def rotate(x, sign):
        front = x[:, : 2 * split]
        partner = jnp.concatenate([front[:, split:], front[:, :split]], axis=1)
        return jnp.concatenate([front * cosine + sign * sine * partner, x[:, 2 * split :]], axis=1)

    up = jnp.dot(normed, w_up, preferred_element_type=f32) + up_bias
    act = gelu_tanh(up).astype(bf16)
    qkv = jnp.dot(normed, w_in, preferred_element_type=f32) + qkv_bias
    query = rotate(qkv[:, :wide], 1.0).astype(bf16)
    key = rotate(qkv[:, wide : 2 * wide], 1.0).astype(bf16)
    value = qkv[:, 2 * wide :].astype(bf16)
    lane = jnp.arange(wide)
    lane_head = jnp.where(lane < 2 * split, (lane % split) // (ROT // 2), (lane - 2 * split) // (HEAD - ROT))
    head_qk = (lane_head[None] == jnp.arange(heads)[:, None]).astype(bf16)
    head_v = ((lane // HEAD)[None] == jnp.arange(heads)[:, None]).astype(bf16)
    block_rows = min(512, group_rows)
    block_ids = jnp.arange(group_rows // block_rows, dtype=jnp.int32)

    def block_scores(start):
        q = lax.dynamic_slice_in_dim(query, start, block_rows)
        seg = lax.dynamic_slice_in_dim(segment, start, block_rows)
        pos = lax.dynamic_slice_in_dim(packed, start, block_rows)
        keep = (seg[:, None] == segment[None, :]) & (packed[None, :] <= pos[:, None])
        scores = jnp.einsum("hqe,ke->hqk", q[None] * head_qk[:, None, :], key, preferred_element_type=f32)
        return q, jnp.where(keep[None], scores * scaling, MASKED)

    def attend(index):
        _, scores = block_scores(index * block_rows)
        top = jnp.max(scores, axis=-1, keepdims=True)
        raised = jnp.exp(scores - top)
        total = jnp.sum(raised, axis=-1, keepdims=True)
        weights = (raised / total).astype(bf16)
        mixed = jnp.einsum("hqk,hke->qe", weights, value[None] * head_v[:, None, :], preferred_element_type=f32)
        return mixed.astype(bf16), (top + jnp.log(total))[..., 0]

    mixed, lse = lax.map(attend, block_ids)
    mixed = mixed.reshape(group_rows, wide)

    branch = lax.dot_general(mixed, w_out, by_columns, preferred_element_type=f32)
    branch = branch + lax.dot_general(act, w_down, by_columns, preferred_element_type=f32)
    branch = turn(scatter_rows(branch.astype(bf16)))
    biases = b_dense.astype(f32) + b_fc2.astype(f32)
    result = (source[:half] + branch + biases).astype(bf16)
    result_other = swap(result, "tp", 1)
    result = halves(jnp.concatenate([result, result_other], axis=0))

    mixed_grad = jnp.dot(grads, w_out, preferred_element_type=f32).astype(bf16)
    act_grad = jnp.dot(grads, w_down, preferred_element_type=f32)
    up_grad = jax.vjp(gelu_tanh, up)[1](act_grad)[0]
    up_grad_low = up_grad.astype(bf16)

    def attend_back(carried, inputs):
        key_grad, value_grad = carried
        index, lse_blk = inputs
        start = index * block_rows
        q, scores = block_scores(start)
        probs = jnp.exp(scores - lse_blk[:, :, None])
        grad = lax.dynamic_slice_in_dim(mixed_grad, start, block_rows)
        grad_h = grad[None] * head_v[:, None, :]
        prob_grad = jnp.einsum("hqe,ke->hqk", grad_h, value, preferred_element_type=f32)
        inner = jnp.sum(probs * prob_grad, axis=-1, keepdims=True)
        score_grad = (probs * (prob_grad - inner)).astype(bf16)
        query_grad = scaling * jnp.einsum(
            "hqk,hke->qe", score_grad, key[None] * head_qk[:, None, :], preferred_element_type=f32
        )
        key_grad = key_grad + scaling * jnp.einsum(
            "hqk,hqe->ke", score_grad, q[None] * head_qk[:, None, :], preferred_element_type=f32
        )
        value_grad = value_grad + jnp.einsum(
            "hqk,hqe->ke", probs.astype(bf16), grad_h, preferred_element_type=f32
        )
        return (key_grad, value_grad), query_grad

    zeros = jnp.zeros((group_rows, wide), f32)
    (key_grad, value_grad), query_grad = lax.scan(attend_back, (zeros, zeros), (block_ids, lse))
    query_grad = query_grad.reshape(group_rows, wide)
    qkv_grad = jnp.concatenate(
        [rotate(query_grad, -1.0), rotate(key_grad, -1.0), value_grad], axis=1
    )
    qkv_grad_low = qkv_grad.astype(bf16)

    normed_grad = lax.dot_general(qkv_grad_low, w_in, by_columns, preferred_element_type=f32)
    normed_grad = normed_grad + lax.dot_general(up_grad_low, w_up, by_columns, preferred_element_type=f32)
    normed_grad = turn(scatter_rows(normed_grad.astype(bf16)))
    d = normed_grad * gain_vec
    xhat_half = xhat[:half]
    input_grad = (
        rstd[:half]
        * (
            d
            - jnp.mean(d, axis=-1, keepdims=True)
            - xhat_half * jnp.mean(d * xhat_half, axis=-1, keepdims=True)
        )
        + grad_own[:half].astype(f32)
    )
    input_grad = halves(jnp.concatenate([input_grad, swap(input_grad, "tp", 1)], axis=0))

    def summed(left, right):
        full = lax.dot_general(left, right, by_rows, preferred_element_type=f32).astype(bf16)
        return line_scatter([full[s * feat : (s + 1) * feat] for s in range(n)]).astype(bf16)

    down_part = spread_columns(summed(grads, act))
    dense_part = spread_columns(summed(grads, mixed))
    qkv_sum = summed(normed, qkv_grad_low)
    qkv_sum = lax.dot_general(qkv_sum, place_of, by_columns, preferred_element_type=f32).astype(bf16)
    qkv_part = spread_columns(qkv_sum)
    up_part = spread_columns(summed(normed, up_grad_low))

    def placed(vector):
        full = jnp.zeros((vector.shape[0] * m,), f32)
        return lax.dynamic_update_slice_in_dim(full, vector, c * vector.shape[0], axis=0)

    qkv_bias_grad = lax.dot_general(
        jnp.sum(qkv_grad, axis=0)[None], place_of.astype(f32), by_columns,
        precision=lax.Precision.HIGHEST, preferred_element_type=f32,
    )[0]
    qkv_bias_grad, up_bias_grad, out_bias_grad = lax.psum(
        (placed(qkv_bias_grad), placed(jnp.sum(up_grad, axis=0)), jnp.sum(grad_own.astype(f32), axis=0)),
        ("fsdp", "ctx"),
    )
    gain_grad, shift_grad = lax.psum(
        (jnp.sum(normed_grad * xhat_half, axis=0), jnp.sum(normed_grad, axis=0)),
        ("fsdp", "ctx", "tp"),
    )
    return (
        result[None],
        input_grad[None],
        gain_grad,
        shift_grad,
        qkv_part,
        qkv_bias_grad,
        dense_part,
        out_bias_grad,
        up_part,
        up_bias_grad,
        down_part,
        out_bias_grad,
    )


def solution(mesh):
    in_specs = (
        P("fsdp", "ctx", None),
        P("fsdp", "ctx", None),
        P(),
        P(),
        P("fsdp", "tp"),
        P("tp"),
        P("fsdp", "tp"),
        P(),
        P("fsdp", "tp"),
        P("tp"),
        P("fsdp", "tp"),
        P(),
        P("fsdp", None),
        P("fsdp", None),
    )
    out_specs = (
        P("fsdp", "ctx", None),
        P("fsdp", "ctx", None),
        P(),
        P(),
        P(("fsdp", "ctx"), "tp"),
        P("tp"),
        P(("fsdp", "ctx"), "tp"),
        P(),
        P(("fsdp", "ctx"), "tp"),
        P("tp"),
        P(("fsdp", "ctx"), "tp"),
        P(),
    )
    return jax.shard_map(shards, mesh=mesh, in_specs=in_specs, out_specs=out_specs, check_vma=False)
```

time: 3620 us -> 1170 us (0.32)
  waiting for transfers between devices: 2900 us -> 194 us
  starting transfers between devices: 16.2 us -> 163 us
  blocking collectives: 79.4 us -> 130 us
    unnamed x7 -> x0, waiting for transfers between devices: 2450 us -> none
    all_gather x4 -> x0, waiting for transfers between devices: 398 us -> none  [the longest x1 208 us: shards(): lax.all_gather(w_qkv, 'fsdp', axis=0, tiled=True)]
    ppermute x0 -> x88, waiting for transfers between devices: none -> 194 us  [the longest x40 76.7 us: swap(): return lax.ppermute(x, axis, [(i, i ^ bit) for i in range(size)])]
    ppermute x0 -> x88, starting transfers between devices: none -> 163 us  [the longest x12 82.7 us: line_scatter(): lax.ppermute(send_up, 'fsdp', [(i, i + 1) for i in range(0, min(s, n - 1))])]
    all_to_all x4 -> x0, waiting for transfers between devices: 57.4 us -> none  [the longest x1 30.7 us: shards(): lax.all_to_all(qkv_low, 'ctx', split_axis=1, concat_axis=0, tiled=True)]
    concatenate x1 -> x8, other arithmetic: 65.5 us -> 9.14 us  [the longest x2 5.56 us: turn(): jnp.concatenate([lax.dynamic_slice_in_dim(x, lax.rem(z - s + n, n) * feat...]
    psum x1 -> x2, blocking collectives: 79.4 us -> 130 us  [the longest x1 91.9 us: shards(): lax.psum((placed(qkv_bias_grad), placed(jnp.sum(up_grad, axis=0)), jnp.su...]
    convert_element_type x7 -> x31, other arithmetic: 1.36 us -> 41.8 us  [the longest x12 26.2 us: add(): return (a.astype(f32) + b.astype(f32)).astype(bf16)]
  transfers between devices with their start and end apart: 10 -> 88, of which waited for: 6 -> 32; matrix products, arithmetic and copies ran while one was open for 14% -> 54% of each run, Pallas kernels for 0% -> 0%
where the time goes in v1:
time: 1170 us; the launch traced here: 1160 us
  matrix products  364 us (31%)
  waiting for transfers between devices  194 us (17%)
  other arithmetic  176 us (15%)
  starting transfers between devices  163 us (14%)
  blocking collectives  130 us (11%)
  local copies, waits for them, and re-layouts  123 us (11%)
    psum x1, blocking collectives, shards(): lax.psum((placed(qkv_bias_grad), placed(jnp.sum(up_grad, axis=0)), jnp.su...  91.9 us
    ppermute x12, starting transfers between devices, line_scatter(): lax.ppermute(send_up, 'fsdp', [(i, i + 1) for i in range(0, min(s, n - 1))])  82.7 us
    ppermute x40, waiting for transfers between devices, swap(): return lax.ppermute(x, axis, [(i, i ^ bit) for i in range(size)])  76.7 us
    ppermute x12, waiting for transfers between devices, line_gather(): down = lax.ppermute(down, 'fsdp', [(i, i - 1) for i in range(1, n - s + 1)])  63.3 us
    dot_general x4, matrix products, attend_back(): jnp.einsum('hqe,ke->hqk', grad_h, value, preferred_element_type=f32)  48.3 us
    convert_element_type x4, other arithmetic, attend_back(): score_grad = (probs * (prob_grad - inner)).astype(bf16)  48.3 us
    dot_general x8, matrix products, block_scores(): jnp.einsum('hqe,ke->hqk', q[None] * head_qk[:, None, :], key, preferred_e...  46.4 us
    dot_general x4, matrix products, summed(): lax.dot_general(left, right, by_rows, preferred_element_type=f32)  44.2 us
  transfers between devices with their start and end apart: 88, of which 32 were waited for; matrix products, arithmetic and copies ran while one was open for 54% of the time, Pallas kernels for 0%

profile of v1, /device:TPU:0, one launch (start us, length us, event | category | flops | bytes accessed | tf_op | source)
XLA Modules:
  0.0 1159.4 jit_solution(13661583166820884172)
XLA Ops:
  46.1 9.0 collective-permute-done.16
  100.3 8.6 collective-permute-done.21
  112.9 9.2 collective-permute-done.10
  125.6 8.1 collective-permute-done.42
  154.0 11.7 %collective-permute-done.26 = bf16[512,1024]{1,0:T(8,128)(2,1)S(1)} collective-permute-done((bf16[512,1024]{1,0:T(8,128)(2,1)S(1)}, bf16[512,1024]{1,0:T(8,128)(2,1)S(1)}, u32[]{:S(2)}, u32[]{:S(2)}) %collective-permute-start.26) | collective-permute-done | bytes 1048608 | tf_op jit(solution)/shard_map/ppermute | solution.py:39
  199.2 23.1 %collective-permute-done.11 = bf16[512,768]{1,0:T(8,128)(2,1)S(1)} collective-permute-done((bf16[512,768]{1,0:T(8,128)(2,1)S(1)}, bf16[512,768]{1,0:T(8,128)(2,1)S(1)}, u32[]{:S(2)}, u32[]{:S(2)}) %collective-permute-start.11) | collective-permute-done | bytes 786464 | tf_op jit(solution)/shard_map/ppermute | solution.py:40
  222.4 12.8 %fusion.171 = (bf16[2048,768]{0,1:T(8,128)(2,1)}, f32[2048,768]{0,1:T(8,128)S(1)}) fusion(f32[768]{0:T(1024)S(1)} %fusion.120, bf16[2048,2048]{1,0:T(8,128)(2,1)} %constant_dynamic-update-slice_fusion.1, bf16[512,768]{1,0:T(8,128)(2,1)S(1)} %broadcast_select_fusion.6, bf16[512,768]{1,0:T(8,128)(2,1)S(1)} %broadcast_select_fusion.7, ...), kind=kOutput, calls=%fused_computation.392 | convolution fusion | flops 6458179584 | bytes 20974592 | tf_op jit(solution)/shard_map/dot_general | solution.py:226
  252.5 67.4 %while.29 = (s32[]{:T(128)}, bf16[4,512,256]{2,1,0:T(8,128)(2,1)}, f32[4,4,512]{2,1,0:T(4,128)S(1)}, s32[4]{0:T(128)S(1)}, s32[2048]{0:T(1024)S(1)}, /*index=5*/...) while((s32[]{:T(128)}, bf16[4,512,256]{2,1,0:T(8,128)(2,1)}, ...), condition=%wide.region_8.9_spmd.clone, body=%wide.region_5.8_spmd.clone.sunk | while | flops 4351199232 | bytes 61971188 | solution.py:254
  319.9 242.1 %while.30 = (s32[]{:T(128)}, f32[2048,256]{1,0:T(8,128)}, f32[2048,256]{1,0:T(8,128)}, f32[4,512,256]{2,1,0:T(8,128)}, s32[4]{0:T(128)S(1)}, /*index=5*/s32[2048...) while((s32[]{:T(128)}, f32[2048,256]{1,0:T(8,128)}, ...), condition=%wide.region_11.12_spmd.clone.clone, body=%wide.region_9.11_spmd.clone.clone.sunk | while | flops 10810427392 | bytes 182031152 | solution.py:293
  323.4 8.2 fusion.221
  331.7 12.1 %multiply_reduce_fusion.6 = (f32[4,512]{1,0:T(4,128)S(1)}, f32[4,512,2048]{2,1,0:T(8,128)}) fusion(f32[4,512,2048]{2,1,0:T(8,128)} %fusion.221, f32[4,512]{1,0:T(4,128)S(1)} %dynamic-slice_bitcast_fusion.10, pred[512,2048]{1,0:T(8,128)(4,1)S(1)} %compare_and_fusion.5, bf16[2048,256]{1,0:T(8,128)(2,1)S(1)} %copy-done.4, ...), kind=kOutput, calls=%fused_computation.32.clone.1 | convolution fusion | flops 2168977408 | bytes 35932160 | tf_op jit(solution)/shard_map/while/body/eval_jaxpr/hqe,ke->hqk/dot_general | solution.py:278
  343.8 12.1 %multiply_convert_fusion.5 = bf16[4,512,2048]{2,1,0:T(8,128)(2,1)S(1)} fusion(f32[4,512,2048]{2,1,0:T(8,128)} %get-tuple-element.706, f32[4,512,2048]{2,1,0:T(8,128)} %fusion.221, f32[4,512]{1,0:T(4,128)S(1)} %get-tuple-element.707, f32[4,512]{1,0:T(4,128)S(1)} %dynamic-slice_bitcast_fusion.10, pred[512,2048]{1,0:T(8,128)(4,1)S(1)} %compare_and_fusion.5), kind=kLoop, calls=%fused_computation.31.clone.1 | loop fusion | flops 25165824 | bytes 43008000 | tf_op jit(solution)/shard_map/while/body/eval_jaxpr/convert_element_type | solution.py:280
  369.7 9.8 fusion.223
  383.0 8.2 fusion.221
  391.2 12.1 %multiply_reduce_fusion.6 = (f32[4,512]{1,0:T(4,128)S(1)}, f32[4,512,2048]{2,1,0:T(8,128)}) fusion(f32[4,512,2048]{2,1,0:T(8,128)} %fusion.221, f32[4,512]{1,0:T(4,128)S(1)} %dynamic-slice_bitcast_fusion.10, pred[512,2048]{1,0:T(8,128)(4,1)S(1)} %compare_and_fusion.5, bf16[2048,256]{1,0:T(8,128)(2,1)S(1)} %copy-done.4, ...), kind=kOutput, calls=%fused_computation.32.clone.1 | convolution fusion | flops 2168977408 | bytes 35932160 | tf_op jit(solution)/shard_map/while/body/eval_jaxpr/hqe,ke->hqk/dot_general | solution.py:278
  403.3 12.1 %multiply_convert_fusion.5 = bf16[4,512,2048]{2,1,0:T(8,128)(2,1)S(1)} fusion(f32[4,512,2048]{2,1,0:T(8,128)} %get-tuple-element.706, f32[4,512,2048]{2,1,0:T(8,128)} %fusion.221, f32[4,512]{1,0:T(4,128)S(1)} %get-tuple-element.707, f32[4,512]{1,0:T(4,128)S(1)} %dynamic-slice_bitcast_fusion.10, pred[512,2048]{1,0:T(8,128)(4,1)S(1)} %compare_and_fusion.5), kind=kLoop, calls=%fused_computation.31.clone.1 | loop fusion | flops 25165824 | bytes 43008000 | tf_op jit(solution)/shard_map/while/body/eval_jaxpr/convert_element_type | solution.py:280
  421.9 8.0 fusion.222
  429.9 10.4 fusion.223
  443.7 8.2 fusion.221
  451.9 12.1 %multiply_reduce_fusion.6 = (f32[4,512]{1,0:T(4,128)S(1)}, f32[4,512,2048]{2,1,0:T(8,128)}) fusion(f32[4,512,2048]{2,1,0:T(8,128)} %fusion.221, f32[4,512]{1,0:T(4,128)S(1)} %dynamic-slice_bitcast_fusion.10, pred[512,2048]{1,0:T(8,128)(4,1)S(1)} %compare_and_fusion.5, bf16[2048,256]{1,0:T(8,128)(2,1)S(1)} %copy-done.4, ...), kind=kOutput, calls=%fused_computation.32.clone.1 | convolution fusion | flops 2168977408 | bytes 35932160 | tf_op jit(solution)/shard_map/while/body/eval_jaxpr/hqe,ke->hqk/dot_general | solution.py:278
  464.0 12.1 %multiply_convert_fusion.5 = bf16[4,512,2048]{2,1,0:T(8,128)(2,1)S(1)} fusion(f32[4,512,2048]{2,1,0:T(8,128)} %get-tuple-element.706, f32[4,512,2048]{2,1,0:T(8,128)} %fusion.221, f32[4,512]{1,0:T(4,128)S(1)} %get-tuple-element.707, f32[4,512]{1,0:T(4,128)S(1)} %dynamic-slice_bitcast_fusion.10, pred[512,2048]{1,0:T(8,128)(4,1)S(1)} %compare_and_fusion.5), kind=kLoop, calls=%fused_computation.31.clone.1 | loop fusion | flops 25165824 | bytes 43008000 | tf_op jit(solution)/shard_map/while/body/eval_jaxpr/convert_element_type | solution.py:280
  482.7 8.0 fusion.222
  490.6 10.4 fusion.223
  504.4 8.2 fusion.221
  512.7 12.1 %multiply_reduce_fusion.6 = (f32[4,512]{1,0:T(4,128)S(1)}, f32[4,512,2048]{2,1,0:T(8,128)}) fusion(f32[4,512,2048]{2,1,0:T(8,128)} %fusion.221, f32[4,512]{1,0:T(4,128)S(1)} %dynamic-slice_bitcast_fusion.10, pred[512,2048]{1,0:T(8,128)(4,1)S(1)} %compare_and_fusion.5, bf16[2048,256]{1,0:T(8,128)(2,1)S(1)} %copy-done.4, ...), kind=kOutput, calls=%fused_computation.32.clone.1 | convolution fusion | flops 2168977408 | bytes 35932160 | tf_op jit(solution)/shard_map/while/body/eval_jaxpr/hqe,ke->hqk/dot_general | solution.py:278
  524.8 12.1 %multiply_convert_fusion.5 = bf16[4,512,2048]{2,1,0:T(8,128)(2,1)S(1)} fusion(f32[4,512,2048]{2,1,0:T(8,128)} %get-tuple-element.706, f32[4,512,2048]{2,1,0:T(8,128)} %fusion.221, f32[4,512]{1,0:T(4,128)S(1)} %get-tuple-element.707, f32[4,512]{1,0:T(4,128)S(1)} %dynamic-slice_bitcast_fusion.10, pred[512,2048]{1,0:T(8,128)(4,1)S(1)} %compare_and_fusion.5), kind=kLoop, calls=%fused_computation.31.clone.1 | loop fusion | flops 25165824 | bytes 43008000 | tf_op jit(solution)/shard_map/while/body/eval_jaxpr/convert_element_type | solution.py:280
  543.4 8.0 fusion.222
  551.4 10.4 fusion.223
  605.0 11.2 convolution_convert_fusion.2
  625.7 14.0 %collective-permute-start.52 = (bf16[512,768]{1,0:T(8,128)(2,1)}, bf16[512,768]{1,0:T(8,128)(2,1)}, u32[]{:S(2)}, u32[]{:S(2)}) collective-permute-start(bf16[512,768]{1,0:T(8,128)(2,1)} %get-tuple-element.443), channel_id=1, source_target_pairs={{0,8},{1,9},{2,10},{3,11},{4,12},{5,13},{6,14},{7,15}} | collective-permute-start | bytes 2359304 | tf_op jit(solution)/shard_map/ppermute | solution.py:53
  647.1 13.8 %fusion.142 = f32[2048,1024]{1,0:T(8,128)} fusion(bf16[2048,2048]{1,0:T(8,128)(2,1)} %constant_dynamic-update-slice_fusion.1, bf16[512,1024]{1,0:T(8,128)(2,1)S(1)} %broadcast_select_fusion.1, bf16[512,1024]{1,0:T(8,128)(2,1)S(1)} %copy-done.36, bf16[512,1024]{1,0:T(8,128)(2,1)S(1)} %broadcast_select_fusion.5, bf16[512,1024]{1,0:T(8,128)(2,1)S(1)} %copy-done.25), kind=kOutput, calls=%fused_computation.226 | convolution fusion | flops 8606711808 | bytes 20971520 | tf_op jit(solution)/shard_map/dot_general | solution.py:224
  661.0 12.9 %convolution_convert_fusion = bf16[2048,1024]{0,1:T(8,128)(2,1)S(1)} fusion(bf16[2048,2048]{1,0:T(8,128)(2,1)S(1)} %bitcast.264, f32[2048,1024]{1,0:T(8,128)} %fusion.142, f32[1024]{0:T(1024)S(1)} %copy-done.67), kind=kOutput, calls=%fused_computation.102 | convolution fusion | flops 8613003264 | bytes 20975616 | tf_op jit(solution)/shard_map/dot_general | solution.py:317
  677.0 21.4 %fusion.172 = (f32[1024]{0:T(1024)S(1)}, bf16[2048,1024]{1,0:T(8,128)(2,1)}) fusion(f32[2048,1024]{1,0:T(8,128)} %fusion.142, f32[1024]{0:T(1024)S(1)} %copy-done.67, bf16[2048,2048]{1,0:T(8,128)(2,1)} %constant_dynamic-update-slice_fusion.10, bf16[512,1024]{1,0:T(8,128)(2,1)} %broadcast_select_fusion, bf16[512,1024]{1,0:T(8,128)(2,1)S(1)} %copy-done.37, ...), kind=kOutput, calls=%fused_computation.393 | convolution fusion | flops 8652848128 | bytes 25174016 | tf_op jit(solution)/shard_map/dot_general | solution.py:266
  698.4 14.1 %convolution_convert_fusion.1 = bf16[2048,1024]{0,1:T(8,128)(2,1)} fusion(bf16[2048,2048]{1,0:T(8,128)(2,1)} %constant_dynamic-update-slice_fusion.1, bf16[2048,1024]{1,0:T(8,128)(2,1)} %get-tuple-element.529), kind=kOutput, calls=%fused_computation.103 | convolution fusion | flops 8592031744 | bytes 16777216 | tf_op jit(solution)/shard_map/dot_general | solution.py:317
  712.5 14.4 %fusion.104 = f32[2048,2048]{1,0:T(8,128)} fusion(bf16[2048,1024]{1,0:T(8,128)(2,1)} %get-tuple-element.529, bf16[512,1024]{1,0:T(8,128)(2,1)S(1)} %copy-done.39, bf16[512,1024]{1,0:T(8,128)(2,1)S(1)} %copy-done.36, bf16[512,1024]{1,0:T(8,128)(2,1)S(1)} %copy-done.41, bf16[512,1024]{1,0:T(8,128)(2,1)S(1)} %copy-done.25), kind=kOutput, calls=%fused_computation.146 | convolution fusion | flops 8606711808 | bytes 25165824 | tf_op jit(solution)/shard_map/dot_general | solution.py:301
  726.9 16.1 %fusion.141 = f32[2048,2048]{1,0:T(8,128)} fusion(bf16[512,1024]{1,0:T(8,128)(2,1)} %broadcast_select_fusion, bf16[512,1024]{1,0:T(8,128)(2,1)S(1)} %copy-done.37, bf16[512,1024]{1,0:T(8,128)(2,1)} %copy-done.42, bf16[512,1024]{1,0:T(8,128)(2,1)S(1)} %copy-done.23, f32[2048,1024]{1,0:T(8,128)} %fusion.142, f32[1024]{0:T(1024)S(1)} %copy-done.67), kind=kOutput, calls=%fused_computation.225 | convolution fusion | flops 8627683328 | bytes 29364224 | tf_op jit(solution)/shard_map/dot_general | solution.py:258
  750.0 15.3 %add_convert_fusion = bf16[2048,2048]{1,0:T(8,128)(2,1)} fusion(f32[2048,2048]{1,0:T(8,128)} %fusion.104, f32[2048,768]{1,0:T(8,128)} %constant_dynamic-update-slice_fusion.19, bf16[512,768]{1,0:T(8,128)(2,1)} %copy-done.45, bf16[512,768]{1,0:T(8,128)(2,1)} %copy-done.44, bf16[512,768]{1,0:T(8,128)(2,1)} %copy-done.46, bf16[512,768]{1,0:T(8,128)(2,1)} %fusion.114), kind=kOutput, calls=%fused_computation.76 | convolution fusion | flops 6464995328 | bytes 34603008 | tf_op jit(solution)/shard_map/dot_general | solution.py:300
  772.4 12.1 %add_convert_fusion.1 = bf16[2048,2048]{1,0:T(8,128)(2,1)} fusion(f32[2048,2048]{1,0:T(8,128)} %fusion.141, bf16[2048,256]{1,0:T(8,128)(2,1)} %bitcast.15, bf16[512,256]{1,0:T(8,128)(2,1)} %copy-done.21, bf16[512,256]{1,0:T(8,128)(2,1)} %copy-done.19, bf16[512,256]{1,0:T(8,128)(2,1)} %copy-done.20, bf16[512,256]{1,0:T(8,128)(2,1)S(1)} %copy-done.18), kind=kOutput, calls=%fused_computation.77 | convolution fusion | flops 2160066560 | bytes 27262976 | tf_op jit(solution)/shard_map/dot_general | solution.py:257
  797.7 13.6 %collective-permute-start.54 = (bf16[512,768]{1,0:T(8,128)(2,1)S(1)}, bf16[512,768]{1,0:T(8,128)(2,1)S(1)}, u32[]{:S(2)}, u32[]{:S(2)}) collective-permute-start(bf16[512,768]{1,0:T(8,128)(2,1)S(1)} %get-tuple-element.439), channel_id=1, source_target_pairs={{0,8},{8,16},{16,24},{1,9},{9,17},{17,25},{2,10},{10,18},{18,26},{... | collective-permute-start | bytes 2359304 | tf_op jit(solution)/shard_map/ppermute | solution.py:53
  818.0 8.0 collective-permute-done.54
  826.0 24.1 %collective-permute-start.80 = (bf16[512,1024]{0,1:T(8,128)(2,1)S(1)}, bf16[512,1024]{0,1:T(8,128)(2,1)S(1)}, u32[]{:S(2)}, u32[]{:S(2)}) collective-permute-start(bf16[512,1024]{0,1:T(8,128)(2,1)S(1)} %get-tuple-element.417), channel_id=1, source_target_pairs={{0,8},{8,16},{1,9},{9,17},{2,10},{10,18},{3,11},{11,19},{4,12},{12... | collective-permute-start | bytes 3145736 | tf_op jit(solution)/shard_map/ppermute | solution.py:53
  863.8 9.8 collective-permute-done.80
  892.3 91.9 %all-reduce.1 = (f32[3072]{0:T(1024)}, f32[2048]{0:T(1024)S(1)}, f32[4096]{0:T(1024)}) all-reduce(f32[3072]{0:T(1024)S(1)} %dynamic_update_slice.18, f32[2048]{0:T(1024)S(1)} %copy-done.59, f32[4096]{0:T(1024)S(1)} %dynamic_update_slice.19), channel_id=1, replica_groups=mesh['fsdp'=4,'ctx'=4,'tp'=2] {'fsdp','ctx'}, use_global_device_ids=true, to_apply=%region_19.20 | all-reduce | flops 9216 | bytes 73728 | tf_op jit(solution)/shard_map/psum | solution.py:335
  1040.1 7.9 collective-permute-done.47
  1054.1 8.8 collective-permute-done.33
  1066.3 19.7 %collective-permute-done.48 = bf16[256,2048]{1,0:T(8,128)(2,1)S(1)} collective-permute-done((bf16[256,2048]{1,0:T(8,128)(2,1)S(1)}, bf16[256,2048]{1,0:T(8,128)(2,1)S(1)}, u32[]{:S(2)}, u32[]{:S(2)}) %collective-permute-start.48) | collective-permute-done | bytes 1048608 | tf_op jit(solution)/shard_map/ppermute | solution.py:30
  1090.1 8.7 collective-permute-done.34
  1111.4 37.8 %all-reduce = (f32[2048]{0:T(1024)}, f32[2048]{0:T(1024)}) all-reduce(f32[2048]{0:T(1024)S(1)} %get-tuple-element.337, f32[2048]{0:T(1024)S(1)} %get-tuple-element.449), channel_id=1, replica_groups=mesh['fsdp'=4,'ctx'=4,'tp'=2] {'fsdp','ctx','tp'}, use_global_device_ids=true, to_apply=%region_15.16 | all-reduce | flops 4096 | bytes 32768 | tf_op jit(solution)/shard_map/psum | solution.py:339
  (604 shorter events, 498.0 us)
Async XLA Ops:
  15.4 66.4 %collective-permute-start.38 = (bf16[256,2048]{1,0:T(8,128)(2,1)}, bf16[256,2048]{1,0:T(8,128)(2,1)}, u32[]{:S(2)}, u32[]{:S(2)}) collective-permute-start(bf16[256,2048]{1,0:T(8,128)(2,1)} %slice.316), channel_id=1, source_target_pairs={{0,2},{2,0},{4,6},{6,4},{1,3},{3,1},{5,7},{7,5},{8,10},{10,8},{12,... | collective-permute-start | bytes 3145736 | tf_op jit(solution)/shard_map/ppermute | solution.py:30
  18.3 64.8 %collective-permute-start.40 = (bf16[256,2048]{1,0:T(8,128)(2,1)}, bf16[256,2048]{1,0:T(8,128)(2,1)}, u32[]{:S(2)}, u32[]{:S(2)}) collective-permute-start(bf16[256,2048]{1,0:T(8,128)(2,1)} %slice.316), channel_id=1, source_target_pairs={{0,4},{2,6},{4,0},{6,2},{1,5},{3,7},{5,1},{7,3},{8,12},{10,14},{12... | collective-permute-start | bytes 3145736 | tf_op jit(solution)/shard_map/ppermute | solution.py:30
  29.2 41.6 %collective-permute-start.9 = (bf16[512,768]{1,0:T(8,128)(2,1)}, bf16[512,768]{1,0:T(8,128)(2,1)}, u32[]{:S(2)}, u32[]{:S(2)}) collective-permute-start(bf16[512,768]{1,0:T(8,128)(2,1)} %fusion.114), channel_id=1, source_target_pairs={{8,0},{16,8},{24,16},{9,1},{17,9},{25,17},{10,2},{18,10},{26,18},{... | collective-permute-start | bytes 2359304 | tf_op jit(solution)/shard_map/ppermute | solution.py:40
  80.5 28.4 %collective-permute-start.21 = (bf16[512,1024]{1,0:T(8,128)(2,1)S(1)}, bf16[512,1024]{1,0:T(8,128)(2,1)S(1)}, u32[]{:S(2)}, u32[]{:S(2)}) collective-permute-start(bf16[512,1024]{1,0:T(8,128)(2,1)S(1)} %constant_dynamic-slice_fusion.39), channel_id=1, source_target_pairs={{8,0},{16,8},{24,16},{9,1},{17,9},{25,17},{10,2},{18,10},{26,18},{... | collective-permute-start | bytes 3145736 | tf_op jit(solution)/shard_map/ppermute | solution.py:40
  81.8 40.2 %collective-permute-start.10 = (bf16[512,768]{1,0:T(8,128)(2,1)}, bf16[512,768]{1,0:T(8,128)(2,1)S(1)}, u32[]{:S(2)}, u32[]{:S(2)}) collective-permute-start(bf16[512,768]{1,0:T(8,128)(2,1)} %collective-permute-done.9), channel_id=1, source_target_pairs={{8,0},{16,8},{9,1},{17,9},{10,2},{18,10},{11,3},{19,11},{12,4},{20... | collective-permute-start | bytes 2359304 | tf_op jit(solution)/shard_map/ppermute | solution.py:40
  83.1 40.2 %collective-permute-start.12 = (bf16[512,768]{1,0:T(8,128)(2,1)}, bf16[512,768]{1,0:T(8,128)(2,1)S(1)}, u32[]{:S(2)}, u32[]{:S(2)}) collective-permute-start(bf16[512,768]{1,0:T(8,128)(2,1)} %collective-permute-done.8), channel_id=1, source_target_pairs={{8,16},{16,24},{9,17},{17,25},{10,18},{18,26},{11,19},{19,27},{12,... | collective-permute-start | bytes 2359304 | tf_op jit(solution)/shard_map/ppermute | solution.py:39
  89.1 34.9 %collective-permute-start.39 = (bf16[256,2048]{1,0:T(8,128)(2,1)}, bf16[256,2048]{1,0:T(8,128)(2,1)S(1)}, u32[]{:S(2)}, u32[]{:S(2)}) collective-permute-start(bf16[256,2048]{1,0:T(8,128)(2,1)} %collective-permute-done.38), channel_id=1, source_target_pairs={{0,1},{1,0},{2,3},{3,2},{4,5},{5,4},{6,7},{7,6},{8,9},{9,8},{10,11... | collective-permute-start | bytes 3145736 | tf_op jit(solution)/shard_map/ppermute | solution.py:30
  93.5 40.1 %collective-permute-start.41 = (bf16[256,2048]{1,0:T(8,128)(2,1)}, bf16[256,2048]{1,0:T(8,128)(2,1)S(1)}, u32[]{:S(2)}, u32[]{:S(2)}) collective-permute-start(bf16[256,2048]{1,0:T(8,128)(2,1)} %collective-permute-done.40), channel_id=1, source_target_pairs={{0,1},{1,0},{2,3},{3,2},{4,5},{5,4},{6,7},{7,6},{8,9},{9,8},{10,11... | collective-permute-start | bytes 3145736 | tf_op jit(solution)/shard_map/ppermute | solution.py:30
  108.9 29.5 %collective-permute-start.20 = (bf16[512,1024]{1,0:T(8,128)(2,1)S(1)}, bf16[512,1024]{1,0:T(8,128)(2,1)S(1)}, u32[]{:S(2)}, u32[]{:S(2)}) collective-permute-start(bf16[512,1024]{1,0:T(8,128)(2,1)S(1)} %constant_dynamic-slice_fusion.39), channel_id=1, source_target_pairs={{0,8},{8,16},{16,24},{1,9},{9,17},{17,25},{2,10},{10,18},{18,26},{... | collective-permute-start | bytes 3145736 | tf_op jit(solution)/shard_map/ppermute | solution.py:39
  138.4 27.3 %collective-permute-start.26 = (bf16[512,1024]{1,0:T(8,128)(2,1)S(1)}, bf16[512,1024]{1,0:T(8,128)(2,1)S(1)}, u32[]{:S(2)}, u32[]{:S(2)}) collective-permute-start(bf16[512,1024]{1,0:T(8,128)(2,1)S(1)} %constant_dynamic-slice_fusion.38), channel_id=1, source_target_pairs={{0,8},{8,16},{16,24},{1,9},{9,17},{17,25},{2,10},{10,18},{18,26},{... | collective-permute-start | bytes 3145736 | tf_op jit(solution)/shard_map/ppermute | solution.py:39
  145.4 24.6 %collective-permute-start.22 = (bf16[512,1024]{1,0:T(8,128)(2,1)S(1)}, bf16[512,1024]{1,0:T(8,128)(2,1)}, u32[]{:S(2)}, u32[]{:S(2)}) collective-permute-start(bf16[512,1024]{1,0:T(8,128)(2,1)S(1)} %collective-permute-done.21), channel_id=1, source_target_pairs={{8,0},{16,8},{9,1},{17,9},{10,2},{18,10},{11,3},{19,11},{12,4},{20... | collective-permute-start | bytes 3145736 | tf_op jit(solution)/shard_map/ppermute | solution.py:40
  165.7 28.2 %collective-permute-start.28 = (bf16[512,1024]{1,0:T(8,128)(2,1)S(1)}, bf16[512,1024]{1,0:T(8,128)(2,1)S(1)}, u32[]{:S(2)}, u32[]{:S(2)}) collective-permute-start(bf16[512,1024]{1,0:T(8,128)(2,1)S(1)} %collective-permute-done.27), channel_id=1, source_target_pairs={{8,0},{16,8},{9,1},{17,9},{10,2},{18,10},{11,3},{19,11},{12,4},{20... | collective-permute-start | bytes 3145736 | tf_op jit(solution)/shard_map/ppermute | solution.py:40
  167.0 28.2 %collective-permute-start.30 = (bf16[512,1024]{1,0:T(8,128)(2,1)S(1)}, bf16[512,1024]{1,0:T(8,128)(2,1)}, u32[]{:S(2)}, u32[]{:S(2)}) collective-permute-start(bf16[512,1024]{1,0:T(8,128)(2,1)S(1)} %collective-permute-done.26), channel_id=1, source_target_pairs={{8,16},{16,24},{9,17},{17,25},{10,18},{18,26},{11,19},{19,27},{12,... | collective-permute-start | bytes 3145736 | tf_op jit(solution)/shard_map/ppermute | solution.py:39
  183.2 39.1 %collective-permute-start.11 = (bf16[512,768]{1,0:T(8,128)(2,1)S(1)}, bf16[512,768]{1,0:T(8,128)(2,1)S(1)}, u32[]{:S(2)}, u32[]{:S(2)}) collective-permute-start(bf16[512,768]{1,0:T(8,128)(2,1)S(1)} %collective-permute-done.10), channel_id=1, source_target_pairs={{8,0},{9,1},{10,2},{11,3},{12,4},{13,5},{14,6},{15,7}} | collective-permute-start | bytes 2359304 | tf_op jit(solution)/shard_map/ppermute | solution.py:40
  185.3 455.5 %collective-permute-start.25 = (bf16[512,1024]{1,0:T(8,128)(2,1)}, bf16[512,1024]{1,0:T(8,128)(2,1)}, u32[]{:S(2)}, u32[]{:S(2)}) collective-permute-start(bf16[512,1024]{1,0:T(8,128)(2,1)} %collective-permute-done.24), channel_id=1, source_target_pairs={{16,24},{17,25},{18,26},{19,27},{20,28},{21,29},{22,30},{23,31}} | collective-permute-start | bytes 3145736 | tf_op jit(solution)/shard_map/ppermute | solution.py:39
  193.9 448.6 %collective-permute-start.23 = (bf16[512,1024]{1,0:T(8,128)(2,1)}, bf16[512,1024]{1,0:T(8,128)(2,1)}, u32[]{:S(2)}, u32[]{:S(2)}) collective-permute-start(bf16[512,1024]{1,0:T(8,128)(2,1)} %collective-permute-done.22), channel_id=1, source_target_pairs={{8,0},{9,1},{10,2},{11,3},{12,4},{13,5},{14,6},{15,7}} | collective-permute-start | bytes 3145736 | tf_op jit(solution)/shard_map/ppermute | solution.py:40
  195.2 478.7 %collective-permute-start.31 = (bf16[512,1024]{1,0:T(8,128)(2,1)}, bf16[512,1024]{1,0:T(8,128)(2,1)}, u32[]{:S(2)}, u32[]{:S(2)}) collective-permute-start(bf16[512,1024]{1,0:T(8,128)(2,1)} %collective-permute-done.30), channel_id=1, source_target_pairs={{16,24},{17,25},{18,26},{19,27},{20,28},{21,29},{22,30},{23,31}} | collective-permute-start | bytes 3145736 | tf_op jit(solution)/shard_map/ppermute | solution.py:39
  573.5 42.8 %collective-permute-start.61 = (bf16[512,256]{0,1:T(8,128)(2,1)}, bf16[512,256]{0,1:T(8,128)(2,1)S(1)}, u32[]{:S(2)}, u32[]{:S(2)}) collective-permute-start(bf16[512,256]{0,1:T(8,128)(2,1)} %get-tuple-element.498), channel_id=1, source_target_pairs={{0,8},{1,9},{2,10},{3,11},{4,12},{5,13},{6,14},{7,15}} | collective-permute-start | bytes 786440 | tf_op jit(solution)/shard_map/ppermute | solution.py:53
  576.1 40.2 %collective-permute-start.64 = (bf16[512,256]{0,1:T(8,128)(2,1)}, bf16[512,256]{0,1:T(8,128)(2,1)}, u32[]{:S(2)}, u32[]{:S(2)}) collective-permute-start(bf16[512,256]{0,1:T(8,128)(2,1)} %get-tuple-element.499), channel_id=1, source_target_pairs={{24,16},{25,17},{26,18},{27,19},{28,20},{29,21},{30,22},{31,23}} | collective-permute-start | bytes 786440 | tf_op jit(solution)/shard_map/ppermute | solution.py:54
  624.4 52.2 %collective-permute-start.29 = (bf16[512,1024]{1,0:T(8,128)(2,1)S(1)}, bf16[512,1024]{1,0:T(8,128)(2,1)S(1)}, u32[]{:S(2)}, u32[]{:S(2)}) collective-permute-start(bf16[512,1024]{1,0:T(8,128)(2,1)S(1)} %copy-done.35), channel_id=1, source_target_pairs={{8,0},{9,1},{10,2},{11,3},{12,4},{13,5},{14,6},{15,7}} | collective-permute-start | bytes 3145736 | tf_op jit(solution)/shard_map/ppermute | solution.py:40
  625.7 139.6 %collective-permute-start.52 = (bf16[512,768]{1,0:T(8,128)(2,1)}, bf16[512,768]{1,0:T(8,128)(2,1)}, u32[]{:S(2)}, u32[]{:S(2)}) collective-permute-start(bf16[512,768]{1,0:T(8,128)(2,1)} %get-tuple-element.443), channel_id=1, source_target_pairs={{0,8},{1,9},{2,10},{3,11},{4,12},{5,13},{6,14},{7,15}} | collective-permute-start | bytes 2359304 | tf_op jit(solution)/shard_map/ppermute | solution.py:53
  640.8 126.2 %collective-permute-start.55 = (bf16[512,768]{1,0:T(8,128)(2,1)}, bf16[512,768]{1,0:T(8,128)(2,1)}, u32[]{:S(2)}, u32[]{:S(2)}) collective-permute-start(bf16[512,768]{1,0:T(8,128)(2,1)} %get-tuple-element.444), channel_id=1, source_target_pairs={{24,16},{25,17},{26,18},{27,19},{28,20},{29,21},{30,22},{31,23}} | collective-permute-start | bytes 2359304 | tf_op jit(solution)/shard_map/ppermute | solution.py:54
  642.5 142.3 %collective-permute-start.63 = (bf16[512,256]{0,1:T(8,128)(2,1)}, bf16[512,256]{0,1:T(8,128)(2,1)}, u32[]{:S(2)}, u32[]{:S(2)}) collective-permute-start(bf16[512,256]{0,1:T(8,128)(2,1)} %get-tuple-element.494), channel_id=1, source_target_pairs={{0,8},{8,16},{16,24},{1,9},{9,17},{17,25},{2,10},{10,18},{18,26},{... | collective-permute-start | bytes 786440 | tf_op jit(solution)/shard_map/ppermute | solution.py:53
  673.9 112.2 %collective-permute-start.66 = (bf16[512,256]{0,1:T(8,128)(2,1)}, bf16[512,256]{0,1:T(8,128)(2,1)}, u32[]{:S(2)}, u32[]{:S(2)}) collective-permute-start(bf16[512,256]{0,1:T(8,128)(2,1)} %get-tuple-element.495), channel_id=1, source_target_pairs={{8,0},{16,8},{24,16},{9,1},{17,9},{25,17},{10,2},{18,10},{26,18},{... | collective-permute-start | bytes 786440 | tf_op jit(solution)/shard_map/ppermute | solution.py:54
  744.5 66.8 %collective-permute-start.79 = (bf16[512,1024]{0,1:T(8,128)(2,1)}, bf16[512,1024]{0,1:T(8,128)(2,1)}, u32[]{:S(2)}, u32[]{:S(2)}) collective-permute-start(bf16[512,1024]{0,1:T(8,128)(2,1)} %get-tuple-element.419), channel_id=1, source_target_pairs={{0,8},{1,9},{2,10},{3,11},{4,12},{5,13},{6,14},{7,15}} | collective-permute-start | bytes 3145736 | tf_op jit(solution)/shard_map/ppermute | solution.py:53
  765.3 47.4 %collective-permute-start.82 = (bf16[512,1024]{0,1:T(8,128)(2,1)}, bf16[512,1024]{0,1:T(8,128)(2,1)}, u32[]{:S(2)}, u32[]{:S(2)}) collective-permute-start(bf16[512,1024]{0,1:T(8,128)(2,1)} %get-tuple-element.420), channel_id=1, source_target_pairs={{24,16},{25,17},{26,18},{27,19},{28,20},{29,21},{30,22},{31,23}} | collective-permute-start | bytes 3145736 | tf_op jit(solution)/shard_map/ppermute | solution.py:54
  784.8 30.8 %collective-permute-start.70 = (bf16[512,1024]{0,1:T(8,128)(2,1)S(1)}, bf16[512,1024]{0,1:T(8,128)(2,1)S(1)}, u32[]{:S(2)}, u32[]{:S(2)}) collective-permute-start(bf16[512,1024]{0,1:T(8,128)(2,1)S(1)} %get-tuple-element.425), channel_id=1, source_target_pairs={{0,8},{1,9},{2,10},{3,11},{4,12},{5,13},{6,14},{7,15}} | collective-permute-start | bytes 3145736 | tf_op jit(solution)/shard_map/ppermute | solution.py:53
  786.2 29.9 %collective-permute-start.73 = (bf16[512,1024]{0,1:T(8,128)(2,1)S(1)}, bf16[512,1024]{0,1:T(8,128)(2,1)S(1)}, u32[]{:S(2)}, u32[]{:S(2)}) collective-permute-start(bf16[512,1024]{0,1:T(8,128)(2,1)S(1)} %get-tuple-element.426), channel_id=1, source_target_pairs={{24,16},{25,17},{26,18},{27,19},{28,20},{29,21},{30,22},{31,23}} | collective-permute-start | bytes 3145736 | tf_op jit(solution)/shard_map/ppermute | solution.py:54
  797.7 28.2 %collective-permute-start.54 = (bf16[512,768]{1,0:T(8,128)(2,1)S(1)}, bf16[512,768]{1,0:T(8,128)(2,1)S(1)}, u32[]{:S(2)}, u32[]{:S(2)}) collective-permute-start(bf16[512,768]{1,0:T(8,128)(2,1)S(1)} %get-tuple-element.439), channel_id=1, source_target_pairs={{0,8},{8,16},{16,24},{1,9},{9,17},{17,25},{2,10},{10,18},{18,26},{... | collective-permute-start | bytes 2359304 | tf_op jit(solution)/shard_map/ppermute | solution.py:53
  811.3 39.2 %collective-permute-start.57 = (bf16[512,768]{1,0:T(8,128)(2,1)S(1)}, bf16[512,768]{1,0:T(8,128)(2,1)S(1)}, u32[]{:S(2)}, u32[]{:S(2)}) collective-permute-start(bf16[512,768]{1,0:T(8,128)(2,1)S(1)} %get-tuple-element.440), channel_id=1, source_target_pairs={{8,0},{16,8},{24,16},{9,1},{17,9},{25,17},{10,2},{18,10},{26,18},{... | collective-permute-start | bytes 2359304 | tf_op jit(solution)/shard_map/ppermute | solution.py:54
  812.7 39.7 %collective-permute-start.67 = (bf16[128,256]{0,1:T(8,128)(2,1)S(1)}, bf16[128,256]{0,1:T(8,128)(2,1)S(1)}, u32[]{:S(2)}, u32[]{:S(2)}) collective-permute-start(bf16[128,256]{0,1:T(8,128)(2,1)S(1)} %get-tuple-element.515), channel_id=1, source_target_pairs={{0,2},{2,0},{4,6},{6,4},{1,3},{3,1},{5,7},{7,5},{8,10},{10,8},{12,... | collective-permute-start | bytes 196616 | tf_op jit(solution)/shard_map/ppermute | solution.py:30
  815.6 37.2 %collective-permute-start.68 = (bf16[128,256]{0,1:T(8,128)(2,1)S(1)}, bf16[128,256]{0,1:T(8,128)(2,1)S(1)}, u32[]{:S(2)}, u32[]{:S(2)}) collective-permute-start(bf16[128,256]{0,1:T(8,128)(2,1)S(1)} %get-tuple-element.514), channel_id=1, source_target_pairs={{0,4},{2,6},{4,0},{6,2},{1,5},{3,7},{5,1},{7,3},{8,12},{10,14},{12... | collective-permute-start | bytes 196616 | tf_op jit(solution)/shard_map/ppermute | solution.py:30
  816.1 211.1 %collective-permute-start.46 = (bf16[4,256,2048]{2,1,0:T(8,128)(2,1)}, bf16[4,256,2048]{2,1,0:T(8,128)(2,1)}, u32[]{:S(2)}, u32[]{:S(2)}) collective-permute-start(bf16[4,256,2048]{2,1,0:T(8,128)(2,1)} %slice_bitcast_fusion), channel_id=1, source_target_pairs={{0,1},{1,0},{2,3},{3,2},{4,5},{5,4},{6,7},{7,6},{8,9},{9,8},{10,11... | collective-permute-start | bytes 12582920 | tf_op jit(solution)/shard_map/ppermute | solution.py:30
  826.0 47.7 %collective-permute-start.80 = (bf16[512,1024]{0,1:T(8,128)(2,1)S(1)}, bf16[512,1024]{0,1:T(8,128)(2,1)S(1)}, u32[]{:S(2)}, u32[]{:S(2)}) collective-permute-start(bf16[512,1024]{0,1:T(8,128)(2,1)S(1)} %get-tuple-element.417), channel_id=1, source_target_pairs={{0,8},{8,16},{1,9},{9,17},{2,10},{10,18},{3,11},{11,19},{4,12},{12... | collective-permute-start | bytes 3145736 | tf_op jit(solution)/shard_map/ppermute | solution.py:53
  850.5 24.8 %collective-permute-start.83 = (bf16[512,1024]{0,1:T(8,128)(2,1)S(1)}, bf16[512,1024]{0,1:T(8,128)(2,1)S(1)}, u32[]{:S(2)}, u32[]{:S(2)}) collective-permute-start(bf16[512,1024]{0,1:T(8,128)(2,1)S(1)} %get-tuple-element.418), channel_id=1, source_target_pairs={{16,8},{24,16},{17,9},{25,17},{18,10},{26,18},{19,11},{27,19},{20,... | collective-permute-start | bytes 3145736 | tf_op jit(solution)/shard_map/ppermute | solution.py:54
  852.8 132.0 %collective-permute-start.71 = (bf16[512,1024]{0,1:T(8,128)(2,1)}, bf16[512,1024]{0,1:T(8,128)(2,1)S(1)}, u32[]{:S(2)}, u32[]{:S(2)}) collective-permute-start(bf16[512,1024]{0,1:T(8,128)(2,1)} %get-tuple-element.423), channel_id=1, source_target_pairs={{0,8},{8,16},{1,9},{9,17},{2,10},{10,18},{3,11},{11,19},{4,12},{12... | collective-permute-start | bytes 3145736 | tf_op jit(solution)/shard_map/ppermute | solution.py:53
  863.8 169.5 %collective-permute-start.32 = (bf16[4,256,2048]{2,1,0:T(8,128)(2,1)}, bf16[4,256,2048]{2,1,0:T(8,128)(2,1)}, u32[]{:S(2)}, u32[]{:S(2)}) collective-permute-start(bf16[4,256,2048]{2,1,0:T(8,128)(2,1)} %slice_bitcast_fusion.2), channel_id=1, source_target_pairs={{0,1},{1,0},{2,3},{3,2},{4,5},{5,4},{6,7},{7,6},{8,9},{9,8},{10,11... | collective-permute-start | bytes 12582920 | tf_op jit(solution)/shard_map/ppermute | solution.py:30
  873.6 113.3 %collective-permute-start.74 = (bf16[512,1024]{0,1:T(8,128)(2,1)}, bf16[512,1024]{0,1:T(8,128)(2,1)}, u32[]{:S(2)}, u32[]{:S(2)}) collective-permute-start(bf16[512,1024]{0,1:T(8,128)(2,1)} %get-tuple-element.424), channel_id=1, source_target_pairs={{16,8},{24,16},{17,9},{25,17},{18,10},{26,18},{19,11},{27,19},{20,... | collective-permute-start | bytes 3145736 | tf_op jit(solution)/shard_map/ppermute | solution.py:54
  881.0 117.2 %collective-permute-start.81 = (bf16[512,1024]{0,1:T(8,128)(2,1)}, bf16[512,1024]{0,1:T(8,128)(2,1)}, u32[]{:S(2)}, u32[]{:S(2)}) collective-permute-start(bf16[512,1024]{0,1:T(8,128)(2,1)} %get-tuple-element.415), channel_id=1, source_target_pairs={{0,8},{8,16},{16,24},{1,9},{9,17},{17,25},{2,10},{10,18},{18,26},{... | collective-permute-start | bytes 3145736 | tf_op jit(solution)/shard_map/ppermute | solution.py:53
  1019.8 31.4 %collective-permute-start.76 = (bf16[128,1024]{0,1:T(8,128)(2,1)}, bf16[128,1024]{0,1:T(8,128)(2,1)}, u32[]{:S(2)}, u32[]{:S(2)}) collective-permute-start(bf16[128,1024]{0,1:T(8,128)(2,1)} %get-tuple-element.493), channel_id=1, source_target_pairs={{0,2},{2,0},{4,6},{6,4},{1,3},{3,1},{5,7},{7,5},{8,10},{10,8},{12,... | collective-permute-start | bytes 786440 | tf_op jit(solution)/shard_map/ppermute | solution.py:30
  1019.8 31.5 %collective-permute-start.77 = (bf16[128,1024]{0,1:T(8,128)(2,1)}, bf16[128,1024]{0,1:T(8,128)(2,1)}, u32[]{:S(2)}, u32[]{:S(2)}) collective-permute-start(bf16[128,1024]{0,1:T(8,128)(2,1)} %get-tuple-element.492), channel_id=1, source_target_pairs={{0,4},{2,6},{4,0},{6,2},{1,5},{3,7},{5,1},{7,3},{8,12},{10,14},{12... | collective-permute-start | bytes 786440 | tf_op jit(solution)/shard_map/ppermute | solution.py:30
  1025.0 27.8 %collective-permute-start.78 = (bf16[128,1024]{0,1:T(8,128)(2,1)}, bf16[128,1024]{0,1:T(8,128)(2,1)}, u32[]{:S(2)}, u32[]{:S(2)}) collective-permute-start(bf16[128,1024]{0,1:T(8,128)(2,1)} %get-tuple-element.491), channel_id=1, source_target_pairs={{0,6},{2,4},{4,2},{6,0},{1,7},{3,5},{5,3},{7,1},{8,14},{10,12},{12... | collective-permute-start | bytes 786440 | tf_op jit(solution)/shard_map/ppermute | solution.py:30
  1051.2 34.7 %collective-permute-start.48 = (bf16[256,2048]{1,0:T(8,128)(2,1)S(1)}, bf16[256,2048]{1,0:T(8,128)(2,1)S(1)}, u32[]{:S(2)}, u32[]{:S(2)}) collective-permute-start(bf16[256,2048]{1,0:T(8,128)(2,1)S(1)} %pad_maximum_fusion.11), channel_id=1, source_target_pairs={{0,2},{2,0},{4,6},{6,4},{1,3},{3,1},{5,7},{7,5},{8,10},{10,8},{12,... | collective-permute-start | bytes 3145736 | tf_op jit(solution)/shard_map/ppermute | solution.py:30
  1051.3 34.7 %collective-permute-start.50 = (bf16[256,2048]{1,0:T(8,128)(2,1)S(1)}, bf16[256,2048]{1,0:T(8,128)(2,1)S(1)}, u32[]{:S(2)}, u32[]{:S(2)}) collective-permute-start(bf16[256,2048]{1,0:T(8,128)(2,1)S(1)} %pad_maximum_fusion.12), channel_id=1, source_target_pairs={{0,4},{2,6},{4,0},{6,2},{1,5},{3,7},{5,1},{7,3},{8,12},{10,14},{12... | collective-permute-start | bytes 3145736 | tf_op jit(solution)/shard_map/ppermute | solution.py:30
  1064.0 34.8 %collective-permute-start.34 = (bf16[256,2048]{1,0:T(8,128)(2,1)S(1)}, bf16[256,2048]{1,0:T(8,128)(2,1)S(1)}, u32[]{:S(2)}, u32[]{:S(2)}) collective-permute-start(bf16[256,2048]{1,0:T(8,128)(2,1)S(1)} %pad_maximum_fusion.9), channel_id=1, source_target_pairs={{0,2},{2,0},{4,6},{6,4},{1,3},{3,1},{5,7},{7,5},{8,10},{10,8},{12,... | collective-permute-start | bytes 3145736 | tf_op jit(solution)/shard_map/ppermute | solution.py:30
  1066.2 32.6 %collective-permute-start.36 = (bf16[256,2048]{1,0:T(8,128)(2,1)S(1)}, bf16[256,2048]{1,0:T(8,128)(2,1)S(1)}, u32[]{:S(2)}, u32[]{:S(2)}) collective-permute-start(bf16[256,2048]{1,0:T(8,128)(2,1)S(1)} %pad_maximum_fusion.10), channel_id=1, source_target_pairs={{0,4},{2,6},{4,0},{6,2},{1,5},{3,7},{5,1},{7,3},{8,12},{10,14},{12... | collective-permute-start | bytes 3145736 | tf_op jit(solution)/shard_map/ppermute | solution.py:30
  1090.1 61.5 %collective-permute-start.51 = (f32[256,2048]{1,0:T(8,128)}, f32[256,2048]{1,0:T(8,128)}, u32[]{:S(2)}, u32[]{:S(2)}) collective-permute-start(f32[256,2048]{1,0:T(8,128)} %convert_add_fusion.8), channel_id=1, source_target_pairs={{0,1},{1,0},{2,3},{3,2},{4,5},{5,4},{6,7},{7,6},{8,9},{9,8},{10,11... | collective-permute-start | bytes 6291464 | tf_op jit(solution)/shard_map/ppermute | solution.py:30
  1099.9 49.4 %collective-permute-start.37 = (bf16[256,2048]{1,0:T(8,128)(2,1)S(1)}, bf16[256,2048]{1,0:T(8,128)(2,1)S(1)}, u32[]{:S(2)}, u32[]{:S(2)}) collective-permute-start(bf16[256,2048]{1,0:T(8,128)(2,1)S(1)} %fusion.100), channel_id=1, source_target_pairs={{0,1},{1,0},{2,3},{3,2},{4,5},{5,4},{6,7},{7,6},{8,9},{9,8},{10,11... | collective-permute-start | bytes 3145736 | tf_op jit(solution)/shard_map/ppermute | solution.py:30
  (131 other events, 3150.0 us)

commit v2 on v1

--- a/solution.py
+++ b/solution.py
@@ -1,8 +1,11 @@
+import functools
 import math
 
 import jax
 import jax.numpy as jnp
 from jax import lax
+from jax.experimental import pallas as pl
+from jax.experimental.pallas import tpu as pltpu
 from jax.sharding import PartitionSpec as P
 
 HEAD = 64
@@ -28,6 +31,15 @@
 def swap(x, axis, bit):
     size = lax.axis_size(axis)
     return lax.ppermute(x, axis, [(i, i ^ bit) for i in range(size)])
+
+
+def everywhere(x, *axes):
+    for axis in axes:
+        bit = 1
+        while bit < lax.axis_size(axis):
+            x = x + swap(x, axis, bit)
+            bit *= 2
+    return x
 
 
 def line_gather(own):
@@ -132,6 +144,253 @@
         base = (head * 3 + 2) * HEAD
         order += list(range(base, base + HEAD))
     return order
+
+
+BLOCK = 256
+NT = (((1,), (1,)), ((), ()))
+
+
+def mm(a, b, dims=(((1,), (0,)), ((), ()))):
+    return lax.dot_general(a, b, dims, preferred_element_type=f32)
+
+
+def turned(x, cosine, sine, split):
+    slab = cosine.shape[1]
+    front = x[:, :slab]
+    if slab == 2 * split:
+        partner = pltpu.roll(front, split, 1)
+    else:
+        lane = lax.broadcasted_iota(jnp.int32, front.shape, 1)
+        partner = jnp.where(
+            lane < split, pltpu.roll(front, slab - split, 1), pltpu.roll(front, split, 1)
+        )
+    front = front * cosine + partner * sine
+    if slab == x.shape[1]:
+        return front
+    return jnp.concatenate([front, x[:, slab:]], axis=1)
+
+
+def to_packed(prow_ref, block, data):
+    shape = (BLOCK, prow_ref.shape[1])
+    at = lax.broadcasted_iota(jnp.int32, shape, 0) + block * BLOCK
+    return mm((at == prow_ref[...]).astype(f32).astype(bf16), data)
+
+
+def to_arrival(pcol_ref, block, data):
+    rows = pl.ds(pl.multiple_of(block * BLOCK, BLOCK), BLOCK)
+    shape = (BLOCK, data.shape[0])
+    at = lax.broadcasted_iota(jnp.int32, shape, 1)
+    return mm((at == pcol_ref[rows, :]).astype(f32).astype(bf16), data)
+
+
+def kept(i, j, start):
+    keys = lax.broadcasted_iota(jnp.int32, (BLOCK, BLOCK), 0) + j * BLOCK
+    queries = lax.broadcasted_iota(jnp.int32, (BLOCK, BLOCK), 1) + i * BLOCK
+    return (keys >= start) & (keys <= queries)
+
+
+def forward_kernel(
+    heads, low_ref, qkv_ref, bias_ref, cos_ref, sin_ref, prow_ref, pcol_ref, start_ref, qmask_ref,
+    packed_ref, outt_ref, lse_ref, mixed_ref, x_ref, vt_ref, mp_ref,
+):
+    rows_all, wide = mixed_ref.shape
+    blocks = rows_all // BLOCK
+    split = ROT // 2 * heads
+
+    @pl.loop(0, blocks)
+    def _(r):
+        rows = pl.ds(pl.multiple_of(r * BLOCK, BLOCK), BLOCK)
+        cosine, sine = cos_ref[rows, :], sin_ref[rows, :]
+        x = qkv_ref[rows, :] + bias_ref[0:1, :]
+        q = turned(x[:, :wide], cosine, sine, split) * (1.0 / math.sqrt(HEAD))
+        k = turned(x[:, wide : 2 * wide], cosine, sine, split)
+        x_ref[rows, :] = jnp.concatenate([q, k, x[:, 2 * wide :]], axis=1).astype(bf16)
+
+    @pl.loop(0, blocks)
+    def _(p):
+        rows = pl.ds(pl.multiple_of(p * BLOCK, BLOCK), BLOCK)
+        y = to_packed(prow_ref, p, x_ref[...])
+        packed_ref[rows, :] = y.astype(bf16)
+        vt_ref[:, rows] = y[:, 2 * wide :].T.astype(bf16)
+
+    @pl.loop(0, blocks)
+    def _(i):
+        rows = pl.ds(pl.multiple_of(i * BLOCK, BLOCK), BLOCK)
+        start = start_ref[0:1, rows]
+        q = packed_ref[rows, :wide]
+        qs = [q * qmask_ref[h] for h in range(heads)]
+
+        def step(j, carried):
+            keys = pl.ds(pl.multiple_of(j * BLOCK, BLOCK), BLOCK)
+            k = packed_ref[keys, wide : 2 * wide]
+            keep = kept(i, j, start)
+            after = []
+            for h in range(heads):
+                top, total, acc = carried[h]
+                s = jnp.where(keep, mm(k, qs[h], NT), MASKED)
+                new_top = jnp.maximum(top, jnp.max(s, axis=0, keepdims=True))
+                p = jnp.exp(s - new_top)
+                alpha = jnp.exp(top - new_top)
+                total = total * alpha + jnp.sum(p, axis=0, keepdims=True)
+                acc = acc * alpha + mm(vt_ref[h * HEAD : (h + 1) * HEAD, keys], p.astype(bf16))
+                after.append((new_top, total, acc))
+            return tuple(after)
+
+        begin = tuple(
+            (
+                jnp.full((1, BLOCK), MASKED, f32),
+                jnp.zeros((1, BLOCK), f32),
+                jnp.zeros((HEAD, BLOCK), f32),
+            )
+            for _ in range(heads)
+        )
+        state = lax.fori_loop(low_ref[i], i + 1, step, begin)
+        out = jnp.concatenate([acc / total for _, total, acc in state], axis=0)
+        outt_ref[:, rows] = out
+        mp_ref[rows, :] = out.T.astype(bf16)
+        lse = [top + jnp.log(total) for top, total, _ in state]
+        lse_ref[:, rows] = jnp.concatenate(lse + [jnp.zeros((8 - heads, BLOCK), f32)], axis=0)
+
+    @pl.loop(0, blocks)
+    def _(r):
+        rows = pl.ds(pl.multiple_of(r * BLOCK, BLOCK), BLOCK)
+        mixed_ref[rows, :] = to_arrival(pcol_ref, r, mp_ref[...]).astype(bf16)
+
+
+def backward_kernel(
+    heads, low_ref, packed_ref, outt_ref, lse_ref, grad_ref, cos_ref, sin_ref, prow_ref, pcol_ref, start_ref,
+    qmask_ref, vmask_ref, ktmask_ref,
+    qkv_grad_ref, bias_grad_ref, kt_ref, dk_ref, dv_ref, dq_ref, gp_ref,
+):
+    rows_all, wide = grad_ref.shape
+    blocks = rows_all // BLOCK
+    split = ROT // 2 * heads
+
+    @pl.loop(0, blocks)
+    def _(p):
+        rows = pl.ds(pl.multiple_of(p * BLOCK, BLOCK), BLOCK)
+        gp_ref[rows, :wide] = to_packed(prow_ref, p, grad_ref[...]).astype(bf16)
+        kt_ref[:, rows] = packed_ref[rows, wide : 2 * wide].astype(f32).T.astype(bf16)
+        dk_ref[rows, :] = jnp.zeros((BLOCK, wide), f32)
+        dv_ref[rows, :] = jnp.zeros((BLOCK, wide), f32)
+
+    @pl.loop(0, blocks)
+    def _(i):
+        rows = pl.ds(pl.multiple_of(i * BLOCK, BLOCK), BLOCK)
+        start = start_ref[0:1, rows]
+        q = packed_ref[rows, :wide]
+        g = gp_ref[rows, :wide]
+        qs = [q * qmask_ref[h] for h in range(heads)]
+        gs = [g * vmask_ref[h] for h in range(heads)]
+        product = g.astype(f32).T * outt_ref[:, rows]
+        inner = [
+            jnp.sum(product[h * HEAD : (h + 1) * HEAD], axis=0, keepdims=True) for h in range(heads)
+        ]
+        lse = [lse_ref[h : h + 1, rows] for h in range(heads)]
+
+        def step(j, dqt):
+            keys = pl.ds(pl.multiple_of(j * BLOCK, BLOCK), BLOCK)
+            k = packed_ref[keys, wide : 2 * wide]
+            v = packed_ref[keys, 2 * wide :]
+            kt = kt_ref[:, keys]
+            keep = kept(i, j, start)
+            dk = dk_ref[keys, :]
+            dv = dv_ref[keys, :]
+            for h in range(heads):
+                s = jnp.where(keep, mm(k, qs[h], NT), MASKED)
+                p = jnp.exp(s - lse[h])
+                dp = mm(v, gs[h], NT)
+                ds = (p * (dp - inner[h])).astype(bf16)
+                dv = dv + mm(p.astype(bf16), gs[h])
+                dk = dk + mm(ds, qs[h])
+                dqt = dqt + mm(kt * ktmask_ref[h], ds)
+            dk_ref[keys, :] = dk
+            dv_ref[keys, :] = dv
+            return dqt
+
+        dqt = lax.fori_loop(low_ref[i], i + 1, step, jnp.zeros((wide, BLOCK), f32))
+        dq_ref[rows, :] = dqt.T * (1.0 / math.sqrt(HEAD))
+
+    bias_grad_ref[...] = jnp.zeros(bias_grad_ref.shape, f32)
+
+    @pl.loop(0, blocks)
+    def _(p):
+        rows = pl.ds(pl.multiple_of(p * BLOCK, BLOCK), BLOCK)
+        cosine, sine = cos_ref[rows, :], -sin_ref[rows, :]
+        dq = turned(dq_ref[rows, :], cosine, sine, split)
+        dk = turned(dk_ref[rows, :], cosine, sine, split)
+        full = jnp.concatenate([dq, dk, dv_ref[rows, :]], axis=1)
+        bias_grad_ref[0:1, :] = bias_grad_ref[0:1, :] + jnp.sum(full, axis=0, keepdims=True)
+        gp_ref[rows, :] = full.astype(bf16)
+
+    @pl.loop(0, blocks)
+    def _(r):
+        rows = pl.ds(pl.multiple_of(r * BLOCK, BLOCK), BLOCK)
+        qkv_grad_ref[rows, :] = to_arrival(pcol_ref, r, gp_ref[...]).astype(bf16)
+
+
+def whole(count):
+    return [pl.BlockSpec(memory_space=pltpu.VMEM)] * count
+
+
+def attend(heads, low, qkv, bias, cosine, sine, prow, pcol, start, qmask):
+    rows, wide = qkv.shape[0], heads * HEAD
+    pairs = (rows // BLOCK) * 4 * heads * BLOCK * BLOCK
+    return pl.pallas_call(
+        functools.partial(forward_kernel, heads),
+        grid_spec=pltpu.PrefetchScalarGridSpec(
+            num_scalar_prefetch=1,
+            grid=(),
+            in_specs=whole(8),
+            out_specs=whole(4),
+            scratch_shapes=[
+                pltpu.VMEM((rows, 3 * wide), bf16),
+                pltpu.VMEM((wide, rows), bf16),
+                pltpu.VMEM((rows, wide), bf16),
+            ],
+        ),
+        out_shape=[
+            jax.ShapeDtypeStruct((rows, 3 * wide), bf16),
+            jax.ShapeDtypeStruct((wide, rows), f32),
+            jax.ShapeDtypeStruct((8, rows), f32),
+            jax.ShapeDtypeStruct((rows, wide), bf16),
+        ],
+        compiler_params=pltpu.CompilerParams(vmem_limit_bytes=40 * 2**20),
+        cost_estimate=pl.CostEstimate(
+            flops=8 * rows * rows * wide + pairs * 4 * wide, bytes_accessed=20 * rows * wide, transcendentals=pairs
+        ),
+        name="attend_forward",
+    )(low, qkv, bias, cosine, sine, prow, pcol, start, qmask)
+
+
+def attend_back(heads, low, packed, outt, lse, grad, cosine, sine, prow, pcol, start, qmask, vmask, ktmask):
+    rows, wide = grad.shape
+    pairs = (rows // BLOCK) * 4 * heads * BLOCK * BLOCK
+    return pl.pallas_call(
+        functools.partial(backward_kernel, heads),
+        grid_spec=pltpu.PrefetchScalarGridSpec(
+            num_scalar_prefetch=1,
+            grid=(),
+            in_specs=whole(12),
+            out_specs=whole(2),
+            scratch_shapes=[
+                pltpu.VMEM((wide, rows), bf16),
+                pltpu.VMEM((rows, wide), f32),
+                pltpu.VMEM((rows, wide), f32),
+                pltpu.VMEM((rows, wide), f32),
+                pltpu.VMEM((rows, 3 * wide), bf16),
+            ],
+        ),
+        out_shape=[
+            jax.ShapeDtypeStruct((rows, 3 * wide), bf16),
+            jax.ShapeDtypeStruct((8, 3 * wide), f32),
+        ],
+        compiler_params=pltpu.CompilerParams(vmem_limit_bytes=40 * 2**20),
+        cost_estimate=pl.CostEstimate(
+            flops=8 * rows * rows * wide + pairs * 10 * wide, bytes_accessed=20 * rows * wide, transcendentals=pairs
+        ),
+        name="attend_backward",
+    )(low, packed, outt, lse, grad, cosine, sine, prow, pcol, start, qmask, vmask, ktmask)
 
 
 def shards(
@@ -163,7 +422,6 @@
     wide = heads * HEAD
     by_columns = (((1,), (1,)), ((), ()))
     by_rows = (((0,), (0,)), ((), ()))
-    scaling = 1.0 / math.sqrt(HEAD)
 
     def turn(x):
         return jnp.concatenate(
@@ -207,52 +465,39 @@
     packed = jnp.concatenate(
         [lax.dynamic_slice_in_dim(assignment[0], at, half) for at in block_of]
     )
-    segment, place = positions(packed, lengths[0])
-    frequency = jnp.power(
-        10000.0, -(jnp.arange(ROT // 2, dtype=f32) * 2.0 / ROT)
-    )
-    angles = place.astype(f32)[:, None] * jnp.tile(frequency, 2 * heads)[None, :]
-    cosine = jnp.cos(angles)
-    sine = jnp.sin(angles) * jnp.where(jnp.arange(ROT * heads) < ROT // 2 * heads, -1.0, 1.0)[None, :]
     split = ROT // 2 * heads
-
-    def rotate(x, sign):
-        front = x[:, : 2 * split]
-        partner = jnp.concatenate([front[:, split:], front[:, :split]], axis=1)
-        return jnp.concatenate([front * cosine + sign * sine * partner, x[:, 2 * split :]], axis=1)
+    slab = 2 * split if 2 * split % 128 == 0 else wide
+    lane = jnp.arange(wide)
+    lane_head = jnp.where(lane < 2 * split, (lane % split) // (ROT // 2), (lane - 2 * split) // (HEAD - ROT))
+    exponent = (lane[:slab] % (ROT // 2)).astype(f32) * 2.0 / ROT
+    frequency = jnp.where(lane[:slab] < 2 * split, jnp.power(10000.0, -exponent), 0.0)
+    sign = jnp.where(lane[:slab] < split, -1.0, 1.0)
+
+    def tables(place):
+        angles = place.astype(f32)[:, None] * frequency[None, :]
+        return jnp.cos(angles), jnp.sin(angles) * sign[None, :]
+
+    ordered = jnp.arange(group_rows, dtype=jnp.int32)
+    place_packed = positions(ordered, lengths[0])[1]
+    start = ordered - place_packed
+    low = start[::BLOCK] // BLOCK
+    start = start[None]
+    cos_arrival, sin_arrival = tables(positions(packed, lengths[0])[1])
+    cos_packed, sin_packed = tables(place_packed)
+    prow, pcol = packed[None], packed[:, None]
+    head_qk = (lane_head[None] == jnp.arange(heads)[:, None]).astype(bf16)
+    head_v = ((lane // HEAD)[None] == jnp.arange(heads)[:, None]).astype(bf16)
+    qmask = jnp.broadcast_to(head_qk[:, None, :], (heads, BLOCK, wide))
+    vmask = jnp.broadcast_to(head_v[:, None, :], (heads, BLOCK, wide))
+    ktmask = jnp.broadcast_to(head_qk[:, :, None], (heads, wide, BLOCK))
 
     up = jnp.dot(normed, w_up, preferred_element_type=f32) + up_bias
     act = gelu_tanh(up).astype(bf16)
-    qkv = jnp.dot(normed, w_in, preferred_element_type=f32) + qkv_bias
-    query = rotate(qkv[:, :wide], 1.0).astype(bf16)
-    key = rotate(qkv[:, wide : 2 * wide], 1.0).astype(bf16)
-    value = qkv[:, 2 * wide :].astype(bf16)
-    lane = jnp.arange(wide)
-    lane_head = jnp.where(lane < 2 * split, (lane % split) // (ROT // 2), (lane - 2 * split) // (HEAD - ROT))
-    head_qk = (lane_head[None] == jnp.arange(heads)[:, None]).astype(bf16)
-    head_v = ((lane // HEAD)[None] == jnp.arange(heads)[:, None]).astype(bf16)
-    block_rows = min(512, group_rows)
-    block_ids = jnp.arange(group_rows // block_rows, dtype=jnp.int32)
-
-    def block_scores(start):
-        q = lax.dynamic_slice_in_dim(query, start, block_rows)
-        seg = lax.dynamic_slice_in_dim(segment, start, block_rows)
-        pos = lax.dynamic_slice_in_dim(packed, start, block_rows)
-        keep = (seg[:, None] == segment[None, :]) & (packed[None, :] <= pos[:, None])
-        scores = jnp.einsum("hqe,ke->hqk", q[None] * head_qk[:, None, :], key, preferred_element_type=f32)
-        return q, jnp.where(keep[None], scores * scaling, MASKED)
-
-    def attend(index):
-        _, scores = block_scores(index * block_rows)
-        top = jnp.max(scores, axis=-1, keepdims=True)
-        raised = jnp.exp(scores - top)
-        total = jnp.sum(raised, axis=-1, keepdims=True)
-        weights = (raised / total).astype(bf16)
-        mixed = jnp.einsum("hqk,hke->qe", weights, value[None] * head_v[:, None, :], preferred_element_type=f32)
-        return mixed.astype(bf16), (top + jnp.log(total))[..., 0]
-
-    mixed, lse = lax.map(attend, block_ids)
-    mixed = mixed.reshape(group_rows, wide)
+    qkv = jnp.dot(normed, w_in, preferred_element_type=f32)
+    qkv_bias = jnp.broadcast_to(qkv_bias, (8, 3 * wide))
+    qkv_packed, outt, lse, mixed = attend(
+        heads, low, qkv, qkv_bias, cos_arrival, sin_arrival, prow, pcol, start, qmask
+    )
 
     branch = lax.dot_general(mixed, w_out, by_columns, preferred_element_type=f32)
     branch = branch + lax.dot_general(act, w_down, by_columns, preferred_element_type=f32)
@@ -267,35 +512,10 @@
     up_grad = jax.vjp(gelu_tanh, up)[1](act_grad)[0]
     up_grad_low = up_grad.astype(bf16)
 
-    def attend_back(carried, inputs):
-        key_grad, value_grad = carried
-        index, lse_blk = inputs
-        start = index * block_rows
-        q, scores = block_scores(start)
-        probs = jnp.exp(scores - lse_blk[:, :, None])
-        grad = lax.dynamic_slice_in_dim(mixed_grad, start, block_rows)
-        grad_h = grad[None] * head_v[:, None, :]
-        prob_grad = jnp.einsum("hqe,ke->hqk", grad_h, value, preferred_element_type=f32)
-        inner = jnp.sum(probs * prob_grad, axis=-1, keepdims=True)
-        score_grad = (probs * (prob_grad - inner)).astype(bf16)
-        query_grad = scaling * jnp.einsum(
-            "hqk,hke->qe", score_grad, key[None] * head_qk[:, None, :], preferred_element_type=f32
-        )
-        key_grad = key_grad + scaling * jnp.einsum(
-            "hqk,hqe->ke", score_grad, q[None] * head_qk[:, None, :], preferred_element_type=f32
-        )
-        value_grad = value_grad + jnp.einsum(
-            "hqk,hqe->ke", probs.astype(bf16), grad_h, preferred_element_type=f32
-        )
-        return (key_grad, value_grad), query_grad
-
-    zeros = jnp.zeros((group_rows, wide), f32)
-    (key_grad, value_grad), query_grad = lax.scan(attend_back, (zeros, zeros), (block_ids, lse))
-    query_grad = query_grad.reshape(group_rows, wide)
-    qkv_grad = jnp.concatenate(
-        [rotate(query_grad, -1.0), rotate(key_grad, -1.0), value_grad], axis=1
-    )
-    qkv_grad_low = qkv_grad.astype(bf16)
+    qkv_grad_low, qkv_bias_sum = attend_back(
+        heads, low, qkv_packed, outt, lse, mixed_grad, cos_packed, sin_packed, prow, pcol, start,
+        qmask, vmask, ktmask,
+    )
 
     normed_grad = lax.dot_general(qkv_grad_low, w_in, by_columns, preferred_element_type=f32)
     normed_grad = normed_grad + lax.dot_general(up_grad_low, w_up, by_columns, preferred_element_type=f32)
@@ -329,17 +549,19 @@
         return lax.dynamic_update_slice_in_dim(full, vector, c * vector.shape[0], axis=0)
 
     qkv_bias_grad = lax.dot_general(
-        jnp.sum(qkv_grad, axis=0)[None], place_of.astype(f32), by_columns,
+        qkv_bias_sum[:1], place_of.astype(f32), by_columns,
         precision=lax.Precision.HIGHEST, preferred_element_type=f32,
     )[0]
-    qkv_bias_grad, up_bias_grad, out_bias_grad = lax.psum(
-        (placed(qkv_bias_grad), placed(jnp.sum(up_grad, axis=0)), jnp.sum(grad_own.astype(f32), axis=0)),
-        ("fsdp", "ctx"),
-    )
-    gain_grad, shift_grad = lax.psum(
-        (jnp.sum(normed_grad * xhat_half, axis=0), jnp.sum(normed_grad, axis=0)),
-        ("fsdp", "ctx", "tp"),
-    )
+    bias_sums = everywhere(
+        jnp.concatenate([placed(qkv_bias_grad), placed(jnp.sum(up_grad, axis=0))]), "ctx", "fsdp"
+    )
+    qkv_bias_grad, up_bias_grad = bias_sums[: 3 * wide * m], bias_sums[3 * wide * m :]
+    out_bias_grad = everywhere(jnp.sum(out_grad[0].astype(f32), axis=0), "ctx", "fsdp")
+    norm_sums = everywhere(
+        jnp.stack([jnp.sum(normed_grad * xhat_half, axis=0), jnp.sum(normed_grad, axis=0)]),
+        "tp", "ctx", "fsdp",
+    )
+    gain_grad, shift_grad = norm_sums[0], norm_sums[1]
     return (
         result[None],
         input_grad[None],

time: 1170 us -> 826 us (0.71)
  matrix products: 364 us -> 149 us
  blocking collectives: 130 us -> 0 us
  other arithmetic: 176 us -> 85.8 us
  Pallas kernels: 0 us -> 89.2 us
  local copies, waits for them, and re-layouts: 123 us -> 76.7 us
  starting transfers between devices: 163 us -> 199 us
  waiting for transfers between devices: 194 us -> 214 us
    dot_general x30 -> x2, matrix products: 216 us -> 12.4 us  [the longest x1 11.3 us: shards(): qkv = jnp.dot(normed, w_in, preferred_element_type=f32)]
    psum x2 -> x0, blocking collectives: 130 us -> none  [the longest x1 91.9 us: shards(): lax.psum((placed(qkv_bias_grad), placed(jnp.sum(up_grad, axis=0)), jnp.su...]
    pallas_call x0 -> x2, Pallas kernels: none -> 89.2 us  [the longest x1 45.3 us: attend_back(): pl.pallas_call(functools.partial(backward_kernel, heads), grid_spec=pltpu...]
    ppermute x40 -> x53, starting transfers between devices: 24.3 us -> 98.6 us  [swap(): return lax.ppermute(x, axis, [(i, i ^ bit) for i in range(size)])]
    ppermute x40 -> x53, waiting for transfers between devices: 76.7 us -> 128 us  [swap(): return lax.ppermute(x, axis, [(i, i ^ bit) for i in range(size)])]
    convert_element_type x5 -> x2, other arithmetic: 48.3 us -> 0.01 us  [the longest x1 0.01 us: tables(): angles = place.astype(f32)[:, None] * frequency[None, :]]
    ppermute x12, starting transfers between devices: 82.7 us -> 47.3 us  [line_scatter(): lax.ppermute(send_up, 'fsdp', [(i, i + 1) for i in range(0, min(s, n - 1))])]
    reduce_sum x6 -> x2, other arithmetic: 26.6 us -> 1.06 us  [the longest x1 0.69 us: shards(): centred = source - jnp.mean(source, axis=-1, keepdims=True)]
  transfers between devices with their start and end apart: 88 -> 101, of which waited for: 32 -> 35; matrix products, arithmetic and copies ran while one was open for 54% -> 36% of each run, Pallas kernels for 0% -> 11%
where the time goes in v2:
time: 826 us; the launch traced here: 817 us
  waiting for transfers between devices  214 us (26%)
  starting transfers between devices  199 us (24%)
  matrix products  149 us (18%)
  Pallas kernels  89.2 us (11%)
  other arithmetic  85.8 us (10%)
  local copies, waits for them, and re-layouts  76.7 us (9%)
    ppermute x53, waiting for transfers between devices, swap(): return lax.ppermute(x, axis, [(i, i ^ bit) for i in range(size)])  128 us
    ppermute x53, starting transfers between devices, swap(): return lax.ppermute(x, axis, [(i, i ^ bit) for i in range(size)])  98.6 us
    ppermute x12, starting transfers between devices, line_scatter(): lax.ppermute(send_up, 'fsdp', [(i, i + 1) for i in range(0, min(s, n - 1))])  47.3 us
    pallas_call x1, Pallas kernels, attend_back(): pl.pallas_call(functools.partial(backward_kernel, heads), grid_spec=pltpu...  45.3 us
    pallas_call x1, Pallas kernels, attend(): pl.pallas_call(functools.partial(forward_kernel, heads), grid_spec=pltpu....  43.9 us
    ppermute x12, waiting for transfers between devices, line_gather(): down = lax.ppermute(down, 'fsdp', [(i, i - 1) for i in range(1, n - s + 1)])  42.7 us
    dot_general x4, matrix products, summed(): lax.dot_general(left, right, by_rows, preferred_element_type=f32)  40.8 us
    unnamed x188, local copies, waits for them, and re-layouts  24.9 us
  transfers between devices with their start and end apart: 101, of which 35 were waited for; matrix products, arithmetic and copies ran while one was open for 36% of the time, Pallas kernels for 11%

profile of v2, /device:TPU:0, one launch (start us, length us, event | category | flops | bytes accessed | tf_op | source)
XLA Modules:
  0.0 816.9 jit_solution(13392574691191460647)
XLA Ops:
  3.1 6.3 collective-permute-start.14
  39.0 5.9 collective-permute-done.79
  68.2 7.4 fusion.34
  76.1 4.3 collective-permute-done.8
  85.4 17.8 %collective-permute-done.2 = bf16[256,2048]{1,0:T(8,128)(2,1)} collective-permute-done((bf16[256,2048]{1,0:T(8,128)(2,1)}, bf16[256,2048]{1,0:T(8,128)(2,1)}, u32[]{:S(2)}, u32[]{:S(2)}) %collective-permute-start.2) | collective-permute-done | bytes 1048608 | tf_op jit(solution)/shard_map/ppermute | solution.py:33
  115.7 6.9 collective-permute-done.10
  126.6 7.1 collective-permute-done.42
  138.7 4.4 collective-permute-start.26
  155.5 10.3 %collective-permute-done.26 = bf16[512,1024]{1,0:T(8,128)(2,1)S(1)} collective-permute-done((bf16[512,1024]{1,0:T(8,128)(2,1)S(1)}, bf16[512,1024]{1,0:T(8,128)(2,1)S(1)}, u32[]{:S(2)}, u32[]{:S(2)}) %collective-permute-start.26) | collective-permute-done | bytes 1048608 | tf_op jit(solution)/shard_map/ppermute | solution.py:51
  173.1 5.8 convolution_convert_fusion.4.grad_ref
  186.9 7.1 collective-permute-done.28
  199.3 22.1 %collective-permute-done.11 = bf16[512,768]{1,0:T(8,128)(2,1)S(1)} collective-permute-done((bf16[512,768]{1,0:T(8,128)(2,1)S(1)}, bf16[512,768]{1,0:T(8,128)(2,1)S(1)}, u32[]{:S(2)}, u32[]{:S(2)}) %collective-permute-start.11) | collective-permute-done | bytes 786464 | tf_op jit(solution)/shard_map/ppermute | solution.py:52
  221.6 11.3 %fusion.44.qkv_ref = f32[2048,768]{1,0:T(8,128)} fusion(bf16[2048,2048]{1,0:T(8,128)(2,1)} %constant_dynamic-update-slice_fusion, bf16[512,768]{1,0:T(8,128)(2,1)S(1)} %broadcast_select_fusion.6, bf16[512,768]{1,0:T(8,128)(2,1)S(1)} %broadcast_select_fusion.7, bf16[512,768]{1,0:T(8,128)(2,1)S(1)} %broadcast_select_fusion.8, bf16[512,768]{1,0:T(8,128)(2,1)} %fusion.25), kind=kOutput, calls=%fused_computation.134 | convolution fusion | flops 6455033856 | bytes 17825792 | tf_op jit(solution)/shard_map/dot_general | solution.py:496
  232.9 43.9 %attend_forward.1 = (bf16[2048,768]{1,0:T(8,128)(2,1)S(1)}, f32[256,2048]{1,0:T(8,128)S(1)}, f32[8,2048]{1,0:T(8,128)S(1)}, bf16[2048,256]{1,0:T(8,128)(2,1)S(1)}) custom-call(s32[8]{0:T(128)S(1)} %and_select_fusion.5.low_ref, f32[2048,768]{1,0:T(8,128)} %fusion.44.qkv_ref, f32[8,768]{1,0:T(8,128)S(1)} %broadcast_in_dim.53.bias_ref, ...), custom_call_target="tpu_custom_call" | custom-call | flops 17179869184 | bytes 10485760 | tf_op jit(solution)/shard_map/attend_forward/pallas_call | solution.py:339
  282.7 45.3 %attend_backward.1 = (bf16[2048,768]{1,0:T(8,128)(2,1)S(1)}, f32[8,768]{1,0:T(8,128)S(1)}) custom-call(s32[8]{0:T(128)S(1)} %and_select_fusion.5.low_ref, bf16[2048,768]{1,0:T(8,128)(2,1)S(1)} %get-tuple-element.19.packed_ref, f32[256,2048]{1,0:T(8,128)S(1)} %get-tuple-element.20.outt_ref, f32[8,2048]{1,0:T(8,128)S(1)} %get-tuple-element.21.lse_ref, ...), custom_call_target="tpu_custom_call" | custom-call | flops 30064771072 | bytes 10485760 | tf_op jit(solution)/shard_map/attend_backward/pallas_call | solution.py:369
  328.1 11.6 %convolution_convert_fusion.2 = bf16[2048,768]{1,0:T(8,128)(2,1)} fusion(bf16[2048,2048]{1,0:T(8,128)(2,1)} %constant_dynamic-update-slice_fusion, bf16[2048,768]{1,0:T(8,128)(2,1)S(1)} %get-tuple-element.22), kind=kOutput, calls=%fused_computation.28 | convolution fusion | flops 6444023808 | bytes 14680064 | tf_op jit(solution)/shard_map/dot_general | solution.py:537
  349.6 12.9 %collective-permute-start.57 = (bf16[512,768]{1,0:T(8,128)(2,1)}, bf16[512,768]{1,0:T(8,128)(2,1)}, u32[]{:S(2)}, u32[]{:S(2)}) collective-permute-start(bf16[512,768]{1,0:T(8,128)(2,1)} %get-tuple-element.61), channel_id=1, source_target_pairs={{0,8},{1,9},{2,10},{3,11},{4,12},{5,13},{6,14},{7,15}} | collective-permute-start | bytes 2359304 | tf_op jit(solution)/shard_map/ppermute | solution.py:65
  370.2 13.4 %fusion.43 = f32[2048,1024]{1,0:T(8,128)} fusion(bf16[2048,2048]{1,0:T(8,128)(2,1)} %constant_dynamic-update-slice_fusion, bf16[512,1024]{1,0:T(8,128)(2,1)S(1)} %broadcast_select_fusion.1, bf16[512,1024]{1,0:T(8,128)(2,1)S(1)} %copy-done.40, bf16[512,1024]{1,0:T(8,128)(2,1)S(1)} %broadcast_select_fusion.5, bf16[512,1024]{1,0:T(8,128)(2,1)S(1)} %copy-done.29), kind=kOutput, calls=%fused_computation.131 | convolution fusion | flops 8606711808 | bytes 20971520 | tf_op jit(solution)/shard_map/dot_general | solution.py:494
  383.6 12.9 %convolution_convert_fusion = bf16[2048,1024]{0,1:T(8,128)(2,1)S(1)} fusion(bf16[2048,2048]{1,0:T(8,128)(2,1)S(1)} %bitcast.195, f32[2048,1024]{1,0:T(8,128)} %fusion.43, f32[1024]{0:T(1024)S(1)} %dynamic-slice_convert_fusion), kind=kOutput, calls=%fused_computation.26 | convolution fusion | flops 8613003264 | bytes 20975616 | tf_op jit(solution)/shard_map/dot_general | solution.py:537
  399.6 20.3 %fusion.81 = (f32[1024]{0:T(1024)S(1)}, bf16[2048,1024]{1,0:T(8,128)(2,1)}) fusion(f32[2048,1024]{1,0:T(8,128)} %fusion.43, f32[1024]{0:T(1024)S(1)} %dynamic-slice_convert_fusion, bf16[2048,2048]{1,0:T(8,128)(2,1)} %constant_dynamic-update-slice_fusion.10, bf16[512,1024]{1,0:T(8,128)(2,1)S(1)} %broadcast_select_fusion, ...), kind=kOutput, calls=%fused_computation.319 | convolution fusion | flops 8652848128 | bytes 25174016 | tf_op jit(solution)/shard_map/dot_general | solution.py:511
  419.8 14.0 %convolution_convert_fusion.1 = bf16[2048,1024]{0,1:T(8,128)(2,1)} fusion(bf16[2048,2048]{1,0:T(8,128)(2,1)} %constant_dynamic-update-slice_fusion, bf16[2048,1024]{1,0:T(8,128)(2,1)} %get-tuple-element.147), kind=kOutput, calls=%fused_computation.27 | convolution fusion | flops 8592031744 | bytes 16777216 | tf_op jit(solution)/shard_map/dot_general | solution.py:537
  433.8 14.0 %fusion.21 = f32[2048,2048]{1,0:T(8,128)} fusion(bf16[2048,1024]{1,0:T(8,128)(2,1)} %get-tuple-element.147, bf16[512,1024]{1,0:T(8,128)(2,1)S(1)} %broadcast_select_fusion.1, bf16[512,1024]{1,0:T(8,128)(2,1)S(1)} %copy-done.40, bf16[512,1024]{1,0:T(8,128)(2,1)S(1)} %broadcast_select_fusion.5, bf16[512,1024]{1,0:T(8,128)(2,1)S(1)} %copy-done.29), kind=kOutput, calls=%fused_computation.69 | convolution fusion | flops 8606711808 | bytes 25165824 | tf_op jit(solution)/shard_map/dot_general | solution.py:521
  447.8 15.6 %fusion.42 = f32[2048,2048]{1,0:T(8,128)} fusion(bf16[512,1024]{1,0:T(8,128)(2,1)S(1)} %broadcast_select_fusion, bf16[512,1024]{1,0:T(8,128)(2,1)S(1)} %copy-done.41, bf16[512,1024]{1,0:T(8,128)(2,1)S(1)} %broadcast_select_fusion.4, bf16[512,1024]{1,0:T(8,128)(2,1)S(1)} %copy-done.31, f32[2048,1024]{1,0:T(8,128)} %fusion.43, ...), kind=kOutput, calls=%fused_computation.130 | convolution fusion | flops 8627683328 | bytes 29364224 | tf_op jit(solution)/shard_map/dot_general | solution.py:503
  464.9 4.5 collective-permute-start.92
  469.5 13.1 %add_convert_fusion = bf16[2048,2048]{1,0:T(8,128)(2,1)} fusion(f32[2048,2048]{1,0:T(8,128)} %fusion.21, bf16[2048,768]{1,0:T(8,128)(2,1)S(1)} %copy-done.5, bf16[512,768]{1,0:T(8,128)(2,1)} %copy-done.47, bf16[512,768]{1,0:T(8,128)(2,1)S(1)} %copy-done.44, bf16[512,768]{1,0:T(8,128)(2,1)} %copy-done.48, bf16[512,768]{1,0:T(8,128)(2,1)} %fusion.25), kind=kOutput, calls=%fused_computation | convolution fusion | flops 6463422464 | bytes 31457280 | tf_op jit(solution)/shard_map/dot_general | solution.py:520
  488.4 10.1 %add_convert_fusion.1 = bf16[2048,2048]{1,0:T(8,128)(2,1)} fusion(f32[2048,2048]{1,0:T(8,128)} %fusion.42, bf16[2048,256]{1,0:T(8,128)(2,1)S(1)} %copy-done.3, bf16[512,256]{1,0:T(8,128)(2,1)S(1)} %copy-done.27, bf16[512,256]{1,0:T(8,128)(2,1)S(1)} %copy-done.23, bf16[512,256]{1,0:T(8,128)(2,1)S(1)} %copy-done.25, bf16[512,256]{1,0:T(8,128)(2,1)S(1)} %copy-done.21), kind=kOutput, calls=%fused_computation.1 | convolution fusion | flops 2160066560 | bytes 27262976 | tf_op jit(solution)/shard_map/dot_general | solution.py:502
  503.1 5.8 collective-permute-done.58
  509.7 5.0 slice_bitcast_fusion
  516.0 10.9 %collective-permute-start.68 = (f32[7168]{0:T(1024)S(1)}, f32[7168]{0:T(1024)S(1)}, u32[]{:S(2)}, u32[]{:S(2)}) collective-permute-start(f32[7168]{0:T(1024)S(1)} %add.492), channel_id=1, source_target_pairs={{0,8},{8,0},{16,24},{24,16},{1,9},{9,1},{17,25},{25,17},{2,10},{10... | collective-permute-start | bytes 86024 | tf_op jit(solution)/shard_map/ppermute | solution.py:33
  529.0 4.6 collective-permute-start.59
  535.0 37.6 %collective-permute-start.82 = (f32[2048]{0:T(1024)S(1)}, f32[2048]{0:T(1024)S(1)}, u32[]{:S(2)}, u32[]{:S(2)}) collective-permute-start(f32[2048]{0:T(1024)S(1)} %copy-done.63), channel_id=1, source_target_pairs={{0,16},{8,24},{16,0},{24,8},{1,17},{9,25},{17,1},{25,9},{2,18},{10... | collective-permute-start | bytes 24584 | tf_op jit(solution)/shard_map/ppermute | solution.py:33
  578.6 7.5 collective-permute-done.82
  599.0 17.4 %collective-permute-done.69 = f32[7168]{0:T(1024)S(1)} collective-permute-done((f32[7168]{0:T(1024)S(1)}, f32[7168]{0:T(1024)S(1)}, u32[]{:S(2)}, u32[]{:S(2)}) %collective-permute-start.69) | collective-permute-done | bytes 28704 | tf_op jit(solution)/shard_map/ppermute | solution.py:33
  626.8 4.9 collective-permute-done.64
  646.0 3.7 collective-permute-done.65
  649.7 9.0 %collective-permute-start.85 = (bf16[512,1024]{0,1:T(8,128)(2,1)S(1)}, bf16[512,1024]{0,1:T(8,128)(2,1)S(1)}, u32[]{:S(2)}, u32[]{:S(2)}) collective-permute-start(bf16[512,1024]{0,1:T(8,128)(2,1)S(1)} %get-tuple-element.39), channel_id=1, source_target_pairs={{0,8},{8,16},{16,24},{1,9},{9,17},{17,25},{2,10},{10,18},{18,26},{... | collective-permute-start | bytes 3145736 | tf_op jit(solution)/shard_map/ppermute | solution.py:65
  662.7 4.0 collective-permute-done.97
  670.0 9.6 %collective-permute-done.85 = bf16[512,1024]{0,1:T(8,128)(2,1)S(1)} collective-permute-done((bf16[512,1024]{0,1:T(8,128)(2,1)S(1)}, bf16[512,1024]{0,1:T(8,128)(2,1)S(1)}, u32[]{:S(2)}, u32[]{:S(2)}) %collective-permute-start.85) | collective-permute-done | bytes 1048608 | tf_op jit(solution)/shard_map/ppermute | solution.py:65
  680.3 7.6 collective-permute-done.88
  694.0 3.7 collective-permute-done.100
  699.9 6.0 fusion.6
  708.5 4.1 fusion.7
  712.8 5.5 collective-permute-done.47
  724.3 8.9 %collective-permute-done.33 = bf16[128,2048]{1,0:T(8,128)(2,1)S(1)} collective-permute-done((bf16[128,2048]{1,0:T(8,128)(2,1)S(1)}, bf16[128,2048]{1,0:T(8,128)(2,1)S(1)}, u32[]{:S(2)}, u32[]{:S(2)}) %collective-permute-start.33) | collective-permute-done | bytes 524320 | tf_op jit(solution)/shard_map/ppermute | solution.py:33
  737.0 20.1 %collective-permute-done.48 = bf16[256,2048]{1,0:T(8,128)(2,1)S(1)} collective-permute-done((bf16[256,2048]{1,0:T(8,128)(2,1)S(1)}, bf16[256,2048]{1,0:T(8,128)(2,1)S(1)}, u32[]{:S(2)}, u32[]{:S(2)}) %collective-permute-start.48) | collective-permute-done | bytes 1048608 | tf_op jit(solution)/shard_map/ppermute | solution.py:33
  761.3 13.3 %collective-permute-done.34 = bf16[256,2048]{1,0:T(8,128)(2,1)S(1)} collective-permute-done((bf16[256,2048]{1,0:T(8,128)(2,1)S(1)}, bf16[256,2048]{1,0:T(8,128)(2,1)S(1)}, u32[]{:S(2)}, u32[]{:S(2)}) %collective-permute-start.34) | collective-permute-done | bytes 1048608 | tf_op jit(solution)/shard_map/ppermute | solution.py:33
  782.9 7.5 collective-permute-start.55
  809.1 6.7 maximum_select_fusion
  (517 shorter events, 262.2 us)
Async XLA Ops:
  1.8 35.1 %collective-permute-start.15 = (bf16[512,256]{1,0:T(8,128)(2,1)S(1)}, bf16[512,256]{1,0:T(8,128)(2,1)}, u32[]{:S(2)}, u32[]{:S(2)}) collective-permute-start(bf16[512,256]{1,0:T(8,128)(2,1)S(1)} %constant_dynamic-slice_fusion.37), channel_id=1, source_target_pairs={{8,0},{16,8},{24,16},{9,1},{17,9},{25,17},{10,2},{18,10},{26,18},{... | collective-permute-start | bytes 786440 | tf_op jit(solution)/shard_map/ppermute | solution.py:52
  3.1 35.1 %collective-permute-start.14 = (bf16[512,256]{1,0:T(8,128)(2,1)S(1)}, bf16[512,256]{1,0:T(8,128)(2,1)}, u32[]{:S(2)}, u32[]{:S(2)}) collective-permute-start(bf16[512,256]{1,0:T(8,128)(2,1)S(1)} %constant_dynamic-slice_fusion.37), channel_id=1, source_target_pairs={{0,8},{8,16},{16,24},{1,9},{9,17},{17,25},{2,10},{10,18},{18,26},{... | collective-permute-start | bytes 786440 | tf_op jit(solution)/shard_map/ppermute | solution.py:51
  19.9 62.7 %collective-permute-start.38 = (bf16[256,2048]{1,0:T(8,128)(2,1)}, bf16[256,2048]{1,0:T(8,128)(2,1)}, u32[]{:S(2)}, u32[]{:S(2)}) collective-permute-start(bf16[256,2048]{1,0:T(8,128)(2,1)} %slice.258), channel_id=1, source_target_pairs={{0,2},{2,0},{4,6},{6,4},{1,3},{3,1},{5,7},{7,5},{8,10},{10,8},{12,... | collective-permute-start | bytes 3145736 | tf_op jit(solution)/shard_map/ppermute | solution.py:33
  23.6 42.9 %collective-permute-start.9 = (bf16[512,768]{1,0:T(8,128)(2,1)}, bf16[512,768]{1,0:T(8,128)(2,1)}, u32[]{:S(2)}, u32[]{:S(2)}) collective-permute-start(bf16[512,768]{1,0:T(8,128)(2,1)} %fusion.25), channel_id=1, source_target_pairs={{8,0},{16,8},{24,16},{9,1},{17,9},{25,17},{10,2},{18,10},{26,18},{... | collective-permute-start | bytes 2359304 | tf_op jit(solution)/shard_map/ppermute | solution.py:52
  58.1 26.4 %collective-permute-start.40 = (bf16[256,2048]{1,0:T(8,128)(2,1)}, bf16[256,2048]{1,0:T(8,128)(2,1)}, u32[]{:S(2)}, u32[]{:S(2)}) collective-permute-start(bf16[256,2048]{1,0:T(8,128)(2,1)} %slice.258), channel_id=1, source_target_pairs={{0,4},{2,6},{4,0},{6,2},{1,5},{3,7},{5,1},{7,3},{8,12},{10,14},{12... | collective-permute-start | bytes 3145736 | tf_op jit(solution)/shard_map/ppermute | solution.py:33
  66.5 36.7 %collective-permute-start.2 = (bf16[256,2048]{1,0:T(8,128)(2,1)}, bf16[256,2048]{1,0:T(8,128)(2,1)}, u32[]{:S(2)}, u32[]{:S(2)}) collective-permute-start(bf16[256,2048]{1,0:T(8,128)(2,1)} %slice.246), channel_id=1, source_target_pairs={{0,4},{2,6},{4,0},{6,2},{1,5},{3,7},{5,1},{7,3},{8,12},{10,14},{12... | collective-permute-start | bytes 3145736 | tf_op jit(solution)/shard_map/ppermute | solution.py:33
  81.3 32.0 %collective-permute-start.21 = (bf16[512,1024]{1,0:T(8,128)(2,1)}, bf16[512,1024]{1,0:T(8,128)(2,1)S(1)}, u32[]{:S(2)}, u32[]{:S(2)}) collective-permute-start(bf16[512,1024]{1,0:T(8,128)(2,1)} %constant_dynamic-slice_fusion.36), channel_id=1, source_target_pairs={{8,0},{16,8},{24,16},{9,1},{17,9},{25,17},{10,2},{18,10},{26,18},{... | collective-permute-start | bytes 3145736 | tf_op jit(solution)/shard_map/ppermute | solution.py:52
  82.7 39.9 %collective-permute-start.10 = (bf16[512,768]{1,0:T(8,128)(2,1)}, bf16[512,768]{1,0:T(8,128)(2,1)S(1)}, u32[]{:S(2)}, u32[]{:S(2)}) collective-permute-start(bf16[512,768]{1,0:T(8,128)(2,1)} %collective-permute-done.9), channel_id=1, source_target_pairs={{8,0},{16,8},{9,1},{17,9},{10,2},{18,10},{11,3},{19,11},{12,4},{20... | collective-permute-start | bytes 2359304 | tf_op jit(solution)/shard_map/ppermute | solution.py:52
  84.5 39.3 %collective-permute-start.12 = (bf16[512,768]{1,0:T(8,128)(2,1)}, bf16[512,768]{1,0:T(8,128)(2,1)S(1)}, u32[]{:S(2)}, u32[]{:S(2)}) collective-permute-start(bf16[512,768]{1,0:T(8,128)(2,1)} %copy-done.45), channel_id=1, source_target_pairs={{8,16},{16,24},{9,17},{17,25},{10,18},{18,26},{11,19},{19,27},{12,... | collective-permute-start | bytes 2359304 | tf_op jit(solution)/shard_map/ppermute | solution.py:51
  85.2 39.3 %collective-permute-start.39 = (bf16[256,2048]{1,0:T(8,128)(2,1)}, bf16[256,2048]{1,0:T(8,128)(2,1)S(1)}, u32[]{:S(2)}, u32[]{:S(2)}) collective-permute-start(bf16[256,2048]{1,0:T(8,128)(2,1)} %collective-permute-done.38), channel_id=1, source_target_pairs={{0,1},{1,0},{2,3},{3,2},{4,5},{5,4},{6,7},{7,6},{8,9},{9,8},{10,11... | collective-permute-start | bytes 3145736 | tf_op jit(solution)/shard_map/ppermute | solution.py:33
  103.2 30.6 %collective-permute-start.41 = (bf16[256,2048]{1,0:T(8,128)(2,1)}, bf16[256,2048]{1,0:T(8,128)(2,1)S(1)}, u32[]{:S(2)}, u32[]{:S(2)}) collective-permute-start(bf16[256,2048]{1,0:T(8,128)(2,1)} %collective-permute-done.40), channel_id=1, source_target_pairs={{0,1},{1,0},{2,3},{3,2},{4,5},{5,4},{6,7},{7,6},{8,9},{9,8},{10,11... | collective-permute-start | bytes 3145736 | tf_op jit(solution)/shard_map/ppermute | solution.py:33
  138.7 27.2 %collective-permute-start.26 = (bf16[512,1024]{1,0:T(8,128)(2,1)S(1)}, bf16[512,1024]{1,0:T(8,128)(2,1)S(1)}, u32[]{:S(2)}, u32[]{:S(2)}) collective-permute-start(bf16[512,1024]{1,0:T(8,128)(2,1)S(1)} %copy-done.30), channel_id=1, source_target_pairs={{0,8},{8,16},{16,24},{1,9},{9,17},{17,25},{2,10},{10,18},{18,26},{... | collective-permute-start | bytes 3145736 | tf_op jit(solution)/shard_map/ppermute | solution.py:51
  165.9 28.2 %collective-permute-start.28 = (bf16[512,1024]{1,0:T(8,128)(2,1)S(1)}, bf16[512,1024]{1,0:T(8,128)(2,1)S(1)}, u32[]{:S(2)}, u32[]{:S(2)}) collective-permute-start(bf16[512,1024]{1,0:T(8,128)(2,1)S(1)} %collective-permute-done.27), channel_id=1, source_target_pairs={{8,0},{16,8},{9,1},{17,9},{10,2},{18,10},{11,3},{19,11},{12,4},{20... | collective-permute-start | bytes 3145736 | tf_op jit(solution)/shard_map/ppermute | solution.py:52
  167.2 28.2 %collective-permute-start.30 = (bf16[512,1024]{1,0:T(8,128)(2,1)S(1)}, bf16[512,1024]{1,0:T(8,128)(2,1)}, u32[]{:S(2)}, u32[]{:S(2)}) collective-permute-start(bf16[512,1024]{1,0:T(8,128)(2,1)S(1)} %collective-permute-done.26), channel_id=1, source_target_pairs={{8,16},{16,24},{9,17},{17,25},{10,18},{18,26},{11,19},{19,27},{12,... | collective-permute-start | bytes 3145736 | tf_op jit(solution)/shard_map/ppermute | solution.py:51
  182.3 39.1 %collective-permute-start.11 = (bf16[512,768]{1,0:T(8,128)(2,1)S(1)}, bf16[512,768]{1,0:T(8,128)(2,1)S(1)}, u32[]{:S(2)}, u32[]{:S(2)}) collective-permute-start(bf16[512,768]{1,0:T(8,128)(2,1)S(1)} %collective-permute-done.10), channel_id=1, source_target_pairs={{8,0},{9,1},{10,2},{11,3},{12,4},{13,5},{14,6},{15,7}} | collective-permute-start | bytes 2359304 | tf_op jit(solution)/shard_map/ppermute | solution.py:52
  184.4 179.0 %collective-permute-start.25 = (bf16[512,1024]{1,0:T(8,128)(2,1)}, bf16[512,1024]{1,0:T(8,128)(2,1)}, u32[]{:S(2)}, u32[]{:S(2)}) collective-permute-start(bf16[512,1024]{1,0:T(8,128)(2,1)} %collective-permute-done.24), channel_id=1, source_target_pairs={{16,24},{17,25},{18,26},{19,27},{20,28},{21,29},{22,30},{23,31}} | collective-permute-start | bytes 3145736 | tf_op jit(solution)/shard_map/ppermute | solution.py:51
  194.1 172.4 %collective-permute-start.23 = (bf16[512,1024]{1,0:T(8,128)(2,1)}, bf16[512,1024]{1,0:T(8,128)(2,1)}, u32[]{:S(2)}, u32[]{:S(2)}) collective-permute-start(bf16[512,1024]{1,0:T(8,128)(2,1)} %collective-permute-done.22), channel_id=1, source_target_pairs={{8,0},{9,1},{10,2},{11,3},{12,4},{13,5},{14,6},{15,7}} | collective-permute-start | bytes 3145736 | tf_op jit(solution)/shard_map/ppermute | solution.py:52
  195.4 201.2 %collective-permute-start.31 = (bf16[512,1024]{1,0:T(8,128)(2,1)}, bf16[512,1024]{1,0:T(8,128)(2,1)}, u32[]{:S(2)}, u32[]{:S(2)}) collective-permute-start(bf16[512,1024]{1,0:T(8,128)(2,1)} %collective-permute-done.30), channel_id=1, source_target_pairs={{16,24},{17,25},{18,26},{19,27},{20,28},{21,29},{22,30},{23,31}} | collective-permute-start | bytes 3145736 | tf_op jit(solution)/shard_map/ppermute | solution.py:51
  280.2 61.0 %collective-permute-start.70 = (bf16[512,256]{0,1:T(8,128)(2,1)}, bf16[512,256]{0,1:T(8,128)(2,1)S(1)}, u32[]{:S(2)}, u32[]{:S(2)}) collective-permute-start(bf16[512,256]{0,1:T(8,128)(2,1)} %get-tuple-element.110), channel_id=1, source_target_pairs={{0,8},{1,9},{2,10},{3,11},{4,12},{5,13},{6,14},{7,15}} | collective-permute-start | bytes 786440 | tf_op jit(solution)/shard_map/ppermute | solution.py:65
  281.6 59.5 %collective-permute-start.73 = (bf16[512,256]{0,1:T(8,128)(2,1)}, bf16[512,256]{0,1:T(8,128)(2,1)S(1)}, u32[]{:S(2)}, u32[]{:S(2)}) collective-permute-start(bf16[512,256]{0,1:T(8,128)(2,1)} %get-tuple-element.111), channel_id=1, source_target_pairs={{24,16},{25,17},{26,18},{27,19},{28,20},{29,21},{30,22},{31,23}} | collective-permute-start | bytes 786440 | tf_op jit(solution)/shard_map/ppermute | solution.py:66
  348.3 50.0 %collective-permute-start.29 = (bf16[512,1024]{1,0:T(8,128)(2,1)}, bf16[512,1024]{1,0:T(8,128)(2,1)S(1)}, u32[]{:S(2)}, u32[]{:S(2)}) collective-permute-start(bf16[512,1024]{1,0:T(8,128)(2,1)} %copy-done.39), channel_id=1, source_target_pairs={{8,0},{9,1},{10,2},{11,3},{12,4},{13,5},{14,6},{15,7}} | collective-permute-start | bytes 3145736 | tf_op jit(solution)/shard_map/ppermute | solution.py:52
  349.6 133.3 %collective-permute-start.57 = (bf16[512,768]{1,0:T(8,128)(2,1)}, bf16[512,768]{1,0:T(8,128)(2,1)}, u32[]{:S(2)}, u32[]{:S(2)}) collective-permute-start(bf16[512,768]{1,0:T(8,128)(2,1)} %get-tuple-element.61), channel_id=1, source_target_pairs={{0,8},{1,9},{2,10},{3,11},{4,12},{5,13},{6,14},{7,15}} | collective-permute-start | bytes 2359304 | tf_op jit(solution)/shard_map/ppermute | solution.py:65
  363.5 120.4 %collective-permute-start.60 = (bf16[512,768]{1,0:T(8,128)(2,1)}, bf16[512,768]{1,0:T(8,128)(2,1)}, u32[]{:S(2)}, u32[]{:S(2)}) collective-permute-start(bf16[512,768]{1,0:T(8,128)(2,1)} %get-tuple-element.62), channel_id=1, source_target_pairs={{24,16},{25,17},{26,18},{27,19},{28,20},{29,21},{30,22},{31,23}} | collective-permute-start | bytes 2359304 | tf_op jit(solution)/shard_map/ppermute | solution.py:66
  366.5 132.6 %collective-permute-start.72 = (bf16[512,256]{0,1:T(8,128)(2,1)}, bf16[512,256]{0,1:T(8,128)(2,1)}, u32[]{:S(2)}, u32[]{:S(2)}) collective-permute-start(bf16[512,256]{0,1:T(8,128)(2,1)} %get-tuple-element.106), channel_id=1, source_target_pairs={{0,8},{8,16},{16,24},{1,9},{9,17},{17,25},{2,10},{10,18},{18,26},{... | collective-permute-start | bytes 786440 | tf_op jit(solution)/shard_map/ppermute | solution.py:65
  396.6 103.8 %collective-permute-start.75 = (bf16[512,256]{0,1:T(8,128)(2,1)}, bf16[512,256]{0,1:T(8,128)(2,1)}, u32[]{:S(2)}, u32[]{:S(2)}) collective-permute-start(bf16[512,256]{0,1:T(8,128)(2,1)} %get-tuple-element.107), channel_id=1, source_target_pairs={{8,0},{16,8},{24,16},{9,1},{17,9},{25,17},{10,2},{18,10},{26,18},{... | collective-permute-start | bytes 786440 | tf_op jit(solution)/shard_map/ppermute | solution.py:66
  464.9 68.7 %collective-permute-start.92 = (bf16[512,1024]{0,1:T(8,128)(2,1)}, bf16[512,1024]{0,1:T(8,128)(2,1)}, u32[]{:S(2)}, u32[]{:S(2)}) collective-permute-start(bf16[512,1024]{0,1:T(8,128)(2,1)} %get-tuple-element.37), channel_id=1, source_target_pairs={{0,8},{1,9},{2,10},{3,11},{4,12},{5,13},{6,14},{7,15}} | collective-permute-start | bytes 3145736 | tf_op jit(solution)/shard_map/ppermute | solution.py:65
  499.7 35.3 %collective-permute-start.95 = (bf16[512,1024]{0,1:T(8,128)(2,1)S(1)}, bf16[512,1024]{0,1:T(8,128)(2,1)S(1)}, u32[]{:S(2)}, u32[]{:S(2)}) collective-permute-start(bf16[512,1024]{0,1:T(8,128)(2,1)S(1)} %copy-done.42), channel_id=1, source_target_pairs={{24,16},{25,17},{26,18},{27,19},{28,20},{29,21},{30,22},{31,23}} | collective-permute-start | bytes 3145736 | tf_op jit(solution)/shard_map/ppermute | solution.py:66
  500.4 74.2 %collective-permute-start.83 = (bf16[512,1024]{0,1:T(8,128)(2,1)S(1)}, bf16[512,1024]{0,1:T(8,128)(2,1)S(1)}, u32[]{:S(2)}, u32[]{:S(2)}) collective-permute-start(bf16[512,1024]{0,1:T(8,128)(2,1)S(1)} %get-tuple-element.43), channel_id=1, source_target_pairs={{0,8},{1,9},{2,10},{3,11},{4,12},{5,13},{6,14},{7,15}} | collective-permute-start | bytes 3145736 | tf_op jit(solution)/shard_map/ppermute | solution.py:65
  502.4 73.4 %collective-permute-start.86 = (bf16[512,1024]{0,1:T(8,128)(2,1)S(1)}, bf16[512,1024]{0,1:T(8,128)(2,1)S(1)}, u32[]{:S(2)}, u32[]{:S(2)}) collective-permute-start(bf16[512,1024]{0,1:T(8,128)(2,1)S(1)} %get-tuple-element.44), channel_id=1, source_target_pairs={{24,16},{25,17},{26,18},{27,19},{28,20},{29,21},{30,22},{31,23}} | collective-permute-start | bytes 3145736 | tf_op jit(solution)/shard_map/ppermute | solution.py:66
  529.0 57.2 %collective-permute-start.59 = (bf16[512,768]{1,0:T(8,128)(2,1)S(1)}, bf16[512,768]{1,0:T(8,128)(2,1)S(1)}, u32[]{:S(2)}, u32[]{:S(2)}) collective-permute-start(bf16[512,768]{1,0:T(8,128)(2,1)S(1)} %get-tuple-element.57), channel_id=1, source_target_pairs={{0,8},{8,16},{16,24},{1,9},{9,17},{17,25},{2,10},{10,18},{18,26},{... | collective-permute-start | bytes 2359304 | tf_op jit(solution)/shard_map/ppermute | solution.py:65
  533.6 54.7 %collective-permute-start.62 = (bf16[512,768]{1,0:T(8,128)(2,1)S(1)}, bf16[512,768]{1,0:T(8,128)(2,1)S(1)}, u32[]{:S(2)}, u32[]{:S(2)}) collective-permute-start(bf16[512,768]{1,0:T(8,128)(2,1)S(1)} %get-tuple-element.58), channel_id=1, source_target_pairs={{8,0},{16,8},{24,16},{9,1},{17,9},{25,17},{10,2},{18,10},{26,18},{... | collective-permute-start | bytes 2359304 | tf_op jit(solution)/shard_map/ppermute | solution.py:66
  535.0 51.1 %collective-permute-start.82 = (f32[2048]{0:T(1024)S(1)}, f32[2048]{0:T(1024)S(1)}, u32[]{:S(2)}, u32[]{:S(2)}) collective-permute-start(f32[2048]{0:T(1024)S(1)} %copy-done.63), channel_id=1, source_target_pairs={{0,16},{8,24},{16,0},{24,8},{1,17},{9,25},{17,1},{25,9},{2,18},{10... | collective-permute-start | bytes 24584 | tf_op jit(solution)/shard_map/ppermute | solution.py:33
  586.1 113.8 %collective-permute-start.46 = (bf16[4,256,2048]{2,1,0:T(8,128)(2,1)}, bf16[4,256,2048]{2,1,0:T(8,128)(2,1)}, u32[]{:S(2)}, u32[]{:S(2)}) collective-permute-start(bf16[4,256,2048]{2,1,0:T(8,128)(2,1)} %slice_bitcast_fusion), channel_id=1, source_target_pairs={{0,1},{1,0},{2,3},{3,2},{4,5},{5,4},{6,7},{7,6},{8,9},{9,8},{10,11... | collective-permute-start | bytes 12582920 | tf_op jit(solution)/shard_map/ppermute | solution.py:33
  586.1 36.5 %collective-permute-start.93 = (bf16[512,1024]{0,1:T(8,128)(2,1)S(1)}, bf16[512,1024]{0,1:T(8,128)(2,1)S(1)}, u32[]{:S(2)}, u32[]{:S(2)}) collective-permute-start(bf16[512,1024]{0,1:T(8,128)(2,1)S(1)} %get-tuple-element.35), channel_id=1, source_target_pairs={{0,8},{8,16},{1,9},{9,17},{2,10},{10,18},{3,11},{11,19},{4,12},{12... | collective-permute-start | bytes 3145736 | tf_op jit(solution)/shard_map/ppermute | solution.py:65
  588.4 35.9 %collective-permute-start.96 = (bf16[512,1024]{0,1:T(8,128)(2,1)S(1)}, bf16[512,1024]{0,1:T(8,128)(2,1)S(1)}, u32[]{:S(2)}, u32[]{:S(2)}) collective-permute-start(bf16[512,1024]{0,1:T(8,128)(2,1)S(1)} %get-tuple-element.36), channel_id=1, source_target_pairs={{16,8},{24,16},{17,9},{25,17},{18,10},{26,18},{19,11},{27,19},{20,... | collective-permute-start | bytes 3145736 | tf_op jit(solution)/shard_map/ppermute | solution.py:66
  595.4 43.3 %collective-permute-start.84 = (bf16[512,1024]{0,1:T(8,128)(2,1)}, bf16[512,1024]{0,1:T(8,128)(2,1)}, u32[]{:S(2)}, u32[]{:S(2)}) collective-permute-start(bf16[512,1024]{0,1:T(8,128)(2,1)} %get-tuple-element.41), channel_id=1, source_target_pairs={{0,8},{8,16},{1,9},{9,17},{2,10},{10,18},{3,11},{11,19},{4,12},{12... | collective-permute-start | bytes 3145736 | tf_op jit(solution)/shard_map/ppermute | solution.py:65
  622.7 85.0 %collective-permute-start.32 = (bf16[4,256,2048]{2,1,0:T(8,128)(2,1)}, bf16[4,256,2048]{2,1,0:T(8,128)(2,1)}, u32[]{:S(2)}, u32[]{:S(2)}) collective-permute-start(bf16[4,256,2048]{2,1,0:T(8,128)(2,1)} %slice_bitcast_fusion.2), channel_id=1, source_target_pairs={{0,1},{1,0},{2,3},{3,2},{4,5},{5,4},{6,7},{7,6},{8,9},{9,8},{10,11... | collective-permute-start | bytes 12582920 | tf_op jit(solution)/shard_map/ppermute | solution.py:33
  631.7 27.0 %collective-permute-start.94 = (bf16[512,1024]{0,1:T(8,128)(2,1)}, bf16[512,1024]{0,1:T(8,128)(2,1)}, u32[]{:S(2)}, u32[]{:S(2)}) collective-permute-start(bf16[512,1024]{0,1:T(8,128)(2,1)} %get-tuple-element.33), channel_id=1, source_target_pairs={{0,8},{8,16},{16,24},{1,9},{9,17},{17,25},{2,10},{10,18},{18,26},{... | collective-permute-start | bytes 3145736 | tf_op jit(solution)/shard_map/ppermute | solution.py:65
  638.7 28.0 %collective-permute-start.97 = (bf16[512,1024]{0,1:T(8,128)(2,1)S(1)}, bf16[512,1024]{0,1:T(8,128)(2,1)S(1)}, u32[]{:S(2)}, u32[]{:S(2)}) collective-permute-start(bf16[512,1024]{0,1:T(8,128)(2,1)S(1)} %get-tuple-element.34), channel_id=1, source_target_pairs={{8,0},{16,8},{24,16},{9,1},{17,9},{25,17},{10,2},{18,10},{26,18},{... | collective-permute-start | bytes 3145736 | tf_op jit(solution)/shard_map/ppermute | solution.py:66
  649.7 29.9 %collective-permute-start.85 = (bf16[512,1024]{0,1:T(8,128)(2,1)S(1)}, bf16[512,1024]{0,1:T(8,128)(2,1)S(1)}, u32[]{:S(2)}, u32[]{:S(2)}) collective-permute-start(bf16[512,1024]{0,1:T(8,128)(2,1)S(1)} %get-tuple-element.39), channel_id=1, source_target_pairs={{0,8},{8,16},{16,24},{1,9},{9,17},{17,25},{2,10},{10,18},{18,26},{... | collective-permute-start | bytes 3145736 | tf_op jit(solution)/shard_map/ppermute | solution.py:65
  658.7 29.1 %collective-permute-start.88 = (bf16[512,1024]{0,1:T(8,128)(2,1)S(1)}, bf16[512,1024]{0,1:T(8,128)(2,1)S(1)}, u32[]{:S(2)}, u32[]{:S(2)}) collective-permute-start(bf16[512,1024]{0,1:T(8,128)(2,1)S(1)} %get-tuple-element.40), channel_id=1, source_target_pairs={{8,0},{16,8},{24,16},{9,1},{17,9},{25,17},{10,2},{18,10},{26,18},{... | collective-permute-start | bytes 3145736 | tf_op jit(solution)/shard_map/ppermute | solution.py:66
  691.6 29.6 %collective-permute-start.89 = (bf16[128,1024]{0,1:T(8,128)(2,1)}, bf16[128,1024]{0,1:T(8,128)(2,1)}, u32[]{:S(2)}, u32[]{:S(2)}) collective-permute-start(bf16[128,1024]{0,1:T(8,128)(2,1)} %get-tuple-element.105), channel_id=1, source_target_pairs={{0,2},{2,0},{4,6},{6,4},{1,3},{3,1},{5,7},{7,5},{8,10},{10,8},{12,... | collective-permute-start | bytes 786440 | tf_op jit(solution)/shard_map/ppermute | solution.py:33
  692.6 29.9 %collective-permute-start.90 = (bf16[128,1024]{0,1:T(8,128)(2,1)}, bf16[128,1024]{0,1:T(8,128)(2,1)}, u32[]{:S(2)}, u32[]{:S(2)}) collective-permute-start(bf16[128,1024]{0,1:T(8,128)(2,1)} %get-tuple-element.104), channel_id=1, source_target_pairs={{0,4},{2,6},{4,0},{6,2},{1,5},{3,7},{5,1},{7,3},{8,12},{10,14},{12... | collective-permute-start | bytes 786440 | tf_op jit(solution)/shard_map/ppermute | solution.py:33
  721.2 35.9 %collective-permute-start.48 = (bf16[256,2048]{1,0:T(8,128)(2,1)S(1)}, bf16[256,2048]{1,0:T(8,128)(2,1)S(1)}, u32[]{:S(2)}, u32[]{:S(2)}) collective-permute-start(bf16[256,2048]{1,0:T(8,128)(2,1)S(1)} %pad_maximum_fusion.9), channel_id=1, source_target_pairs={{0,2},{2,0},{4,6},{6,4},{1,3},{3,1},{5,7},{7,5},{8,10},{10,8},{12,... | collective-permute-start | bytes 3145736 | tf_op jit(solution)/shard_map/ppermute | solution.py:33
  722.5 34.6 %collective-permute-start.50 = (bf16[256,2048]{1,0:T(8,128)(2,1)S(1)}, bf16[256,2048]{1,0:T(8,128)(2,1)S(1)}, u32[]{:S(2)}, u32[]{:S(2)}) collective-permute-start(bf16[256,2048]{1,0:T(8,128)(2,1)S(1)} %pad_maximum_fusion.10), channel_id=1, source_target_pairs={{0,4},{2,6},{4,0},{6,2},{1,5},{3,7},{5,1},{7,3},{8,12},{10,14},{12... | collective-permute-start | bytes 3145736 | tf_op jit(solution)/shard_map/ppermute | solution.py:33
  735.2 39.5 %collective-permute-start.34 = (bf16[256,2048]{1,0:T(8,128)(2,1)S(1)}, bf16[256,2048]{1,0:T(8,128)(2,1)S(1)}, u32[]{:S(2)}, u32[]{:S(2)}) collective-permute-start(bf16[256,2048]{1,0:T(8,128)(2,1)S(1)} %pad_maximum_fusion.7), channel_id=1, source_target_pairs={{0,2},{2,0},{4,6},{6,4},{1,3},{3,1},{5,7},{7,5},{8,10},{10,8},{12,... | collective-permute-start | bytes 3145736 | tf_op jit(solution)/shard_map/ppermute | solution.py:33
  736.1 38.5 %collective-permute-start.36 = (bf16[256,2048]{1,0:T(8,128)(2,1)S(1)}, bf16[256,2048]{1,0:T(8,128)(2,1)S(1)}, u32[]{:S(2)}, u32[]{:S(2)}) collective-permute-start(bf16[256,2048]{1,0:T(8,128)(2,1)S(1)} %pad_maximum_fusion.8), channel_id=1, source_target_pairs={{0,4},{2,6},{4,0},{6,2},{1,5},{3,7},{5,1},{7,3},{8,12},{10,14},{12... | collective-permute-start | bytes 3145736 | tf_op jit(solution)/shard_map/ppermute | solution.py:33
  761.2 47.8 %collective-permute-start.51 = (f32[256,2048]{1,0:T(8,128)}, f32[256,2048]{1,0:T(8,128)}, u32[]{:S(2)}, u32[]{:S(2)}) collective-permute-start(f32[256,2048]{1,0:T(8,128)} %convert_add_fusion.8), channel_id=1, source_target_pairs={{0,1},{1,0},{2,3},{3,2},{4,5},{5,4},{6,7},{7,6},{8,9},{9,8},{10,11... | collective-permute-start | bytes 6291464 | tf_op jit(solution)/shard_map/ppermute | solution.py:33
  (137 other events, 2721.8 us)

commit v3 on v2

--- a/solution.py
+++ b/solution.py
@@ -42,94 +42,183 @@
     return x
 
 
-def line_gather(own):
-    n = lax.axis_size("fsdp")
-    z = lax.axis_index("fsdp")
-    up = down = own
-    ups, downs = [None], [None]
-    for s in range(1, n):
-        up = lax.ppermute(up, "fsdp", [(i, i + 1) for i in range(s - 1, n - 1)])
-        down = lax.ppermute(down, "fsdp", [(i, i - 1) for i in range(1, n - s + 1)])
-        ups.append(up)
-        downs.append(down)
-    return [own] + [jnp.where(s <= z, ups[s], downs[n - s]) for s in range(1, n)]
-
-
-def line_scatter(parts):
-    n = lax.axis_size("fsdp")
-    up = down = None
-    for s in range(1, n):
-        send_up, send_down = parts[s], parts[n - s]
-        if s > 1:
-            send_up, send_down = add(send_up, up), add(send_down, down)
-        up = lax.ppermute(send_up, "fsdp", [(i, i + 1) for i in range(0, min(s, n - 1))])
-        down = lax.ppermute(send_down, "fsdp", [(i, i - 1) for i in range(max(n - s, 1), n)])
-    return parts[0].astype(f32) + up.astype(f32) + down.astype(f32)
+def after(x, *before):
+    before = [item for item in before if item is not None]
+    return lax.optimization_barrier((x, *before))[0] if before else x
+
+
+class Order:
+    def __init__(self):
+        self.last = ()
+
+    def then(self, x):
+        return after(x, *self.last)
+
+    def did(self, *values):
+        self.last = values
+
+    def arrive(self, values):
+        values = after(values, *self.last)
+        self.last = self.last + tuple(jax.tree.leaves(values))
+        return values
+
+
+def line_up(x, first, last):
+    return lax.ppermute(x, "fsdp", [(i, i + 1) for i in range(first, last)])
+
+
+def line_down(x, first, last):
+    return lax.ppermute(x, "fsdp", [(i, i - 1) for i in range(first, last)])
+
+
+class Gather:
+    def __init__(self, own):
+        self.ups, self.downs = [own], [own]
+
+    def start(self):
+        n, s = lax.axis_size("fsdp"), len(self.ups)
+        if s < n:
+            self.ups.append(line_up(self.ups[-1], s - 1, n - 1))
+            self.downs.append(line_down(self.downs[-1], 1, n - s + 1))
+
+    def arrive(self, order):
+        self.ups[-1], self.downs[-1] = order.arrive((self.ups[-1], self.downs[-1]))
+
+    def rest(self, order):
+        for _ in range(len(self.ups), lax.axis_size("fsdp")):
+            self.start()
+            self.arrive(order)
+
+    def sources(self):
+        return self.ups + self.downs[1:]
+
+
+class Scatter:
+    def __init__(self, parts):
+        self.parts, self.sums, self.step = parts, None, 1
+
+    def start(self):
+        n, s = lax.axis_size("fsdp"), self.step
+        if s < n:
+            up, down = self.parts[s], self.parts[n - s]
+            if self.sums is not None:
+                up, down = add(up, self.sums[0]), add(down, self.sums[1])
+            self.sums = line_up(up, 0, min(s, n - 1)), line_down(down, max(n - s, 1), n)
+            self.step += 1
+
+    def arrive(self, order):
+        self.sums = order.arrive(self.sums)
+
+    def rest(self, order):
+        for _ in range(self.step, lax.axis_size("fsdp")):
+            self.start()
+            self.arrive(order)
+
+    def total(self):
+        up, down = self.sums
+        return (self.parts[0].astype(f32) + up.astype(f32) + down.astype(f32)).astype(bf16)
+
+
+class Rows:
+    def __init__(self, own):
+        self.own = own
+        self.half = own.shape[0] // 2
+
+    def start(self):
+        mine = self.own[: self.half]
+        self.got = [swap(mine, "ctx", 1 << k) for k in range(lax.axis_size("ctx").bit_length() - 1)]
+
+    def arrive(self, order):
+        self.got = order.arrive(self.got)
+
+    def start_far(self):
+        m, quarter = lax.axis_size("ctx"), self.half // 2
+        if m == 4:
+            first, second = self.got
+            self.far = [swap(first[:quarter], "ctx", 2), swap(second[quarter:], "ctx", 1)]
+            self.near = [first, second]
+        else:
+            mine = self.own[: self.half]
+            self.near = self.got
+            self.far = [swap(mine, "ctx", j) for j in range(1, m) if j & (j - 1)]
+        self.near_other = [swap(piece, "tp", 1) for piece in self.near]
+
+    def arrive_far(self, order):
+        self.far, self.near_other = order.arrive((self.far, self.near_other))
+
+    def start_last(self):
+        self.far_other = [swap(piece, "tp", 1) for piece in self.far]
+
+    def arrive_last(self, order):
+        self.far_other = order.arrive(self.far_other)
+
+    def blocks(self):
+        m = lax.axis_size("ctx")
+        near = list(zip(self.near, self.near_other))
+        far = list(zip(self.far, self.far_other))
+        blocks = [self.own]
+        for j in range(1, m):
+            if j & (j - 1) == 0:
+                blocks += near.pop(0)
+            elif m == 4:
+                blocks += [far[0][0], far[1][0], far[0][1], far[1][1]]
+            else:
+                blocks += far.pop(0)
+        return blocks
+
+
+class RowSums:
+    def __init__(self, slots):
+        self.slots = [slots[j] for j in range(slots.shape[0])]
+
+    def start(self):
+        m, slots = len(self.slots), self.slots
+        quarter = slots[0].shape[0] // 2
+        if m == 4:
+            self.got = [swap(slots[3][:quarter], "ctx", 2), swap(slots[3][quarter:], "ctx", 1)]
+        else:
+            self.got = [swap(slots[j], "ctx", j) for j in range(1, m) if j & (j - 1)]
+
+    def arrive(self, order):
+        self.got = order.arrive(self.got)
+
+    def start_last(self):
+        m, slots = len(self.slots), self.slots
+        quarter = slots[0].shape[0] // 2
+        if m == 4:
+            first = jnp.concatenate([add(slots[1][:quarter], self.got[0]), slots[1][quarter:]], axis=0)
+            second = jnp.concatenate([slots[2][:quarter], add(slots[2][quarter:], self.got[1])], axis=0)
+            self.last, self.got = [swap(first, "ctx", 1), swap(second, "ctx", 2)], []
+        else:
+            self.last = [swap(slots[j], "ctx", j) for j in range(1, m) if j & (j - 1) == 0]
+
+    def arrive_last(self, order):
+        self.last, self.slots[0] = order.arrive((self.last, self.slots[0]))
+
+    def total(self):
+        return sum((x.astype(f32) for x in self.got + self.last), self.slots[0].astype(f32))
 
 
 def add(a, b):
     return (a.astype(f32) + b.astype(f32)).astype(bf16)
 
 
-def gather_rows(rows):
-    m = lax.axis_size("ctx")
-    half = rows.shape[0] // 2
-    mine = rows[:half]
-    if m == 4:
-        quarter = half // 2
-        first = swap(mine, "ctx", 1)
-        second = swap(mine, "ctx", 2)
-        third_a = swap(first[:quarter], "ctx", 2)
-        third_b = swap(second[quarter:], "ctx", 1)
-        got = [[first], [second], [third_a, third_b]]
-    else:
-        slots = [mine]
-        bit = 1
-        while bit < m:
-            slots = slots + [swap(piece, "ctx", bit) for piece in slots]
-            bit *= 2
-        got = [[piece] for piece in slots[1:]]
-    blocks = [rows]
-    for pieces in got:
-        blocks = blocks + pieces + [swap(piece, "tp", 1) for piece in pieces]
-    return jnp.concatenate(blocks, axis=0)
-
-
-def scatter_rows(part):
-    m = lax.axis_size("ctx")
-    half = part.shape[0] // (2 * m)
-    blocks = part.reshape(m, 2, half, part.shape[1])
-    slots = add(blocks[:, 0], swap(blocks[:, 1], "tp", 1))
-    if m == 4:
-        quarter = half // 2
-        to_second = swap(slots[3, :quarter], "ctx", 2)
-        to_first = swap(slots[3, quarter:], "ctx", 1)
-        first = jnp.concatenate([add(slots[1, :quarter], to_second), slots[1, quarter:]], axis=0)
-        second = jnp.concatenate([slots[2, :quarter], add(slots[2, quarter:], to_first)], axis=0)
-        return (
-            slots[0].astype(f32)
-            + swap(first, "ctx", 1).astype(f32)
-            + swap(second, "ctx", 2).astype(f32)
-        )
-    bit = m // 2
-    while bit >= 1:
-        slots = add(slots[:bit], swap(slots[bit : 2 * bit], "ctx", bit))
-        bit //= 2
-    return slots[0].astype(f32)
-
-
-def spread_columns(block):
+def spread_start(block):
     m = lax.axis_size("ctx")
     c = lax.axis_index("ctx")
-    rows, cols = block.shape[0] // m, block.shape[1]
+    rows = block.shape[0] // m
     pieces = []
     for j in range(m):
         piece = lax.dynamic_slice_in_dim(block, (c ^ j) * rows, rows, axis=0)
         pieces.append(piece if j == 0 else swap(piece, "ctx", j))
+    return pieces
+
+
+def side_by_side(pieces):
+    m = lax.axis_size("ctx")
+    c = lax.axis_index("ctx")
     stacked = jnp.stack(pieces)
-    ordered = [
-        lax.dynamic_index_in_dim(stacked, c ^ k, axis=0, keepdims=False) for k in range(m)
-    ]
+    ordered = [lax.dynamic_index_in_dim(stacked, c ^ k, axis=0, keepdims=False) for k in range(m)]
     return jnp.concatenate(ordered, axis=1).astype(f32)
 
 
@@ -189,29 +278,143 @@
     return (keys >= start) & (keys <= queries)
 
 
+def fetch(z_ref, sources, weight_ref, sems, first):
+    n = (len(sources) + 1) // 2
+    feat, cols = weight_ref.shape[0] // n, weight_ref.shape[1]
+
+    def copy(source, s):
+        rows = pl.ds(s * feat, feat)
+        return pltpu.make_async_copy(
+            source.at[:, pl.ds(first, cols)], weight_ref.at[rows, :], sems.at[s]
+        )
+
+    def each(do):
+        do(copy(sources[0], 0))
+        for s in range(1, n):
+
+            @pl.when(z_ref[0] >= s)
+            def _():
+                do(copy(sources[s], s))
+
+            @pl.when(z_ref[0] < s)
+            def _():
+                do(copy(sources[2 * n - 1 - s], s))
+
+    each(lambda c: c.start())
+    each(lambda c: c.wait())
+
+
+def pack_kernel(heads, count, z_ref, x_in_ref, bias_ref, cos_ref, sin_ref, prow_ref, *rest):
+    sources, (packed_ref, vt_ref, x_ref, weight_ref, sems) = rest[:count], rest[count:]
+    wide = vt_ref.shape[0]
+    blocks = x_ref.shape[0] // BLOCK
+    split = ROT // 2 * heads
+    r = pl.program_id(0)
+
+    @pl.when(r == 0)
+    def _():
+        fetch(z_ref, sources, weight_ref, sems, 0)
+
+    rows = pl.ds(pl.multiple_of(r * BLOCK, BLOCK), BLOCK)
+    cosine, sine = cos_ref[rows, :], sin_ref[rows, :]
+    x_in = x_in_ref[...]
+    for part in range(3):
+        at = slice(part * wide, (part + 1) * wide)
+        x = mm(x_in, weight_ref[:, at]) + bias_ref[0:1, at]
+        if part < 2:
+            x = turned(x, cosine, sine, split)
+        if part == 0:
+            x = x * (1.0 / math.sqrt(HEAD))
+        x_ref[rows, at] = x.astype(bf16)
+
+    @pl.when(r == blocks - 1)
+    def _():
+        @pl.loop(0, blocks)
+        def _(p):
+            rows = pl.ds(pl.multiple_of(p * BLOCK, BLOCK), BLOCK)
+            y = to_packed(prow_ref, p, x_ref[...])
+            packed_ref[rows, :] = y.astype(bf16)
+            vt_ref[:, rows] = y[:, 2 * wide :].T.astype(bf16)
+
+
+def curve(u):
+    square = u * u
+    return jnp.tanh(math.sqrt(2.0 / math.pi) * (u + 0.044715 * (square * u))), square
+
+
+def up_kernel(count, z_ref, x_ref, bias_ref, *rest):
+    sources, (up_ref, act_ref, weight_ref, sems) = rest[:count], rest[count:]
+
+    @pl.when(pl.program_id(0) == 0)
+    def _():
+        fetch(z_ref, sources, weight_ref, sems, 0)
+
+    x = x_ref[...]
+    step = min(256, up_ref.shape[1])
+    for at in range(0, up_ref.shape[1], step):
+        at = slice(at, at + step)
+        u = mm(x, weight_ref[:, at]) + bias_ref[0:1, at]
+        up_ref[:, at] = u
+        act_ref[:, at] = (0.5 * u * (1.0 + curve(u)[0])).astype(bf16)
+
+
+def up_back_kernel(count, z_ref, x_ref, up_ref, *rest):
+    sources, (grad_ref, sum_ref, weight_ref, sems) = rest[:count], rest[count:]
+
+    @pl.when(pl.program_id(0) == 0)
+    def _():
+        fetch(z_ref, sources, weight_ref, sems, 0)
+        sum_ref[...] = jnp.zeros(sum_ref.shape, f32)
+
+    x = x_ref[...]
+    step = min(256, grad_ref.shape[1])
+    for at in range(0, grad_ref.shape[1], step):
+        at = slice(at, at + step)
+        u = up_ref[:, at]
+        bend, square = curve(u)
+        slope = 0.5 * (1.0 + bend) + (0.5 * math.sqrt(2.0 / math.pi)) * u * (
+            (1.0 - bend * bend) * (1.0 + (3.0 * 0.044715) * square)
+        )
+        grad = mm(x, weight_ref[:, at]) * slope
+        grad_ref[:, at] = grad.astype(bf16)
+        sum_ref[0:1, at] = sum_ref[0:1, at] + jnp.sum(grad, axis=0, keepdims=True)
+
+
+def plain_kernel(count, first, z_ref, x_ref, *rest):
+    sources, (out_ref, weight_ref, sems) = rest[:count], rest[count:]
+
+    @pl.when(pl.program_id(0) == 0)
+    def _():
+        fetch(z_ref, sources, weight_ref, sems, first)
+
+    out_ref[...] = mm(x_ref[...], weight_ref[...]).astype(bf16)
+
+
+def spread_kernel(count, first, z_ref, a_ref, b_ref, *rest):
+    a_sources, b_sources = rest[:count], rest[count : 2 * count]
+    keep_ref, send_ref, a_weight_ref, b_weight_ref, sems = rest[2 * count :]
+
+    @pl.when(pl.program_id(0) == 0)
+    def _():
+        fetch(z_ref, a_sources, a_weight_ref, sems, first)
+        fetch(z_ref, b_sources, b_weight_ref, sems, 0)
+
+    half = keep_ref.shape[1]
+    for h, out_ref in ((0, keep_ref), (1, send_ref)):
+        rows = slice(h * half, (h + 1) * half)
+        a, b = a_ref[rows, :], b_ref[rows, :]
+        for at in range(0, out_ref.shape[2], 256):
+            at = slice(at, at + 256)
+            out = mm(a, a_weight_ref[at, :], NT) + mm(b, b_weight_ref[at, :], NT)
+            out_ref[0, :, at] = out.astype(bf16)
+
+
 def forward_kernel(
-    heads, low_ref, qkv_ref, bias_ref, cos_ref, sin_ref, prow_ref, pcol_ref, start_ref, qmask_ref,
-    packed_ref, outt_ref, lse_ref, mixed_ref, x_ref, vt_ref, mp_ref,
+    heads, low_ref, packed_ref, vt_ref, pcol_ref, start_ref, qmask_ref,
+    outt_ref, lse_ref, mixed_ref, mp_ref,
 ):
     rows_all, wide = mixed_ref.shape
     blocks = rows_all // BLOCK
-    split = ROT // 2 * heads
-
-    @pl.loop(0, blocks)
-    def _(r):
-        rows = pl.ds(pl.multiple_of(r * BLOCK, BLOCK), BLOCK)
-        cosine, sine = cos_ref[rows, :], sin_ref[rows, :]
-        x = qkv_ref[rows, :] + bias_ref[0:1, :]
-        q = turned(x[:, :wide], cosine, sine, split) * (1.0 / math.sqrt(HEAD))
-        k = turned(x[:, wide : 2 * wide], cosine, sine, split)
-        x_ref[rows, :] = jnp.concatenate([q, k, x[:, 2 * wide :]], axis=1).astype(bf16)
-
-    @pl.loop(0, blocks)
-    def _(p):
-        rows = pl.ds(pl.multiple_of(p * BLOCK, BLOCK), BLOCK)
-        y = to_packed(prow_ref, p, x_ref[...])
-        packed_ref[rows, :] = y.astype(bf16)
-        vt_ref[:, rows] = y[:, 2 * wide :].T.astype(bf16)
 
     @pl.loop(0, blocks)
     def _(i):
@@ -333,34 +536,199 @@
     return [pl.BlockSpec(memory_space=pltpu.VMEM)] * count
 
 
-def attend(heads, low, qkv, bias, cosine, sine, prow, pcol, start, qmask):
-    rows, wide = qkv.shape[0], heads * HEAD
+COST = 0.05
+
+
+def blocks_call(kernel, name, z, ins, in_specs, sources, outs, out_specs, scratch, steps, flops, weight_shapes):
+    sems = len(sources[0]) // 2 + 1
+    return pl.pallas_call(
+        kernel,
+        grid_spec=pltpu.PrefetchScalarGridSpec(
+            num_scalar_prefetch=1,
+            grid=(steps,),
+            in_specs=in_specs + [pl.BlockSpec(memory_space=pl.ANY)] * sum(map(len, sources)),
+            out_specs=out_specs,
+            scratch_shapes=scratch
+            + [pltpu.VMEM(shape, bf16) for shape in weight_shapes]
+            + [pltpu.SemaphoreType.DMA((sems,))],
+        ),
+        out_shape=outs,
+        compiler_params=pltpu.CompilerParams(vmem_limit_bytes=48 * 2**20),
+        cost_estimate=pl.CostEstimate(flops=int(COST * flops), bytes_accessed=2**20, transcendentals=0),
+        name=name,
+    )(z, *ins, *[x for group in sources for x in group])
+
+
+def fixed(shape):
+    return pl.BlockSpec(shape, lambda *_: (0,) * len(shape))
+
+
+def by_row(rows, cols):
+    return pl.BlockSpec((rows, cols), lambda i, *_: (i, 0))
+
+
+def prepare_kernel(norm, slots, at_ref, x_ref, gain_ref, shift_ref, out_ref, *rest):
+    rows, width = x_ref.shape
+    half, step = rows // 2, 64
+    feat = width // slots
+    if not norm:
+        rest[0][...] = jnp.zeros(rest[0].shape, f32)
+
+    @pl.loop(0, rows // step)
+    def _(b):
+        source = pl.ds(pl.multiple_of(b * step, step), step)
+        first = b * step
+        second = (first >= half).astype(jnp.int32)
+        place = (second ^ at_ref[1]) * half + first - second * half
+        target = pl.ds(pl.multiple_of(place, step), step)
+        x = x_ref[source, :].astype(f32)
+        if norm:
+            mean = jnp.mean(x, axis=-1, keepdims=True)
+            centred = x - mean
+            rstd = lax.rsqrt(jnp.mean(centred * centred, axis=-1, keepdims=True) + EPSILON)
+        else:
+            rest[0][0:1, :] = rest[0][0:1, :] + jnp.sum(x, axis=0, keepdims=True)
+        for s in range(slots):
+            block = lax.rem(at_ref[0] - s + slots, slots)
+            columns = pl.ds(pl.multiple_of(block * feat, feat), feat)
+            y = x_ref[source, columns]
+            if norm:
+                y = (y.astype(f32) - mean) * rstd * gain_ref[0:1, columns] + shift_ref[0:1, columns]
+            out_ref[target, s * feat : (s + 1) * feat] = y.astype(bf16)
+
+
+def prepare(norm, at, x, gain, shift, n):
+    rows, width = x.shape
+    out = [jax.ShapeDtypeStruct((rows, width), bf16)]
+    if not norm:
+        out.append(jax.ShapeDtypeStruct((8, width), f32))
+    return pl.pallas_call(
+        functools.partial(prepare_kernel, norm, n),
+        grid_spec=pltpu.PrefetchScalarGridSpec(
+            num_scalar_prefetch=1, grid=(), in_specs=whole(3), out_specs=whole(len(out))
+        ),
+        out_shape=out,
+        compiler_params=pltpu.CompilerParams(vmem_limit_bytes=40 * 2**20),
+        cost_estimate=pl.CostEstimate(flops=2**20, bytes_accessed=2**20, transcendentals=0),
+        name="prepare",
+    )(at, x, gain, shift)
+
+
+def assemble_kernel(*refs):
+    *pieces, out_ref, sems = refs
+
+    def each(do):
+        first = 0
+        for k, piece in enumerate(pieces):
+            count = piece.shape[0]
+            do(pltpu.make_async_copy(piece, out_ref.at[pl.ds(first, count), :], sems.at[k]))
+            first += count
+
+    each(lambda copy: copy.start())
+    each(lambda copy: copy.wait())
+
+
+def assemble(pieces):
+    rows = sum(piece.shape[0] for piece in pieces)
+    return pl.pallas_call(
+        assemble_kernel,
+        in_specs=whole(len(pieces)),
+        out_specs=pl.BlockSpec(memory_space=pl.ANY),
+        scratch_shapes=[pltpu.SemaphoreType.DMA((len(pieces),))],
+        out_shape=jax.ShapeDtypeStruct((rows, pieces[0].shape[1]), bf16),
+        compiler_params=pltpu.CompilerParams(vmem_limit_bytes=40 * 2**20),
+        cost_estimate=pl.CostEstimate(flops=2**20, bytes_accessed=2**20, transcendentals=0),
+        name="assemble",
+    )(*pieces)
+
+
+def pack(heads, z, normed, bias, cosine, sine, prow, sources):
+    rows, width = normed.shape
+    wide = heads * HEAD
+    slab = cosine.shape[1]
+    return blocks_call(
+        functools.partial(pack_kernel, heads, len(sources)), "pack", z,
+        [normed, bias, cosine, sine, prow],
+        [by_row(BLOCK, width), fixed(bias.shape), fixed((rows, slab)), fixed((rows, slab)), fixed(prow.shape)],
+        [sources],
+        [jax.ShapeDtypeStruct((rows, 3 * wide), bf16), jax.ShapeDtypeStruct((wide, rows), bf16)],
+        [fixed((rows, 3 * wide)), fixed((wide, rows))],
+        [pltpu.VMEM((rows, 3 * wide), bf16)],
+        rows // BLOCK, 12 * rows * rows * wide, [(width, 3 * wide)],
+    )
+
+
+def up_forward(z, normed, bias, sources):
+    rows, width = normed.shape
+    cols = bias.shape[1]
+    return blocks_call(
+        functools.partial(up_kernel, len(sources)), "up", z,
+        [normed, bias], [by_row(512, width), fixed(bias.shape)], [sources],
+        [jax.ShapeDtypeStruct((rows, cols), f32), jax.ShapeDtypeStruct((rows, cols), bf16)],
+        [by_row(512, cols), by_row(512, cols)], [],
+        rows // 512, 2 * rows * width * cols, [(width, cols)],
+    )
+
+
+def up_backward(z, grads, up, sources):
+    rows, width = grads.shape
+    cols = up.shape[1]
+    return blocks_call(
+        functools.partial(up_back_kernel, len(sources)), "up_back", z,
+        [grads, up], [by_row(512, width), by_row(512, cols)], [sources],
+        [jax.ShapeDtypeStruct((rows, cols), bf16), jax.ShapeDtypeStruct((8, cols), f32)],
+        [by_row(512, cols), fixed((8, cols))], [],
+        rows // 512, 2 * rows * width * cols, [(width, cols)],
+    )
+
+
+def times(z, x, sources, first, cols):
+    rows, width = x.shape
+    return blocks_call(
+        functools.partial(plain_kernel, len(sources), first), "times", z,
+        [x], [by_row(512, width)], [sources],
+        [jax.ShapeDtypeStruct((rows, cols), bf16)], [by_row(512, cols)], [],
+        rows // 512, 2 * rows * width * cols, [(width, cols)],
+    )[0]
+
+
+def to_features(z, a, a_sources, first, b, b_sources, half, width):
+    rows = a.shape[0]
+    slots = rows // (2 * half)
+    a_cols, b_cols = a.shape[1], b.shape[1]
+    out = jax.ShapeDtypeStruct((slots, half, width), bf16)
+    spec = pl.BlockSpec((1, half, width), lambda i, *_: (i, 0, 0))
+    return blocks_call(
+        functools.partial(spread_kernel, len(a_sources), first), "to_features", z,
+        [a, b], [by_row(2 * half, a_cols), by_row(2 * half, b_cols)], [a_sources, b_sources],
+        [out, out], [spec, spec], [],
+        slots, 2 * rows * width * (a_cols + b_cols), [(width, a_cols), (width, b_cols)],
+    )
+
+
+def attend(heads, low, packed, vt, pcol, start, qmask):
+    rows, wide = packed.shape[0], heads * HEAD
     pairs = (rows // BLOCK) * 4 * heads * BLOCK * BLOCK
     return pl.pallas_call(
         functools.partial(forward_kernel, heads),
         grid_spec=pltpu.PrefetchScalarGridSpec(
             num_scalar_prefetch=1,
             grid=(),
-            in_specs=whole(8),
-            out_specs=whole(4),
-            scratch_shapes=[
-                pltpu.VMEM((rows, 3 * wide), bf16),
-                pltpu.VMEM((wide, rows), bf16),
-                pltpu.VMEM((rows, wide), bf16),
-            ],
+            in_specs=whole(5),
+            out_specs=whole(3),
+            scratch_shapes=[pltpu.VMEM((rows, wide), bf16)],
         ),
         out_shape=[
-            jax.ShapeDtypeStruct((rows, 3 * wide), bf16),
             jax.ShapeDtypeStruct((wide, rows), f32),
             jax.ShapeDtypeStruct((8, rows), f32),
             jax.ShapeDtypeStruct((rows, wide), bf16),
         ],
         compiler_params=pltpu.CompilerParams(vmem_limit_bytes=40 * 2**20),
         cost_estimate=pl.CostEstimate(
-            flops=8 * rows * rows * wide + pairs * 4 * wide, bytes_accessed=20 * rows * wide, transcendentals=pairs
+            flops=2 * rows * rows * wide + pairs * 4 * wide, bytes_accessed=20 * rows * wide, transcendentals=pairs
         ),
         name="attend_forward",
-    )(low, qkv, bias, cosine, sine, prow, pcol, start, qmask)
+    )(low, packed, vt, pcol, start, qmask)
 
 
 def attend_back(heads, low, packed, outt, lse, grad, cosine, sine, prow, pcol, start, qmask, vmask, ktmask):
@@ -429,37 +797,37 @@
             axis=1,
         )
 
-    def halves(x):
-        return jnp.where(t == 0, x, jnp.concatenate([x[half:], x[:half]], axis=0))
-
     def mine(weight):
         share = weight.shape[-1] // m
         return lax.dynamic_slice_in_dim(weight, c * share, share, axis=weight.ndim - 1)
 
-    order = jnp.array(column_order(heads), jnp.int32)
-    place_of = (jnp.arange(3 * wide, dtype=jnp.int32)[:, None] == order[None, :]).astype(bf16)
+    listed = jnp.array(column_order(heads), jnp.int32)
+    place_of = (jnp.arange(3 * wide, dtype=jnp.int32)[:, None] == listed[None, :]).astype(bf16)
     qkv_own = jnp.dot(mine(w_qkv), place_of, preferred_element_type=f32).astype(bf16)
     qkv_bias = jnp.dot(mine(b_qkv)[None], place_of, preferred_element_type=f32)
     up_bias = mine(b_fc1).astype(f32)
 
-    up_slots = line_gather(mine(w_fc1))
-    qkv_slots = line_gather(qkv_own)
-    dense_slots = line_gather(mine(w_dense))
-    down_slots = line_gather(mine(w_fc2))
-    w_up = jnp.concatenate(up_slots, axis=0)
-    w_in = jnp.concatenate(qkv_slots, axis=0)
-    w_out = jnp.concatenate(dense_slots, axis=0)
-    w_down = jnp.concatenate(down_slots, axis=0)
-
-    source = halves(hidden_in[0]).astype(f32)
+    order = Order()
+    z_ref = jnp.full((1,), z, jnp.int32)
+    first = Gather(jnp.concatenate([qkv_own, mine(w_dense)], axis=1))
+    first.start()
+
+    at = jnp.stack([z, t]).astype(jnp.int32)
     gain_vec = ln_gain.astype(f32)
     shift_vec = ln_bias.astype(f32)
-    centred = source - jnp.mean(source, axis=-1, keepdims=True)
-    rstd = lax.rsqrt(jnp.mean(centred * centred, axis=-1, keepdims=True) + EPSILON)
-    xhat = centred * rstd
-    normed = gather_rows(turn((xhat * gain_vec + shift_vec).astype(bf16)))
-    grad_own = halves(out_grad[0])
-    grads = gather_rows(turn(grad_own))
+    gain_row = jnp.broadcast_to(gain_vec[None], (8, width))
+    shift_row = jnp.broadcast_to(shift_vec[None], (8, width))
+    normed_own = prepare(True, at, after(hidden_in[0], first.ups[0]), gain_row, shift_row, n)[0]
+    order.did(normed_own)
+    rows_in = Rows(normed_own)
+    rows_in.start()
+    first.arrive(order)
+    first.start()
+    grads_own, out_sum = prepare(False, at, order.then(out_grad[0]), gain_row, shift_row, n)
+    order.did(grads_own)
+    assignment, lengths, w_fc1, w_fc2 = order.then((assignment, lengths, w_fc1, w_fc2))
+    second = Gather(mine(w_fc1))
+    third = Gather(mine(w_fc2))
 
     block_of = [((c ^ j) * 2 + (t ^ h)) * half for j in range(m) for h in range(2)]
     packed = jnp.concatenate(
@@ -491,59 +859,177 @@
     vmask = jnp.broadcast_to(head_v[:, None, :], (heads, BLOCK, wide))
     ktmask = jnp.broadcast_to(head_qk[:, :, None], (heads, wide, BLOCK))
 
-    up = jnp.dot(normed, w_up, preferred_element_type=f32) + up_bias
-    act = gelu_tanh(up).astype(bf16)
-    qkv = jnp.dot(normed, w_in, preferred_element_type=f32)
+    order.did(second.ups[0], third.ups[0], cos_arrival, sin_arrival, cos_packed, sin_packed)
+    first.arrive(order)
+    rows_in.arrive(order)
+
+    first.start()
+    rows_in.start_far()
+    first.arrive(order)
+    rows_in.arrive_far(order)
+    first.rest(order)
+
+    second.start()
+    rows_in.start_last()
+    rows_grad = Rows(order.then(grads_own))
+    rows_grad.start()
+    rows_in.arrive_last(order)
+    normed = assemble(order.then(rows_in.blocks()))
+    order.did(normed)
     qkv_bias = jnp.broadcast_to(qkv_bias, (8, 3 * wide))
-    qkv_packed, outt, lse, mixed = attend(
-        heads, low, qkv, qkv_bias, cos_arrival, sin_arrival, prow, pcol, start, qmask
-    )
-
-    branch = lax.dot_general(mixed, w_out, by_columns, preferred_element_type=f32)
-    branch = branch + lax.dot_general(act, w_down, by_columns, preferred_element_type=f32)
-    branch = turn(scatter_rows(branch.astype(bf16)))
+    qkv_packed, vt = pack(
+        heads, z_ref, order.then(normed), qkv_bias, cos_arrival, sin_arrival, prow, first.sources()
+    )
+    order.did(qkv_packed)
+    second.arrive(order)
+    rows_grad.arrive(order)
+
+    second.start()
+    rows_grad.start_far()
+    outt, lse, mixed = attend(heads, low, order.then(qkv_packed), vt, pcol, start, qmask)
+    order.did(mixed)
+    second.arrive(order)
+    rows_grad.arrive_far(order)
+
+    second.start()
+    rows_grad.start_last()
+    rows_grad.arrive_last(order)
+    grads = assemble(order.then(rows_grad.blocks()))
+    order.did(grads)
+    mixed_grad = times(z_ref, order.then(grads), first.sources(), 3 * wide, wide)
+    order.did(mixed_grad)
+    dense_grad = lax.dot_general(grads, order.then(mixed), by_rows, preferred_element_type=f32).astype(bf16)
+    order.did(dense_grad)
+    second.arrive(order)
+    second.rest(order)
+
+    third.start()
+    up_bias = jnp.broadcast_to(up_bias[None], (8, up_bias.shape[0]))
+    up, act = up_forward(z_ref, order.then(normed), up_bias, second.sources())
+    order.did(act)
+    down_grad = lax.dot_general(grads, order.then(act), by_rows, preferred_element_type=f32).astype(bf16)
+    down_sum = Scatter([down_grad[s * feat : (s + 1) * feat] for s in range(n)])
+    order.did(*down_sum.parts)
+    third.arrive(order)
+
+    third.start()
+    down_sum.start()
+    qkv_grad_low, qkv_bias_sum = attend_back(
+        heads, low, order.then(qkv_packed), outt, lse, mixed_grad, cos_packed, sin_packed, prow, pcol, start,
+        qmask, vmask, ktmask,
+    )
+    order.did(qkv_grad_low)
+    third.arrive(order)
+    down_sum.arrive(order)
+
+    third.start()
+    down_sum.start()
+    qkv_weight = lax.dot_general(
+        normed, order.then(qkv_grad_low), by_rows, preferred_element_type=f32
+    ).astype(bf16)
+    first_sum = Scatter(
+        [
+            jnp.concatenate([x[s * feat : (s + 1) * feat] for x in (qkv_weight, dense_grad)], axis=1)
+            for s in range(n)
+        ]
+    )
+    order.did(*first_sum.parts)
+    third.arrive(order)
+    down_sum.arrive(order)
+    third.rest(order)
+
+    down_sum.start()
+    first_sum.start()
+    branch_keep, branch_send = to_features(
+        z_ref, order.then(mixed), first.sources(), 3 * wide, act, third.sources(), half, width
+    )
+    order.did(branch_keep)
+    branch_other = swap(branch_send, "tp", 1)
+    up_grad_low, up_bias_sum = up_backward(z_ref, grads, order.then(up), third.sources())
+    order.did(up_grad_low)
+    down_sum.arrive(order)
+    first_sum.arrive(order)
+    branch_keep, branch_other = order.arrive((branch_keep, branch_other))
+    down_sum.rest(order)
+
+    first_sum.start()
+    branch_sum = RowSums(add(branch_keep, branch_other))
+    branch_sum.start()
+    up_weight = lax.dot_general(
+        normed, order.then(up_grad_low), by_rows, preferred_element_type=f32
+    ).astype(bf16)
+    up_sum = Scatter([up_weight[s * feat : (s + 1) * feat] for s in range(n)])
+    order.did(*up_sum.parts)
+    first_sum.arrive(order)
+    branch_sum.arrive(order)
+
+    first_sum.start()
+    up_sum.start()
+    branch_sum.start_last()
+    keep, send = to_features(
+        z_ref, order.then(qkv_grad_low), first.sources(), 0, up_grad_low, second.sources(), half, width
+    )
+    order.did(keep)
+    other = swap(send, "tp", 1)
+    up_sum.arrive(order)
+    first_sum.arrive(order)
+    branch_sum.arrive_last(order)
+    keep, other = order.arrive((keep, other))
+    first_sum.rest(order)
+
+    up_sum.start()
+    row_sum = RowSums(add(keep, other))
+    row_sum.start()
+    down_pieces = spread_start(order.then(down_sum.total()))
+    branch = turn(branch_sum.total())
+    source = lax.dynamic_slice_in_dim(hidden_in[0], t * half, half).astype(f32)
     biases = b_dense.astype(f32) + b_fc2.astype(f32)
-    result = (source[:half] + branch + biases).astype(bf16)
-    result_other = swap(result, "tp", 1)
-    result = halves(jnp.concatenate([result, result_other], axis=0))
-
-    mixed_grad = jnp.dot(grads, w_out, preferred_element_type=f32).astype(bf16)
-    act_grad = jnp.dot(grads, w_down, preferred_element_type=f32)
-    up_grad = jax.vjp(gelu_tanh, up)[1](act_grad)[0]
-    up_grad_low = up_grad.astype(bf16)
-
-    qkv_grad_low, qkv_bias_sum = attend_back(
-        heads, low, qkv_packed, outt, lse, mixed_grad, cos_packed, sin_packed, prow, pcol, start,
-        qmask, vmask, ktmask,
-    )
-
-    normed_grad = lax.dot_general(qkv_grad_low, w_in, by_columns, preferred_element_type=f32)
-    normed_grad = normed_grad + lax.dot_general(up_grad_low, w_up, by_columns, preferred_element_type=f32)
-    normed_grad = turn(scatter_rows(normed_grad.astype(bf16)))
+    result = (source + branch + biases).astype(bf16)
+    first_total = first_sum.total()
+    qkv_sum = lax.dot_general(
+        first_total[:, : 3 * wide], place_of, by_columns, preferred_element_type=f32
+    ).astype(bf16)
+    first_total = jnp.concatenate([qkv_sum, first_total[:, 3 * wide :]], axis=1)
+    order.did(result, first_total)
+    up_sum.arrive(order)
+    row_sum.arrive(order)
+    down_pieces = order.arrive(down_pieces)
+
+    up_sum.start()
+    row_sum.start_last()
+    result_other = swap(order.then(result), "tp", 1)
+    qkv_pieces = spread_start(order.then(first_total))
+    down_part = side_by_side(down_pieces)
+    centred = order.then(source)
+    centred = centred - jnp.mean(centred, axis=-1, keepdims=True)
+    rstd = lax.rsqrt(jnp.mean(centred * centred, axis=-1, keepdims=True) + EPSILON)
+    xhat = centred * rstd
+    order.did(down_part, xhat)
+    row_sum.arrive_last(order)
+    up_sum.arrive(order)
+    up_sum.rest(order)
+    result_other, qkv_pieces = order.arrive((result_other, qkv_pieces))
+
+    up_pieces = spread_start(order.then(up_sum.total()))
+    normed_grad = turn(row_sum.total())
     d = normed_grad * gain_vec
-    xhat_half = xhat[:half]
-    input_grad = (
-        rstd[:half]
-        * (
-            d
-            - jnp.mean(d, axis=-1, keepdims=True)
-            - xhat_half * jnp.mean(d * xhat_half, axis=-1, keepdims=True)
+    input_grad = rstd * (
+        d - jnp.mean(d, axis=-1, keepdims=True) - xhat * jnp.mean(d * xhat, axis=-1, keepdims=True)
+    ) + lax.dynamic_slice_in_dim(out_grad[0], t * half, half).astype(f32)
+    input_other = swap(input_grad, "tp", 1)
+    norm_sums = jnp.concatenate([jnp.sum(normed_grad * xhat, axis=0), jnp.sum(normed_grad, axis=0)])
+    order.did(input_grad, norm_sums)
+    qkv_part = side_by_side([x[:, : 3 * wide] for x in qkv_pieces])
+    dense_part = side_by_side([x[:, 3 * wide :] for x in qkv_pieces])
+    up_part = side_by_side(up_pieces)
+
+    def in_rows(own_half, other_half):
+        return jnp.concatenate(
+            [jnp.where(t == 0, own_half, other_half), jnp.where(t == 0, other_half, own_half)], axis=0
         )
-        + grad_own[:half].astype(f32)
-    )
-    input_grad = halves(jnp.concatenate([input_grad, swap(input_grad, "tp", 1)], axis=0))
-
-    def summed(left, right):
-        full = lax.dot_general(left, right, by_rows, preferred_element_type=f32).astype(bf16)
-        return line_scatter([full[s * feat : (s + 1) * feat] for s in range(n)]).astype(bf16)
-
-    down_part = spread_columns(summed(grads, act))
-    dense_part = spread_columns(summed(grads, mixed))
-    qkv_sum = summed(normed, qkv_grad_low)
-    qkv_sum = lax.dot_general(qkv_sum, place_of, by_columns, preferred_element_type=f32).astype(bf16)
-    qkv_part = spread_columns(qkv_sum)
-    up_part = spread_columns(summed(normed, up_grad_low))
-
+
+    result = in_rows(result, result_other)
+    input_grad = in_rows(input_grad, input_other)
     def placed(vector):
         full = jnp.zeros((vector.shape[0] * m,), f32)
         return lax.dynamic_update_slice_in_dim(full, vector, c * vector.shape[0], axis=0)
@@ -552,16 +1038,13 @@
         qkv_bias_sum[:1], place_of.astype(f32), by_columns,
         precision=lax.Precision.HIGHEST, preferred_element_type=f32,
     )[0]
-    bias_sums = everywhere(
-        jnp.concatenate([placed(qkv_bias_grad), placed(jnp.sum(up_grad, axis=0))]), "ctx", "fsdp"
-    )
-    qkv_bias_grad, up_bias_grad = bias_sums[: 3 * wide * m], bias_sums[3 * wide * m :]
-    out_bias_grad = everywhere(jnp.sum(out_grad[0].astype(f32), axis=0), "ctx", "fsdp")
-    norm_sums = everywhere(
-        jnp.stack([jnp.sum(normed_grad * xhat_half, axis=0), jnp.sum(normed_grad, axis=0)]),
-        "tp", "ctx", "fsdp",
-    )
-    gain_grad, shift_grad = norm_sums[0], norm_sums[1]
+    norm_sums = norm_sums + swap(norm_sums, "tp", 1)
+    sums = everywhere(
+        jnp.concatenate([norm_sums, out_sum[0], placed(qkv_bias_grad), placed(up_bias_sum[0])]), "ctx", "fsdp"
+    )
+    gain_grad, shift_grad, out_bias_grad = sums[:width], sums[width : 2 * width], sums[2 * width : 3 * width]
+    qkv_bias_grad = sums[3 * width : 3 * width + 3 * wide * m]
+    up_bias_grad = sums[3 * width + 3 * wide * m :]
     return (
         result[None],
         input_grad[None],

time: 826 us -> 666 us (0.81)
  matrix products: 149 us -> 44.7 us
  Pallas kernels: 89.2 us -> 185 us
  waiting for transfers between devices: 214 us -> 128 us
  starting transfers between devices: 199 us -> 166 us
  local copies, waits for them, and re-layouts: 76.7 us -> 54.4 us
  other arithmetic: 85.8 us -> 76.8 us
    pallas_call x0 -> x10, Pallas kernels: none -> 119 us  [the longest x6 104 us: blocks_call(): pl.pallas_call(kernel, grid_spec=pltpu.PrefetchScalarGridSpec(num_scalar_...]
    dot_general x13 -> x5, matrix products: 145 us -> 41.5 us  [the longest x1 12.8 us: shards(): lax.dot_general(grads, order.then(act), by_rows, preferred_element_type=f32)]
    ppermute x53 -> x42, waiting for transfers between devices: 128 us -> 60.4 us  [swap(): return lax.ppermute(x, axis, [(i, i ^ bit) for i in range(size)])]
    ppermute x53 -> x42, starting transfers between devices: 98.6 us -> 37.6 us  [swap(): return lax.ppermute(x, axis, [(i, i ^ bit) for i in range(size)])]
    ppermute x48 -> x36, starting transfers between devices: 100 us -> 128 us  [the longest x18 102 us: line_up(): return lax.ppermute(x, 'fsdp', [(i, i + 1) for i in range(first, last)])]
    select_n x15 -> x2, other arithmetic: 21.2 us -> 0.64 us  [in_rows(): jnp.where(t == 0, own_half, other_half)]
    ppermute x48 -> x36, waiting for transfers between devices: 86.8 us -> 67.5 us  [the longest x18 34.9 us: line_down(): return lax.ppermute(x, 'fsdp', [(i, i - 1) for i in range(first, last)])]
    pallas_call x1, Pallas kernels: 43.9 us -> 26.5 us  [attend(): pl.pallas_call(functools.partial(forward_kernel, heads), grid_spec=pltpu....]
  transfers between devices with their start and end apart: 101 -> 78, of which waited for: 35 -> 26; matrix products, arithmetic and copies ran while one was open for 36% -> 21% of each run, Pallas kernels for 11% -> 25%
where the time goes in v3:
time: 666 us; the launch traced here: 658 us
  Pallas kernels  185 us (28%)
  starting transfers between devices  166 us (25%)
  waiting for transfers between devices  128 us (19%)
  other arithmetic  76.8 us (12%)
  local copies, waits for them, and re-layouts  54.4 us (8%)
  matrix products  44.7 us (7%)
    pallas_call x6, Pallas kernels, blocks_call(): pl.pallas_call(kernel, grid_spec=pltpu.PrefetchScalarGridSpec(num_scalar_...  104 us
    ppermute x18, starting transfers between devices, line_up(): return lax.ppermute(x, 'fsdp', [(i, i + 1) for i in range(first, last)])  102 us
    ppermute x42, waiting for transfers between devices, swap(): return lax.ppermute(x, axis, [(i, i ^ bit) for i in range(size)])  60.4 us
    pallas_call x1, Pallas kernels, attend_back(): pl.pallas_call(functools.partial(backward_kernel, heads), grid_spec=pltpu...  40 us
    ppermute x42, starting transfers between devices, swap(): return lax.ppermute(x, axis, [(i, i ^ bit) for i in range(size)])  37.6 us
    ppermute x18, waiting for transfers between devices, line_down(): return lax.ppermute(x, 'fsdp', [(i, i - 1) for i in range(first, last)])  34.9 us
    ppermute x18, waiting for transfers between devices, line_up(): return lax.ppermute(x, 'fsdp', [(i, i + 1) for i in range(first, last)])  32.6 us
    convert_element_type x11, other arithmetic, add(): return (a.astype(f32) + b.astype(f32)).astype(bf16)  31.1 us
  transfers between devices with their start and end apart: 78, of which 26 were waited for; matrix products, arithmetic and copies ran while one was open for 21% of the time, Pallas kernels for 25%

profile of v3, /device:TPU:0, one launch (start us, length us, event | category | flops | bytes accessed | tf_op | source)
XLA Modules:
  0.0 657.7 jit_solution(11629906812613017095)
XLA Ops:
  4.3 5.0 collective-permute-start
  20.9 10.7 %collective-permute-done.rest_1_ = bf16[512,1024]{1,0:T(8,128)(2,1)S(1)} collective-permute-done((bf16[512,1024]{1,0:T(8,128)(2,1)S(1)}, bf16[512,1024]{1,0:T(8,128)(2,1)S(1)}, u32[]{:S(2)}, u32[]{:S(2)}) %collective-permute-start) | collective-permute-done | bytes 1048608 | tf_op jit(solution)/shard_map/ppermute | solution.py:67
  31.7 4.2 collective-permute-done.1.rest_4_
  46.9 9.1 %fusion.21 = (f32[2048,128]{1,0:T(8,128)}, f32[2048,128]{1,0:T(8,128)}, f32[2048,128]{1,0:T(8,128)S(1)}, f32[2048,128]{1,0:T(8,128)S(1)}) fusion(f32[2048]{0:T(1024)S(1)} %get-tuple-element.387, f32[128]{0:T(128)S(1)} %get-tuple-element.383, f32[128]{0:T(128)S(1)} %get-tuple-element.384, f32[2048]{0:T(1024)S(1)} %get-tuple-element.388), kind=kLoop, calls=%fused_computation.59 | loop fusion | flops 1048576 | bytes 4211712 | tf_op jit(solution)/shard_map/mul | solution.py:846
  56.1 9.6 %collective-permute-done.5.rest_5_ = bf16[512,1024]{1,0:T(8,128)(2,1)} collective-permute-done((bf16[512,1024]{1,0:T(8,128)(2,1)S(1)}, bf16[512,1024]{1,0:T(8,128)(2,1)}, u32[]{:S(2)}, u32[]{:S(2)}) %collective-permute-start.5) | collective-permute-done | bytes 1048608 | tf_op jit(solution)/shard_map/ppermute | solution.py:71
  72.1 8.5 %collective-permute-done.6.refs_5_ = bf16[128,2048]{1,0:T(8,128)(2,1)S(1)} collective-permute-done((bf16[128,2048]{1,0:T(8,128)(2,1)S(1)}, bf16[128,2048]{1,0:T(8,128)(2,1)S(1)}, u32[]{:S(2)}, u32[]{:S(2)}) %collective-permute-start.6) | collective-permute-done | bytes 524320 | tf_op jit(solution)/shard_map/ppermute | solution.py:33
  82.1 5.3 collective-permute-start.14
  87.4 4.1 collective-permute-done.11.rest_6_
  98.7 5.0 assemble.2.x_in_ref.x_ref
  103.8 22.3 %pack.1 = (bf16[2048,768]{1,0:T(8,128)(2,1)}, bf16[256,2048]{1,0:T(8,128)(2,1)S(1)}) custom-call(s32[1]{0:T(128)} %bitcast.1.z_ref, bf16[2048,2048]{1,0:T(8,128)(2,1)} %assemble.2.x_in_ref.x_ref, f32[8,768]{1,0:T(8,128)S(1)} %broadcast_in_dim.71.bias_ref, f32[2048,128]{1,0:T(8,128)S(1)} %get-tuple-element.381.cos_ref, ...), custom_call_target="tpu_custom_call" | custom-call | flops 644245120 | bytes 1048576 | tf_op jit(solution)/shard_map/pack/pallas_call | solution.py:544
  138.0 26.5 %attend_forward.1 = (f32[256,2048]{1,0:T(8,128)S(1)}, f32[8,2048]{1,0:T(8,128)S(1)}, bf16[2048,256]{1,0:T(8,128)(2,1)S(1)}) custom-call(s32[8]{0:T(128)S(1)} %and_select_fusion.5.low_ref, bf16[2048,768]{1,0:T(8,128)(2,1)S(1)} %copy-done.37, bf16[256,2048]{1,0:T(8,128)(2,1)S(1)} %copy-done.40, s32[2048,1]{1,0:T(8,128)S(1)} %copy-done.35, ...), custom_call_target="tpu_custom_call" | custom-call | flops 10737418240 | bytes 10485760 | tf_op jit(solution)/shard_map/attend_forward/pallas_call | solution.py:712
  169.3 24.0 %collective-permute-start.28 = (bf16[512,1024]{1,0:T(8,128)(2,1)S(1)}, bf16[512,1024]{1,0:T(8,128)(2,1)S(1)}, u32[]{:S(2)}, u32[]{:S(2)}) collective-permute-start(bf16[512,1024]{1,0:T(8,128)(2,1)S(1)} %copy-done.10), channel_id=1, source_target_pairs={{0,8},{8,16},{16,24},{1,9},{9,17},{17,25},{2,10},{10,18},{18,26},{... | collective-permute-start | bytes 3145736 | tf_op jit(solution)/shard_map/ppermute | solution.py:67
  194.8 5.6 assemble.3.x_ref
  200.4 6.9 %times.1.grad_ref = bf16[2048,256]{1,0:T(8,128)(2,1)S(1)} custom-call(s32[1]{0:T(128)} %bitcast.1.z_ref, bf16[2048,2048]{1,0:T(8,128)(2,1)} %assemble.3.x_ref, bf16[512,1024]{1,0:T(8,128)(2,1)S(1)} %pad_maximum_fusion.1.rest_0_, bf16[512,1024]{1,0:T(8,128)(2,1)S(1)} %collective-permute-done.rest_1_, bf16[512,1024]{1,0:T(8,128)(2,1)} %collective-permute-done.4.rest_2_, ...), custom_call_target="tpu_custom_call" | custom-call | flops 107374184 | bytes 1048576 | tf_op jit(solution)/shard_map/times/pallas_call | solution.py:544
  207.3 6.9 %convolution_convert_fusion.3 = bf16[2048,256]{0,1:T(8,128)(2,1)} fusion(bf16[2048,2048]{1,0:T(8,128)(2,1)} %assemble.3.x_ref, bf16[2048,256]{1,0:T(8,128)(2,1)S(1)} %get-tuple-element.225.a_ref), kind=kOutput, calls=%fused_computation.12 | convolution fusion | flops 2148007936 | bytes 10485760 | tf_op jit(solution)/shard_map/dot_general | solution.py:901
  215.5 16.3 %up.1 = (f32[2048,1024]{1,0:T(8,128)}, bf16[2048,1024]{1,0:T(8,128)(2,1)}) custom-call(s32[1]{0:T(128)} %bitcast.1.z_ref, bf16[2048,2048]{1,0:T(8,128)(2,1)} %assemble.2.x_in_ref.x_ref, f32[8,1024]{1,0:T(8,128)S(1)} %broadcast_in_dim.76.bias_ref, bf16[512,1024]{1,0:T(8,128)(2,1)S(1)} %copy-done.9, bf16[512,1024]{1,0:T(8,128)(2,1)} %collective-permute-done.14.rest_1_.rest_8_, ...), custom_call_target="tpu_custom_call" | custom-call | flops 429496736 | bytes 1048576 | tf_op jit(solution)/shard_map/up/pallas_call | solution.py:544
  231.8 12.8 %convolution_convert_fusion.1 = bf16[2048,1024]{1,0:T(8,128)(2,1)S(1)} fusion(bf16[2048,2048]{1,0:T(8,128)(2,1)} %assemble.3.x_ref, bf16[2048,1024]{1,0:T(8,128)(2,1)} %get-tuple-element.209.b_ref), kind=kOutput, calls=%fused_computation.4 | convolution fusion | flops 8592031744 | bytes 16777216 | tf_op jit(solution)/shard_map/dot_general | solution.py:910
  250.1 12.7 %collective-permute-start.32 = (bf16[512,1024]{1,0:T(8,128)(2,1)}, bf16[512,1024]{1,0:T(8,128)(2,1)S(1)}, u32[]{:S(2)}, u32[]{:S(2)}) collective-permute-start(bf16[512,1024]{1,0:T(8,128)(2,1)} %get-tuple-element.316), channel_id=1, source_target_pairs={{0,8},{1,9},{2,10},{3,11},{4,12},{5,13},{6,14},{7,15}} | collective-permute-start | bytes 3145736 | tf_op jit(solution)/shard_map/ppermute | solution.py:67
  265.2 40.0 %attend_backward.1 = (bf16[2048,768]{1,0:T(8,128)(2,1)S(1)}, f32[8,768]{1,0:T(8,128)S(1)}) custom-call(s32[8]{0:T(128)S(1)} %and_select_fusion.5.low_ref, bf16[2048,768]{1,0:T(8,128)(2,1)S(1)} %copy-done.38, f32[256,2048]{1,0:T(8,128)S(1)} %copy-done.42, f32[8,2048]{1,0:T(8,128)S(1)} %get-tuple-element.214.lse_ref, bf16[2048,256]{1,0:T(8,128)(2,1)S(1)} %times.1.grad_ref, ...), custom_call_target="tpu_custom_call" | custom-call | flops 30064771072 | bytes 10485760 | tf_op jit(solution)/shard_map/attend_backward/pallas_call | solution.py:737
  308.1 3.2 fusion.5
  313.4 4.7 collective-permute-start.36
  319.7 9.2 %convolution_convert_fusion.2 = bf16[2048,768]{0,1:T(8,128)(2,1)S(1)} fusion(bf16[2048,2048]{1,0:T(8,128)(2,1)} %assemble.2.x_in_ref.x_ref, bf16[2048,768]{1,0:T(8,128)(2,1)S(1)} %get-tuple-element.242.a_ref), kind=kOutput, calls=%fused_computation.5 | convolution fusion | flops 6444023808 | bytes 14680064 | tf_op jit(solution)/shard_map/dot_general | solution.py:927
  332.5 5.4 collective-permute-done.35.rest_13_.rest_6_
  340.1 17.6 %to_features.2 = (bf16[4,256,2048]{2,1,0:T(8,128)(2,1)}, bf16[4,256,2048]{2,1,0:T(8,128)(2,1)}) custom-call(s32[1]{0:T(128)} %bitcast.1.z_ref, bf16[2048,256]{1,0:T(8,128)(2,1)S(1)} %get-tuple-element.225.a_ref, bf16[2048,1024]{1,0:T(8,128)(2,1)} %get-tuple-element.209.b_ref, bf16[512,1024]{1,0:T(8,128)(2,1)S(1)} %pad_maximum_fusion.1.rest_0_, ...), custom_call_target="tpu_custom_call" | custom-call | flops 536870912 | bytes 1048576 | tf_op jit(solution)/shard_map/to_features/pallas_call | solution.py:544
  357.9 3.6 add_convert_fusion.9
  361.5 12.1 %collective-permute-start.39 = (bf16[512,1024]{1,0:T(8,128)(2,1)}, bf16[512,1024]{1,0:T(8,128)(2,1)}, u32[]{:S(2)}, u32[]{:S(2)}) collective-permute-start(bf16[512,1024]{1,0:T(8,128)(2,1)} %get-tuple-element.311), channel_id=1, source_target_pairs={{0,8},{8,16},{16,24},{1,9},{9,17},{17,25},{2,10},{10,18},{18,26},{... | collective-permute-start | bytes 3145736 | tf_op jit(solution)/shard_map/ppermute | solution.py:67
  376.7 5.5 collective-permute-start.41
  392.7 18.4 %up_back.1 = (bf16[2048,1024]{1,0:T(8,128)(2,1)}, f32[8,1024]{1,0:T(8,128)S(1)}) custom-call(s32[1]{0:T(128)} %bitcast.1.z_ref, bf16[2048,2048]{1,0:T(8,128)(2,1)} %assemble.3.x_ref, f32[2048,1024]{1,0:T(8,128)} %get-tuple-element.229.up_ref, bf16[512,1024]{1,0:T(8,128)(2,1)S(1)} %copy-done.11, bf16[512,1024]{1,0:T(8,128)(2,1)S(1)} %copy-done.25, ...), custom_call_target="tpu_custom_call" | custom-call | flops 429496736 | bytes 1048576 | tf_op jit(solution)/shard_map/up_back/pallas_call | solution.py:544
  411.4 7.0 %collective-permute-done.41 = bf16[512,1024]{0,1:T(8,128)(2,1)} collective-permute-done((bf16[512,1024]{0,1:T(8,128)(2,1)}, bf16[512,1024]{0,1:T(8,128)(2,1)}, u32[]{:S(2)}, u32[]{:S(2)}) %collective-permute-start.41) | collective-permute-done | bytes 1048608 | tf_op jit(solution)/shard_map/ppermute | solution.py:67
  418.4 3.4 fusion.7
  421.8 4.4 collective-permute-start.45
  428.1 3.5 add_convert_fusion.5
  431.6 11.8 %convolution_convert_fusion = bf16[2048,1024]{1,0:T(8,128)(2,1)S(1)} fusion(bf16[2048,2048]{1,0:T(8,128)(2,1)} %assemble.2.x_in_ref.x_ref, bf16[2048,1024]{1,0:T(8,128)(2,1)S(1)} %copy-done.63), kind=kOutput, calls=%fused_computation.3 | convolution fusion | flops 8592031744 | bytes 16777216 | tf_op jit(solution)/shard_map/dot_general | solution.py:958
  443.4 5.6 add_convert_fusion.1
  452.4 4.5 collective-permute-start.49
  462.9 22.4 %to_features.3 = (bf16[4,256,2048]{2,1,0:T(8,128)(2,1)}, bf16[4,256,2048]{2,1,0:T(8,128)(2,1)}) custom-call(s32[1]{0:T(128)} %bitcast.1.z_ref, bf16[2048,768]{1,0:T(8,128)(2,1)} %copy-done.32, bf16[2048,1024]{1,0:T(8,128)(2,1)} %get-tuple-element.237.b_ref, bf16[512,1024]{1,0:T(8,128)(2,1)S(1)} %pad_maximum_fusion.1.rest_0_, ...), custom_call_target="tpu_custom_call" | custom-call | flops 751619264 | bytes 1048576 | tf_op jit(solution)/shard_map/to_features/pallas_call | solution.py:544
  488.7 4.8 collective-permute-start.51
  499.7 3.7 fusion.9
  503.4 11.3 %collective-permute-done.52 = bf16[512,1024]{0,1:T(8,128)(2,1)S(1)} collective-permute-done((bf16[512,1024]{0,1:T(8,128)(2,1)S(1)}, bf16[512,1024]{0,1:T(8,128)(2,1)S(1)}, u32[]{:S(2)}, u32[]{:S(2)}) %collective-permute-start.52) | collective-permute-done | bytes 1048608 | tf_op jit(solution)/shard_map/ppermute | solution.py:71
  514.7 4.8 collective-permute-start.53
  527.8 13.6 %collective-permute-done.53 = bf16[512,1024]{1,0:T(8,128)(2,1)} collective-permute-done((bf16[512,1024]{1,0:T(8,128)(2,1)}, bf16[512,1024]{1,0:T(8,128)(2,1)}, u32[]{:S(2)}, u32[]{:S(2)}) %collective-permute-start.53) | collective-permute-done | bytes 1048608 | tf_op jit(solution)/shard_map/ppermute | solution.py:67
  541.4 3.9 add_convert_fusion.3
  545.3 8.5 %collective-permute-start.67 = (bf16[512,1024]{1,0:T(8,128)(2,1)}, bf16[512,1024]{1,0:T(8,128)(2,1)}, u32[]{:S(2)}, u32[]{:S(2)}) collective-permute-start(bf16[512,1024]{1,0:T(8,128)(2,1)} %get-tuple-element.291), channel_id=1, source_target_pairs={{0,8},{8,16},{16,24},{1,9},{9,17},{17,25},{2,10},{10,18},{18,26},{... | collective-permute-start | bytes 3145736 | tf_op jit(solution)/shard_map/ppermute | solution.py:67
  555.1 4.1 add_convert_fusion
  564.2 7.2 %collective-permute-done.56 = bf16[128,2048]{1,0:T(8,128)(2,1)S(1)} collective-permute-done((bf16[128,2048]{1,0:T(8,128)(2,1)S(1)}, bf16[128,2048]{1,0:T(8,128)(2,1)S(1)}, u32[]{:S(2)}, u32[]{:S(2)}) %collective-permute-start.56) | collective-permute-done | bytes 524320 | tf_op jit(solution)/shard_map/ppermute | solution.py:33
  583.3 3.8 collective-permute-done.60
  591.4 14.7 %collective-permute-done.66 = bf16[256,2048]{1,0:T(8,128)(2,1)} collective-permute-done((bf16[256,2048]{1,0:T(8,128)(2,1)}, bf16[256,2048]{1,0:T(8,128)(2,1)}, u32[]{:S(2)}, u32[]{:S(2)}) %collective-permute-start.66) | collective-permute-done | bytes 1048608 | tf_op jit(solution)/shard_map/ppermute | solution.py:33
  633.3 3.1 collective-permute-done.71
  (442 shorter events, 193.7 us)
Async XLA Ops:
  4.3 27.3 %collective-permute-start = (bf16[512,1024]{1,0:T(8,128)(2,1)S(1)}, bf16[512,1024]{1,0:T(8,128)(2,1)S(1)}, u32[]{:S(2)}, u32[]{:S(2)}) collective-permute-start(bf16[512,1024]{1,0:T(8,128)(2,1)S(1)} %pad_maximum_fusion.1.rest_0_), channel_id=1, source_target_pairs={{0,8},{8,16},{16,24},{1,9},{9,17},{17,25},{2,10},{10,18},{18,26},{... | collective-permute-start | bytes 3145736 | tf_op jit(solution)/shard_map/ppermute | solution.py:67
  9.3 26.5 %collective-permute-start.1 = (bf16[512,1024]{1,0:T(8,128)(2,1)S(1)}, bf16[512,1024]{1,0:T(8,128)(2,1)S(1)}, u32[]{:S(2)}, u32[]{:S(2)}) collective-permute-start(bf16[512,1024]{1,0:T(8,128)(2,1)S(1)} %pad_maximum_fusion.1.rest_0_), channel_id=1, source_target_pairs={{8,0},{16,8},{24,16},{9,1},{17,9},{25,17},{10,2},{18,10},{26,18},{... | collective-permute-start | bytes 3145736 | tf_op jit(solution)/shard_map/ppermute | solution.py:71
  17.9 49.9 %collective-permute-start.2 = (bf16[256,2048]{1,0:T(8,128)(2,1)}, bf16[256,2048]{1,0:T(8,128)(2,1)}, u32[]{:S(2)}, u32[]{:S(2)}) collective-permute-start(bf16[256,2048]{1,0:T(8,128)(2,1)} %slice.286), channel_id=1, source_target_pairs={{0,2},{2,0},{4,6},{6,4},{1,3},{3,1},{5,7},{7,5},{8,10},{10,8},{12,... | collective-permute-start | bytes 3145736 | tf_op jit(solution)/shard_map/ppermute | solution.py:33
  19.4 48.4 %collective-permute-start.3 = (bf16[256,2048]{1,0:T(8,128)(2,1)}, bf16[256,2048]{1,0:T(8,128)(2,1)}, u32[]{:S(2)}, u32[]{:S(2)}) collective-permute-start(bf16[256,2048]{1,0:T(8,128)(2,1)} %slice.286), channel_id=1, source_target_pairs={{0,4},{2,6},{4,0},{6,2},{1,5},{3,7},{5,1},{7,3},{8,12},{10,14},{12... | collective-permute-start | bytes 3145736 | tf_op jit(solution)/shard_map/ppermute | solution.py:33
  37.5 28.1 %collective-permute-start.5 = (bf16[512,1024]{1,0:T(8,128)(2,1)S(1)}, bf16[512,1024]{1,0:T(8,128)(2,1)}, u32[]{:S(2)}, u32[]{:S(2)}) collective-permute-start(bf16[512,1024]{1,0:T(8,128)(2,1)S(1)} %collective-permute-done.1.rest_4_), channel_id=1, source_target_pairs={{8,0},{16,8},{9,1},{17,9},{10,2},{18,10},{11,3},{19,11},{12,4},{20... | collective-permute-start | bytes 3145736 | tf_op jit(solution)/shard_map/ppermute | solution.py:71
  66.5 25.0 %collective-permute-start.11 = (bf16[512,1024]{1,0:T(8,128)(2,1)}, bf16[512,1024]{1,0:T(8,128)(2,1)S(1)}, u32[]{:S(2)}, u32[]{:S(2)}) collective-permute-start(bf16[512,1024]{1,0:T(8,128)(2,1)} %collective-permute-done.5.rest_5_), channel_id=1, source_target_pairs={{8,0},{9,1},{10,2},{11,3},{12,4},{13,5},{14,6},{15,7}} | collective-permute-start | bytes 3145736 | tf_op jit(solution)/shard_map/ppermute | solution.py:71
  82.1 44.9 %collective-permute-start.14 = (bf16[512,1024]{1,0:T(8,128)(2,1)S(1)}, bf16[512,1024]{1,0:T(8,128)(2,1)}, u32[]{:S(2)}, u32[]{:S(2)}) collective-permute-start(bf16[512,1024]{1,0:T(8,128)(2,1)S(1)} %constant_dynamic-slice_fusion.28.rest_0_.rest_7_), channel_id=1, source_target_pairs={{0,8},{8,16},{16,24},{1,9},{9,17},{17,25},{2,10},{10,18},{18,26},{... | collective-permute-start | bytes 3145736 | tf_op jit(solution)/shard_map/ppermute | solution.py:67
  91.5 35.6 %collective-permute-start.15 = (bf16[512,1024]{1,0:T(8,128)(2,1)S(1)}, bf16[512,1024]{1,0:T(8,128)(2,1)S(1)}, u32[]{:S(2)}, u32[]{:S(2)}) collective-permute-start(bf16[512,1024]{1,0:T(8,128)(2,1)S(1)} %constant_dynamic-slice_fusion.28.rest_0_.rest_7_), channel_id=1, source_target_pairs={{8,0},{16,8},{24,16},{9,1},{17,9},{25,17},{10,2},{18,10},{26,18},{... | collective-permute-start | bytes 3145736 | tf_op jit(solution)/shard_map/ppermute | solution.py:71
  94.4 35.8 %collective-permute-start.16 = (bf16[256,2048]{1,0:T(8,128)(2,1)}, bf16[256,2048]{1,0:T(8,128)(2,1)}, u32[]{:S(2)}, u32[]{:S(2)}) collective-permute-start(bf16[256,2048]{1,0:T(8,128)(2,1)} %slice.227), channel_id=1, source_target_pairs={{0,2},{2,0},{4,6},{6,4},{1,3},{3,1},{5,7},{7,5},{8,10},{10,8},{12,... | collective-permute-start | bytes 3145736 | tf_op jit(solution)/shard_map/ppermute | solution.py:33
  95.9 34.3 %collective-permute-start.17 = (bf16[256,2048]{1,0:T(8,128)(2,1)}, bf16[256,2048]{1,0:T(8,128)(2,1)}, u32[]{:S(2)}, u32[]{:S(2)}) collective-permute-start(bf16[256,2048]{1,0:T(8,128)(2,1)} %slice.227), channel_id=1, source_target_pairs={{0,4},{2,6},{4,0},{6,2},{1,5},{3,7},{5,1},{7,3},{8,12},{10,14},{12... | collective-permute-start | bytes 3145736 | tf_op jit(solution)/shard_map/ppermute | solution.py:33
  128.9 37.0 %collective-permute-start.23 = (bf16[512,1024]{1,0:T(8,128)(2,1)}, bf16[512,1024]{1,0:T(8,128)(2,1)}, u32[]{:S(2)}, u32[]{:S(2)}) collective-permute-start(bf16[512,1024]{1,0:T(8,128)(2,1)} %copy-done.19), channel_id=1, source_target_pairs={{8,0},{16,8},{9,1},{17,9},{10,2},{18,10},{11,3},{19,11},{12,4},{20... | collective-permute-start | bytes 3145736 | tf_op jit(solution)/shard_map/ppermute | solution.py:71
  130.2 35.7 %collective-permute-start.20 = (bf16[256,2048]{1,0:T(8,128)(2,1)}, bf16[256,2048]{1,0:T(8,128)(2,1)}, u32[]{:S(2)}, u32[]{:S(2)}) collective-permute-start(bf16[256,2048]{1,0:T(8,128)(2,1)} %collective-permute-done.16.refs_1_), channel_id=1, source_target_pairs={{0,1},{1,0},{2,3},{3,2},{4,5},{5,4},{6,7},{7,6},{8,9},{9,8},{10,11... | collective-permute-start | bytes 3145736 | tf_op jit(solution)/shard_map/ppermute | solution.py:33
  130.3 35.6 %collective-permute-start.21 = (bf16[256,2048]{1,0:T(8,128)(2,1)}, bf16[256,2048]{1,0:T(8,128)(2,1)}, u32[]{:S(2)}, u32[]{:S(2)}) collective-permute-start(bf16[256,2048]{1,0:T(8,128)(2,1)} %collective-permute-done.17.refs_3_), channel_id=1, source_target_pairs={{0,1},{1,0},{2,3},{3,2},{4,5},{5,4},{6,7},{7,6},{8,9},{9,8},{10,11... | collective-permute-start | bytes 3145736 | tf_op jit(solution)/shard_map/ppermute | solution.py:33
  134.5 31.4 %collective-permute-start.18 = (bf16[128,2048]{1,0:T(8,128)(2,1)S(1)}, bf16[128,2048]{1,0:T(8,128)(2,1)S(1)}, u32[]{:S(2)}, u32[]{:S(2)}) collective-permute-start(bf16[128,2048]{1,0:T(8,128)(2,1)S(1)} %slice.228), channel_id=1, source_target_pairs={{0,4},{2,6},{4,0},{6,2},{1,5},{3,7},{5,1},{7,3},{8,12},{10,14},{12... | collective-permute-start | bytes 1572872 | tf_op jit(solution)/shard_map/ppermute | solution.py:33
  135.1 30.8 %collective-permute-start.19 = (bf16[128,2048]{1,0:T(8,128)(2,1)S(1)}, bf16[128,2048]{1,0:T(8,128)(2,1)S(1)}, u32[]{:S(2)}, u32[]{:S(2)}) collective-permute-start(bf16[128,2048]{1,0:T(8,128)(2,1)S(1)} %slice.229), channel_id=1, source_target_pairs={{0,2},{2,0},{4,6},{6,4},{1,3},{3,1},{5,7},{7,5},{8,10},{10,8},{12,... | collective-permute-start | bytes 1572872 | tf_op jit(solution)/shard_map/ppermute | solution.py:33
  165.9 27.3 %collective-permute-start.24 = (bf16[128,2048]{1,0:T(8,128)(2,1)S(1)}, bf16[128,2048]{1,0:T(8,128)(2,1)S(1)}, u32[]{:S(2)}, u32[]{:S(2)}) collective-permute-start(bf16[128,2048]{1,0:T(8,128)(2,1)S(1)} %collective-permute-done.18.refs_5_), channel_id=1, source_target_pairs={{0,1},{1,0},{2,3},{3,2},{4,5},{5,4},{6,7},{7,6},{8,9},{9,8},{10,11... | collective-permute-start | bytes 1572872 | tf_op jit(solution)/shard_map/ppermute | solution.py:33
  166.0 28.8 %collective-permute-start.25 = (bf16[128,2048]{1,0:T(8,128)(2,1)S(1)}, bf16[128,2048]{1,0:T(8,128)(2,1)S(1)}, u32[]{:S(2)}, u32[]{:S(2)}) collective-permute-start(bf16[128,2048]{1,0:T(8,128)(2,1)S(1)} %collective-permute-done.19.refs_6_), channel_id=1, source_target_pairs={{0,1},{1,0},{2,3},{3,2},{4,5},{5,4},{6,7},{7,6},{8,9},{9,8},{10,11... | collective-permute-start | bytes 1572872 | tf_op jit(solution)/shard_map/ppermute | solution.py:33
  166.5 47.6 %collective-permute-start.26 = (bf16[512,1024]{1,0:T(8,128)(2,1)S(1)}, bf16[512,1024]{1,0:T(8,128)(2,1)S(1)}, u32[]{:S(2)}, u32[]{:S(2)}) collective-permute-start(bf16[512,1024]{1,0:T(8,128)(2,1)S(1)} %copy-done.22), channel_id=1, source_target_pairs={{16,24},{17,25},{18,26},{19,27},{20,28},{21,29},{22,30},{23,31}} | collective-permute-start | bytes 3145736 | tf_op jit(solution)/shard_map/ppermute | solution.py:67
  167.2 47.3 %collective-permute-start.27 = (bf16[512,1024]{1,0:T(8,128)(2,1)}, bf16[512,1024]{1,0:T(8,128)(2,1)S(1)}, u32[]{:S(2)}, u32[]{:S(2)}) collective-permute-start(bf16[512,1024]{1,0:T(8,128)(2,1)} %collective-permute-done.23.rest_5_.rest_12_), channel_id=1, source_target_pairs={{8,0},{9,1},{10,2},{11,3},{12,4},{13,5},{14,6},{15,7}} | collective-permute-start | bytes 3145736 | tf_op jit(solution)/shard_map/ppermute | solution.py:71
  169.3 78.5 %collective-permute-start.28 = (bf16[512,1024]{1,0:T(8,128)(2,1)S(1)}, bf16[512,1024]{1,0:T(8,128)(2,1)S(1)}, u32[]{:S(2)}, u32[]{:S(2)}) collective-permute-start(bf16[512,1024]{1,0:T(8,128)(2,1)S(1)} %copy-done.10), channel_id=1, source_target_pairs={{0,8},{8,16},{16,24},{1,9},{9,17},{17,25},{2,10},{10,18},{18,26},{... | collective-permute-start | bytes 3145736 | tf_op jit(solution)/shard_map/ppermute | solution.py:67
  193.3 54.5 %collective-permute-start.29 = (bf16[512,1024]{1,0:T(8,128)(2,1)S(1)}, bf16[512,1024]{1,0:T(8,128)(2,1)S(1)}, u32[]{:S(2)}, u32[]{:S(2)}) collective-permute-start(bf16[512,1024]{1,0:T(8,128)(2,1)S(1)} %copy-done.10), channel_id=1, source_target_pairs={{8,0},{16,8},{24,16},{9,1},{17,9},{25,17},{10,2},{18,10},{26,18},{... | collective-permute-start | bytes 3145736 | tf_op jit(solution)/shard_map/ppermute | solution.py:71
  247.8 60.3 %collective-permute-start.30 = (bf16[512,1024]{1,0:T(8,128)(2,1)S(1)}, bf16[512,1024]{1,0:T(8,128)(2,1)S(1)}, u32[]{:S(2)}, u32[]{:S(2)}) collective-permute-start(bf16[512,1024]{1,0:T(8,128)(2,1)S(1)} %collective-permute-done.28.rest_8_.rest_1_), channel_id=1, source_target_pairs={{8,16},{16,24},{9,17},{17,25},{10,18},{18,26},{11,19},{19,27},{12,... | collective-permute-start | bytes 3145736 | tf_op jit(solution)/shard_map/ppermute | solution.py:67
  248.6 59.4 %collective-permute-start.31 = (bf16[512,1024]{1,0:T(8,128)(2,1)S(1)}, bf16[512,1024]{1,0:T(8,128)(2,1)S(1)}, u32[]{:S(2)}, u32[]{:S(2)}) collective-permute-start(bf16[512,1024]{1,0:T(8,128)(2,1)S(1)} %collective-permute-done.29.rest_11_.rest_4_), channel_id=1, source_target_pairs={{8,0},{16,8},{9,1},{17,9},{10,2},{18,10},{11,3},{19,11},{12,4},{20... | collective-permute-start | bytes 3145736 | tf_op jit(solution)/shard_map/ppermute | solution.py:71
  250.1 58.0 %collective-permute-start.32 = (bf16[512,1024]{1,0:T(8,128)(2,1)}, bf16[512,1024]{1,0:T(8,128)(2,1)S(1)}, u32[]{:S(2)}, u32[]{:S(2)}) collective-permute-start(bf16[512,1024]{1,0:T(8,128)(2,1)} %get-tuple-element.316), channel_id=1, source_target_pairs={{0,8},{1,9},{2,10},{3,11},{4,12},{5,13},{6,14},{7,15}} | collective-permute-start | bytes 3145736 | tf_op jit(solution)/shard_map/ppermute | solution.py:67
  262.8 45.3 %collective-permute-start.33 = (bf16[512,1024]{1,0:T(8,128)(2,1)}, bf16[512,1024]{1,0:T(8,128)(2,1)}, u32[]{:S(2)}, u32[]{:S(2)}) collective-permute-start(bf16[512,1024]{1,0:T(8,128)(2,1)} %get-tuple-element.314), channel_id=1, source_target_pairs={{24,16},{25,17},{26,18},{27,19},{28,20},{29,21},{30,22},{31,23}} | collective-permute-start | bytes 3145736 | tf_op jit(solution)/shard_map/ppermute | solution.py:71
  312.1 25.8 %collective-permute-start.35 = (bf16[512,1024]{1,0:T(8,128)(2,1)S(1)}, bf16[512,1024]{1,0:T(8,128)(2,1)S(1)}, u32[]{:S(2)}, u32[]{:S(2)}) collective-permute-start(bf16[512,1024]{1,0:T(8,128)(2,1)S(1)} %collective-permute-done.31.rest_12_.rest_5_), channel_id=1, source_target_pairs={{8,0},{9,1},{10,2},{11,3},{12,4},{13,5},{14,6},{15,7}} | collective-permute-start | bytes 3145736 | tf_op jit(solution)/shard_map/ppermute | solution.py:71
  313.4 25.8 %collective-permute-start.36 = (bf16[512,1024]{1,0:T(8,128)(2,1)S(1)}, bf16[512,1024]{1,0:T(8,128)(2,1)S(1)}, u32[]{:S(2)}, u32[]{:S(2)}) collective-permute-start(bf16[512,1024]{1,0:T(8,128)(2,1)S(1)} %get-tuple-element.313), channel_id=1, source_target_pairs={{0,8},{8,16},{1,9},{9,17},{2,10},{10,18},{3,11},{11,19},{4,12},{12... | collective-permute-start | bytes 3145736 | tf_op jit(solution)/shard_map/ppermute | solution.py:67
  357.8 73.8 %collective-permute-start.38 = (bf16[4,256,2048]{2,1,0:T(8,128)(2,1)}, bf16[4,256,2048]{2,1,0:T(8,128)(2,1)}, u32[]{:S(2)}, u32[]{:S(2)}) collective-permute-start(bf16[4,256,2048]{2,1,0:T(8,128)(2,1)} %get-tuple-element.227), channel_id=1, source_target_pairs={{0,1},{1,0},{2,3},{3,2},{4,5},{5,4},{6,7},{7,6},{8,9},{9,8},{10,11... | collective-permute-start | bytes 12582920 | tf_op jit(solution)/shard_map/ppermute | solution.py:33
  361.5 50.0 %collective-permute-start.39 = (bf16[512,1024]{1,0:T(8,128)(2,1)}, bf16[512,1024]{1,0:T(8,128)(2,1)}, u32[]{:S(2)}, u32[]{:S(2)}) collective-permute-start(bf16[512,1024]{1,0:T(8,128)(2,1)} %get-tuple-element.311), channel_id=1, source_target_pairs={{0,8},{8,16},{16,24},{1,9},{9,17},{17,25},{2,10},{10,18},{18,26},{... | collective-permute-start | bytes 3145736 | tf_op jit(solution)/shard_map/ppermute | solution.py:67
  373.6 37.8 %collective-permute-start.40 = (bf16[512,1024]{1,0:T(8,128)(2,1)}, bf16[512,1024]{1,0:T(8,128)(2,1)}, u32[]{:S(2)}, u32[]{:S(2)}) collective-permute-start(bf16[512,1024]{1,0:T(8,128)(2,1)} %get-tuple-element.310), channel_id=1, source_target_pairs={{8,0},{16,8},{24,16},{9,1},{17,9},{25,17},{10,2},{18,10},{26,18},{... | collective-permute-start | bytes 3145736 | tf_op jit(solution)/shard_map/ppermute | solution.py:71
  375.0 36.4 %collective-permute-start.42 = (bf16[512,1024]{0,1:T(8,128)(2,1)}, bf16[512,1024]{0,1:T(8,128)(2,1)}, u32[]{:S(2)}, u32[]{:S(2)}) collective-permute-start(bf16[512,1024]{0,1:T(8,128)(2,1)} %pad_maximum_fusion.5), channel_id=1, source_target_pairs={{24,16},{25,17},{26,18},{27,19},{28,20},{29,21},{30,22},{31,23}} | collective-permute-start | bytes 3145736 | tf_op jit(solution)/shard_map/ppermute | solution.py:71
  376.7 41.7 %collective-permute-start.41 = (bf16[512,1024]{0,1:T(8,128)(2,1)}, bf16[512,1024]{0,1:T(8,128)(2,1)}, u32[]{:S(2)}, u32[]{:S(2)}) collective-permute-start(bf16[512,1024]{0,1:T(8,128)(2,1)} %pad_maximum_fusion.3), channel_id=1, source_target_pairs={{0,8},{1,9},{2,10},{3,11},{4,12},{5,13},{6,14},{7,15}} | collective-permute-start | bytes 3145736 | tf_op jit(solution)/shard_map/ppermute | solution.py:67
  421.8 35.1 %collective-permute-start.45 = (bf16[512,1024]{0,1:T(8,128)(2,1)}, bf16[512,1024]{0,1:T(8,128)(2,1)S(1)}, u32[]{:S(2)}, u32[]{:S(2)}) collective-permute-start(bf16[512,1024]{0,1:T(8,128)(2,1)} %get-tuple-element.353), channel_id=1, source_target_pairs={{0,8},{8,16},{1,9},{9,17},{2,10},{10,18},{3,11},{11,19},{4,12},{12... | collective-permute-start | bytes 3145736 | tf_op jit(solution)/shard_map/ppermute | solution.py:67
  426.3 32.3 %collective-permute-start.46 = (bf16[512,1024]{0,1:T(8,128)(2,1)}, bf16[512,1024]{0,1:T(8,128)(2,1)}, u32[]{:S(2)}, u32[]{:S(2)}) collective-permute-start(bf16[512,1024]{0,1:T(8,128)(2,1)} %get-tuple-element.352), channel_id=1, source_target_pairs={{16,8},{24,16},{17,9},{25,17},{18,10},{26,18},{19,11},{27,19},{20,... | collective-permute-start | bytes 3145736 | tf_op jit(solution)/shard_map/ppermute | solution.py:71
  452.4 44.8 %collective-permute-start.49 = (bf16[512,1024]{1,0:T(8,128)(2,1)}, bf16[512,1024]{1,0:T(8,128)(2,1)}, u32[]{:S(2)}, u32[]{:S(2)}) collective-permute-start(bf16[512,1024]{1,0:T(8,128)(2,1)} %get-tuple-element.308), channel_id=1, source_target_pairs={{0,8},{1,9},{2,10},{3,11},{4,12},{5,13},{6,14},{7,15}} | collective-permute-start | bytes 3145736 | tf_op jit(solution)/shard_map/ppermute | solution.py:67
  456.9 41.7 %collective-permute-start.50 = (bf16[512,1024]{1,0:T(8,128)(2,1)}, bf16[512,1024]{1,0:T(8,128)(2,1)}, u32[]{:S(2)}, u32[]{:S(2)}) collective-permute-start(bf16[512,1024]{1,0:T(8,128)(2,1)} %get-tuple-element.306), channel_id=1, source_target_pairs={{24,16},{25,17},{26,18},{27,19},{28,20},{29,21},{30,22},{31,23}} | collective-permute-start | bytes 3145736 | tf_op jit(solution)/shard_map/ppermute | solution.py:71
  485.3 69.8 %collective-permute-start.55 = (bf16[4,256,2048]{2,1,0:T(8,128)(2,1)}, bf16[4,256,2048]{2,1,0:T(8,128)(2,1)}, u32[]{:S(2)}, u32[]{:S(2)}) collective-permute-start(bf16[4,256,2048]{2,1,0:T(8,128)(2,1)} %get-tuple-element.253), channel_id=1, source_target_pairs={{0,1},{1,0},{2,3},{3,2},{4,5},{5,4},{6,7},{7,6},{8,9},{9,8},{10,11... | collective-permute-start | bytes 12582920 | tf_op jit(solution)/shard_map/ppermute | solution.py:33
  487.4 27.3 %collective-permute-start.52 = (bf16[512,1024]{0,1:T(8,128)(2,1)S(1)}, bf16[512,1024]{0,1:T(8,128)(2,1)S(1)}, u32[]{:S(2)}, u32[]{:S(2)}) collective-permute-start(bf16[512,1024]{0,1:T(8,128)(2,1)S(1)} %add_convert_fusion.7), channel_id=1, source_target_pairs={{8,0},{16,8},{24,16},{9,1},{17,9},{25,17},{10,2},{18,10},{26,18},{... | collective-permute-start | bytes 3145736 | tf_op jit(solution)/shard_map/ppermute | solution.py:71
  488.7 30.8 %collective-permute-start.51 = (bf16[512,1024]{0,1:T(8,128)(2,1)S(1)}, bf16[512,1024]{0,1:T(8,128)(2,1)S(1)}, u32[]{:S(2)}, u32[]{:S(2)}) collective-permute-start(bf16[512,1024]{0,1:T(8,128)(2,1)S(1)} %add_convert_fusion.8), channel_id=1, source_target_pairs={{0,8},{8,16},{16,24},{1,9},{9,17},{17,25},{2,10},{10,18},{18,26},{... | collective-permute-start | bytes 3145736 | tf_op jit(solution)/shard_map/ppermute | solution.py:67
  497.2 26.6 %collective-permute-start.48 = (bf16[256,2048]{1,0:T(8,128)(2,1)}, bf16[256,2048]{1,0:T(8,128)(2,1)}, u32[]{:S(2)}, u32[]{:S(2)}) collective-permute-start(bf16[256,2048]{1,0:T(8,128)(2,1)} %pad_maximum_fusion.7), channel_id=1, source_target_pairs={{0,4},{2,6},{4,0},{6,2},{1,5},{3,7},{5,1},{7,3},{8,12},{10,14},{12... | collective-permute-start | bytes 3145736 | tf_op jit(solution)/shard_map/ppermute | solution.py:33
  498.7 25.1 %collective-permute-start.47 = (bf16[256,2048]{1,0:T(8,128)(2,1)}, bf16[256,2048]{1,0:T(8,128)(2,1)}, u32[]{:S(2)}, u32[]{:S(2)}) collective-permute-start(bf16[256,2048]{1,0:T(8,128)(2,1)} %pad_maximum_fusion.6), channel_id=1, source_target_pairs={{0,2},{2,0},{4,6},{6,4},{1,3},{3,1},{5,7},{7,5},{8,10},{10,8},{12,... | collective-permute-start | bytes 3145736 | tf_op jit(solution)/shard_map/ppermute | solution.py:33
  514.7 26.7 %collective-permute-start.53 = (bf16[512,1024]{1,0:T(8,128)(2,1)}, bf16[512,1024]{1,0:T(8,128)(2,1)}, u32[]{:S(2)}, u32[]{:S(2)}) collective-permute-start(bf16[512,1024]{1,0:T(8,128)(2,1)} %get-tuple-element.299), channel_id=1, source_target_pairs={{0,8},{8,16},{1,9},{9,17},{2,10},{10,18},{3,11},{11,19},{4,12},{12... | collective-permute-start | bytes 3145736 | tf_op jit(solution)/shard_map/ppermute | solution.py:67
  545.3 63.3 %collective-permute-start.67 = (bf16[512,1024]{1,0:T(8,128)(2,1)}, bf16[512,1024]{1,0:T(8,128)(2,1)}, u32[]{:S(2)}, u32[]{:S(2)}) collective-permute-start(bf16[512,1024]{1,0:T(8,128)(2,1)} %get-tuple-element.291), channel_id=1, source_target_pairs={{0,8},{8,16},{16,24},{1,9},{9,17},{17,25},{2,10},{10,18},{18,26},{... | collective-permute-start | bytes 3145736 | tf_op jit(solution)/shard_map/ppermute | solution.py:67
  553.8 55.8 %collective-permute-start.68 = (bf16[512,1024]{1,0:T(8,128)(2,1)}, bf16[512,1024]{1,0:T(8,128)(2,1)}, u32[]{:S(2)}, u32[]{:S(2)}) collective-permute-start(bf16[512,1024]{1,0:T(8,128)(2,1)} %get-tuple-element.290), channel_id=1, source_target_pairs={{8,0},{16,8},{24,16},{9,1},{17,9},{25,17},{10,2},{18,10},{26,18},{... | collective-permute-start | bytes 3145736 | tf_op jit(solution)/shard_map/ppermute | solution.py:71
  588.0 30.7 %collective-permute-start.61 = (bf16[256,2048]{1,0:T(8,128)(2,1)S(1)}, bf16[256,2048]{1,0:T(8,128)(2,1)S(1)}, u32[]{:S(2)}, u32[]{:S(2)}) collective-permute-start(bf16[256,2048]{1,0:T(8,128)(2,1)S(1)} %fusion.11), channel_id=1, source_target_pairs={{0,1},{1,0},{2,3},{3,2},{4,5},{5,4},{6,7},{7,6},{8,9},{9,8},{10,11... | collective-permute-start | bytes 3145736 | tf_op jit(solution)/shard_map/ppermute | solution.py:33
  621.0 30.9 %collective-permute-start.75 = (bf16[128,1024]{1,0:T(8,128)(2,1)S(1)}, bf16[128,1024]{1,0:T(8,128)(2,1)S(1)}, u32[]{:S(2)}, u32[]{:S(2)}) collective-permute-start(bf16[128,1024]{1,0:T(8,128)(2,1)S(1)} %get-tuple-element.339), channel_id=1, source_target_pairs={{0,2},{2,0},{4,6},{6,4},{1,3},{3,1},{5,7},{7,5},{8,10},{10,8},{12,... | collective-permute-start | bytes 786440 | tf_op jit(solution)/shard_map/ppermute | solution.py:33
  622.1 29.8 %collective-permute-start.76 = (bf16[128,1024]{1,0:T(8,128)(2,1)S(1)}, bf16[128,1024]{1,0:T(8,128)(2,1)S(1)}, u32[]{:S(2)}, u32[]{:S(2)}) collective-permute-start(bf16[128,1024]{1,0:T(8,128)(2,1)S(1)} %get-tuple-element.338), channel_id=1, source_target_pairs={{0,4},{2,6},{4,0},{6,2},{1,5},{3,7},{5,1},{7,3},{8,12},{10,14},{12... | collective-permute-start | bytes 786440 | tf_op jit(solution)/shard_map/ppermute | solution.py:33
  623.4 28.5 %collective-permute-start.77 = (bf16[128,1024]{1,0:T(8,128)(2,1)S(1)}, bf16[128,1024]{1,0:T(8,128)(2,1)S(1)}, u32[]{:S(2)}, u32[]{:S(2)}) collective-permute-start(bf16[128,1024]{1,0:T(8,128)(2,1)S(1)} %get-tuple-element.337), channel_id=1, source_target_pairs={{0,6},{2,4},{4,2},{6,0},{1,7},{3,5},{5,3},{7,1},{8,14},{10,12},{12... | collective-permute-start | bytes 786440 | tf_op jit(solution)/shard_map/ppermute | solution.py:33
  (119 other events, 1675.2 us)

commit v4 on v3

--- a/solution.py
+++ b/solution.py
@@ -75,18 +75,19 @@
     def __init__(self, own):
         self.ups, self.downs = [own], [own]
 
-    def start(self):
+    def start(self, order):
         n, s = lax.axis_size("fsdp"), len(self.ups)
         if s < n:
-            self.ups.append(line_up(self.ups[-1], s - 1, n - 1))
-            self.downs.append(line_down(self.downs[-1], 1, n - s + 1))
+            up, down = order.then((self.ups[-1], self.downs[-1]))
+            self.ups.append(line_up(up, s - 1, n - 1))
+            self.downs.append(line_down(down, 1, n - s + 1))
 
     def arrive(self, order):
         self.ups[-1], self.downs[-1] = order.arrive((self.ups[-1], self.downs[-1]))
 
     def rest(self, order):
         for _ in range(len(self.ups), lax.axis_size("fsdp")):
-            self.start()
+            self.start(order)
             self.arrive(order)
 
     def sources(self):
@@ -97,12 +98,12 @@
     def __init__(self, parts):
         self.parts, self.sums, self.step = parts, None, 1
 
-    def start(self):
+    def start(self, order):
         n, s = lax.axis_size("fsdp"), self.step
         if s < n:
-            up, down = self.parts[s], self.parts[n - s]
+            up, down = order.then((self.parts[s], self.parts[n - s]))
             if self.sums is not None:
-                up, down = add(up, self.sums[0]), add(down, self.sums[1])
+                up, down = order.arrive((add(up, self.sums[0]), add(down, self.sums[1])))
             self.sums = line_up(up, 0, min(s, n - 1)), line_down(down, max(n - s, 1), n)
             self.step += 1
 
@@ -111,7 +112,7 @@
 
     def rest(self, order):
         for _ in range(self.step, lax.axis_size("fsdp")):
-            self.start()
+            self.start(order)
             self.arrive(order)
 
     def total(self):
@@ -120,59 +121,59 @@
 
 
 class Rows:
-    def __init__(self, own):
-        self.own = own
-        self.half = own.shape[0] // 2
-
-    def start(self):
-        mine = self.own[: self.half]
-        self.got = [swap(mine, "ctx", 1 << k) for k in range(lax.axis_size("ctx").bit_length() - 1)]
+    def __init__(self, mine):
+        self.mine = mine
+
+    def start(self, order):
+        mine = order.then(self.mine)
+        self.near = [swap(mine, "ctx", 1 << k) for k in range(lax.axis_size("ctx").bit_length() - 1)]
 
     def arrive(self, order):
-        self.got = order.arrive(self.got)
+        self.near = order.arrive(self.near)
 
     def start_far(self):
-        m, quarter = lax.axis_size("ctx"), self.half // 2
+        m, quarter = lax.axis_size("ctx"), self.mine.shape[0] // 2
         if m == 4:
-            first, second = self.got
+            first, second = self.near
             self.far = [swap(first[:quarter], "ctx", 2), swap(second[quarter:], "ctx", 1)]
-            self.near = [first, second]
         else:
-            mine = self.own[: self.half]
-            self.near = self.got
-            self.far = [swap(mine, "ctx", j) for j in range(1, m) if j & (j - 1)]
-        self.near_other = [swap(piece, "tp", 1) for piece in self.near]
+            self.far = [swap(self.mine, "ctx", j) for j in range(1, m) if j & (j - 1)]
 
     def arrive_far(self, order):
-        self.far, self.near_other = order.arrive((self.far, self.near_other))
-
-    def start_last(self):
-        self.far_other = [swap(piece, "tp", 1) for piece in self.far]
-
-    def arrive_last(self, order):
-        self.far_other = order.arrive(self.far_other)
-
-    def blocks(self):
+        self.far = order.arrive(self.far)
+
+    def halves(self, order):
         m = lax.axis_size("ctx")
-        near = list(zip(self.near, self.near_other))
-        far = list(zip(self.far, self.far_other))
-        blocks = [self.own]
+        near, far = list(self.near), list(self.far)
+        blocks = [self.mine]
         for j in range(1, m):
             if j & (j - 1) == 0:
-                blocks += near.pop(0)
+                blocks.append(near.pop(0))
             elif m == 4:
-                blocks += [far[0][0], far[1][0], far[0][1], far[1][1]]
+                blocks += far
             else:
-                blocks += far.pop(0)
-        return blocks
+                blocks.append(far.pop(0))
+        self.here = assemble(order.then(blocks))
+        order.did(self.here)
+
+    def start_last(self, order):
+        self.there = swap(order.then(self.here), "tp", 1)
+
+    def arrive_last(self, order):
+        self.there = order.arrive(self.there)
+
+    def all(self, order):
+        full = assemble(order.then([self.here, self.there]))
+        order.did(full)
+        return full
 
 
 class RowSums:
     def __init__(self, slots):
         self.slots = [slots[j] for j in range(slots.shape[0])]
 
-    def start(self):
-        m, slots = len(self.slots), self.slots
+    def start(self, order):
+        m, slots = len(self.slots), order.then(self.slots)
         quarter = slots[0].shape[0] // 2
         if m == 4:
             self.got = [swap(slots[3][:quarter], "ctx", 2), swap(slots[3][quarter:], "ctx", 1)]
@@ -182,12 +183,13 @@
     def arrive(self, order):
         self.got = order.arrive(self.got)
 
-    def start_last(self):
-        m, slots = len(self.slots), self.slots
+    def start_last(self, order):
+        m, slots = len(self.slots), order.then(self.slots)
         quarter = slots[0].shape[0] // 2
         if m == 4:
             first = jnp.concatenate([add(slots[1][:quarter], self.got[0]), slots[1][quarter:]], axis=0)
             second = jnp.concatenate([slots[2][:quarter], add(slots[2][quarter:], self.got[1])], axis=0)
+            first, second = order.arrive((first, second))
             self.last, self.got = [swap(first, "ctx", 1), swap(second, "ctx", 2)], []
         else:
             self.last = [swap(slots[j], "ctx", j) for j in range(1, m) if j & (j - 1) == 0]
@@ -212,14 +214,6 @@
         piece = lax.dynamic_slice_in_dim(block, (c ^ j) * rows, rows, axis=0)
         pieces.append(piece if j == 0 else swap(piece, "ctx", j))
     return pieces
-
-
-def side_by_side(pieces):
-    m = lax.axis_size("ctx")
-    c = lax.axis_index("ctx")
-    stacked = jnp.stack(pieces)
-    ordered = [lax.dynamic_index_in_dim(stacked, c ^ k, axis=0, keepdims=False) for k in range(m)]
-    return jnp.concatenate(ordered, axis=1).astype(f32)
 
 
 def column_order(heads):
@@ -279,8 +273,10 @@
 
 
 def fetch(z_ref, sources, weight_ref, sems, first):
-    n = (len(sources) + 1) // 2
-    feat, cols = weight_ref.shape[0] // n, weight_ref.shape[1]
+    feat, cols = sources[0].shape[0], weight_ref.shape[1]
+    if len(sources) == 1:
+        feat = weight_ref.shape[0] // sems.shape[0]
+    n = weight_ref.shape[0] // feat
 
     def copy(source, s):
         rows = pl.ds(s * feat, feat)
@@ -289,6 +285,11 @@
         )
 
     def each(do):
+        if len(sources) == 1:
+            for s in range(n):
+                block = pl.multiple_of(lax.rem(z_ref[0] - s + n, n) * feat, feat)
+                do(copy(sources[0].at[pl.ds(block, feat), :], s))
+            return
         do(copy(sources[0], 0))
         for s in range(1, n):
 
@@ -391,22 +392,33 @@
 
 
 def spread_kernel(count, first, z_ref, a_ref, b_ref, *rest):
-    a_sources, b_sources = rest[:count], rest[count : 2 * count]
-    keep_ref, send_ref, a_weight_ref, b_weight_ref, sems = rest[2 * count :]
+    a_sources, b_sources = rest[: count[0]], rest[count[0] : sum(count)]
+    keep_ref, send_ref, a_weight_ref, b_weight_ref, sems = rest[sum(count) :]
 
     @pl.when(pl.program_id(0) == 0)
     def _():
         fetch(z_ref, a_sources, a_weight_ref, sems, first)
         fetch(z_ref, b_sources, b_weight_ref, sems, 0)
 
-    half = keep_ref.shape[1]
-    for h, out_ref in ((0, keep_ref), (1, send_ref)):
-        rows = slice(h * half, (h + 1) * half)
-        a, b = a_ref[rows, :], b_ref[rows, :]
-        for at in range(0, out_ref.shape[2], 256):
-            at = slice(at, at + 256)
-            out = mm(a, a_weight_ref[at, :], NT) + mm(b, b_weight_ref[at, :], NT)
-            out_ref[0, :, at] = out.astype(bf16)
+    slots, half, width = keep_ref.shape
+    steps = pl.num_programs(0) // 2
+
+    def write(out_ref):
+        for slot in range(slots):
+            rows = slice(slot * half, (slot + 1) * half)
+            a, b = a_ref[rows, :], b_ref[rows, :]
+            for at in range(0, width, 256):
+                at = slice(at, at + 256)
+                out = mm(a, a_weight_ref[at, :], NT) + mm(b, b_weight_ref[at, :], NT)
+                out_ref[slot, :, at] = out.astype(bf16)
+
+    @pl.when(pl.program_id(0) < steps)
+    def _():
+        write(keep_ref)
+
+    @pl.when(pl.program_id(0) >= steps)
+    def _():
+        write(send_ref)
 
 
 def forward_kernel(
@@ -421,16 +433,17 @@
         rows = pl.ds(pl.multiple_of(i * BLOCK, BLOCK), BLOCK)
         start = start_ref[0:1, rows]
         q = packed_ref[rows, :wide]
-        qs = [q * qmask_ref[h] for h in range(heads)]
+        qs = jnp.concatenate([q * qmask_ref[h] for h in range(heads)], axis=0)
 
         def step(j, carried):
             keys = pl.ds(pl.multiple_of(j * BLOCK, BLOCK), BLOCK)
             k = packed_ref[keys, wide : 2 * wide]
             keep = kept(i, j, start)
+            scores = mm(k, qs, NT)
             after = []
             for h in range(heads):
                 top, total, acc = carried[h]
-                s = jnp.where(keep, mm(k, qs[h], NT), MASKED)
+                s = jnp.where(keep, scores[:, h * BLOCK : (h + 1) * BLOCK], MASKED)
                 new_top = jnp.maximum(top, jnp.max(s, axis=0, keepdims=True))
                 p = jnp.exp(s - new_top)
                 alpha = jnp.exp(top - new_top)
@@ -483,8 +496,8 @@
         start = start_ref[0:1, rows]
         q = packed_ref[rows, :wide]
         g = gp_ref[rows, :wide]
-        qs = [q * qmask_ref[h] for h in range(heads)]
-        gs = [g * vmask_ref[h] for h in range(heads)]
+        qs = jnp.concatenate([q * qmask_ref[h] for h in range(heads)], axis=0)
+        gs = jnp.concatenate([g * vmask_ref[h] for h in range(heads)], axis=0)
         product = g.astype(f32).T * outt_ref[:, rows]
         inner = [
             jnp.sum(product[h * HEAD : (h + 1) * HEAD], axis=0, keepdims=True) for h in range(heads)
@@ -497,19 +510,18 @@
             v = packed_ref[keys, 2 * wide :]
             kt = kt_ref[:, keys]
             keep = kept(i, j, start)
-            dk = dk_ref[keys, :]
-            dv = dv_ref[keys, :]
+            scores = mm(k, qs, NT)
+            slopes = mm(v, gs, NT)
+            probs, flows = [], []
             for h in range(heads):
-                s = jnp.where(keep, mm(k, qs[h], NT), MASKED)
-                p = jnp.exp(s - lse[h])
-                dp = mm(v, gs[h], NT)
-                ds = (p * (dp - inner[h])).astype(bf16)
-                dv = dv + mm(p.astype(bf16), gs[h])
-                dk = dk + mm(ds, qs[h])
-                dqt = dqt + mm(kt * ktmask_ref[h], ds)
-            dk_ref[keys, :] = dk
-            dv_ref[keys, :] = dv
-            return dqt
+                at = slice(h * BLOCK, (h + 1) * BLOCK)
+                p = jnp.exp(jnp.where(keep, scores[:, at], MASKED) - lse[h])
+                probs.append(p.astype(bf16))
+                flows.append((p * (slopes[:, at] - inner[h])).astype(bf16))
+            dv_ref[keys, :] = dv_ref[keys, :] + mm(jnp.concatenate(probs, axis=1), gs)
+            dk_ref[keys, :] = dk_ref[keys, :] + mm(jnp.concatenate(flows, axis=1), qs)
+            kts = jnp.concatenate([kt * ktmask_ref[h] for h in range(heads)], axis=1)
+            return dqt + mm(kts, jnp.concatenate(flows, axis=0))
 
         dqt = lax.fori_loop(low_ref[i], i + 1, step, jnp.zeros((wide, BLOCK), f32))
         dq_ref[rows, :] = dqt.T * (1.0 / math.sqrt(HEAD))
@@ -540,7 +552,7 @@
 
 
 def blocks_call(kernel, name, z, ins, in_specs, sources, outs, out_specs, scratch, steps, flops, weight_shapes):
-    sems = len(sources[0]) // 2 + 1
+    sems = lax.axis_size("fsdp")
     return pl.pallas_call(
         kernel,
         grid_spec=pltpu.PrefetchScalarGridSpec(
@@ -571,23 +583,16 @@
     rows, width = x_ref.shape
     half, step = rows // 2, 64
     feat = width // slots
-    if not norm:
-        rest[0][...] = jnp.zeros(rest[0].shape, f32)
-
-    @pl.loop(0, rows // step)
+
+    @pl.loop(0, half // step)
     def _(b):
-        source = pl.ds(pl.multiple_of(b * step, step), step)
-        first = b * step
-        second = (first >= half).astype(jnp.int32)
-        place = (second ^ at_ref[1]) * half + first - second * half
-        target = pl.ds(pl.multiple_of(place, step), step)
-        x = x_ref[source, :].astype(f32)
+        source = pl.ds(pl.multiple_of(at_ref[1] * half + b * step, step), step)
+        target = pl.ds(pl.multiple_of(b * step, step), step)
         if norm:
+            x = x_ref[source, :].astype(f32)
             mean = jnp.mean(x, axis=-1, keepdims=True)
             centred = x - mean
             rstd = lax.rsqrt(jnp.mean(centred * centred, axis=-1, keepdims=True) + EPSILON)
-        else:
-            rest[0][0:1, :] = rest[0][0:1, :] + jnp.sum(x, axis=0, keepdims=True)
         for s in range(slots):
             block = lax.rem(at_ref[0] - s + slots, slots)
             columns = pl.ds(pl.multiple_of(block * feat, feat), feat)
@@ -596,10 +601,20 @@
                 y = (y.astype(f32) - mean) * rstd * gain_ref[0:1, columns] + shift_ref[0:1, columns]
             out_ref[target, s * feat : (s + 1) * feat] = y.astype(bf16)
 
+    if not norm:
+        sum_ref = rest[0]
+        sum_ref[...] = jnp.zeros(sum_ref.shape, f32)
+
+        @pl.loop(0, rows // step)
+        def _(b):
+            source = pl.ds(pl.multiple_of(b * step, step), step)
+            x = x_ref[source, :].astype(f32)
+            sum_ref[0:1, :] = sum_ref[0:1, :] + jnp.sum(x, axis=0, keepdims=True)
+
 
 def prepare(norm, at, x, gain, shift, n):
     rows, width = x.shape
-    out = [jax.ShapeDtypeStruct((rows, width), bf16)]
+    out = [jax.ShapeDtypeStruct((rows // 2, width), bf16)]
     if not norm:
         out.append(jax.ShapeDtypeStruct((8, width), f32))
     return pl.pallas_call(
@@ -612,6 +627,79 @@
         cost_estimate=pl.CostEstimate(flops=2**20, bytes_accessed=2**20, transcendentals=0),
         name="prepare",
     )(at, x, gain, shift)
+
+
+def place_kernel(count, at_ref, *refs):
+    pieces, outs = refs[:count], refs[count:]
+    for j, piece in enumerate(pieces):
+        first = 0
+        for out_ref in outs:
+            cols = out_ref.shape[1] // count
+            target = pl.ds(pl.multiple_of((at_ref[0] ^ j) * cols, cols), cols)
+            out_ref[:, target] = piece[:, first : first + cols].astype(f32)
+            first += cols
+
+
+def place(c, pieces, widths):
+    count, rows = len(pieces), pieces[0].shape[0]
+    return pl.pallas_call(
+        functools.partial(place_kernel, count),
+        grid_spec=pltpu.PrefetchScalarGridSpec(
+            num_scalar_prefetch=1, grid=(), in_specs=whole(count), out_specs=whole(len(widths))
+        ),
+        out_shape=[jax.ShapeDtypeStruct((rows, count * cols), f32) for cols in widths],
+        compiler_params=pltpu.CompilerParams(vmem_limit_bytes=40 * 2**20),
+        cost_estimate=pl.CostEstimate(flops=2**20, bytes_accessed=2**20, transcendentals=0),
+        name="place",
+    )(c, *pieces)
+
+
+def join_kernel(a_ref, b_ref, *outs):
+    cols = a_ref.shape[1]
+    for s, out_ref in enumerate(outs):
+
+        @pl.when(pl.program_id(0) == s)
+        def _():
+            out_ref[:, :cols] = a_ref[...]
+            out_ref[:, cols:] = b_ref[...]
+
+
+def join(a, b, n):
+    rows, cols = a.shape[0] // n, a.shape[1] + b.shape[1]
+    return pl.pallas_call(
+        join_kernel,
+        grid=(n,),
+        in_specs=[
+            pl.BlockSpec((rows, a.shape[1]), lambda i: (i, 0)),
+            pl.BlockSpec((rows, b.shape[1]), lambda i: (i, 0)),
+        ],
+        out_specs=[pl.BlockSpec((rows, cols), lambda i: (0, 0))] * n,
+        out_shape=[jax.ShapeDtypeStruct((rows, cols), bf16)] * n,
+        compiler_params=pltpu.CompilerParams(vmem_limit_bytes=40 * 2**20),
+        cost_estimate=pl.CostEstimate(flops=2**20, bytes_accessed=2**20, transcendentals=0),
+        name="join",
+    )(a, b)
+
+
+def reorder(order, x, blocks):
+    rows, cols = x.shape[0] // blocks, x.shape[1]
+
+    def copy_kernel(order_ref, x_ref, out_ref):
+        out_ref[...] = x_ref[...]
+
+    return pl.pallas_call(
+        copy_kernel,
+        grid_spec=pltpu.PrefetchScalarGridSpec(
+            num_scalar_prefetch=1,
+            grid=(blocks,),
+            in_specs=[pl.BlockSpec((rows, cols), lambda i, order_ref: (order_ref[i], 0))],
+            out_specs=pl.BlockSpec((rows, cols), lambda i, order_ref: (i, 0)),
+        ),
+        out_shape=jax.ShapeDtypeStruct(x.shape, x.dtype),
+        compiler_params=pltpu.CompilerParams(vmem_limit_bytes=40 * 2**20),
+        cost_estimate=pl.CostEstimate(flops=2**20, bytes_accessed=2**20, transcendentals=0),
+        name="reorder",
+    )(order, x)
 
 
 def assemble_kernel(*refs):
@@ -694,15 +782,20 @@
 
 def to_features(z, a, a_sources, first, b, b_sources, half, width):
     rows = a.shape[0]
-    slots = rows // (2 * half)
+    slots, each = rows // (2 * half), 512 // half
+    steps = slots // each
     a_cols, b_cols = a.shape[1], b.shape[1]
     out = jax.ShapeDtypeStruct((slots, half, width), bf16)
-    spec = pl.BlockSpec((1, half, width), lambda i, *_: (i, 0, 0))
+    block = (each, half, width)
     return blocks_call(
-        functools.partial(spread_kernel, len(a_sources), first), "to_features", z,
-        [a, b], [by_row(2 * half, a_cols), by_row(2 * half, b_cols)], [a_sources, b_sources],
-        [out, out], [spec, spec], [],
-        slots, 2 * rows * width * (a_cols + b_cols), [(width, a_cols), (width, b_cols)],
+        functools.partial(spread_kernel, (len(a_sources), len(b_sources)), first), "to_features", z,
+        [a, b], [by_row(512, a_cols), by_row(512, b_cols)], [a_sources, b_sources],
+        [out, out],
+        [
+            pl.BlockSpec(block, lambda i, *_: (jnp.minimum(i, steps - 1), 0, 0)),
+            pl.BlockSpec(block, lambda i, *_: (jnp.maximum(i - steps, 0), 0, 0)),
+        ],
+        [], 2 * steps, 2 * rows * width * (a_cols + b_cols), [(width, a_cols), (width, b_cols)],
     )
 
 
@@ -723,7 +816,7 @@
             jax.ShapeDtypeStruct((8, rows), f32),
             jax.ShapeDtypeStruct((rows, wide), bf16),
         ],
-        compiler_params=pltpu.CompilerParams(vmem_limit_bytes=40 * 2**20),
+        compiler_params=pltpu.CompilerParams(vmem_limit_bytes=60 * 2**20),
         cost_estimate=pl.CostEstimate(
             flops=2 * rows * rows * wide + pairs * 4 * wide, bytes_accessed=20 * rows * wide, transcendentals=pairs
         ),
@@ -753,7 +846,7 @@
             jax.ShapeDtypeStruct((rows, 3 * wide), bf16),
             jax.ShapeDtypeStruct((8, 3 * wide), f32),
         ],
-        compiler_params=pltpu.CompilerParams(vmem_limit_bytes=40 * 2**20),
+        compiler_params=pltpu.CompilerParams(vmem_limit_bytes=60 * 2**20),
         cost_estimate=pl.CostEstimate(
             flops=8 * rows * rows * wide + pairs * 10 * wide, bytes_accessed=20 * rows * wide, transcendentals=pairs
         ),
@@ -797,20 +890,28 @@
             axis=1,
         )
 
+    def by_slots(left, right):
+        return [
+            lax.dot_general(
+                left[:, s * feat : (s + 1) * feat], right, by_rows, preferred_element_type=f32
+            ).astype(bf16)
+            for s in range(n)
+        ]
+
     def mine(weight):
         share = weight.shape[-1] // m
         return lax.dynamic_slice_in_dim(weight, c * share, share, axis=weight.ndim - 1)
 
     listed = jnp.array(column_order(heads), jnp.int32)
     place_of = (jnp.arange(3 * wide, dtype=jnp.int32)[:, None] == listed[None, :]).astype(bf16)
-    qkv_own = jnp.dot(mine(w_qkv), place_of, preferred_element_type=f32).astype(bf16)
     qkv_bias = jnp.dot(mine(b_qkv)[None], place_of, preferred_element_type=f32)
     up_bias = mine(b_fc1).astype(f32)
 
     order = Order()
     z_ref = jnp.full((1,), z, jnp.int32)
+    qkv_own = jnp.dot(mine(w_qkv), place_of, preferred_element_type=f32).astype(bf16)
     first = Gather(jnp.concatenate([qkv_own, mine(w_dense)], axis=1))
-    first.start()
+    first.start(order)
 
     at = jnp.stack([z, t]).astype(jnp.int32)
     gain_vec = ln_gain.astype(f32)
@@ -820,16 +921,19 @@
     normed_own = prepare(True, at, after(hidden_in[0], first.ups[0]), gain_row, shift_row, n)[0]
     order.did(normed_own)
     rows_in = Rows(normed_own)
-    rows_in.start()
-    first.arrive(order)
-    first.start()
+    rows_in.start(order)
     grads_own, out_sum = prepare(False, at, order.then(out_grad[0]), gain_row, shift_row, n)
     order.did(grads_own)
-    assignment, lengths, w_fc1, w_fc2 = order.then((assignment, lengths, w_fc1, w_fc2))
+    grads_all = lax.all_gather(grads_own, ("ctx", "tp"), axis=0, tiled=True)
+    first.arrive(order)
+
+    first.start(order)
+    w_fc1, w_fc2 = order.then((w_fc1, w_fc2))
     second = Gather(mine(w_fc1))
-    third = Gather(mine(w_fc2))
-
-    block_of = [((c ^ j) * 2 + (t ^ h)) * half for j in range(m) for h in range(2)]
+    third_own = mine(w_fc2)
+    assignment, lengths = order.then((assignment, lengths))
+
+    block_of = [((c ^ j) * 2 + (t ^ h)) * half for h in range(2) for j in range(m)]
     packed = jnp.concatenate(
         [lax.dynamic_slice_in_dim(assignment[0], at, half) for at in block_of]
     )
@@ -859,42 +963,37 @@
     vmask = jnp.broadcast_to(head_v[:, None, :], (heads, BLOCK, wide))
     ktmask = jnp.broadcast_to(head_qk[:, :, None], (heads, wide, BLOCK))
 
-    order.did(second.ups[0], third.ups[0], cos_arrival, sin_arrival, cos_packed, sin_packed)
+    order.did(second.ups[0], third_own, cos_arrival, sin_arrival, cos_packed, sin_packed)
+    rows_in.arrive(order)
     first.arrive(order)
-    rows_in.arrive(order)
-
-    first.start()
+
+    first.start(order)
     rows_in.start_far()
+    rows_in.arrive_far(order)
+    rows_in.halves(order)
     first.arrive(order)
-    rows_in.arrive_far(order)
     first.rest(order)
 
-    second.start()
-    rows_in.start_last()
-    rows_grad = Rows(order.then(grads_own))
-    rows_grad.start()
+    second.start(order)
+    rows_in.start_last(order)
     rows_in.arrive_last(order)
-    normed = assemble(order.then(rows_in.blocks()))
-    order.did(normed)
+    normed = rows_in.all(order)
+
     qkv_bias = jnp.broadcast_to(qkv_bias, (8, 3 * wide))
     qkv_packed, vt = pack(
         heads, z_ref, order.then(normed), qkv_bias, cos_arrival, sin_arrival, prow, first.sources()
     )
     order.did(qkv_packed)
     second.arrive(order)
-    rows_grad.arrive(order)
-
-    second.start()
-    rows_grad.start_far()
+
+    second.start(order)
     outt, lse, mixed = attend(heads, low, order.then(qkv_packed), vt, pcol, start, qmask)
     order.did(mixed)
     second.arrive(order)
-    rows_grad.arrive_far(order)
-
-    second.start()
-    rows_grad.start_last()
-    rows_grad.arrive_last(order)
-    grads = assemble(order.then(rows_grad.blocks()))
+
+    second.start(order)
+    by_block = jnp.stack([at // half for at in block_of]).astype(jnp.int32)
+    grads = reorder(by_block, order.then(grads_all), 2 * m)
     order.did(grads)
     mixed_grad = times(z_ref, order.then(grads), first.sources(), 3 * wide, wide)
     order.did(mixed_grad)
@@ -903,125 +1002,109 @@
     second.arrive(order)
     second.rest(order)
 
-    third.start()
+    third = lax.all_gather(order.then(third_own), "fsdp", axis=0, tiled=True)
     up_bias = jnp.broadcast_to(up_bias[None], (8, up_bias.shape[0]))
     up, act = up_forward(z_ref, order.then(normed), up_bias, second.sources())
     order.did(act)
+    to_slots = jnp.stack([lax.rem(z - f + n, n) for f in range(n)]).astype(jnp.int32)
     down_grad = lax.dot_general(grads, order.then(act), by_rows, preferred_element_type=f32).astype(bf16)
-    down_sum = Scatter([down_grad[s * feat : (s + 1) * feat] for s in range(n)])
-    order.did(*down_sum.parts)
-    third.arrive(order)
-
-    third.start()
-    down_sum.start()
+    order.did(down_grad)
+    down_grad = reorder(to_slots, down_grad, n)
+    order.did(down_grad)
+    down_total = lax.psum_scatter(order.then(down_grad), "fsdp", scatter_dimension=0, tiled=True)
+
     qkv_grad_low, qkv_bias_sum = attend_back(
         heads, low, order.then(qkv_packed), outt, lse, mixed_grad, cos_packed, sin_packed, prow, pcol, start,
         qmask, vmask, ktmask,
     )
     order.did(qkv_grad_low)
-    third.arrive(order)
-    down_sum.arrive(order)
-
-    third.start()
-    down_sum.start()
     qkv_weight = lax.dot_general(
         normed, order.then(qkv_grad_low), by_rows, preferred_element_type=f32
     ).astype(bf16)
-    first_sum = Scatter(
-        [
-            jnp.concatenate([x[s * feat : (s + 1) * feat] for x in (qkv_weight, dense_grad)], axis=1)
-            for s in range(n)
-        ]
-    )
+    first_sum = Scatter(join(qkv_weight, dense_grad, n))
     order.did(*first_sum.parts)
-    third.arrive(order)
-    down_sum.arrive(order)
-    third.rest(order)
-
-    down_sum.start()
-    first_sum.start()
-    branch_keep, branch_send = to_features(
-        z_ref, order.then(mixed), first.sources(), 3 * wide, act, third.sources(), half, width
-    )
-    order.did(branch_keep)
-    branch_other = swap(branch_send, "tp", 1)
-    up_grad_low, up_bias_sum = up_backward(z_ref, grads, order.then(up), third.sources())
+
+    third_sources = [order.arrive(third)]
+    first_sum.start(order)
+    up_grad_low, up_bias_sum = up_backward(z_ref, grads, order.then(up), third_sources)
     order.did(up_grad_low)
-    down_sum.arrive(order)
+    keep, send = to_features(
+        z_ref, order.then(mixed), first.sources(), 3 * wide, act, third_sources, half, width
+    )
+    order.did(keep)
     first_sum.arrive(order)
-    branch_keep, branch_other = order.arrive((branch_keep, branch_other))
-    down_sum.rest(order)
-
-    first_sum.start()
-    branch_sum = RowSums(add(branch_keep, branch_other))
-    branch_sum.start()
+
+    first_sum.start(order)
+    other = swap(order.then(send), "tp", 1)
     up_weight = lax.dot_general(
         normed, order.then(up_grad_low), by_rows, preferred_element_type=f32
     ).astype(bf16)
-    up_sum = Scatter([up_weight[s * feat : (s + 1) * feat] for s in range(n)])
-    order.did(*up_sum.parts)
-    first_sum.arrive(order)
-    branch_sum.arrive(order)
-
-    first_sum.start()
-    up_sum.start()
-    branch_sum.start_last()
+    order.did(up_weight)
+    up_weight = reorder(to_slots, order.then(up_weight), n)
+    order.did(up_weight)
+    up_total = lax.psum_scatter(order.then(up_weight), "fsdp", scatter_dimension=0, tiled=True)
+    keep, other = order.arrive((keep, other))
+
+    branch_sum = RowSums(order.arrive(add(keep, other)))
+    branch_sum.start(order)
     keep, send = to_features(
         z_ref, order.then(qkv_grad_low), first.sources(), 0, up_grad_low, second.sources(), half, width
     )
     order.did(keep)
-    other = swap(send, "tp", 1)
-    up_sum.arrive(order)
+    branch_sum.arrive(order)
     first_sum.arrive(order)
+    down_total = order.arrive(down_total)
+
+    first_sum.start(order)
+    other = swap(order.then(send), "tp", 1)
+    branch_sum.start_last(order)
+    source = order.then(lax.dynamic_slice_in_dim(hidden_in[0], t * half, half)).astype(f32)
+    centred = source - jnp.mean(source, axis=-1, keepdims=True)
+    rstd = lax.rsqrt(jnp.mean(centred * centred, axis=-1, keepdims=True) + EPSILON)
+    xhat = centred * rstd
+    order.did(xhat)
+    keep, other = order.arrive((keep, other))
+    row_sum = RowSums(order.arrive(add(keep, other)))
     branch_sum.arrive_last(order)
-    keep, other = order.arrive((keep, other))
+    first_sum.arrive(order)
     first_sum.rest(order)
 
-    up_sum.start()
-    row_sum = RowSums(add(keep, other))
-    row_sum.start()
-    down_pieces = spread_start(order.then(down_sum.total()))
-    branch = turn(branch_sum.total())
-    source = lax.dynamic_slice_in_dim(hidden_in[0], t * half, half).astype(f32)
-    biases = b_dense.astype(f32) + b_fc2.astype(f32)
-    result = (source + branch + biases).astype(bf16)
-    first_total = first_sum.total()
+    row_sum.start(order)
+    first_total = order.then(first_sum.total())
     qkv_sum = lax.dot_general(
         first_total[:, : 3 * wide], place_of, by_columns, preferred_element_type=f32
     ).astype(bf16)
-    first_total = jnp.concatenate([qkv_sum, first_total[:, 3 * wide :]], axis=1)
-    order.did(result, first_total)
-    up_sum.arrive(order)
+    both = jnp.concatenate([qkv_sum, first_total[:, 3 * wide :], down_total], axis=1)
+    order.did(both)
+    pieces = spread_start(both)
+    branch = turn(order.then(branch_sum.total()))
+    biases = b_dense.astype(f32) + b_fc2.astype(f32)
+    result = (source + branch + biases).astype(bf16)
+    order.did(result)
     row_sum.arrive(order)
-    down_pieces = order.arrive(down_pieces)
-
-    up_sum.start()
-    row_sum.start_last()
+    pieces = order.arrive(pieces)
+
+    row_sum.start_last(order)
     result_other = swap(order.then(result), "tp", 1)
-    qkv_pieces = spread_start(order.then(first_total))
-    down_part = side_by_side(down_pieces)
-    centred = order.then(source)
-    centred = centred - jnp.mean(centred, axis=-1, keepdims=True)
-    rstd = lax.rsqrt(jnp.mean(centred * centred, axis=-1, keepdims=True) + EPSILON)
-    xhat = centred * rstd
-    order.did(down_part, xhat)
+    c_ref = jnp.full((1,), c, jnp.int32)
+    qkv_part, dense_part, down_part = place(
+        c_ref, order.then(pieces), [3 * wide, wide, w_fc2.shape[1] // m]
+    )
+    order.did(qkv_part)
+    up_total = order.arrive(up_total)
     row_sum.arrive_last(order)
-    up_sum.arrive(order)
-    up_sum.rest(order)
-    result_other, qkv_pieces = order.arrive((result_other, qkv_pieces))
-
-    up_pieces = spread_start(order.then(up_sum.total()))
+
+    up_pieces = spread_start(order.then(up_total))
     normed_grad = turn(row_sum.total())
-    d = normed_grad * gain_vec
+    d = order.then(normed_grad) * gain_vec
     input_grad = rstd * (
         d - jnp.mean(d, axis=-1, keepdims=True) - xhat * jnp.mean(d * xhat, axis=-1, keepdims=True)
     ) + lax.dynamic_slice_in_dim(out_grad[0], t * half, half).astype(f32)
-    input_other = swap(input_grad, "tp", 1)
     norm_sums = jnp.concatenate([jnp.sum(normed_grad * xhat, axis=0), jnp.sum(normed_grad, axis=0)])
     order.did(input_grad, norm_sums)
-    qkv_part = side_by_side([x[:, : 3 * wide] for x in qkv_pieces])
-    dense_part = side_by_side([x[:, 3 * wide :] for x in qkv_pieces])
-    up_part = side_by_side(up_pieces)
+    input_other = swap(order.then(input_grad), "tp", 1)
+    norm_sums = order.then(norm_sums)
+    up_part = place(c_ref, order.arrive(up_pieces), [w_fc1.shape[1] // m])[0]
 
     def in_rows(own_half, other_half):
         return jnp.concatenate(
@@ -1040,7 +1123,7 @@
     )[0]
     norm_sums = norm_sums + swap(norm_sums, "tp", 1)
     sums = everywhere(
-        jnp.concatenate([norm_sums, out_sum[0], placed(qkv_bias_grad), placed(up_bias_sum[0])]), "ctx", "fsdp"
+        jnp.concatenate([norm_sums, out_sum[0], placed(qkv_bias_grad), placed(up_bias_sum[0])]), "fsdp", "ctx"
     )
     gain_grad, shift_grad, out_bias_grad = sums[:width], sums[width : 2 * width], sums[2 * width : 3 * width]
     qkv_bias_grad = sums[3 * width : 3 * width + 3 * wide * m]

time: 666 us -> 620 us (0.931)
  starting transfers between devices: 166 us -> 64.5 us
  waiting for transfers between devices: 128 us -> 192 us
  other arithmetic: 76.8 us -> 52.3 us
  Pallas kernels: 185 us -> 203 us
  local copies, waits for them, and re-layouts: 54.4 us -> 38.9 us
  between operations: 2.8 us -> 15.7 us
    ppermute x18 -> x9, starting transfers between devices: 102 us -> 22.3 us  [line_up(): return lax.ppermute(x, 'fsdp', [(i, i + 1) for i in range(first, last)])]
    ppermute x42 -> x28, waiting for transfers between devices: 60.4 us -> 94.2 us  [swap(): return lax.ppermute(x, axis, [(i, i ^ bit) for i in range(size)])]
    ppermute x18 -> x9, waiting for transfers between devices: 34.9 us -> 57 us  [line_down(): return lax.ppermute(x, 'fsdp', [(i, i - 1) for i in range(first, last)])]
    ppermute x18 -> x9, starting transfers between devices: 26.5 us -> 12 us  [line_down(): return lax.ppermute(x, 'fsdp', [(i, i - 1) for i in range(first, last)])]
    pallas_call x0 -> x6, Pallas kernels: none -> 12.2 us  [the longest x3 8.14 us: reorder(): pl.pallas_call(copy_kernel, grid_spec=pltpu.PrefetchScalarGridSpec(num_sc...]
    convert_element_type x11 -> x10, other arithmetic: 31.1 us -> 20.6 us  [add(): return (a.astype(f32) + b.astype(f32)).astype(bf16)]
    slice x8 -> x5, local copies, waits for them, and re-layouts: 9.51 us -> 0.28 us  [the longest x2 0.17 us: start(): slots[3][quarter:]]
    convert_element_type x5 -> x0, other arithmetic: 7.99 us -> none  [the longest x4 5.19 us: side_by_side(): return jnp.concatenate(ordered, axis=1).astype(f32)]
  transfers between devices with their start and end apart: 78 -> 50, of which waited for: 26 -> 25; matrix products, arithmetic and copies ran while one was open for 21% -> 17% of each run, Pallas kernels for 25% -> 32%
where the time goes in v4:
time: 620 us; the launch traced here: 612 us
  Pallas kernels  203 us (33%)
  waiting for transfers between devices  192 us (31%)
  starting transfers between devices  64.5 us (10%)
  other arithmetic  52.3 us (8%)
  matrix products  46 us (7%)
  local copies, waits for them, and re-layouts  38.9 us (6%)
  between operations  15.7 us (3%)
    pallas_call x6, Pallas kernels, blocks_call(): pl.pallas_call(kernel, grid_spec=pltpu.PrefetchScalarGridSpec(num_scalar_...  108 us
    ppermute x28, waiting for transfers between devices, swap(): return lax.ppermute(x, axis, [(i, i ^ bit) for i in range(size)])  94.2 us
    ppermute x9, waiting for transfers between devices, line_down(): return lax.ppermute(x, 'fsdp', [(i, i - 1) for i in range(first, last)])  57 us
    pallas_call x1, Pallas kernels, attend_back(): pl.pallas_call(functools.partial(backward_kernel, heads), grid_spec=pltpu...  43.1 us
    ppermute x9, waiting for transfers between devices, line_up(): return lax.ppermute(x, 'fsdp', [(i, i + 1) for i in range(first, last)])  36.2 us
    ppermute x28, starting transfers between devices, swap(): return lax.ppermute(x, axis, [(i, i ^ bit) for i in range(size)])  29.6 us
    pallas_call x1, Pallas kernels, attend(): pl.pallas_call(functools.partial(forward_kernel, heads), grid_spec=pltpu....  25.6 us
    ppermute x9, starting transfers between devices, line_up(): return lax.ppermute(x, 'fsdp', [(i, i + 1) for i in range(first, last)])  22.3 us
  transfers between devices with their start and end apart: 50, of which 25 were waited for; matrix products, arithmetic and copies ran while one was open for 17% of the time, Pallas kernels for 32%

profile of v4, /device:TPU:0, one launch (start us, length us, event | category | flops | bytes accessed | tf_op | source)
XLA Modules:
  0.0 612.4 jit_solution(9917685665565338551)
XLA Ops:
  17.1 5.0 collective-permute-start
  26.5 18.3 %collective-permute-done.rest_1_ = bf16[512,1024]{1,0:T(8,128)(2,1)S(1)} collective-permute-done((bf16[512,1024]{1,0:T(8,128)(2,1)}, bf16[512,1024]{1,0:T(8,128)(2,1)S(1)}, u32[]{:S(2)}, u32[]{:S(2)}) %collective-permute-start) | collective-permute-done | bytes 1048608 | tf_op jit(solution)/shard_map/ppermute | solution.py:67
  44.8 4.1 collective-permute-done.1.rest_4_
  52.4 3.0 constant_dynamic-slice_fusion.24
  55.5 8.9 %fusion.18 = (f32[2048,128]{1,0:T(8,128)}, f32[2048,128]{1,0:T(8,128)}, f32[2048,128]{1,0:T(8,128)}, f32[2048,128]{1,0:T(8,128)}) fusion(f32[2048]{0:T(1024)S(1)} %get-tuple-element.373, f32[128]{0:T(128)S(1)} %get-tuple-element.369, f32[128]{0:T(128)S(1)} %get-tuple-element.370, f32[2048]{0:T(1024)S(1)} %get-tuple-element.374), kind=kLoop, calls=%fused_computation.47 | loop fusion | flops 1048576 | bytes 4211712 | tf_op jit(solution)/shard_map/mul | solution.py:950
  64.4 14.4 %collective-permute-done.7.rest_5_ = bf16[512,1024]{1,0:T(8,128)(2,1)} collective-permute-done((bf16[512,1024]{1,0:T(8,128)(2,1)S(1)}, bf16[512,1024]{1,0:T(8,128)(2,1)}, u32[]{:S(2)}, u32[]{:S(2)}) %collective-permute-start.7) | collective-permute-done | bytes 1048608 | tf_op jit(solution)/shard_map/ppermute | solution.py:71
  86.0 8.9 %collective-permute-done.4.refs_3_ = bf16[128,2048]{1,0:T(8,128)(2,1)S(1)} collective-permute-done((bf16[128,2048]{1,0:T(8,128)(2,1)S(1)}, bf16[128,2048]{1,0:T(8,128)(2,1)S(1)}, u32[]{:S(2)}, u32[]{:S(2)}) %collective-permute-start.4) | collective-permute-done | bytes 524320 | tf_op jit(solution)/shard_map/ppermute | solution.py:33
  98.4 3.3 assemble.2.refs_0_
  101.7 3.9 collective-permute-done.9.rest_6_
  105.6 2.4 collective-permute-start.11
  110.8 2.3 collective-permute-done.10.refs_1_
  113.1 6.8 %assemble.3.x_in_ref.x_ref = bf16[2048,2048]{1,0:T(8,128)(2,1)} custom-call(bf16[1024,2048]{1,0:T(8,128)(2,1)} %assemble.2.refs_0_, bf16[1024,2048]{1,0:T(8,128)(2,1)} %collective-permute-done.10.refs_1_), custom_call_target="tpu_custom_call" | custom-call | flops 1048576 | bytes 1048576 | tf_op jit(solution)/shard_map/assemble/pallas_call | solution.py:721
  120.0 22.2 %pack.1 = (bf16[2048,768]{1,0:T(8,128)(2,1)}, bf16[256,2048]{1,0:T(8,128)(2,1)S(1)}) custom-call(s32[1]{0:T(128)} %bitcast.1.z_ref, bf16[2048,2048]{1,0:T(8,128)(2,1)} %assemble.3.x_in_ref.x_ref, f32[8,768]{1,0:T(8,128)S(1)} %broadcast_in_dim.73.bias_ref, f32[2048,128]{1,0:T(8,128)S(1)} %copy-done.20, f32[2048,128]{1,0:T(8,128)S(1)} %copy-done.21, ...), custom_call_target="tpu_custom_call" | custom-call | flops 644245120 | bytes 1048576 | tf_op jit(solution)/shard_map/pack/pallas_call | solution.py:556
  148.9 25.6 %attend_forward.1 = (f32[256,2048]{1,0:T(8,128)}, f32[8,2048]{1,0:T(8,128)}, bf16[2048,256]{1,0:T(8,128)(2,1)}) custom-call(s32[8]{0:T(128)} %and_select_fusion.5.low_ref, bf16[2048,768]{1,0:T(8,128)(2,1)} %get-tuple-element.215.packed_ref, bf16[256,2048]{1,0:T(8,128)(2,1)} %copy-done.39, s32[2048,1]{1,0:T(8,128)} %copy.29.pcol_ref, s32[1,2048]{1,0:T(1,128)} %bitcast.82, ...), custom_call_target="tpu_custom_call" | custom-call | flops 10737418240 | bytes 10485760 | tf_op jit(solution)/shard_map/attend_forward/pallas_call | solution.py:805
  178.0 6.4 %reorder.3.x_ref = bf16[2048,2048]{1,0:T(8,128)(2,1)S(1)} custom-call(s32[8]{0:T(128)S(1)} %stack.64.order_ref, bf16[2048,2048]{1,0:T(8,128)(2,1)} %all-gather.3.cloned.1.call-done.x_ref), custom_call_target="tpu_custom_call" | custom-call | flops 1048576 | bytes 1048576 | tf_op jit(solution)/shard_map/reorder/pallas_call | solution.py:690
  184.3 3.3 copy-done.2
  187.6 6.9 %times.1.grad_ref = bf16[2048,256]{1,0:T(8,128)(2,1)S(1)} custom-call(s32[1]{0:T(128)} %bitcast.1.z_ref, bf16[2048,2048]{1,0:T(8,128)(2,1)} %copy-done.2, bf16[512,1024]{1,0:T(8,128)(2,1)S(1)} %copy-done.4, bf16[512,1024]{1,0:T(8,128)(2,1)S(1)} %copy-done.9, bf16[512,1024]{1,0:T(8,128)(2,1)} %collective-permute-done.6.rest_2_, ...), custom_call_target="tpu_custom_call" | custom-call | flops 107374184 | bytes 1048576 | tf_op jit(solution)/shard_map/times/pallas_call | solution.py:556
  194.6 7.3 %convolution_convert_fusion.3.b_ref = bf16[2048,256]{1,0:T(8,128)(2,1)} fusion(bf16[2048,2048]{1,0:T(8,128)(2,1)} %copy-done.2, bf16[2048,256]{1,0:T(8,128)(2,1)S(1)} %copy-done.29), kind=kOutput, calls=%fused_computation.9 | convolution fusion | flops 2148007936 | bytes 10485760 | tf_op jit(solution)/shard_map/dot_general | solution.py:1000
  204.4 17.0 %up.1 = (f32[2048,1024]{1,0:T(8,128)}, bf16[2048,1024]{1,0:T(8,128)(2,1)}) custom-call(s32[1]{0:T(128)} %bitcast.1.z_ref, bf16[2048,2048]{1,0:T(8,128)(2,1)} %assemble.3.x_in_ref.x_ref, f32[8,1024]{1,0:T(8,128)S(1)} %broadcast_in_dim.78.bias_ref, bf16[512,1024]{1,0:T(8,128)(2,1)} %get-tuple-element.195.rest_0_.rest_7_, ...), custom_call_target="tpu_custom_call" | custom-call | flops 429496736 | bytes 1048576 | tf_op jit(solution)/shard_map/up/pallas_call | solution.py:556
  221.4 12.7 %convolution_convert_fusion.1.x_ref = bf16[2048,1024]{1,0:T(8,128)(2,1)S(1)} fusion(bf16[2048,2048]{1,0:T(8,128)(2,1)} %copy-done.2, bf16[2048,1024]{1,0:T(8,128)(2,1)} %get-tuple-element.214.b_ref), kind=kOutput, calls=%fused_computation.4 | convolution fusion | flops 8592031744 | bytes 16777216 | tf_op jit(solution)/shard_map/dot_general | solution.py:1010
  238.9 43.1 %attend_backward.1 = (bf16[2048,768]{1,0:T(8,128)(2,1)}, f32[8,768]{1,0:T(8,128)}) custom-call(s32[8]{0:T(128)} %and_select_fusion.5.low_ref, bf16[2048,768]{1,0:T(8,128)(2,1)} %get-tuple-element.215.packed_ref, f32[256,2048]{1,0:T(8,128)} %get-tuple-element.216.outt_ref, f32[8,2048]{1,0:T(8,128)} %get-tuple-element.217.lse_ref, ...), custom_call_target="tpu_custom_call" | custom-call | flops 30064771072 | bytes 10485760 | tf_op jit(solution)/shard_map/attend_backward/pallas_call | solution.py:830
  282.5 10.3 %convolution_convert_fusion.2.a_ref = bf16[2048,768]{1,0:T(8,128)(2,1)S(1)} fusion(bf16[2048,2048]{1,0:T(8,128)(2,1)} %assemble.3.x_in_ref.x_ref, bf16[2048,768]{1,0:T(8,128)(2,1)} %get-tuple-element.245.a_ref), kind=kOutput, calls=%fused_computation.5 | convolution fusion | flops 6444023808 | bytes 14680064 | tf_op jit(solution)/shard_map/dot_general | solution.py:1021
  299.3 18.5 %up_back.1 = (bf16[2048,1024]{1,0:T(8,128)(2,1)S(1)}, f32[8,1024]{1,0:T(8,128)S(1)}) custom-call(s32[1]{0:T(128)} %bitcast.1.z_ref, bf16[2048,2048]{1,0:T(8,128)(2,1)} %copy-done.2, f32[2048,1024]{1,0:T(8,128)} %get-tuple-element.227.up_ref, bf16[2048,1024]{1,0:T(8,128)(2,1)} %all-gather.5.cloned.1.call-done.rest_0_.rest_7_), custom_call_target="tpu_custom_call" | custom-call | flops 429496736 | bytes 1048576 | tf_op jit(solution)/shard_map/up_back/pallas_call | solution.py:556
  317.8 19.5 %to_features.2 = (bf16[4,256,2048]{2,1,0:T(8,128)(2,1)}, bf16[4,256,2048]{2,1,0:T(8,128)(2,1)}) custom-call(s32[1]{0:T(128)} %bitcast.1.z_ref, bf16[2048,256]{1,0:T(8,128)(2,1)S(1)} %copy-done.30, bf16[2048,1024]{1,0:T(8,128)(2,1)} %get-tuple-element.214.b_ref, bf16[512,1024]{1,0:T(8,128)(2,1)S(1)} %copy-done.5, bf16[512,1024]{1,0:T(8,128)(2,1)S(1)} %copy-done.10, ...), custom_call_target="tpu_custom_call" | custom-call | flops 536870912 | bytes 1048576 | tf_op jit(solution)/shard_map/to_features/pallas_call | solution.py:556
  337.4 6.9 %collective-permute-done.17 = bf16[512,1024]{1,0:T(8,128)(2,1)S(1)} collective-permute-done((bf16[512,1024]{1,0:T(8,128)(2,1)}, bf16[512,1024]{1,0:T(8,128)(2,1)S(1)}, u32[]{:S(2)}, u32[]{:S(2)}) %collective-permute-start.17) | collective-permute-done | bytes 1048608 | tf_op jit(solution)/shard_map/ppermute | solution.py:67
  347.1 5.2 collective-permute-start.22
  354.1 11.6 %convolution_convert_fusion.x_ref = bf16[2048,1024]{1,0:T(8,128)(2,1)S(1)} fusion(bf16[2048,2048]{1,0:T(8,128)(2,1)} %assemble.3.x_in_ref.x_ref, bf16[2048,1024]{1,0:T(8,128)(2,1)S(1)} %get-tuple-element.239.b_ref), kind=kOutput, calls=%fused_computation.3 | convolution fusion | flops 8592031744 | bytes 16777216 | tf_op jit(solution)/shard_map/dot_general | solution.py:1039
  368.6 5.4 add_convert_fusion.1
  378.9 23.7 %to_features.3 = (bf16[4,256,2048]{2,1,0:T(8,128)(2,1)}, bf16[4,256,2048]{2,1,0:T(8,128)(2,1)}) custom-call(s32[1]{0:T(128)} %bitcast.1.z_ref, bf16[2048,768]{1,0:T(8,128)(2,1)} %get-tuple-element.245.a_ref, bf16[2048,1024]{1,0:T(8,128)(2,1)} %copy-done.24, bf16[512,1024]{1,0:T(8,128)(2,1)S(1)} %copy-done.6, bf16[512,1024]{1,0:T(8,128)(2,1)S(1)} %copy-done.11, ...), custom_call_target="tpu_custom_call" | custom-call | flops 751619264 | bytes 1048576 | tf_op jit(solution)/shard_map/to_features/pallas_call | solution.py:556
  402.6 4.6 reduce-scatter.3.cloned.1.call-done
  407.3 2.9 add_convert_fusion.4
  410.2 2.7 add_convert_fusion.3
  422.7 4.2 add_convert_fusion
  426.9 17.7 %collective-permute-done.24 = bf16[256,2048]{1,0:T(8,128)(2,1)S(1)} collective-permute-done((bf16[256,2048]{1,0:T(8,128)(2,1)S(1)}, bf16[256,2048]{1,0:T(8,128)(2,1)S(1)}, u32[]{:S(2)}, u32[]{:S(2)}) %collective-permute-start.24) | collective-permute-done | bytes 1048608 | tf_op jit(solution)/shard_map/ppermute | solution.py:33
  445.8 11.0 %collective-permute-done.27 = bf16[512,1024]{1,0:T(8,128)(2,1)S(1)} collective-permute-done((bf16[512,1024]{1,0:T(8,128)(2,1)}, bf16[512,1024]{1,0:T(8,128)(2,1)S(1)}, u32[]{:S(2)}, u32[]{:S(2)}) %collective-permute-start.27) | collective-permute-done | bytes 1048608 | tf_op jit(solution)/shard_map/ppermute | solution.py:67
  456.8 32.8 %collective-permute-done.28 = bf16[512,1024]{1,0:T(8,128)(2,1)S(1)} collective-permute-done((bf16[512,1024]{1,0:T(8,128)(2,1)}, bf16[512,1024]{1,0:T(8,128)(2,1)S(1)}, u32[]{:S(2)}, u32[]{:S(2)}) %collective-permute-start.28) | collective-permute-done | bytes 1048608 | tf_op jit(solution)/shard_map/ppermute | solution.py:71
  499.2 2.4 collective-permute-start.33
  503.1 6.6 %collective-permute-done.29 = bf16[128,2048]{1,0:T(8,128)(2,1)S(1)} collective-permute-done((bf16[128,2048]{1,0:T(8,128)(2,1)S(1)}, bf16[128,2048]{1,0:T(8,128)(2,1)S(1)}, u32[]{:S(2)}, u32[]{:S(2)}) %collective-permute-start.29) | collective-permute-done | bytes 524320 | tf_op jit(solution)/shard_map/ppermute | solution.py:33
  511.2 11.2 %collective-permute-done.31.refs_1_ = bf16[128,2048]{1,0:T(8,128)(2,1)S(1)} collective-permute-done((bf16[128,2048]{1,0:T(8,128)(2,1)S(1)}, bf16[128,2048]{1,0:T(8,128)(2,1)S(1)}, u32[]{:S(2)}, u32[]{:S(2)}) %collective-permute-start.31) | collective-permute-done | bytes 524320 | tf_op jit(solution)/shard_map/ppermute | solution.py:33
  522.4 10.1 %collective-permute-done.33.refs_3_ = bf16[128,2048]{1,0:T(8,128)(2,1)S(1)} collective-permute-done((bf16[128,2048]{1,0:T(8,128)(2,1)S(1)}, bf16[128,2048]{1,0:T(8,128)(2,1)S(1)}, u32[]{:S(2)}, u32[]{:S(2)}) %collective-permute-start.33) | collective-permute-done | bytes 524320 | tf_op jit(solution)/shard_map/ppermute | solution.py:33
  538.0 2.2 place.2
  540.2 19.2 %collective-permute-done.35 = bf16[256,2048]{1,0:T(8,128)(2,1)} collective-permute-done((bf16[256,2048]{1,0:T(8,128)(2,1)}, bf16[256,2048]{1,0:T(8,128)(2,1)}, u32[]{:S(2)}, u32[]{:S(2)}) %collective-permute-start.35) | collective-permute-done | bytes 1048608 | tf_op jit(solution)/shard_map/ppermute | solution.py:33
  560.6 2.4 convert_add_fusion.2
  572.9 3.4 collective-permute-done.39
  579.8 2.2 collective-permute-done.40
  586.7 5.3 collective-permute-done.41
  599.5 2.7 broadcast_select_fusion.1
  602.2 2.5 maximum_bitcast_fusion
  (309 shorter events, 123.4 us)
Async XLA Ops:
  7.2 170.7 %all-gather.3.cloned.1.call-start = ((), (), s32[]{:S(2)}) async-start(), calls=%async_computation.2 | async-start | bytes 9437184 | tf_op jit(solution)/shard_map/all_gather | solution.py:927
  17.1 280.1 %all-gather.5.cloned.1.call-start = ((), (), s32[]{:S(2)}) async-start(), calls=%async_computation.3 | async-start | bytes 5242880 | tf_op jit(solution)/shard_map/all_gather | solution.py:1005
  17.1 27.7 %collective-permute-start = (bf16[512,1024]{1,0:T(8,128)(2,1)}, bf16[512,1024]{1,0:T(8,128)(2,1)S(1)}, u32[]{:S(2)}, u32[]{:S(2)}) collective-permute-start(bf16[512,1024]{1,0:T(8,128)(2,1)} %pad_maximum_fusion.2.rest_0_), channel_id=1, source_target_pairs={{0,8},{8,16},{16,24},{1,9},{9,17},{17,25},{2,10},{10,18},{18,26},{... | collective-permute-start | bytes 3145736 | tf_op jit(solution)/shard_map/ppermute | solution.py:67
  22.1 26.8 %collective-permute-start.1 = (bf16[512,1024]{1,0:T(8,128)(2,1)}, bf16[512,1024]{1,0:T(8,128)(2,1)S(1)}, u32[]{:S(2)}, u32[]{:S(2)}) collective-permute-start(bf16[512,1024]{1,0:T(8,128)(2,1)} %pad_maximum_fusion.2.rest_0_), channel_id=1, source_target_pairs={{8,0},{16,8},{24,16},{9,1},{17,9},{25,17},{10,2},{18,10},{26,18},{... | collective-permute-start | bytes 3145736 | tf_op jit(solution)/shard_map/ppermute | solution.py:71
  23.4 40.9 %collective-permute-start.2 = (bf16[256,2048]{1,0:T(8,128)(2,1)}, bf16[256,2048]{1,0:T(8,128)(2,1)S(1)}, u32[]{:S(2)}, u32[]{:S(2)}) collective-permute-start(bf16[256,2048]{1,0:T(8,128)(2,1)} %copy-done.25), channel_id=1, source_target_pairs={{0,2},{2,0},{4,6},{6,4},{1,3},{3,1},{5,7},{7,5},{8,10},{10,8},{12,... | collective-permute-start | bytes 3145736 | tf_op jit(solution)/shard_map/ppermute | solution.py:33
  25.0 39.4 %collective-permute-start.3 = (bf16[256,2048]{1,0:T(8,128)(2,1)}, bf16[256,2048]{1,0:T(8,128)(2,1)}, u32[]{:S(2)}, u32[]{:S(2)}) collective-permute-start(bf16[256,2048]{1,0:T(8,128)(2,1)} %copy-done.25), channel_id=1, source_target_pairs={{0,4},{2,6},{4,0},{6,2},{1,5},{3,7},{5,1},{7,3},{8,12},{10,14},{12... | collective-permute-start | bytes 3145736 | tf_op jit(solution)/shard_map/ppermute | solution.py:33
  49.1 15.3 %collective-permute-start.6 = (bf16[512,1024]{1,0:T(8,128)(2,1)S(1)}, bf16[512,1024]{1,0:T(8,128)(2,1)}, u32[]{:S(2)}, u32[]{:S(2)}) collective-permute-start(bf16[512,1024]{1,0:T(8,128)(2,1)S(1)} %collective-permute-done.rest_1_), channel_id=1, source_target_pairs={{8,16},{16,24},{9,17},{17,25},{10,18},{18,26},{11,19},{19,27},{12,... | collective-permute-start | bytes 3145736 | tf_op jit(solution)/shard_map/ppermute | solution.py:67
  50.7 28.1 %collective-permute-start.7 = (bf16[512,1024]{1,0:T(8,128)(2,1)S(1)}, bf16[512,1024]{1,0:T(8,128)(2,1)}, u32[]{:S(2)}, u32[]{:S(2)}) collective-permute-start(bf16[512,1024]{1,0:T(8,128)(2,1)S(1)} %collective-permute-done.1.rest_4_), channel_id=1, source_target_pairs={{8,0},{16,8},{9,1},{17,9},{10,2},{18,10},{11,3},{19,11},{12,4},{20... | collective-permute-start | bytes 3145736 | tf_op jit(solution)/shard_map/ppermute | solution.py:71
  78.8 22.8 %collective-permute-start.8 = (bf16[512,1024]{1,0:T(8,128)(2,1)}, bf16[512,1024]{1,0:T(8,128)(2,1)}, u32[]{:S(2)}, u32[]{:S(2)}) collective-permute-start(bf16[512,1024]{1,0:T(8,128)(2,1)} %collective-permute-done.6.rest_2_), channel_id=1, source_target_pairs={{16,24},{17,25},{18,26},{19,27},{20,28},{21,29},{22,30},{23,31}} | collective-permute-start | bytes 3145736 | tf_op jit(solution)/shard_map/ppermute | solution.py:67
  80.5 25.1 %collective-permute-start.9 = (bf16[512,1024]{1,0:T(8,128)(2,1)}, bf16[512,1024]{1,0:T(8,128)(2,1)}, u32[]{:S(2)}, u32[]{:S(2)}) collective-permute-start(bf16[512,1024]{1,0:T(8,128)(2,1)} %collective-permute-done.7.rest_5_), channel_id=1, source_target_pairs={{8,0},{9,1},{10,2},{11,3},{12,4},{13,5},{14,6},{15,7}} | collective-permute-start | bytes 3145736 | tf_op jit(solution)/shard_map/ppermute | solution.py:71
  83.0 12.0 %collective-permute-start.4 = (bf16[128,2048]{1,0:T(8,128)(2,1)S(1)}, bf16[128,2048]{1,0:T(8,128)(2,1)S(1)}, u32[]{:S(2)}, u32[]{:S(2)}) collective-permute-start(bf16[128,2048]{1,0:T(8,128)(2,1)S(1)} %slice.112), channel_id=1, source_target_pairs={{0,4},{2,6},{4,0},{6,2},{1,5},{3,7},{5,1},{7,3},{8,12},{10,14},{12... | collective-permute-start | bytes 1572872 | tf_op jit(solution)/shard_map/ppermute | solution.py:33
  84.5 11.4 %collective-permute-start.5 = (bf16[128,2048]{1,0:T(8,128)(2,1)S(1)}, bf16[128,2048]{1,0:T(8,128)(2,1)S(1)}, u32[]{:S(2)}, u32[]{:S(2)}) collective-permute-start(bf16[128,2048]{1,0:T(8,128)(2,1)S(1)} %slice.113), channel_id=1, source_target_pairs={{0,2},{2,0},{4,6},{6,4},{1,3},{3,1},{5,7},{7,5},{8,10},{10,8},{12,... | collective-permute-start | bytes 1572872 | tf_op jit(solution)/shard_map/ppermute | solution.py:33
  105.6 7.5 %collective-permute-start.10 = (bf16[1024,2048]{1,0:T(8,128)(2,1)}, bf16[1024,2048]{1,0:T(8,128)(2,1)}, u32[]{:S(2)}, u32[]{:S(2)}) collective-permute-start(bf16[1024,2048]{1,0:T(8,128)(2,1)} %assemble.2.refs_0_), channel_id=1, source_target_pairs={{0,1},{1,0},{2,3},{3,2},{4,5},{5,4},{6,7},{7,6},{8,9},{9,8},{10,11... | collective-permute-start | bytes 12582920 | tf_op jit(solution)/shard_map/ppermute | solution.py:33
  105.6 37.6 %collective-permute-start.11 = (bf16[512,1024]{1,0:T(8,128)(2,1)}, bf16[512,1024]{1,0:T(8,128)(2,1)}, u32[]{:S(2)}, u32[]{:S(2)}) collective-permute-start(bf16[512,1024]{1,0:T(8,128)(2,1)} %get-tuple-element.195.rest_0_.rest_7_), channel_id=1, source_target_pairs={{0,8},{8,16},{16,24},{1,9},{9,17},{17,25},{2,10},{10,18},{18,26},{... | collective-permute-start | bytes 3145736 | tf_op jit(solution)/shard_map/ppermute | solution.py:67
  108.0 35.2 %collective-permute-start.12 = (bf16[512,1024]{1,0:T(8,128)(2,1)}, bf16[512,1024]{1,0:T(8,128)(2,1)}, u32[]{:S(2)}, u32[]{:S(2)}) collective-permute-start(bf16[512,1024]{1,0:T(8,128)(2,1)} %get-tuple-element.195.rest_0_.rest_7_), channel_id=1, source_target_pairs={{8,0},{16,8},{24,16},{9,1},{17,9},{25,17},{10,2},{18,10},{26,18},{... | collective-permute-start | bytes 3145736 | tf_op jit(solution)/shard_map/ppermute | solution.py:71
  143.2 31.3 %collective-permute-start.13 = (bf16[512,1024]{1,0:T(8,128)(2,1)}, bf16[512,1024]{1,0:T(8,128)(2,1)}, u32[]{:S(2)}, u32[]{:S(2)}) collective-permute-start(bf16[512,1024]{1,0:T(8,128)(2,1)} %collective-permute-done.11.rest_1_.rest_8_), channel_id=1, source_target_pairs={{8,16},{16,24},{9,17},{17,25},{10,18},{18,26},{11,19},{19,27},{12,... | collective-permute-start | bytes 3145736 | tf_op jit(solution)/shard_map/ppermute | solution.py:67
  144.8 29.7 %collective-permute-start.14 = (bf16[512,1024]{1,0:T(8,128)(2,1)}, bf16[512,1024]{1,0:T(8,128)(2,1)}, u32[]{:S(2)}, u32[]{:S(2)}) collective-permute-start(bf16[512,1024]{1,0:T(8,128)(2,1)} %collective-permute-done.12.rest_4_.rest_11_), channel_id=1, source_target_pairs={{8,0},{16,8},{9,1},{17,9},{10,2},{18,10},{11,3},{19,11},{12,4},{20... | collective-permute-start | bytes 3145736 | tf_op jit(solution)/shard_map/ppermute | solution.py:71
  174.5 27.4 %collective-permute-start.15 = (bf16[512,1024]{1,0:T(8,128)(2,1)}, bf16[512,1024]{1,0:T(8,128)(2,1)}, u32[]{:S(2)}, u32[]{:S(2)}) collective-permute-start(bf16[512,1024]{1,0:T(8,128)(2,1)} %collective-permute-done.13.rest_2_.rest_9_), channel_id=1, source_target_pairs={{16,24},{17,25},{18,26},{19,27},{20,28},{21,29},{22,30},{23,31}} | collective-permute-start | bytes 3145736 | tf_op jit(solution)/shard_map/ppermute | solution.py:67
  176.2 27.4 %collective-permute-start.16 = (bf16[512,1024]{1,0:T(8,128)(2,1)}, bf16[512,1024]{1,0:T(8,128)(2,1)}, u32[]{:S(2)}, u32[]{:S(2)}) collective-permute-start(bf16[512,1024]{1,0:T(8,128)(2,1)} %collective-permute-done.14.rest_5_.rest_12_), channel_id=1, source_target_pairs={{8,0},{9,1},{10,2},{11,3},{12,4},{13,5},{14,6},{15,7}} | collective-permute-start | bytes 3145736 | tf_op jit(solution)/shard_map/ppermute | solution.py:71
  203.6 203.7 %reduce-scatter.3.cloned.1.call-start = ((), (), s32[]{:S(2)}) async-start(), calls=%async_computation.4 | async-start | bytes 5242880 | tf_op jit(solution)/shard_map/reduce_scatter | solution.py:1014
  282.1 258.2 %reduce-scatter.5.cloned.1.call-start = ((), (), s32[]{:S(2)}) async-start(), calls=%async_computation.5 | async-start | bytes 5242880 | tf_op jit(solution)/shard_map/reduce_scatter | solution.py:1045
  297.2 47.1 %collective-permute-start.17 = (bf16[512,1024]{1,0:T(8,128)(2,1)}, bf16[512,1024]{1,0:T(8,128)(2,1)S(1)}, u32[]{:S(2)}, u32[]{:S(2)}) collective-permute-start(bf16[512,1024]{1,0:T(8,128)(2,1)} %copy-done.31), channel_id=1, source_target_pairs={{0,8},{1,9},{2,10},{3,11},{4,12},{5,13},{6,14},{7,15}} | collective-permute-start | bytes 3145736 | tf_op jit(solution)/shard_map/ppermute | solution.py:67
  298.5 45.7 %collective-permute-start.18 = (bf16[512,1024]{1,0:T(8,128)(2,1)}, bf16[512,1024]{1,0:T(8,128)(2,1)S(1)}, u32[]{:S(2)}, u32[]{:S(2)}) collective-permute-start(bf16[512,1024]{1,0:T(8,128)(2,1)} %copy-done.33), channel_id=1, source_target_pairs={{24,16},{25,17},{26,18},{27,19},{28,20},{29,21},{30,22},{31,23}} | collective-permute-start | bytes 3145736 | tf_op jit(solution)/shard_map/ppermute | solution.py:71
  347.1 21.5 %collective-permute-start.19 = (bf16[4,256,2048]{2,1,0:T(8,128)(2,1)}, bf16[4,256,2048]{2,1,0:T(8,128)(2,1)}, u32[]{:S(2)}, u32[]{:S(2)}) collective-permute-start(bf16[4,256,2048]{2,1,0:T(8,128)(2,1)} %get-tuple-element.241), channel_id=1, source_target_pairs={{0,1},{1,0},{2,3},{3,2},{4,5},{5,4},{6,7},{7,6},{8,9},{9,8},{10,11... | collective-permute-start | bytes 12582920 | tf_op jit(solution)/shard_map/ppermute | solution.py:33
  347.1 55.5 %collective-permute-start.22 = (bf16[512,1024]{1,0:T(8,128)(2,1)}, bf16[512,1024]{1,0:T(8,128)(2,1)}, u32[]{:S(2)}, u32[]{:S(2)}) collective-permute-start(bf16[512,1024]{1,0:T(8,128)(2,1)} %add_convert_fusion.6), channel_id=1, source_target_pairs={{0,8},{8,16},{1,9},{9,17},{2,10},{10,18},{3,11},{11,19},{4,12},{12... | collective-permute-start | bytes 3145736 | tf_op jit(solution)/shard_map/ppermute | solution.py:67
  352.3 50.3 %collective-permute-start.23 = (bf16[512,1024]{1,0:T(8,128)(2,1)}, bf16[512,1024]{1,0:T(8,128)(2,1)}, u32[]{:S(2)}, u32[]{:S(2)}) collective-permute-start(bf16[512,1024]{1,0:T(8,128)(2,1)} %add_convert_fusion.5), channel_id=1, source_target_pairs={{16,8},{24,16},{17,9},{25,17},{18,10},{26,18},{19,11},{27,19},{20,... | collective-permute-start | bytes 3145736 | tf_op jit(solution)/shard_map/ppermute | solution.py:71
  375.8 26.8 %collective-permute-start.20 = (bf16[128,2048]{1,0:T(8,128)(2,1)S(1)}, bf16[128,2048]{1,0:T(8,128)(2,1)}, u32[]{:S(2)}, u32[]{:S(2)}) collective-permute-start(bf16[128,2048]{1,0:T(8,128)(2,1)S(1)} %get-tuple-element.351), channel_id=1, source_target_pairs={{0,4},{2,6},{4,0},{6,2},{1,5},{3,7},{5,1},{7,3},{8,12},{10,14},{12... | collective-permute-start | bytes 1572872 | tf_op jit(solution)/shard_map/ppermute | solution.py:33
  377.4 25.2 %collective-permute-start.21 = (bf16[128,2048]{1,0:T(8,128)(2,1)S(1)}, bf16[128,2048]{1,0:T(8,128)(2,1)}, u32[]{:S(2)}, u32[]{:S(2)}) collective-permute-start(bf16[128,2048]{1,0:T(8,128)(2,1)S(1)} %get-tuple-element.350), channel_id=1, source_target_pairs={{0,2},{2,0},{4,6},{6,4},{1,3},{3,1},{5,7},{7,5},{8,10},{10,8},{12,... | collective-permute-start | bytes 1572872 | tf_op jit(solution)/shard_map/ppermute | solution.py:33
  413.0 9.7 %collective-permute-start.26 = (bf16[4,256,2048]{2,1,0:T(8,128)(2,1)}, bf16[4,256,2048]{2,1,0:T(8,128)(2,1)}, u32[]{:S(2)}, u32[]{:S(2)}) collective-permute-start(bf16[4,256,2048]{2,1,0:T(8,128)(2,1)} %get-tuple-element.264), channel_id=1, source_target_pairs={{0,1},{1,0},{2,3},{3,2},{4,5},{5,4},{6,7},{7,6},{8,9},{9,8},{10,11... | collective-permute-start | bytes 12582920 | tf_op jit(solution)/shard_map/ppermute | solution.py:33
  413.2 43.6 %collective-permute-start.27 = (bf16[512,1024]{1,0:T(8,128)(2,1)}, bf16[512,1024]{1,0:T(8,128)(2,1)S(1)}, u32[]{:S(2)}, u32[]{:S(2)}) collective-permute-start(bf16[512,1024]{1,0:T(8,128)(2,1)} %add_convert_fusion.4), channel_id=1, source_target_pairs={{0,8},{8,16},{16,24},{1,9},{9,17},{17,25},{2,10},{10,18},{18,26},{... | collective-permute-start | bytes 3145736 | tf_op jit(solution)/shard_map/ppermute | solution.py:67
  414.9 74.7 %collective-permute-start.28 = (bf16[512,1024]{1,0:T(8,128)(2,1)}, bf16[512,1024]{1,0:T(8,128)(2,1)S(1)}, u32[]{:S(2)}, u32[]{:S(2)}) collective-permute-start(bf16[512,1024]{1,0:T(8,128)(2,1)} %add_convert_fusion.3), channel_id=1, source_target_pairs={{8,0},{16,8},{24,16},{9,1},{17,9},{25,17},{10,2},{18,10},{26,18},{... | collective-permute-start | bytes 3145736 | tf_op jit(solution)/shard_map/ppermute | solution.py:71
  419.0 25.6 %collective-permute-start.24 = (bf16[256,2048]{1,0:T(8,128)(2,1)S(1)}, bf16[256,2048]{1,0:T(8,128)(2,1)S(1)}, u32[]{:S(2)}, u32[]{:S(2)}) collective-permute-start(bf16[256,2048]{1,0:T(8,128)(2,1)S(1)} %pad_maximum_fusion.3), channel_id=1, source_target_pairs={{0,2},{2,0},{4,6},{6,4},{1,3},{3,1},{5,7},{7,5},{8,10},{10,8},{12,... | collective-permute-start | bytes 3145736 | tf_op jit(solution)/shard_map/ppermute | solution.py:33
  420.5 25.3 %collective-permute-start.25 = (bf16[256,2048]{1,0:T(8,128)(2,1)S(1)}, bf16[256,2048]{1,0:T(8,128)(2,1)S(1)}, u32[]{:S(2)}, u32[]{:S(2)}) collective-permute-start(bf16[256,2048]{1,0:T(8,128)(2,1)S(1)} %pad_maximum_fusion.4), channel_id=1, source_target_pairs={{0,4},{2,6},{4,0},{6,2},{1,5},{3,7},{5,1},{7,3},{8,12},{10,14},{12... | collective-permute-start | bytes 3145736 | tf_op jit(solution)/shard_map/ppermute | solution.py:33
  494.9 14.8 %collective-permute-start.29 = (bf16[128,2048]{1,0:T(8,128)(2,1)S(1)}, bf16[128,2048]{1,0:T(8,128)(2,1)S(1)}, u32[]{:S(2)}, u32[]{:S(2)}) collective-permute-start(bf16[128,2048]{1,0:T(8,128)(2,1)S(1)} %get-tuple-element.349), channel_id=1, source_target_pairs={{0,4},{2,6},{4,0},{6,2},{1,5},{3,7},{5,1},{7,3},{8,12},{10,14},{12... | collective-permute-start | bytes 1572872 | tf_op jit(solution)/shard_map/ppermute | solution.py:33
  496.4 14.8 %collective-permute-start.30 = (bf16[128,2048]{1,0:T(8,128)(2,1)S(1)}, bf16[128,2048]{1,0:T(8,128)(2,1)S(1)}, u32[]{:S(2)}, u32[]{:S(2)}) collective-permute-start(bf16[128,2048]{1,0:T(8,128)(2,1)S(1)} %get-tuple-element.348), channel_id=1, source_target_pairs={{0,2},{2,0},{4,6},{6,4},{1,3},{3,1},{5,7},{7,5},{8,10},{10,8},{12,... | collective-permute-start | bytes 1572872 | tf_op jit(solution)/shard_map/ppermute | solution.py:33
  498.0 24.4 %collective-permute-start.31 = (bf16[128,2048]{1,0:T(8,128)(2,1)S(1)}, bf16[128,2048]{1,0:T(8,128)(2,1)S(1)}, u32[]{:S(2)}, u32[]{:S(2)}) collective-permute-start(bf16[128,2048]{1,0:T(8,128)(2,1)S(1)} %get-tuple-element.338), channel_id=1, source_target_pairs={{0,2},{2,0},{4,6},{6,4},{1,3},{3,1},{5,7},{7,5},{8,10},{10,8},{12,... | collective-permute-start | bytes 1572872 | tf_op jit(solution)/shard_map/ppermute | solution.py:33
  498.7 23.8 %collective-permute-start.32 = (bf16[128,2048]{1,0:T(8,128)(2,1)S(1)}, bf16[128,2048]{1,0:T(8,128)(2,1)S(1)}, u32[]{:S(2)}, u32[]{:S(2)}) collective-permute-start(bf16[128,2048]{1,0:T(8,128)(2,1)S(1)} %get-tuple-element.337), channel_id=1, source_target_pairs={{0,4},{2,6},{4,0},{6,2},{1,5},{3,7},{5,1},{7,3},{8,12},{10,14},{12... | collective-permute-start | bytes 1572872 | tf_op jit(solution)/shard_map/ppermute | solution.py:33
  499.2 33.3 %collective-permute-start.33 = (bf16[128,2048]{1,0:T(8,128)(2,1)S(1)}, bf16[128,2048]{1,0:T(8,128)(2,1)S(1)}, u32[]{:S(2)}, u32[]{:S(2)}) collective-permute-start(bf16[128,2048]{1,0:T(8,128)(2,1)S(1)} %get-tuple-element.336), channel_id=1, source_target_pairs={{0,6},{2,4},{4,2},{6,0},{1,7},{3,5},{5,3},{7,1},{8,14},{10,12},{12... | collective-permute-start | bytes 1572872 | tf_op jit(solution)/shard_map/ppermute | solution.py:33
  535.1 24.4 %collective-permute-start.35 = (bf16[256,2048]{1,0:T(8,128)(2,1)}, bf16[256,2048]{1,0:T(8,128)(2,1)}, u32[]{:S(2)}, u32[]{:S(2)}) collective-permute-start(bf16[256,2048]{1,0:T(8,128)(2,1)} %pad_maximum_fusion.5), channel_id=1, source_target_pairs={{0,2},{2,0},{4,6},{6,4},{1,3},{3,1},{5,7},{7,5},{8,10},{10,8},{12,... | collective-permute-start | bytes 3145736 | tf_op jit(solution)/shard_map/ppermute | solution.py:33
  536.5 24.1 %collective-permute-start.36 = (bf16[256,2048]{1,0:T(8,128)(2,1)}, bf16[256,2048]{1,0:T(8,128)(2,1)}, u32[]{:S(2)}, u32[]{:S(2)}) collective-permute-start(bf16[256,2048]{1,0:T(8,128)(2,1)} %pad_maximum_fusion.6), channel_id=1, source_target_pairs={{0,4},{2,6},{4,0},{6,2},{1,5},{3,7},{5,1},{7,3},{8,12},{10,14},{12... | collective-permute-start | bytes 3145736 | tf_op jit(solution)/shard_map/ppermute | solution.py:33
  538.0 45.5 %collective-permute-start.34 = (bf16[256,2048]{1,0:T(8,128)(2,1)}, bf16[256,2048]{1,0:T(8,128)(2,1)}, u32[]{:S(2)}, u32[]{:S(2)}) collective-permute-start(bf16[256,2048]{1,0:T(8,128)(2,1)} %fusion.8), channel_id=1, source_target_pairs={{0,1},{1,0},{2,3},{3,2},{4,5},{5,4},{6,7},{7,6},{8,9},{9,8},{10,11... | collective-permute-start | bytes 3145736 | tf_op jit(solution)/shard_map/ppermute | solution.py:33
  568.3 31.2 %collective-permute-start.37 = (f32[256,2048]{1,0:T(8,128)}, f32[256,2048]{1,0:T(8,128)}, u32[]{:S(2)}, u32[]{:S(2)}) collective-permute-start(f32[256,2048]{1,0:T(8,128)} %convert_add_fusion.1), channel_id=1, source_target_pairs={{0,1},{1,0},{2,3},{3,2},{4,5},{5,4},{6,7},{7,6},{8,9},{9,8},{10,11... | collective-permute-start | bytes 6291464 | tf_op jit(solution)/shard_map/ppermute | solution.py:33
  572.1 4.2 collective-permute-start.39
  576.3 5.7 collective-permute-start.40
  577.7 20.3 %collective-permute-start.43 = (bf16[128,1024]{1,0:T(8,128)(2,1)S(1)}, bf16[128,1024]{1,0:T(8,128)(2,1)S(1)}, u32[]{:S(2)}, u32[]{:S(2)}) collective-permute-start(bf16[128,1024]{1,0:T(8,128)(2,1)S(1)} %get-tuple-element.346), channel_id=1, source_target_pairs={{0,2},{2,0},{4,6},{6,4},{1,3},{3,1},{5,7},{7,5},{8,10},{10,8},{12,... | collective-permute-start | bytes 786440 | tf_op jit(solution)/shard_map/ppermute | solution.py:33
  578.3 19.7 %collective-permute-start.44 = (bf16[128,1024]{1,0:T(8,128)(2,1)S(1)}, bf16[128,1024]{1,0:T(8,128)(2,1)S(1)}, u32[]{:S(2)}, u32[]{:S(2)}) collective-permute-start(bf16[128,1024]{1,0:T(8,128)(2,1)S(1)} %get-tuple-element.345), channel_id=1, source_target_pairs={{0,4},{2,6},{4,0},{6,2},{1,5},{3,7},{5,1},{7,3},{8,12},{10,14},{12... | collective-permute-start | bytes 786440 | tf_op jit(solution)/shard_map/ppermute | solution.py:33
  582.0 16.1 %collective-permute-start.45 = (bf16[128,1024]{1,0:T(8,128)(2,1)S(1)}, bf16[128,1024]{1,0:T(8,128)(2,1)S(1)}, u32[]{:S(2)}, u32[]{:S(2)}) collective-permute-start(bf16[128,1024]{1,0:T(8,128)(2,1)S(1)} %get-tuple-element.344), channel_id=1, source_target_pairs={{0,6},{2,4},{4,2},{6,0},{1,7},{3,5},{5,3},{7,1},{8,14},{10,12},{12... | collective-permute-start | bytes 786440 | tf_op jit(solution)/shard_map/ppermute | solution.py:33
  583.5 8.5 %collective-permute-start.41 = (f32[13312]{0:T(1024)S(1)}, f32[13312]{0:T(1024)S(1)}, u32[]{:S(2)}, u32[]{:S(2)}) collective-permute-start(f32[13312]{0:T(1024)S(1)} %add.332), channel_id=1, source_target_pairs={{0,2},{2,0},{4,6},{6,4},{1,3},{3,1},{5,7},{7,5},{8,10},{10,8},{12,... | collective-permute-start | bytes 159752 | tf_op jit(solution)/shard_map/ppermute | solution.py:33
  (62 other events, 738.9 us)
Sparse Core Ops, SparseCore 0:
  17.2 68.6 all-gather.2
  203.7 81.5 all-gather.4
  287.6 119.5 reduce-scatter.2
  413.3 100.0 reduce-scatter.4

commit v5 on v4

--- a/solution.py
+++ b/solution.py
@@ -171,6 +171,10 @@
 class RowSums:
     def __init__(self, slots):
         self.slots = [slots[j] for j in range(slots.shape[0])]
+
+    def start_direct(self, order):
+        slots = order.then(self.slots)
+        self.got, self.last = [], [swap(slots[j], "ctx", j) for j in range(1, len(slots))]
 
     def start(self, order):
         m, slots = len(self.slots), order.then(self.slots)
@@ -1046,18 +1050,16 @@
     keep, other = order.arrive((keep, other))
 
     branch_sum = RowSums(order.arrive(add(keep, other)))
-    branch_sum.start(order)
+    branch_sum.start_direct(order)
     keep, send = to_features(
         z_ref, order.then(qkv_grad_low), first.sources(), 0, up_grad_low, second.sources(), half, width
     )
     order.did(keep)
-    branch_sum.arrive(order)
     first_sum.arrive(order)
     down_total = order.arrive(down_total)
 
     first_sum.start(order)
     other = swap(order.then(send), "tp", 1)
-    branch_sum.start_last(order)
     source = order.then(lax.dynamic_slice_in_dim(hidden_in[0], t * half, half)).astype(f32)
     centred = source - jnp.mean(source, axis=-1, keepdims=True)
     rstd = lax.rsqrt(jnp.mean(centred * centred, axis=-1, keepdims=True) + EPSILON)
@@ -1066,10 +1068,20 @@
     keep, other = order.arrive((keep, other))
     row_sum = RowSums(order.arrive(add(keep, other)))
     branch_sum.arrive_last(order)
+
+    row_sum.start(order)
+    branch = turn(order.then(branch_sum.total()))
+    biases = b_dense.astype(f32) + b_fc2.astype(f32)
+    result = (source + branch + biases).astype(bf16)
+    order.did(result)
+    row_sum.arrive(order)
+
+    row_sum.start_last(order)
+    result_other = swap(order.then(result), "tp", 1)
     first_sum.arrive(order)
     first_sum.rest(order)
-
-    row_sum.start(order)
+    row_sum.arrive_last(order)
+    up_total = order.arrive(up_total)
     first_total = order.then(first_sum.total())
     qkv_sum = lax.dot_general(
         first_total[:, : 3 * wide], place_of, by_columns, preferred_element_type=f32
@@ -1077,24 +1089,6 @@
     both = jnp.concatenate([qkv_sum, first_total[:, 3 * wide :], down_total], axis=1)
     order.did(both)
     pieces = spread_start(both)
-    branch = turn(order.then(branch_sum.total()))
-    biases = b_dense.astype(f32) + b_fc2.astype(f32)
-    result = (source + branch + biases).astype(bf16)
-    order.did(result)
-    row_sum.arrive(order)
-    pieces = order.arrive(pieces)
-
-    row_sum.start_last(order)
-    result_other = swap(order.then(result), "tp", 1)
-    c_ref = jnp.full((1,), c, jnp.int32)
-    qkv_part, dense_part, down_part = place(
-        c_ref, order.then(pieces), [3 * wide, wide, w_fc2.shape[1] // m]
-    )
-    order.did(qkv_part)
-    up_total = order.arrive(up_total)
-    row_sum.arrive_last(order)
-
-    up_pieces = spread_start(order.then(up_total))
     normed_grad = turn(row_sum.total())
     d = order.then(normed_grad) * gain_vec
     input_grad = rstd * (
@@ -1102,7 +1096,14 @@
     ) + lax.dynamic_slice_in_dim(out_grad[0], t * half, half).astype(f32)
     norm_sums = jnp.concatenate([jnp.sum(normed_grad * xhat, axis=0), jnp.sum(normed_grad, axis=0)])
     order.did(input_grad, norm_sums)
+    pieces = order.arrive(pieces)
+    up_pieces = spread_start(order.then(up_total))
     input_other = swap(order.then(input_grad), "tp", 1)
+    c_ref = jnp.full((1,), c, jnp.int32)
+    qkv_part, dense_part, down_part = place(
+        c_ref, order.then(pieces), [3 * wide, wide, w_fc2.shape[1] // m]
+    )
+    order.did(qkv_part)
     norm_sums = order.then(norm_sums)
     up_part = place(c_ref, order.arrive(up_pieces), [w_fc1.shape[1] // m])[0]
 

time: 620 us -> 597 us (0.963)
  waiting for transfers between devices: 192 us -> 170 us
  Pallas kernels: 203 us -> 194 us
    ppermute x9, waiting for transfers between devices: 57 us -> 35.9 us  [line_down(): return lax.ppermute(x, 'fsdp', [(i, i - 1) for i in range(first, last)])]
    ppermute x9, waiting for transfers between devices: 36.2 us -> 24.9 us  [line_up(): return lax.ppermute(x, 'fsdp', [(i, i + 1) for i in range(first, last)])]
    reduce_scatter x1, waiting for transfers between devices: 4.63 us -> 11.7 us  [shards(): lax.psum_scatter(order.then(down_grad), 'fsdp', scatter_dimension=0, tile...]
    ppermute x28 -> x27, waiting for transfers between devices: 94.2 us -> 96.5 us  [swap(): return lax.ppermute(x, axis, [(i, i ^ bit) for i in range(size)])]
    ppermute x28 -> x27, starting transfers between devices: 29.6 us -> 29.3 us  [swap(): return lax.ppermute(x, axis, [(i, i ^ bit) for i in range(size)])]
    convert_element_type x10 -> x8, other arithmetic: 20.6 us -> 20.6 us  [add(): return (a.astype(f32) + b.astype(f32)).astype(bf16)]
    unnamed x128 -> x126, local copies, waits for them, and re-layouts: 20.2 us -> 20.2 us
  transfers between devices with their start and end apart: 50 -> 49, of which waited for: 25 -> 24; matrix products, arithmetic and copies ran while one was open for 17% -> 18% of each run, Pallas kernels for 32% -> 32%
where the time goes in v5:
time: 597 us; the launch traced here: 589 us
  Pallas kernels  194 us (32%)
  waiting for transfers between devices  170 us (28%)
  starting transfers between devices  68.1 us (11%)
  other arithmetic  54.5 us (9%)
  matrix products  47.2 us (8%)
  local copies, waits for them, and re-layouts  39.1 us (7%)
  between operations  15.6 us (3%)
    pallas_call x6, Pallas kernels, blocks_call(): pl.pallas_call(kernel, grid_spec=pltpu.PrefetchScalarGridSpec(num_scalar_...  108 us
    ppermute x27, waiting for transfers between devices, swap(): return lax.ppermute(x, axis, [(i, i ^ bit) for i in range(size)])  96.5 us
    pallas_call x1, Pallas kernels, attend_back(): pl.pallas_call(functools.partial(backward_kernel, heads), grid_spec=pltpu...  38.4 us
    ppermute x9, waiting for transfers between devices, line_down(): return lax.ppermute(x, 'fsdp', [(i, i - 1) for i in range(first, last)])  35.9 us
    ppermute x27, starting transfers between devices, swap(): return lax.ppermute(x, axis, [(i, i ^ bit) for i in range(size)])  29.3 us
    ppermute x9, starting transfers between devices, line_up(): return lax.ppermute(x, 'fsdp', [(i, i + 1) for i in range(first, last)])  26.3 us
    ppermute x9, waiting for transfers between devices, line_up(): return lax.ppermute(x, 'fsdp', [(i, i + 1) for i in range(first, last)])  24.9 us
    pallas_call x1, Pallas kernels, attend(): pl.pallas_call(functools.partial(forward_kernel, heads), grid_spec=pltpu....  22 us
  transfers between devices with their start and end apart: 49, of which 24 were waited for; matrix products, arithmetic and copies ran while one was open for 18% of the time, Pallas kernels for 32%

profile of v5, /device:TPU:0, one launch (start us, length us, event | category | flops | bytes accessed | tf_op | source)
XLA Modules:
  0.0 589.1 jit_solution(17122827090882704966)
XLA Ops:
  17.1 5.0 collective-permute-start
  26.5 18.3 %collective-permute-done.rest_1_ = bf16[512,1024]{1,0:T(8,128)(2,1)S(1)} collective-permute-done((bf16[512,1024]{1,0:T(8,128)(2,1)}, bf16[512,1024]{1,0:T(8,128)(2,1)S(1)}, u32[]{:S(2)}, u32[]{:S(2)}) %collective-permute-start) | collective-permute-done | bytes 1048608 | tf_op jit(solution)/shard_map/ppermute | solution.py:67
  44.8 4.1 collective-permute-done.1.rest_4_
  52.4 3.0 constant_dynamic-slice_fusion.24
  55.5 8.9 %fusion.18 = (f32[2048,128]{1,0:T(8,128)}, f32[2048,128]{1,0:T(8,128)}, f32[2048,128]{1,0:T(8,128)}, f32[2048,128]{1,0:T(8,128)}) fusion(f32[2048]{0:T(1024)S(1)} %get-tuple-element.365, f32[128]{0:T(128)S(1)} %get-tuple-element.361, f32[128]{0:T(128)S(1)} %get-tuple-element.362, f32[2048]{0:T(1024)S(1)} %get-tuple-element.366), kind=kLoop, calls=%fused_computation.47 | loop fusion | flops 1048576 | bytes 4211712 | tf_op jit(solution)/shard_map/mul | solution.py:954
  64.3 14.4 %collective-permute-done.7.rest_5_ = bf16[512,1024]{1,0:T(8,128)(2,1)} collective-permute-done((bf16[512,1024]{1,0:T(8,128)(2,1)S(1)}, bf16[512,1024]{1,0:T(8,128)(2,1)}, u32[]{:S(2)}, u32[]{:S(2)}) %collective-permute-start.7) | collective-permute-done | bytes 1048608 | tf_op jit(solution)/shard_map/ppermute | solution.py:71
  85.9 8.9 %collective-permute-done.4.refs_3_ = bf16[128,2048]{1,0:T(8,128)(2,1)S(1)} collective-permute-done((bf16[128,2048]{1,0:T(8,128)(2,1)S(1)}, bf16[128,2048]{1,0:T(8,128)(2,1)S(1)}, u32[]{:S(2)}, u32[]{:S(2)}) %collective-permute-start.4) | collective-permute-done | bytes 524320 | tf_op jit(solution)/shard_map/ppermute | solution.py:33
  98.3 3.3 assemble.2.refs_0_
  101.6 3.9 collective-permute-done.9.rest_6_
  105.5 2.4 collective-permute-start.11
  110.7 2.3 collective-permute-done.10.refs_1_
  113.0 6.8 %assemble.3.x_in_ref.x_ref = bf16[2048,2048]{1,0:T(8,128)(2,1)} custom-call(bf16[1024,2048]{1,0:T(8,128)(2,1)} %assemble.2.refs_0_, bf16[1024,2048]{1,0:T(8,128)(2,1)} %collective-permute-done.10.refs_1_), custom_call_target="tpu_custom_call" | custom-call | flops 1048576 | bytes 1048576 | tf_op jit(solution)/shard_map/assemble/pallas_call | solution.py:725
  119.9 22.2 %pack.1 = (bf16[2048,768]{1,0:T(8,128)(2,1)}, bf16[256,2048]{1,0:T(8,128)(2,1)S(1)}) custom-call(s32[1]{0:T(128)} %bitcast.1.z_ref, bf16[2048,2048]{1,0:T(8,128)(2,1)} %assemble.3.x_in_ref.x_ref, f32[8,768]{1,0:T(8,128)S(1)} %broadcast_in_dim.73.bias_ref, f32[2048,128]{1,0:T(8,128)S(1)} %copy-done.20, f32[2048,128]{1,0:T(8,128)S(1)} %copy-done.21, ...), custom_call_target="tpu_custom_call" | custom-call | flops 644245120 | bytes 1048576 | tf_op jit(solution)/shard_map/pack/pallas_call | solution.py:560
  148.8 22.0 %attend_forward.1 = (f32[256,2048]{1,0:T(8,128)}, f32[8,2048]{1,0:T(8,128)}, bf16[2048,256]{1,0:T(8,128)(2,1)}) custom-call(s32[8]{0:T(128)} %and_select_fusion.5.low_ref, bf16[2048,768]{1,0:T(8,128)(2,1)} %get-tuple-element.212.packed_ref, bf16[256,2048]{1,0:T(8,128)(2,1)} %copy-done.39, s32[2048,1]{1,0:T(8,128)} %copy.29.pcol_ref, s32[1,2048]{1,0:T(1,128)} %bitcast.82, ...), custom_call_target="tpu_custom_call" | custom-call | flops 10737418240 | bytes 10485760 | tf_op jit(solution)/shard_map/attend_forward/pallas_call | solution.py:809
  175.6 6.4 %reorder.3.x_ref = bf16[2048,2048]{1,0:T(8,128)(2,1)S(1)} custom-call(s32[8]{0:T(128)S(1)} %stack.64.order_ref, bf16[2048,2048]{1,0:T(8,128)(2,1)} %all-gather.3.cloned.1.call-done.x_ref), custom_call_target="tpu_custom_call" | custom-call | flops 1048576 | bytes 1048576 | tf_op jit(solution)/shard_map/reorder/pallas_call | solution.py:694
  182.0 3.3 copy-done.2
  185.3 6.9 %times.1.grad_ref = bf16[2048,256]{1,0:T(8,128)(2,1)S(1)} custom-call(s32[1]{0:T(128)} %bitcast.1.z_ref, bf16[2048,2048]{1,0:T(8,128)(2,1)} %copy-done.2, bf16[512,1024]{1,0:T(8,128)(2,1)S(1)} %copy-done.4, bf16[512,1024]{1,0:T(8,128)(2,1)S(1)} %copy-done.9, bf16[512,1024]{1,0:T(8,128)(2,1)} %collective-permute-done.6.rest_2_, ...), custom_call_target="tpu_custom_call" | custom-call | flops 107374184 | bytes 1048576 | tf_op jit(solution)/shard_map/times/pallas_call | solution.py:560
  192.3 7.3 %convolution_convert_fusion.3.b_ref = bf16[2048,256]{1,0:T(8,128)(2,1)} fusion(bf16[2048,2048]{1,0:T(8,128)(2,1)} %copy-done.2, bf16[2048,256]{1,0:T(8,128)(2,1)S(1)} %copy-done.29), kind=kOutput, calls=%fused_computation.9 | convolution fusion | flops 2148007936 | bytes 10485760 | tf_op jit(solution)/shard_map/dot_general | solution.py:1004
  201.2 17.0 %up.1 = (f32[2048,1024]{1,0:T(8,128)}, bf16[2048,1024]{1,0:T(8,128)(2,1)}) custom-call(s32[1]{0:T(128)} %bitcast.1.z_ref, bf16[2048,2048]{1,0:T(8,128)(2,1)} %assemble.3.x_in_ref.x_ref, f32[8,1024]{1,0:T(8,128)S(1)} %broadcast_in_dim.78.bias_ref, bf16[512,1024]{1,0:T(8,128)(2,1)} %get-tuple-element.192.rest_0_.rest_7_, ...), custom_call_target="tpu_custom_call" | custom-call | flops 429496736 | bytes 1048576 | tf_op jit(solution)/shard_map/up/pallas_call | solution.py:560
  218.2 12.7 %convolution_convert_fusion.1.x_ref = bf16[2048,1024]{1,0:T(8,128)(2,1)S(1)} fusion(bf16[2048,2048]{1,0:T(8,128)(2,1)} %copy-done.2, bf16[2048,1024]{1,0:T(8,128)(2,1)} %get-tuple-element.211.b_ref), kind=kOutput, calls=%fused_computation.4 | convolution fusion | flops 8592031744 | bytes 16777216 | tf_op jit(solution)/shard_map/dot_general | solution.py:1014
  235.8 38.4 %attend_backward.1 = (bf16[2048,768]{1,0:T(8,128)(2,1)}, f32[8,768]{1,0:T(8,128)}) custom-call(s32[8]{0:T(128)} %and_select_fusion.5.low_ref, bf16[2048,768]{1,0:T(8,128)(2,1)} %get-tuple-element.212.packed_ref, f32[256,2048]{1,0:T(8,128)} %get-tuple-element.213.outt_ref, f32[8,2048]{1,0:T(8,128)} %get-tuple-element.214.lse_ref, ...), custom_call_target="tpu_custom_call" | custom-call | flops 30064771072 | bytes 10485760 | tf_op jit(solution)/shard_map/attend_backward/pallas_call | solution.py:834
  274.7 10.3 %convolution_convert_fusion.2.a_ref = bf16[2048,768]{1,0:T(8,128)(2,1)S(1)} fusion(bf16[2048,2048]{1,0:T(8,128)(2,1)} %assemble.3.x_in_ref.x_ref, bf16[2048,768]{1,0:T(8,128)(2,1)} %get-tuple-element.242.a_ref), kind=kOutput, calls=%fused_computation.5 | convolution fusion | flops 6444023808 | bytes 14680064 | tf_op jit(solution)/shard_map/dot_general | solution.py:1025
  289.3 4.8 collective-permute-start.17
  294.9 18.5 %up_back.1 = (bf16[2048,1024]{1,0:T(8,128)(2,1)S(1)}, f32[8,1024]{1,0:T(8,128)S(1)}) custom-call(s32[1]{0:T(128)} %bitcast.1.z_ref, bf16[2048,2048]{1,0:T(8,128)(2,1)} %copy-done.2, f32[2048,1024]{1,0:T(8,128)} %get-tuple-element.224.up_ref, bf16[2048,1024]{1,0:T(8,128)(2,1)} %all-gather.5.cloned.1.call-done.rest_0_.rest_7_), custom_call_target="tpu_custom_call" | custom-call | flops 429496736 | bytes 1048576 | tf_op jit(solution)/shard_map/up_back/pallas_call | solution.py:560
  313.4 19.6 %to_features.2 = (bf16[4,256,2048]{2,1,0:T(8,128)(2,1)}, bf16[4,256,2048]{2,1,0:T(8,128)(2,1)}) custom-call(s32[1]{0:T(128)} %bitcast.1.z_ref, bf16[2048,256]{1,0:T(8,128)(2,1)S(1)} %copy-done.30, bf16[2048,1024]{1,0:T(8,128)(2,1)} %get-tuple-element.211.b_ref, bf16[512,1024]{1,0:T(8,128)(2,1)S(1)} %copy-done.5, bf16[512,1024]{1,0:T(8,128)(2,1)S(1)} %copy-done.10, ...), custom_call_target="tpu_custom_call" | custom-call | flops 536870912 | bytes 1048576 | tf_op jit(solution)/shard_map/to_features/pallas_call | solution.py:560
  333.0 6.6 %collective-permute-done.17 = bf16[512,1024]{1,0:T(8,128)(2,1)S(1)} collective-permute-done((bf16[512,1024]{1,0:T(8,128)(2,1)}, bf16[512,1024]{1,0:T(8,128)(2,1)S(1)}, u32[]{:S(2)}, u32[]{:S(2)}) %collective-permute-start.17) | collective-permute-done | bytes 1048608 | tf_op jit(solution)/shard_map/ppermute | solution.py:67
  342.4 5.3 collective-permute-start.20
  349.4 11.5 %convolution_convert_fusion.x_ref = bf16[2048,1024]{1,0:T(8,128)(2,1)S(1)} fusion(bf16[2048,2048]{1,0:T(8,128)(2,1)} %assemble.3.x_in_ref.x_ref, bf16[2048,1024]{1,0:T(8,128)(2,1)S(1)} %get-tuple-element.236.b_ref), kind=kOutput, calls=%fused_computation.3 | convolution fusion | flops 8592031744 | bytes 16777216 | tf_op jit(solution)/shard_map/dot_general | solution.py:1043
  363.9 7.9 %add_convert_fusion.1 = bf16[4,256,2048]{2,1,0:T(8,128)(2,1)} fusion(bf16[4,256,2048]{2,1,0:T(8,128)(2,1)} %collective-permute-done.19, bf16[4,256,2048]{2,1,0:T(8,128)(2,1)} %get-tuple-element.239), kind=kLoop, calls=%fused_computation.1 | loop fusion | flops 8388608 | bytes 12582912 | tf_op jit(solution)/shard_map/convert_element_type | solution.py:209
  371.8 23.6 %to_features.3 = (bf16[4,256,2048]{2,1,0:T(8,128)(2,1)}, bf16[4,256,2048]{2,1,0:T(8,128)(2,1)}) custom-call(s32[1]{0:T(128)} %bitcast.1.z_ref, bf16[2048,768]{1,0:T(8,128)(2,1)} %get-tuple-element.242.a_ref, bf16[2048,1024]{1,0:T(8,128)(2,1)} %copy-done.24, bf16[512,1024]{1,0:T(8,128)(2,1)S(1)} %copy-done.6, bf16[512,1024]{1,0:T(8,128)(2,1)S(1)} %copy-done.11, ...), custom_call_target="tpu_custom_call" | custom-call | flops 751619264 | bytes 1048576 | tf_op jit(solution)/shard_map/to_features/pallas_call | solution.py:560
  395.5 11.7 %reduce-scatter.3.cloned.1.call-done = bf16[512,1024]{1,0:T(8,128)(2,1)} async-done(((bf16[2048,1024]{1,0:T(8,128)(2,1)}), bf16[512,1024]{1,0:T(8,128)(2,1)}) %reduce-scatter.3.cloned.1.call-update) | async-done | bytes 1048592 | tf_op jit(solution)/shard_map/reduce_scatter | solution.py:1018
  407.2 2.9 add_convert_fusion.4
  410.1 2.6 add_convert_fusion.3
  416.7 2.8 slice_bitcast_fusion.4
  425.3 4.1 add_convert_fusion
  429.4 16.3 %collective-permute-done.22 = bf16[256,2048]{1,0:T(8,128)(2,1)S(1)} collective-permute-done((bf16[256,2048]{1,0:T(8,128)(2,1)S(1)}, bf16[256,2048]{1,0:T(8,128)(2,1)S(1)}, u32[]{:S(2)}, u32[]{:S(2)}) %collective-permute-start.22) | collective-permute-done | bytes 1048608 | tf_op jit(solution)/shard_map/ppermute | solution.py:33
  445.6 22.3 %collective-permute-done.23 = bf16[256,2048]{1,0:T(8,128)(2,1)S(1)} collective-permute-done((bf16[256,2048]{1,0:T(8,128)(2,1)S(1)}, bf16[256,2048]{1,0:T(8,128)(2,1)S(1)}, u32[]{:S(2)}, u32[]{:S(2)}) %collective-permute-start.23) | collective-permute-done | bytes 1048608 | tf_op jit(solution)/shard_map/ppermute | solution.py:33
  473.9 8.9 %collective-permute-done.26 = bf16[128,2048]{1,0:T(8,128)(2,1)S(1)} collective-permute-done((bf16[128,2048]{1,0:T(8,128)(2,1)S(1)}, bf16[128,2048]{1,0:T(8,128)(2,1)S(1)}, u32[]{:S(2)}, u32[]{:S(2)}) %collective-permute-start.26) | collective-permute-done | bytes 524320 | tf_op jit(solution)/shard_map/ppermute | solution.py:33
  488.5 11.2 %collective-permute-done.32 = bf16[512,1024]{1,0:T(8,128)(2,1)} collective-permute-done((bf16[512,1024]{1,0:T(8,128)(2,1)}, bf16[512,1024]{1,0:T(8,128)(2,1)}, u32[]{:S(2)}, u32[]{:S(2)}) %collective-permute-start.32) | collective-permute-done | bytes 1048608 | tf_op jit(solution)/shard_map/ppermute | solution.py:71
  499.7 3.1 add_convert_fusion.2
  502.8 5.6 collective-permute-done.29
  523.6 9.1 %collective-permute-done.33.refs_1_ = bf16[128,2048]{1,0:T(8,128)(2,1)S(1)} collective-permute-done((bf16[128,2048]{1,0:T(8,128)(2,1)S(1)}, bf16[128,2048]{1,0:T(8,128)(2,1)S(1)}, u32[]{:S(2)}, u32[]{:S(2)}) %collective-permute-start.33) | collective-permute-done | bytes 524320 | tf_op jit(solution)/shard_map/ppermute | solution.py:33
  532.8 11.3 %collective-permute-done.34.refs_2_ = bf16[128,2048]{1,0:T(8,128)(2,1)S(1)} collective-permute-done((bf16[128,2048]{1,0:T(8,128)(2,1)S(1)}, bf16[128,2048]{1,0:T(8,128)(2,1)S(1)}, u32[]{:S(2)}, u32[]{:S(2)}) %collective-permute-start.34) | collective-permute-done | bytes 524320 | tf_op jit(solution)/shard_map/ppermute | solution.py:33
  550.5 2.7 collective-permute-done.38
  553.2 2.8 collective-permute-start.39
  566.2 6.7 %collective-permute-done.41 = f32[13312]{0:T(1024)S(1)} collective-permute-done((f32[13312]{0:T(1024)S(1)}, f32[13312]{0:T(1024)S(1)}, u32[]{:S(2)}, u32[]{:S(2)}) %collective-permute-start.41) | collective-permute-done | bytes 53280 | tf_op jit(solution)/shard_map/ppermute | solution.py:33
  576.2 2.7 broadcast_select_fusion.1
  578.9 2.5 maximum_bitcast_fusion
  (299 shorter events, 118.5 us)
Async XLA Ops:
  7.2 168.4 %all-gather.3.cloned.1.call-start = ((), (), s32[]{:S(2)}) async-start(), calls=%async_computation.2 | async-start | bytes 9437184 | tf_op jit(solution)/shard_map/all_gather | solution.py:931
  17.1 272.3 %all-gather.5.cloned.1.call-start = ((), (), s32[]{:S(2)}) async-start(), calls=%async_computation.3 | async-start | bytes 5242880 | tf_op jit(solution)/shard_map/all_gather | solution.py:1009
  17.1 27.7 %collective-permute-start = (bf16[512,1024]{1,0:T(8,128)(2,1)}, bf16[512,1024]{1,0:T(8,128)(2,1)S(1)}, u32[]{:S(2)}, u32[]{:S(2)}) collective-permute-start(bf16[512,1024]{1,0:T(8,128)(2,1)} %pad_maximum_fusion.2.rest_0_), channel_id=1, source_target_pairs={{0,8},{8,16},{16,24},{1,9},{9,17},{17,25},{2,10},{10,18},{18,26},{... | collective-permute-start | bytes 3145736 | tf_op jit(solution)/shard_map/ppermute | solution.py:67
  22.1 26.8 %collective-permute-start.1 = (bf16[512,1024]{1,0:T(8,128)(2,1)}, bf16[512,1024]{1,0:T(8,128)(2,1)S(1)}, u32[]{:S(2)}, u32[]{:S(2)}) collective-permute-start(bf16[512,1024]{1,0:T(8,128)(2,1)} %pad_maximum_fusion.2.rest_0_), channel_id=1, source_target_pairs={{8,0},{16,8},{24,16},{9,1},{17,9},{25,17},{10,2},{18,10},{26,18},{... | collective-permute-start | bytes 3145736 | tf_op jit(solution)/shard_map/ppermute | solution.py:71
  23.4 40.9 %collective-permute-start.2 = (bf16[256,2048]{1,0:T(8,128)(2,1)}, bf16[256,2048]{1,0:T(8,128)(2,1)S(1)}, u32[]{:S(2)}, u32[]{:S(2)}) collective-permute-start(bf16[256,2048]{1,0:T(8,128)(2,1)} %copy-done.25), channel_id=1, source_target_pairs={{0,2},{2,0},{4,6},{6,4},{1,3},{3,1},{5,7},{7,5},{8,10},{10,8},{12,... | collective-permute-start | bytes 3145736 | tf_op jit(solution)/shard_map/ppermute | solution.py:33
  25.0 39.4 %collective-permute-start.3 = (bf16[256,2048]{1,0:T(8,128)(2,1)}, bf16[256,2048]{1,0:T(8,128)(2,1)}, u32[]{:S(2)}, u32[]{:S(2)}) collective-permute-start(bf16[256,2048]{1,0:T(8,128)(2,1)} %copy-done.25), channel_id=1, source_target_pairs={{0,4},{2,6},{4,0},{6,2},{1,5},{3,7},{5,1},{7,3},{8,12},{10,14},{12... | collective-permute-start | bytes 3145736 | tf_op jit(solution)/shard_map/ppermute | solution.py:33
  49.1 15.3 %collective-permute-start.6 = (bf16[512,1024]{1,0:T(8,128)(2,1)S(1)}, bf16[512,1024]{1,0:T(8,128)(2,1)}, u32[]{:S(2)}, u32[]{:S(2)}) collective-permute-start(bf16[512,1024]{1,0:T(8,128)(2,1)S(1)} %collective-permute-done.rest_1_), channel_id=1, source_target_pairs={{8,16},{16,24},{9,17},{17,25},{10,18},{18,26},{11,19},{19,27},{12,... | collective-permute-start | bytes 3145736 | tf_op jit(solution)/shard_map/ppermute | solution.py:67
  50.7 28.1 %collective-permute-start.7 = (bf16[512,1024]{1,0:T(8,128)(2,1)S(1)}, bf16[512,1024]{1,0:T(8,128)(2,1)}, u32[]{:S(2)}, u32[]{:S(2)}) collective-permute-start(bf16[512,1024]{1,0:T(8,128)(2,1)S(1)} %collective-permute-done.1.rest_4_), channel_id=1, source_target_pairs={{8,0},{16,8},{9,1},{17,9},{10,2},{18,10},{11,3},{19,11},{12,4},{20... | collective-permute-start | bytes 3145736 | tf_op jit(solution)/shard_map/ppermute | solution.py:71
  78.8 22.8 %collective-permute-start.8 = (bf16[512,1024]{1,0:T(8,128)(2,1)}, bf16[512,1024]{1,0:T(8,128)(2,1)}, u32[]{:S(2)}, u32[]{:S(2)}) collective-permute-start(bf16[512,1024]{1,0:T(8,128)(2,1)} %collective-permute-done.6.rest_2_), channel_id=1, source_target_pairs={{16,24},{17,25},{18,26},{19,27},{20,28},{21,29},{22,30},{23,31}} | collective-permute-start | bytes 3145736 | tf_op jit(solution)/shard_map/ppermute | solution.py:67
  80.4 25.1 %collective-permute-start.9 = (bf16[512,1024]{1,0:T(8,128)(2,1)}, bf16[512,1024]{1,0:T(8,128)(2,1)}, u32[]{:S(2)}, u32[]{:S(2)}) collective-permute-start(bf16[512,1024]{1,0:T(8,128)(2,1)} %collective-permute-done.7.rest_5_), channel_id=1, source_target_pairs={{8,0},{9,1},{10,2},{11,3},{12,4},{13,5},{14,6},{15,7}} | collective-permute-start | bytes 3145736 | tf_op jit(solution)/shard_map/ppermute | solution.py:71
  82.9 12.0 %collective-permute-start.4 = (bf16[128,2048]{1,0:T(8,128)(2,1)S(1)}, bf16[128,2048]{1,0:T(8,128)(2,1)S(1)}, u32[]{:S(2)}, u32[]{:S(2)}) collective-permute-start(bf16[128,2048]{1,0:T(8,128)(2,1)S(1)} %slice.94), channel_id=1, source_target_pairs={{0,4},{2,6},{4,0},{6,2},{1,5},{3,7},{5,1},{7,3},{8,12},{10,14},{12... | collective-permute-start | bytes 1572872 | tf_op jit(solution)/shard_map/ppermute | solution.py:33
  84.5 11.4 %collective-permute-start.5 = (bf16[128,2048]{1,0:T(8,128)(2,1)S(1)}, bf16[128,2048]{1,0:T(8,128)(2,1)S(1)}, u32[]{:S(2)}, u32[]{:S(2)}) collective-permute-start(bf16[128,2048]{1,0:T(8,128)(2,1)S(1)} %slice.95), channel_id=1, source_target_pairs={{0,2},{2,0},{4,6},{6,4},{1,3},{3,1},{5,7},{7,5},{8,10},{10,8},{12,... | collective-permute-start | bytes 1572872 | tf_op jit(solution)/shard_map/ppermute | solution.py:33
  105.5 7.5 %collective-permute-start.10 = (bf16[1024,2048]{1,0:T(8,128)(2,1)}, bf16[1024,2048]{1,0:T(8,128)(2,1)}, u32[]{:S(2)}, u32[]{:S(2)}) collective-permute-start(bf16[1024,2048]{1,0:T(8,128)(2,1)} %assemble.2.refs_0_), channel_id=1, source_target_pairs={{0,1},{1,0},{2,3},{3,2},{4,5},{5,4},{6,7},{7,6},{8,9},{9,8},{10,11... | collective-permute-start | bytes 12582920 | tf_op jit(solution)/shard_map/ppermute | solution.py:33
  105.5 37.6 %collective-permute-start.11 = (bf16[512,1024]{1,0:T(8,128)(2,1)}, bf16[512,1024]{1,0:T(8,128)(2,1)}, u32[]{:S(2)}, u32[]{:S(2)}) collective-permute-start(bf16[512,1024]{1,0:T(8,128)(2,1)} %get-tuple-element.192.rest_0_.rest_7_), channel_id=1, source_target_pairs={{0,8},{8,16},{16,24},{1,9},{9,17},{17,25},{2,10},{10,18},{18,26},{... | collective-permute-start | bytes 3145736 | tf_op jit(solution)/shard_map/ppermute | solution.py:67
  107.9 35.2 %collective-permute-start.12 = (bf16[512,1024]{1,0:T(8,128)(2,1)}, bf16[512,1024]{1,0:T(8,128)(2,1)}, u32[]{:S(2)}, u32[]{:S(2)}) collective-permute-start(bf16[512,1024]{1,0:T(8,128)(2,1)} %get-tuple-element.192.rest_0_.rest_7_), channel_id=1, source_target_pairs={{8,0},{16,8},{24,16},{9,1},{17,9},{25,17},{10,2},{18,10},{26,18},{... | collective-permute-start | bytes 3145736 | tf_op jit(solution)/shard_map/ppermute | solution.py:71
  143.1 27.7 %collective-permute-start.13 = (bf16[512,1024]{1,0:T(8,128)(2,1)}, bf16[512,1024]{1,0:T(8,128)(2,1)}, u32[]{:S(2)}, u32[]{:S(2)}) collective-permute-start(bf16[512,1024]{1,0:T(8,128)(2,1)} %collective-permute-done.11.rest_1_.rest_8_), channel_id=1, source_target_pairs={{8,16},{16,24},{9,17},{17,25},{10,18},{18,26},{11,19},{19,27},{12,... | collective-permute-start | bytes 3145736 | tf_op jit(solution)/shard_map/ppermute | solution.py:67
  144.8 27.4 %collective-permute-start.14 = (bf16[512,1024]{1,0:T(8,128)(2,1)}, bf16[512,1024]{1,0:T(8,128)(2,1)}, u32[]{:S(2)}, u32[]{:S(2)}) collective-permute-start(bf16[512,1024]{1,0:T(8,128)(2,1)} %collective-permute-done.12.rest_4_.rest_11_), channel_id=1, source_target_pairs={{8,0},{16,8},{9,1},{17,9},{10,2},{18,10},{11,3},{19,11},{12,4},{20... | collective-permute-start | bytes 3145736 | tf_op jit(solution)/shard_map/ppermute | solution.py:71
  172.2 27.4 %collective-permute-start.15 = (bf16[512,1024]{1,0:T(8,128)(2,1)}, bf16[512,1024]{1,0:T(8,128)(2,1)}, u32[]{:S(2)}, u32[]{:S(2)}) collective-permute-start(bf16[512,1024]{1,0:T(8,128)(2,1)} %collective-permute-done.13.rest_2_.rest_9_), channel_id=1, source_target_pairs={{16,24},{17,25},{18,26},{19,27},{20,28},{21,29},{22,30},{23,31}} | collective-permute-start | bytes 3145736 | tf_op jit(solution)/shard_map/ppermute | solution.py:67
  173.8 26.6 %collective-permute-start.16 = (bf16[512,1024]{1,0:T(8,128)(2,1)}, bf16[512,1024]{1,0:T(8,128)(2,1)}, u32[]{:S(2)}, u32[]{:S(2)}) collective-permute-start(bf16[512,1024]{1,0:T(8,128)(2,1)} %collective-permute-done.14.rest_5_.rest_12_), channel_id=1, source_target_pairs={{8,0},{9,1},{10,2},{11,3},{12,4},{13,5},{14,6},{15,7}} | collective-permute-start | bytes 3145736 | tf_op jit(solution)/shard_map/ppermute | solution.py:71
  200.4 206.8 %reduce-scatter.3.cloned.1.call-start = ((), (), s32[]{:S(2)}) async-start(), calls=%async_computation.4 | async-start | bytes 5242880 | tf_op jit(solution)/shard_map/reduce_scatter | solution.py:1018
  274.2 238.8 %reduce-scatter.5.cloned.1.call-start = ((), (), s32[]{:S(2)}) async-start(), calls=%async_computation.5 | async-start | bytes 5242880 | tf_op jit(solution)/shard_map/reduce_scatter | solution.py:1049
  289.3 50.3 %collective-permute-start.17 = (bf16[512,1024]{1,0:T(8,128)(2,1)}, bf16[512,1024]{1,0:T(8,128)(2,1)S(1)}, u32[]{:S(2)}, u32[]{:S(2)}) collective-permute-start(bf16[512,1024]{1,0:T(8,128)(2,1)} %copy-done.32), channel_id=1, source_target_pairs={{0,8},{1,9},{2,10},{3,11},{4,12},{5,13},{6,14},{7,15}} | collective-permute-start | bytes 3145736 | tf_op jit(solution)/shard_map/ppermute | solution.py:67
  294.1 45.5 %collective-permute-start.18 = (bf16[512,1024]{1,0:T(8,128)(2,1)}, bf16[512,1024]{1,0:T(8,128)(2,1)S(1)}, u32[]{:S(2)}, u32[]{:S(2)}) collective-permute-start(bf16[512,1024]{1,0:T(8,128)(2,1)} %copy-done.34), channel_id=1, source_target_pairs={{24,16},{25,17},{26,18},{27,19},{28,20},{29,21},{30,22},{31,23}} | collective-permute-start | bytes 3145736 | tf_op jit(solution)/shard_map/ppermute | solution.py:71
  342.4 21.5 %collective-permute-start.19 = (bf16[4,256,2048]{2,1,0:T(8,128)(2,1)}, bf16[4,256,2048]{2,1,0:T(8,128)(2,1)}, u32[]{:S(2)}, u32[]{:S(2)}) collective-permute-start(bf16[4,256,2048]{2,1,0:T(8,128)(2,1)} %get-tuple-element.238), channel_id=1, source_target_pairs={{0,1},{1,0},{2,3},{3,2},{4,5},{5,4},{6,7},{7,6},{8,9},{9,8},{10,11... | collective-permute-start | bytes 12582920 | tf_op jit(solution)/shard_map/ppermute | solution.py:33
  342.4 53.1 %collective-permute-start.20 = (bf16[512,1024]{1,0:T(8,128)(2,1)}, bf16[512,1024]{1,0:T(8,128)(2,1)}, u32[]{:S(2)}, u32[]{:S(2)}) collective-permute-start(bf16[512,1024]{1,0:T(8,128)(2,1)} %add_convert_fusion.6), channel_id=1, source_target_pairs={{0,8},{8,16},{1,9},{9,17},{2,10},{10,18},{3,11},{11,19},{4,12},{12... | collective-permute-start | bytes 3145736 | tf_op jit(solution)/shard_map/ppermute | solution.py:67
  347.6 47.9 %collective-permute-start.21 = (bf16[512,1024]{1,0:T(8,128)(2,1)}, bf16[512,1024]{1,0:T(8,128)(2,1)}, u32[]{:S(2)}, u32[]{:S(2)}) collective-permute-start(bf16[512,1024]{1,0:T(8,128)(2,1)} %add_convert_fusion.5), channel_id=1, source_target_pairs={{16,8},{24,16},{17,9},{25,17},{18,10},{26,18},{19,11},{27,19},{20,... | collective-permute-start | bytes 3145736 | tf_op jit(solution)/shard_map/ppermute | solution.py:71
  412.7 11.0 %collective-permute-start.25 = (bf16[4,256,2048]{2,1,0:T(8,128)(2,1)}, bf16[4,256,2048]{2,1,0:T(8,128)(2,1)}, u32[]{:S(2)}, u32[]{:S(2)}) collective-permute-start(bf16[4,256,2048]{2,1,0:T(8,128)(2,1)} %get-tuple-element.257), channel_id=1, source_target_pairs={{0,1},{1,0},{2,3},{3,2},{4,5},{5,4},{6,7},{7,6},{8,9},{9,8},{10,11... | collective-permute-start | bytes 12582920 | tf_op jit(solution)/shard_map/ppermute | solution.py:33
  414.5 74.0 %collective-permute-start.31 = (bf16[512,1024]{1,0:T(8,128)(2,1)}, bf16[512,1024]{1,0:T(8,128)(2,1)}, u32[]{:S(2)}, u32[]{:S(2)}) collective-permute-start(bf16[512,1024]{1,0:T(8,128)(2,1)} %add_convert_fusion.4), channel_id=1, source_target_pairs={{0,8},{8,16},{16,24},{1,9},{9,17},{17,25},{2,10},{10,18},{18,26},{... | collective-permute-start | bytes 3145736 | tf_op jit(solution)/shard_map/ppermute | solution.py:67
  419.5 26.1 %collective-permute-start.22 = (bf16[256,2048]{1,0:T(8,128)(2,1)S(1)}, bf16[256,2048]{1,0:T(8,128)(2,1)S(1)}, u32[]{:S(2)}, u32[]{:S(2)}) collective-permute-start(bf16[256,2048]{1,0:T(8,128)(2,1)S(1)} %get-tuple-element.253), channel_id=1, source_target_pairs={{0,2},{2,0},{4,6},{6,4},{1,3},{3,1},{5,7},{7,5},{8,10},{10,8},{12,... | collective-permute-start | bytes 3145736 | tf_op jit(solution)/shard_map/ppermute | solution.py:33
  421.0 46.9 %collective-permute-start.23 = (bf16[256,2048]{1,0:T(8,128)(2,1)S(1)}, bf16[256,2048]{1,0:T(8,128)(2,1)S(1)}, u32[]{:S(2)}, u32[]{:S(2)}) collective-permute-start(bf16[256,2048]{1,0:T(8,128)(2,1)S(1)} %get-tuple-element.254), channel_id=1, source_target_pairs={{0,4},{2,6},{4,0},{6,2},{1,5},{3,7},{5,1},{7,3},{8,12},{10,14},{12... | collective-permute-start | bytes 3145736 | tf_op jit(solution)/shard_map/ppermute | solution.py:33
  422.5 45.4 %collective-permute-start.24 = (bf16[256,2048]{1,0:T(8,128)(2,1)S(1)}, bf16[256,2048]{1,0:T(8,128)(2,1)S(1)}, u32[]{:S(2)}, u32[]{:S(2)}) collective-permute-start(bf16[256,2048]{1,0:T(8,128)(2,1)S(1)} %get-tuple-element.255), channel_id=1, source_target_pairs={{0,6},{2,4},{4,2},{6,0},{1,7},{3,5},{5,3},{7,1},{8,14},{10,12},{12... | collective-permute-start | bytes 3145736 | tf_op jit(solution)/shard_map/ppermute | solution.py:33
  423.7 76.0 %collective-permute-start.32 = (bf16[512,1024]{1,0:T(8,128)(2,1)}, bf16[512,1024]{1,0:T(8,128)(2,1)}, u32[]{:S(2)}, u32[]{:S(2)}) collective-permute-start(bf16[512,1024]{1,0:T(8,128)(2,1)} %add_convert_fusion.3), channel_id=1, source_target_pairs={{8,0},{16,8},{24,16},{9,1},{17,9},{25,17},{10,2},{18,10},{26,18},{... | collective-permute-start | bytes 3145736 | tf_op jit(solution)/shard_map/ppermute | solution.py:71
  470.2 12.6 %collective-permute-start.26 = (bf16[128,2048]{1,0:T(8,128)(2,1)S(1)}, bf16[128,2048]{1,0:T(8,128)(2,1)S(1)}, u32[]{:S(2)}, u32[]{:S(2)}) collective-permute-start(bf16[128,2048]{1,0:T(8,128)(2,1)S(1)} %get-tuple-element.343), channel_id=1, source_target_pairs={{0,4},{2,6},{4,0},{6,2},{1,5},{3,7},{5,1},{7,3},{8,12},{10,14},{12... | collective-permute-start | bytes 1572872 | tf_op jit(solution)/shard_map/ppermute | solution.py:33
  471.8 11.3 %collective-permute-start.27 = (bf16[128,2048]{1,0:T(8,128)(2,1)S(1)}, bf16[128,2048]{1,0:T(8,128)(2,1)S(1)}, u32[]{:S(2)}, u32[]{:S(2)}) collective-permute-start(bf16[128,2048]{1,0:T(8,128)(2,1)S(1)} %get-tuple-element.342), channel_id=1, source_target_pairs={{0,2},{2,0},{4,6},{6,4},{1,3},{3,1},{5,7},{7,5},{8,10},{10,8},{12,... | collective-permute-start | bytes 1572872 | tf_op jit(solution)/shard_map/ppermute | solution.py:33
  485.6 22.9 %collective-permute-start.29 = (bf16[256,2048]{1,0:T(8,128)(2,1)}, bf16[256,2048]{1,0:T(8,128)(2,1)S(1)}, u32[]{:S(2)}, u32[]{:S(2)}) collective-permute-start(bf16[256,2048]{1,0:T(8,128)(2,1)} %pad_maximum_fusion.3), channel_id=1, source_target_pairs={{0,2},{2,0},{4,6},{6,4},{1,3},{3,1},{5,7},{7,5},{8,10},{10,8},{12,... | collective-permute-start | bytes 3145736 | tf_op jit(solution)/shard_map/ppermute | solution.py:33
  487.0 22.8 %collective-permute-start.30 = (bf16[256,2048]{1,0:T(8,128)(2,1)}, bf16[256,2048]{1,0:T(8,128)(2,1)}, u32[]{:S(2)}, u32[]{:S(2)}) collective-permute-start(bf16[256,2048]{1,0:T(8,128)(2,1)} %pad_maximum_fusion.4), channel_id=1, source_target_pairs={{0,4},{2,6},{4,0},{6,2},{1,5},{3,7},{5,1},{7,3},{8,12},{10,14},{12... | collective-permute-start | bytes 3145736 | tf_op jit(solution)/shard_map/ppermute | solution.py:33
  488.4 67.5 %collective-permute-start.28 = (bf16[256,2048]{1,0:T(8,128)(2,1)}, bf16[256,2048]{1,0:T(8,128)(2,1)}, u32[]{:S(2)}, u32[]{:S(2)}) collective-permute-start(bf16[256,2048]{1,0:T(8,128)(2,1)} %fusion.8), channel_id=1, source_target_pairs={{0,1},{1,0},{2,3},{3,2},{4,5},{5,4},{6,7},{7,6},{8,9},{9,8},{10,11... | collective-permute-start | bytes 3145736 | tf_op jit(solution)/shard_map/ppermute | solution.py:33
  517.9 14.9 %collective-permute-start.33 = (bf16[128,2048]{1,0:T(8,128)(2,1)S(1)}, bf16[128,2048]{1,0:T(8,128)(2,1)S(1)}, u32[]{:S(2)}, u32[]{:S(2)}) collective-permute-start(bf16[128,2048]{1,0:T(8,128)(2,1)S(1)} %get-tuple-element.326), channel_id=1, source_target_pairs={{0,2},{2,0},{4,6},{6,4},{1,3},{3,1},{5,7},{7,5},{8,10},{10,8},{12,... | collective-permute-start | bytes 1572872 | tf_op jit(solution)/shard_map/ppermute | solution.py:33
  519.4 24.7 %collective-permute-start.34 = (bf16[128,2048]{1,0:T(8,128)(2,1)S(1)}, bf16[128,2048]{1,0:T(8,128)(2,1)S(1)}, u32[]{:S(2)}, u32[]{:S(2)}) collective-permute-start(bf16[128,2048]{1,0:T(8,128)(2,1)S(1)} %get-tuple-element.325), channel_id=1, source_target_pairs={{0,4},{2,6},{4,0},{6,2},{1,5},{3,7},{5,1},{7,3},{8,12},{10,14},{12... | collective-permute-start | bytes 1572872 | tf_op jit(solution)/shard_map/ppermute | solution.py:33
  520.9 23.2 %collective-permute-start.35 = (bf16[128,2048]{1,0:T(8,128)(2,1)S(1)}, bf16[128,2048]{1,0:T(8,128)(2,1)S(1)}, u32[]{:S(2)}, u32[]{:S(2)}) collective-permute-start(bf16[128,2048]{1,0:T(8,128)(2,1)S(1)} %get-tuple-element.324), channel_id=1, source_target_pairs={{0,6},{2,4},{4,2},{6,0},{1,7},{3,5},{5,3},{7,1},{8,14},{10,12},{12... | collective-permute-start | bytes 1572872 | tf_op jit(solution)/shard_map/ppermute | solution.py:33
  544.1 32.1 %collective-permute-start.36 = (f32[256,2048]{1,0:T(8,128)}, f32[256,2048]{1,0:T(8,128)}, u32[]{:S(2)}, u32[]{:S(2)}) collective-permute-start(f32[256,2048]{1,0:T(8,128)} %convert_add_fusion.1), channel_id=1, source_target_pairs={{0,1},{1,0},{2,3},{3,2},{4,5},{5,4},{6,7},{7,6},{8,9},{9,8},{10,11... | collective-permute-start | bytes 6291464 | tf_op jit(solution)/shard_map/ppermute | solution.py:33
  548.9 4.2 collective-permute-start.38
  553.2 5.1 collective-permute-start.39
  558.3 4.9 collective-permute-start.40
  559.6 15.1 %collective-permute-start.42 = (bf16[128,1024]{1,0:T(8,128)(2,1)S(1)}, bf16[128,1024]{1,0:T(8,128)(2,1)S(1)}, u32[]{:S(2)}, u32[]{:S(2)}) collective-permute-start(bf16[128,1024]{1,0:T(8,128)(2,1)S(1)} %get-tuple-element.340), channel_id=1, source_target_pairs={{0,2},{2,0},{4,6},{6,4},{1,3},{3,1},{5,7},{7,5},{8,10},{10,8},{12,... | collective-permute-start | bytes 786440 | tf_op jit(solution)/shard_map/ppermute | solution.py:33
  560.5 14.2 %collective-permute-start.43 = (bf16[128,1024]{1,0:T(8,128)(2,1)S(1)}, bf16[128,1024]{1,0:T(8,128)(2,1)S(1)}, u32[]{:S(2)}, u32[]{:S(2)}) collective-permute-start(bf16[128,1024]{1,0:T(8,128)(2,1)S(1)} %get-tuple-element.339), channel_id=1, source_target_pairs={{0,4},{2,6},{4,0},{6,2},{1,5},{3,7},{5,1},{7,3},{8,12},{10,14},{12... | collective-permute-start | bytes 786440 | tf_op jit(solution)/shard_map/ppermute | solution.py:33
  562.0 12.7 %collective-permute-start.44 = (bf16[128,1024]{1,0:T(8,128)(2,1)S(1)}, bf16[128,1024]{1,0:T(8,128)(2,1)S(1)}, u32[]{:S(2)}, u32[]{:S(2)}) collective-permute-start(bf16[128,1024]{1,0:T(8,128)(2,1)S(1)} %get-tuple-element.338), channel_id=1, source_target_pairs={{0,6},{2,4},{4,2},{6,0},{1,7},{3,5},{5,3},{7,1},{8,14},{10,12},{12... | collective-permute-start | bytes 786440 | tf_op jit(solution)/shard_map/ppermute | solution.py:33
  563.2 9.7 %collective-permute-start.41 = (f32[13312]{0:T(1024)S(1)}, f32[13312]{0:T(1024)S(1)}, u32[]{:S(2)}, u32[]{:S(2)}) collective-permute-start(f32[13312]{0:T(1024)S(1)} %add.329), channel_id=1, source_target_pairs={{0,4},{2,6},{4,0},{6,2},{1,5},{3,7},{5,1},{7,3},{8,12},{10,14},{12... | collective-permute-start | bytes 159752 | tf_op jit(solution)/shard_map/ppermute | solution.py:33
  (61 other events, 783.6 us)
Sparse Core Ops, SparseCore 0:
  17.2 68.7 all-gather.2
  200.5 84.6 all-gather.4
  287.6 119.5 reduce-scatter.2
  412.9 100.0 reduce-scatter.4

commit v6 on v5

--- a/solution.py
+++ b/solution.py
@@ -700,7 +700,7 @@
             out_specs=pl.BlockSpec((rows, cols), lambda i, order_ref: (i, 0)),
         ),
         out_shape=jax.ShapeDtypeStruct(x.shape, x.dtype),
-        compiler_params=pltpu.CompilerParams(vmem_limit_bytes=40 * 2**20),
+        compiler_params=pltpu.CompilerParams(vmem_limit_bytes=60 * 2**20),
         cost_estimate=pl.CostEstimate(flops=2**20, bytes_accessed=2**20, transcendentals=0),
         name="reorder",
     )(order, x)
@@ -728,7 +728,7 @@
         out_specs=pl.BlockSpec(memory_space=pl.ANY),
         scratch_shapes=[pltpu.SemaphoreType.DMA((len(pieces),))],
         out_shape=jax.ShapeDtypeStruct((rows, pieces[0].shape[1]), bf16),
-        compiler_params=pltpu.CompilerParams(vmem_limit_bytes=40 * 2**20),
+        compiler_params=pltpu.CompilerParams(vmem_limit_bytes=60 * 2**20),
         cost_estimate=pl.CostEstimate(flops=2**20, bytes_accessed=2**20, transcendentals=0),
         name="assemble",
     )(*pieces)

time: 597 us -> 596 us (level)
  Pallas kernels: 194 us -> 212 us
  waiting for transfers between devices: 170 us -> 158 us
    pallas_call x3, Pallas kernels: 8.14 us -> 20.9 us  [reorder(): pl.pallas_call(copy_kernel, grid_spec=pltpu.PrefetchScalarGridSpec(num_sc...]
    reduce_scatter x1, waiting for transfers between devices: 11.7 us -> 0.02 us  [shards(): lax.psum_scatter(order.then(down_grad), 'fsdp', scatter_dimension=0, tile...]
    unnamed x126 -> x108, local copies, waits for them, and re-layouts: 20.2 us -> 12.8 us
  transfers between devices with their start and end apart: 49 -> 49, of which waited for: 24 -> 21; matrix products, arithmetic and copies ran while one was open for 18% -> 18% of each run, Pallas kernels for 32% -> 36%
where the time goes in v6:
time: 596 us; the launch traced here: 587 us
  Pallas kernels  212 us (36%)
  waiting for transfers between devices  158 us (27%)
  starting transfers between devices  66.1 us (11%)
  other arithmetic  54.1 us (9%)
  matrix products  46 us (8%)
  local copies, waits for them, and re-layouts  34.1 us (6%)
  between operations  15.5 us (3%)
    pallas_call x6, Pallas kernels, blocks_call(): pl.pallas_call(kernel, grid_spec=pltpu.PrefetchScalarGridSpec(num_scalar_...  108 us
    ppermute x27, waiting for transfers between devices, swap(): return lax.ppermute(x, axis, [(i, i ^ bit) for i in range(size)])  97.4 us
    pallas_call x1, Pallas kernels, attend_back(): pl.pallas_call(functools.partial(backward_kernel, heads), grid_spec=pltpu...  41.2 us
    ppermute x9, waiting for transfers between devices, line_down(): return lax.ppermute(x, 'fsdp', [(i, i - 1) for i in range(first, last)])  35.5 us
    ppermute x27, starting transfers between devices, swap(): return lax.ppermute(x, axis, [(i, i ^ bit) for i in range(size)])  29.6 us
    ppermute x9, waiting for transfers between devices, line_up(): return lax.ppermute(x, 'fsdp', [(i, i + 1) for i in range(first, last)])  25.3 us
    pallas_call x1, Pallas kernels, attend(): pl.pallas_call(functools.partial(forward_kernel, heads), grid_spec=pltpu....  24.2 us
    ppermute x9, starting transfers between devices, line_up(): return lax.ppermute(x, 'fsdp', [(i, i + 1) for i in range(first, last)])  24 us
  transfers between devices with their start and end apart: 49, of which 21 were waited for; matrix products, arithmetic and copies ran while one was open for 18% of the time, Pallas kernels for 36%

profile of v6, /device:TPU:0, one launch (start us, length us, event | category | flops | bytes accessed | tf_op | source)
XLA Modules:
  0.0 586.7 jit_solution(7146692931867488478)
XLA Ops:
  15.2 5.0 collective-permute-start
  24.6 18.0 %collective-permute-done.rest_1_ = bf16[512,1024]{1,0:T(8,128)(2,1)S(1)} collective-permute-done((bf16[512,1024]{1,0:T(8,128)(2,1)S(1)}, bf16[512,1024]{1,0:T(8,128)(2,1)S(1)}, u32[]{:S(2)}, u32[]{:S(2)}) %collective-permute-start) | collective-permute-done | bytes 1048608 | tf_op jit(solution)/shard_map/ppermute | solution.py:67
  42.6 4.2 collective-permute-done.1.rest_4_
  50.3 3.0 constant_dynamic-slice_fusion.24
  53.3 8.9 %fusion.18 = (f32[2048,128]{1,0:T(8,128)}, f32[2048,128]{1,0:T(8,128)}, f32[2048,128]{1,0:T(8,128)}, f32[2048,128]{1,0:T(8,128)}) fusion(f32[2048]{0:T(1024)S(1)} %get-tuple-element.365, f32[128]{0:T(128)S(1)} %get-tuple-element.361, f32[128]{0:T(128)S(1)} %get-tuple-element.362, f32[2048]{0:T(1024)S(1)} %get-tuple-element.366), kind=kLoop, calls=%fused_computation.47 | loop fusion | flops 1048576 | bytes 4211712 | tf_op jit(solution)/shard_map/mul | solution.py:954
  62.2 14.5 %collective-permute-done.7.rest_5_ = bf16[512,1024]{1,0:T(8,128)(2,1)} collective-permute-done((bf16[512,1024]{1,0:T(8,128)(2,1)S(1)}, bf16[512,1024]{1,0:T(8,128)(2,1)}, u32[]{:S(2)}, u32[]{:S(2)}) %collective-permute-start.7) | collective-permute-done | bytes 1048608 | tf_op jit(solution)/shard_map/ppermute | solution.py:71
  84.0 9.0 %collective-permute-done.4.refs_3_ = bf16[128,2048]{1,0:T(8,128)(2,1)S(1)} collective-permute-done((bf16[128,2048]{1,0:T(8,128)(2,1)S(1)}, bf16[128,2048]{1,0:T(8,128)(2,1)S(1)}, u32[]{:S(2)}, u32[]{:S(2)}) %collective-permute-start.4) | collective-permute-done | bytes 524320 | tf_op jit(solution)/shard_map/ppermute | solution.py:33
  93.9 4.2 assemble.2.refs_0_
  98.2 4.3 collective-permute-done.9.rest_6_
  102.5 2.4 collective-permute-start.11
  110.0 6.8 %assemble.3.x_in_ref.x_ref = bf16[2048,2048]{1,0:T(8,128)(2,1)} custom-call(bf16[1024,2048]{1,0:T(8,128)(2,1)} %assemble.2.refs_0_, bf16[1024,2048]{1,0:T(8,128)(2,1)} %collective-permute-done.10.refs_1_), custom_call_target="tpu_custom_call" | custom-call | flops 1048576 | bytes 1048576 | tf_op jit(solution)/shard_map/assemble/pallas_call | solution.py:725
  119.3 22.3 %pack.1 = (bf16[2048,768]{1,0:T(8,128)(2,1)}, bf16[256,2048]{1,0:T(8,128)(2,1)S(1)}) custom-call(s32[1]{0:T(128)} %bitcast.1.z_ref, bf16[2048,2048]{1,0:T(8,128)(2,1)} %assemble.3.x_in_ref.x_ref, f32[8,768]{1,0:T(8,128)S(1)} %broadcast_in_dim.73.bias_ref, f32[2048,128]{1,0:T(8,128)S(1)} %copy-done.11, f32[2048,128]{1,0:T(8,128)S(1)} %copy-done.12, ...), custom_call_target="tpu_custom_call" | custom-call | flops 644245120 | bytes 1048576 | tf_op jit(solution)/shard_map/pack/pallas_call | solution.py:560
  147.3 24.2 %attend_forward.1 = (f32[256,2048]{1,0:T(8,128)}, f32[8,2048]{1,0:T(8,128)}, bf16[2048,256]{1,0:T(8,128)(2,1)}) custom-call(s32[8]{0:T(128)} %and_select_fusion.5.low_ref, bf16[2048,768]{1,0:T(8,128)(2,1)} %get-tuple-element.212.packed_ref, bf16[256,2048]{1,0:T(8,128)(2,1)} %copy-done.28, s32[2048,1]{1,0:T(8,128)} %copy.29.pcol_ref, s32[1,2048]{1,0:T(1,128)} %bitcast.82, ...), custom_call_target="tpu_custom_call" | custom-call | flops 10737418240 | bytes 10485760 | tf_op jit(solution)/shard_map/attend_forward/pallas_call | solution.py:809
  175.5 9.9 %reorder.3.x_ref = bf16[2048,2048]{1,0:T(8,128)(2,1)} custom-call(s32[8]{0:T(128)} %stack.64.order_ref, bf16[2048,2048]{1,0:T(8,128)(2,1)} %all-gather.3.cloned.1.call-done.x_ref), custom_call_target="tpu_custom_call" | custom-call | flops 1048576 | bytes 1048576 | tf_op jit(solution)/shard_map/reorder/pallas_call | solution.py:694
  185.4 7.8 %times.1.grad_ref = bf16[2048,256]{1,0:T(8,128)(2,1)S(1)} custom-call(s32[1]{0:T(128)} %bitcast.1.z_ref, bf16[2048,2048]{1,0:T(8,128)(2,1)} %reorder.3.x_ref, bf16[512,1024]{1,0:T(8,128)(2,1)S(1)} %pad_maximum_fusion.2.rest_0_, bf16[512,1024]{1,0:T(8,128)(2,1)S(1)} %collective-permute-done.rest_1_, bf16[512,1024]{1,0:T(8,128)(2,1)} %collective-permute-done.6.rest_2_, ...), custom_call_target="tpu_custom_call" | custom-call | flops 107374184 | bytes 1048576 | tf_op jit(solution)/shard_map/times/pallas_call | solution.py:560
  193.2 3.6 convolution_convert_fusion.3.b_ref
  196.9 3.7 collective-permute-done.16.rest_6_.rest_13_
  203.1 16.9 %up.1 = (f32[2048,1024]{1,0:T(8,128)}, bf16[2048,1024]{1,0:T(8,128)(2,1)}) custom-call(s32[1]{0:T(128)} %bitcast.1.z_ref, bf16[2048,2048]{1,0:T(8,128)(2,1)} %assemble.3.x_in_ref.x_ref, f32[8,1024]{1,0:T(8,128)S(1)} %broadcast_in_dim.78.bias_ref, bf16[512,1024]{1,0:T(8,128)(2,1)S(1)} %copy-done.6, bf16[512,1024]{1,0:T(8,128)(2,1)} %collective-permute-done.11.rest_1_.rest_8_, ...), custom_call_target="tpu_custom_call" | custom-call | flops 429496736 | bytes 1048576 | tf_op jit(solution)/shard_map/up/pallas_call | solution.py:560
  220.0 14.0 %convolution_convert_fusion.1.x_ref = bf16[2048,1024]{1,0:T(8,128)(2,1)} fusion(bf16[2048,2048]{1,0:T(8,128)(2,1)} %reorder.3.x_ref, bf16[2048,1024]{1,0:T(8,128)(2,1)} %get-tuple-element.211.b_ref), kind=kOutput, calls=%fused_computation.4 | convolution fusion | flops 8592031744 | bytes 16777216 | tf_op jit(solution)/shard_map/dot_general | solution.py:1014
  234.0 5.5 reorder.4
  241.4 41.2 %attend_backward.1 = (bf16[2048,768]{1,0:T(8,128)(2,1)}, f32[8,768]{1,0:T(8,128)}) custom-call(s32[8]{0:T(128)} %and_select_fusion.5.low_ref, bf16[2048,768]{1,0:T(8,128)(2,1)} %get-tuple-element.212.packed_ref, f32[256,2048]{1,0:T(8,128)} %get-tuple-element.213.outt_ref, f32[8,2048]{1,0:T(8,128)} %get-tuple-element.214.lse_ref, ...), custom_call_target="tpu_custom_call" | custom-call | flops 30064771072 | bytes 10485760 | tf_op jit(solution)/shard_map/attend_backward/pallas_call | solution.py:834
  283.1 10.3 %convolution_convert_fusion.2.a_ref = bf16[2048,768]{1,0:T(8,128)(2,1)S(1)} fusion(bf16[2048,2048]{1,0:T(8,128)(2,1)} %assemble.3.x_in_ref.x_ref, bf16[2048,768]{1,0:T(8,128)(2,1)} %get-tuple-element.242.a_ref), kind=kOutput, calls=%fused_computation.5 | convolution fusion | flops 6444023808 | bytes 14680064 | tf_op jit(solution)/shard_map/dot_general | solution.py:1025
  299.8 17.9 %up_back.1 = (bf16[2048,1024]{1,0:T(8,128)(2,1)S(1)}, f32[8,1024]{1,0:T(8,128)S(1)}) custom-call(s32[1]{0:T(128)} %bitcast.1.z_ref, bf16[2048,2048]{1,0:T(8,128)(2,1)} %reorder.3.x_ref, f32[2048,1024]{1,0:T(8,128)} %get-tuple-element.224.up_ref, bf16[2048,1024]{1,0:T(8,128)(2,1)} %all-gather.5.cloned.1.call-done.rest_0_.rest_7_), custom_call_target="tpu_custom_call" | custom-call | flops 429496736 | bytes 1048576 | tf_op jit(solution)/shard_map/up_back/pallas_call | solution.py:560
  317.8 19.6 %to_features.2 = (bf16[4,256,2048]{2,1,0:T(8,128)(2,1)}, bf16[4,256,2048]{2,1,0:T(8,128)(2,1)}) custom-call(s32[1]{0:T(128)} %bitcast.1.z_ref, bf16[2048,256]{1,0:T(8,128)(2,1)S(1)} %copy-done.18, bf16[2048,1024]{1,0:T(8,128)(2,1)} %get-tuple-element.211.b_ref, bf16[512,1024]{1,0:T(8,128)(2,1)S(1)} %pad_maximum_fusion.2.rest_0_, ...), custom_call_target="tpu_custom_call" | custom-call | flops 536870912 | bytes 1048576 | tf_op jit(solution)/shard_map/to_features/pallas_call | solution.py:560
  337.4 7.3 %collective-permute-done.17 = bf16[512,1024]{1,0:T(8,128)(2,1)S(1)} collective-permute-done((bf16[512,1024]{1,0:T(8,128)(2,1)}, bf16[512,1024]{1,0:T(8,128)(2,1)S(1)}, u32[]{:S(2)}, u32[]{:S(2)}) %collective-permute-start.17) | collective-permute-done | bytes 1048608 | tf_op jit(solution)/shard_map/ppermute | solution.py:67
  347.5 5.3 collective-permute-start.20
  354.6 12.7 %convolution_convert_fusion.x_ref = bf16[2048,1024]{1,0:T(8,128)(2,1)} fusion(bf16[2048,2048]{1,0:T(8,128)(2,1)} %assemble.3.x_in_ref.x_ref, bf16[2048,1024]{1,0:T(8,128)(2,1)S(1)} %get-tuple-element.236.b_ref), kind=kOutput, calls=%fused_computation.3 | convolution fusion | flops 8592031744 | bytes 16777216 | tf_op jit(solution)/shard_map/dot_general | solution.py:1043
  367.3 5.5 reorder.5
  372.8 7.8 %add_convert_fusion.1 = bf16[4,256,2048]{2,1,0:T(8,128)(2,1)} fusion(bf16[4,256,2048]{2,1,0:T(8,128)(2,1)} %collective-permute-done.19, bf16[4,256,2048]{2,1,0:T(8,128)(2,1)} %get-tuple-element.239), kind=kLoop, calls=%fused_computation.1 | loop fusion | flops 8388608 | bytes 12582912 | tf_op jit(solution)/shard_map/convert_element_type | solution.py:209
  380.7 23.6 %to_features.3 = (bf16[4,256,2048]{2,1,0:T(8,128)(2,1)}, bf16[4,256,2048]{2,1,0:T(8,128)(2,1)}) custom-call(s32[1]{0:T(128)} %bitcast.1.z_ref, bf16[2048,768]{1,0:T(8,128)(2,1)} %get-tuple-element.242.a_ref, bf16[2048,1024]{1,0:T(8,128)(2,1)} %copy-done.15, bf16[512,1024]{1,0:T(8,128)(2,1)S(1)} %pad_maximum_fusion.2.rest_0_, ...), custom_call_target="tpu_custom_call" | custom-call | flops 751619264 | bytes 1048576 | tf_op jit(solution)/shard_map/to_features/pallas_call | solution.py:560
  404.3 3.0 add_convert_fusion.4
  407.3 2.6 add_convert_fusion.3
  411.7 4.2 collective-permute-start.31
  416.0 3.5 slice_bitcast_fusion.4
  425.3 4.2 add_convert_fusion
  429.5 16.1 %collective-permute-done.22 = bf16[256,2048]{1,0:T(8,128)(2,1)S(1)} collective-permute-done((bf16[256,2048]{1,0:T(8,128)(2,1)S(1)}, bf16[256,2048]{1,0:T(8,128)(2,1)S(1)}, u32[]{:S(2)}, u32[]{:S(2)}) %collective-permute-start.22) | collective-permute-done | bytes 1048608 | tf_op jit(solution)/shard_map/ppermute | solution.py:33
  445.6 22.3 %collective-permute-done.23 = bf16[256,2048]{1,0:T(8,128)(2,1)S(1)} collective-permute-done((bf16[256,2048]{1,0:T(8,128)(2,1)S(1)}, bf16[256,2048]{1,0:T(8,128)(2,1)S(1)}, u32[]{:S(2)}, u32[]{:S(2)}) %collective-permute-start.23) | collective-permute-done | bytes 1048608 | tf_op jit(solution)/shard_map/ppermute | solution.py:33
  473.9 9.0 %collective-permute-done.26 = bf16[128,2048]{1,0:T(8,128)(2,1)S(1)} collective-permute-done((bf16[128,2048]{1,0:T(8,128)(2,1)S(1)}, bf16[128,2048]{1,0:T(8,128)(2,1)S(1)}, u32[]{:S(2)}, u32[]{:S(2)}) %collective-permute-start.26) | collective-permute-done | bytes 524320 | tf_op jit(solution)/shard_map/ppermute | solution.py:33
  488.7 8.8 %collective-permute-done.32 = bf16[512,1024]{1,0:T(8,128)(2,1)} collective-permute-done((bf16[512,1024]{1,0:T(8,128)(2,1)}, bf16[512,1024]{1,0:T(8,128)(2,1)}, u32[]{:S(2)}, u32[]{:S(2)}) %collective-permute-start.32) | collective-permute-done | bytes 1048608 | tf_op jit(solution)/shard_map/ppermute | solution.py:71
  497.6 3.1 add_convert_fusion.2
  500.7 8.1 %collective-permute-done.29 = bf16[256,2048]{1,0:T(8,128)(2,1)S(1)} collective-permute-done((bf16[256,2048]{1,0:T(8,128)(2,1)}, bf16[256,2048]{1,0:T(8,128)(2,1)S(1)}, u32[]{:S(2)}, u32[]{:S(2)}) %collective-permute-start.29) | collective-permute-done | bytes 1048608 | tf_op jit(solution)/shard_map/ppermute | solution.py:33
  523.0 9.2 %collective-permute-done.33.refs_1_ = bf16[128,2048]{1,0:T(8,128)(2,1)S(1)} collective-permute-done((bf16[128,2048]{1,0:T(8,128)(2,1)S(1)}, bf16[128,2048]{1,0:T(8,128)(2,1)S(1)}, u32[]{:S(2)}, u32[]{:S(2)}) %collective-permute-start.33) | collective-permute-done | bytes 524320 | tf_op jit(solution)/shard_map/ppermute | solution.py:33
  532.2 9.5 %collective-permute-done.34.refs_2_ = bf16[128,2048]{1,0:T(8,128)(2,1)S(1)} collective-permute-done((bf16[128,2048]{1,0:T(8,128)(2,1)S(1)}, bf16[128,2048]{1,0:T(8,128)(2,1)S(1)}, u32[]{:S(2)}, u32[]{:S(2)}) %collective-permute-start.34) | collective-permute-done | bytes 524320 | tf_op jit(solution)/shard_map/ppermute | solution.py:33
  548.1 2.6 collective-permute-done.38
  550.8 2.8 collective-permute-start.39
  563.8 6.7 %collective-permute-done.41 = f32[13312]{0:T(1024)S(1)} collective-permute-done((f32[13312]{0:T(1024)S(1)}, f32[13312]{0:T(1024)S(1)}, u32[]{:S(2)}, u32[]{:S(2)}) %collective-permute-start.41) | collective-permute-done | bytes 53280 | tf_op jit(solution)/shard_map/ppermute | solution.py:33
  573.8 2.7 broadcast_select_fusion.1
  576.5 2.5 maximum_bitcast_fusion
  (281 shorter events, 110.5 us)
Async XLA Ops:
  7.2 168.3 %all-gather.3.cloned.1.call-start = ((), (), s32[]{:S(2)}) async-start(), calls=%async_computation.2 | async-start | bytes 9437184 | tf_op jit(solution)/shard_map/all_gather | solution.py:931
  15.2 282.6 %all-gather.5.cloned.1.call-start = ((), (), s32[]{:S(2)}) async-start(), calls=%async_computation.3 | async-start | bytes 5242880 | tf_op jit(solution)/shard_map/all_gather | solution.py:1009
  15.2 27.4 %collective-permute-start = (bf16[512,1024]{1,0:T(8,128)(2,1)S(1)}, bf16[512,1024]{1,0:T(8,128)(2,1)S(1)}, u32[]{:S(2)}, u32[]{:S(2)}) collective-permute-start(bf16[512,1024]{1,0:T(8,128)(2,1)S(1)} %pad_maximum_fusion.2.rest_0_), channel_id=1, source_target_pairs={{0,8},{8,16},{16,24},{1,9},{9,17},{17,25},{2,10},{10,18},{18,26},{... | collective-permute-start | bytes 3145736 | tf_op jit(solution)/shard_map/ppermute | solution.py:67
  20.2 26.5 %collective-permute-start.1 = (bf16[512,1024]{1,0:T(8,128)(2,1)S(1)}, bf16[512,1024]{1,0:T(8,128)(2,1)S(1)}, u32[]{:S(2)}, u32[]{:S(2)}) collective-permute-start(bf16[512,1024]{1,0:T(8,128)(2,1)S(1)} %pad_maximum_fusion.2.rest_0_), channel_id=1, source_target_pairs={{8,0},{16,8},{24,16},{9,1},{17,9},{25,17},{10,2},{18,10},{26,18},{... | collective-permute-start | bytes 3145736 | tf_op jit(solution)/shard_map/ppermute | solution.py:71
  21.5 40.7 %collective-permute-start.2 = (bf16[256,2048]{1,0:T(8,128)(2,1)}, bf16[256,2048]{1,0:T(8,128)(2,1)}, u32[]{:S(2)}, u32[]{:S(2)}) collective-permute-start(bf16[256,2048]{1,0:T(8,128)(2,1)} %copy-done.16), channel_id=1, source_target_pairs={{0,2},{2,0},{4,6},{6,4},{1,3},{3,1},{5,7},{7,5},{8,10},{10,8},{12,... | collective-permute-start | bytes 3145736 | tf_op jit(solution)/shard_map/ppermute | solution.py:33
  23.1 39.1 %collective-permute-start.3 = (bf16[256,2048]{1,0:T(8,128)(2,1)}, bf16[256,2048]{1,0:T(8,128)(2,1)}, u32[]{:S(2)}, u32[]{:S(2)}) collective-permute-start(bf16[256,2048]{1,0:T(8,128)(2,1)} %copy-done.16), channel_id=1, source_target_pairs={{0,4},{2,6},{4,0},{6,2},{1,5},{3,7},{5,1},{7,3},{8,12},{10,14},{12... | collective-permute-start | bytes 3145736 | tf_op jit(solution)/shard_map/ppermute | solution.py:33
  46.9 15.2 %collective-permute-start.6 = (bf16[512,1024]{1,0:T(8,128)(2,1)S(1)}, bf16[512,1024]{1,0:T(8,128)(2,1)}, u32[]{:S(2)}, u32[]{:S(2)}) collective-permute-start(bf16[512,1024]{1,0:T(8,128)(2,1)S(1)} %collective-permute-done.rest_1_), channel_id=1, source_target_pairs={{8,16},{16,24},{9,17},{17,25},{10,18},{18,26},{11,19},{19,27},{12,... | collective-permute-start | bytes 3145736 | tf_op jit(solution)/shard_map/ppermute | solution.py:67
  48.6 28.1 %collective-permute-start.7 = (bf16[512,1024]{1,0:T(8,128)(2,1)S(1)}, bf16[512,1024]{1,0:T(8,128)(2,1)}, u32[]{:S(2)}, u32[]{:S(2)}) collective-permute-start(bf16[512,1024]{1,0:T(8,128)(2,1)S(1)} %collective-permute-done.1.rest_4_), channel_id=1, source_target_pairs={{8,0},{16,8},{9,1},{17,9},{10,2},{18,10},{11,3},{19,11},{12,4},{20... | collective-permute-start | bytes 3145736 | tf_op jit(solution)/shard_map/ppermute | solution.py:71
  76.7 21.5 %collective-permute-start.8 = (bf16[512,1024]{1,0:T(8,128)(2,1)}, bf16[512,1024]{1,0:T(8,128)(2,1)S(1)}, u32[]{:S(2)}, u32[]{:S(2)}) collective-permute-start(bf16[512,1024]{1,0:T(8,128)(2,1)} %collective-permute-done.6.rest_2_), channel_id=1, source_target_pairs={{16,24},{17,25},{18,26},{19,27},{20,28},{21,29},{22,30},{23,31}} | collective-permute-start | bytes 3145736 | tf_op jit(solution)/shard_map/ppermute | solution.py:67
  77.4 25.1 %collective-permute-start.9 = (bf16[512,1024]{1,0:T(8,128)(2,1)}, bf16[512,1024]{1,0:T(8,128)(2,1)}, u32[]{:S(2)}, u32[]{:S(2)}) collective-permute-start(bf16[512,1024]{1,0:T(8,128)(2,1)} %collective-permute-done.7.rest_5_), channel_id=1, source_target_pairs={{8,0},{9,1},{10,2},{11,3},{12,4},{13,5},{14,6},{15,7}} | collective-permute-start | bytes 3145736 | tf_op jit(solution)/shard_map/ppermute | solution.py:71
  80.9 12.1 %collective-permute-start.4 = (bf16[128,2048]{1,0:T(8,128)(2,1)S(1)}, bf16[128,2048]{1,0:T(8,128)(2,1)S(1)}, u32[]{:S(2)}, u32[]{:S(2)}) collective-permute-start(bf16[128,2048]{1,0:T(8,128)(2,1)S(1)} %slice.94), channel_id=1, source_target_pairs={{0,4},{2,6},{4,0},{6,2},{1,5},{3,7},{5,1},{7,3},{8,12},{10,14},{12... | collective-permute-start | bytes 1572872 | tf_op jit(solution)/shard_map/ppermute | solution.py:33
  82.4 11.5 %collective-permute-start.5 = (bf16[128,2048]{1,0:T(8,128)(2,1)S(1)}, bf16[128,2048]{1,0:T(8,128)(2,1)}, u32[]{:S(2)}, u32[]{:S(2)}) collective-permute-start(bf16[128,2048]{1,0:T(8,128)(2,1)S(1)} %slice.95), channel_id=1, source_target_pairs={{0,2},{2,0},{4,6},{6,4},{1,3},{3,1},{5,7},{7,5},{8,10},{10,8},{12,... | collective-permute-start | bytes 1572872 | tf_op jit(solution)/shard_map/ppermute | solution.py:33
  102.5 7.5 %collective-permute-start.10 = (bf16[1024,2048]{1,0:T(8,128)(2,1)}, bf16[1024,2048]{1,0:T(8,128)(2,1)}, u32[]{:S(2)}, u32[]{:S(2)}) collective-permute-start(bf16[1024,2048]{1,0:T(8,128)(2,1)} %assemble.2.refs_0_), channel_id=1, source_target_pairs={{0,1},{1,0},{2,3},{3,2},{4,5},{5,4},{6,7},{7,6},{8,9},{9,8},{10,11... | collective-permute-start | bytes 12582920 | tf_op jit(solution)/shard_map/ppermute | solution.py:33
  102.5 39.1 %collective-permute-start.11 = (bf16[512,1024]{1,0:T(8,128)(2,1)}, bf16[512,1024]{1,0:T(8,128)(2,1)}, u32[]{:S(2)}, u32[]{:S(2)}) collective-permute-start(bf16[512,1024]{1,0:T(8,128)(2,1)} %get-tuple-element.192.rest_0_.rest_7_), channel_id=1, source_target_pairs={{0,8},{8,16},{16,24},{1,9},{9,17},{17,25},{2,10},{10,18},{18,26},{... | collective-permute-start | bytes 3145736 | tf_op jit(solution)/shard_map/ppermute | solution.py:67
  104.9 36.7 %collective-permute-start.12 = (bf16[512,1024]{1,0:T(8,128)(2,1)}, bf16[512,1024]{1,0:T(8,128)(2,1)}, u32[]{:S(2)}, u32[]{:S(2)}) collective-permute-start(bf16[512,1024]{1,0:T(8,128)(2,1)} %get-tuple-element.192.rest_0_.rest_7_), channel_id=1, source_target_pairs={{8,0},{16,8},{24,16},{9,1},{17,9},{25,17},{10,2},{18,10},{26,18},{... | collective-permute-start | bytes 3145736 | tf_op jit(solution)/shard_map/ppermute | solution.py:71
  141.6 29.9 %collective-permute-start.13 = (bf16[512,1024]{1,0:T(8,128)(2,1)}, bf16[512,1024]{1,0:T(8,128)(2,1)}, u32[]{:S(2)}, u32[]{:S(2)}) collective-permute-start(bf16[512,1024]{1,0:T(8,128)(2,1)} %collective-permute-done.11.rest_1_.rest_8_), channel_id=1, source_target_pairs={{8,16},{16,24},{9,17},{17,25},{10,18},{18,26},{11,19},{19,27},{12,... | collective-permute-start | bytes 3145736 | tf_op jit(solution)/shard_map/ppermute | solution.py:67
  143.3 28.2 %collective-permute-start.14 = (bf16[512,1024]{1,0:T(8,128)(2,1)}, bf16[512,1024]{1,0:T(8,128)(2,1)}, u32[]{:S(2)}, u32[]{:S(2)}) collective-permute-start(bf16[512,1024]{1,0:T(8,128)(2,1)} %collective-permute-done.12.rest_4_.rest_11_), channel_id=1, source_target_pairs={{8,0},{16,8},{9,1},{17,9},{10,2},{18,10},{11,3},{19,11},{12,4},{20... | collective-permute-start | bytes 3145736 | tf_op jit(solution)/shard_map/ppermute | solution.py:71
  171.5 25.4 %collective-permute-start.15 = (bf16[512,1024]{1,0:T(8,128)(2,1)}, bf16[512,1024]{1,0:T(8,128)(2,1)}, u32[]{:S(2)}, u32[]{:S(2)}) collective-permute-start(bf16[512,1024]{1,0:T(8,128)(2,1)} %collective-permute-done.13.rest_2_.rest_9_), channel_id=1, source_target_pairs={{16,24},{17,25},{18,26},{19,27},{20,28},{21,29},{22,30},{23,31}} | collective-permute-start | bytes 3145736 | tf_op jit(solution)/shard_map/ppermute | solution.py:67
  173.1 27.4 %collective-permute-start.16 = (bf16[512,1024]{1,0:T(8,128)(2,1)}, bf16[512,1024]{1,0:T(8,128)(2,1)}, u32[]{:S(2)}, u32[]{:S(2)}) collective-permute-start(bf16[512,1024]{1,0:T(8,128)(2,1)} %collective-permute-done.14.rest_5_.rest_12_), channel_id=1, source_target_pairs={{8,0},{9,1},{10,2},{11,3},{12,4},{13,5},{14,6},{15,7}} | collective-permute-start | bytes 3145736 | tf_op jit(solution)/shard_map/ppermute | solution.py:71
  200.6 203.8 %reduce-scatter.3.cloned.1.call-start = ((), (), s32[]{:S(2)}) async-start(), calls=%async_computation.4 | async-start | bytes 5242880 | tf_op jit(solution)/shard_map/reduce_scatter | solution.py:1018
  282.6 229.7 %reduce-scatter.5.cloned.1.call-start = ((), (), s32[]{:S(2)}) async-start(), calls=%async_computation.5 | async-start | bytes 5242880 | tf_op jit(solution)/shard_map/reduce_scatter | solution.py:1049
  297.7 47.0 %collective-permute-start.17 = (bf16[512,1024]{1,0:T(8,128)(2,1)}, bf16[512,1024]{1,0:T(8,128)(2,1)S(1)}, u32[]{:S(2)}, u32[]{:S(2)}) collective-permute-start(bf16[512,1024]{1,0:T(8,128)(2,1)} %copy-done.20), channel_id=1, source_target_pairs={{0,8},{1,9},{2,10},{3,11},{4,12},{5,13},{6,14},{7,15}} | collective-permute-start | bytes 3145736 | tf_op jit(solution)/shard_map/ppermute | solution.py:67
  299.1 45.7 %collective-permute-start.18 = (bf16[512,1024]{1,0:T(8,128)(2,1)}, bf16[512,1024]{1,0:T(8,128)(2,1)S(1)}, u32[]{:S(2)}, u32[]{:S(2)}) collective-permute-start(bf16[512,1024]{1,0:T(8,128)(2,1)} %copy-done.22), channel_id=1, source_target_pairs={{24,16},{25,17},{26,18},{27,19},{28,20},{29,21},{30,22},{31,23}} | collective-permute-start | bytes 3145736 | tf_op jit(solution)/shard_map/ppermute | solution.py:71
  347.5 25.3 %collective-permute-start.19 = (bf16[4,256,2048]{2,1,0:T(8,128)(2,1)}, bf16[4,256,2048]{2,1,0:T(8,128)(2,1)}, u32[]{:S(2)}, u32[]{:S(2)}) collective-permute-start(bf16[4,256,2048]{2,1,0:T(8,128)(2,1)} %get-tuple-element.238), channel_id=1, source_target_pairs={{0,1},{1,0},{2,3},{3,2},{4,5},{5,4},{6,7},{7,6},{8,9},{9,8},{10,11... | collective-permute-start | bytes 12582920 | tf_op jit(solution)/shard_map/ppermute | solution.py:33
  347.5 56.8 %collective-permute-start.20 = (bf16[512,1024]{1,0:T(8,128)(2,1)}, bf16[512,1024]{1,0:T(8,128)(2,1)}, u32[]{:S(2)}, u32[]{:S(2)}) collective-permute-start(bf16[512,1024]{1,0:T(8,128)(2,1)} %add_convert_fusion.6), channel_id=1, source_target_pairs={{0,8},{8,16},{1,9},{9,17},{2,10},{10,18},{3,11},{11,19},{4,12},{12... | collective-permute-start | bytes 3145736 | tf_op jit(solution)/shard_map/ppermute | solution.py:67
  352.8 51.5 %collective-permute-start.21 = (bf16[512,1024]{1,0:T(8,128)(2,1)}, bf16[512,1024]{1,0:T(8,128)(2,1)}, u32[]{:S(2)}, u32[]{:S(2)}) collective-permute-start(bf16[512,1024]{1,0:T(8,128)(2,1)} %add_convert_fusion.5), channel_id=1, source_target_pairs={{16,8},{24,16},{17,9},{25,17},{18,10},{26,18},{19,11},{27,19},{20,... | collective-permute-start | bytes 3145736 | tf_op jit(solution)/shard_map/ppermute | solution.py:71
  410.0 13.7 %collective-permute-start.25 = (bf16[4,256,2048]{2,1,0:T(8,128)(2,1)}, bf16[4,256,2048]{2,1,0:T(8,128)(2,1)}, u32[]{:S(2)}, u32[]{:S(2)}) collective-permute-start(bf16[4,256,2048]{2,1,0:T(8,128)(2,1)} %get-tuple-element.257), channel_id=1, source_target_pairs={{0,1},{1,0},{2,3},{3,2},{4,5},{5,4},{6,7},{7,6},{8,9},{9,8},{10,11... | collective-permute-start | bytes 12582920 | tf_op jit(solution)/shard_map/ppermute | solution.py:33
  411.7 77.0 %collective-permute-start.31 = (bf16[512,1024]{1,0:T(8,128)(2,1)}, bf16[512,1024]{1,0:T(8,128)(2,1)}, u32[]{:S(2)}, u32[]{:S(2)}) collective-permute-start(bf16[512,1024]{1,0:T(8,128)(2,1)} %add_convert_fusion.4), channel_id=1, source_target_pairs={{0,8},{8,16},{16,24},{1,9},{9,17},{17,25},{2,10},{10,18},{18,26},{... | collective-permute-start | bytes 3145736 | tf_op jit(solution)/shard_map/ppermute | solution.py:67
  419.5 26.1 %collective-permute-start.22 = (bf16[256,2048]{1,0:T(8,128)(2,1)S(1)}, bf16[256,2048]{1,0:T(8,128)(2,1)S(1)}, u32[]{:S(2)}, u32[]{:S(2)}) collective-permute-start(bf16[256,2048]{1,0:T(8,128)(2,1)S(1)} %get-tuple-element.253), channel_id=1, source_target_pairs={{0,2},{2,0},{4,6},{6,4},{1,3},{3,1},{5,7},{7,5},{8,10},{10,8},{12,... | collective-permute-start | bytes 3145736 | tf_op jit(solution)/shard_map/ppermute | solution.py:33
  420.8 47.1 %collective-permute-start.23 = (bf16[256,2048]{1,0:T(8,128)(2,1)S(1)}, bf16[256,2048]{1,0:T(8,128)(2,1)S(1)}, u32[]{:S(2)}, u32[]{:S(2)}) collective-permute-start(bf16[256,2048]{1,0:T(8,128)(2,1)S(1)} %get-tuple-element.254), channel_id=1, source_target_pairs={{0,4},{2,6},{4,0},{6,2},{1,5},{3,7},{5,1},{7,3},{8,12},{10,14},{12... | collective-permute-start | bytes 3145736 | tf_op jit(solution)/shard_map/ppermute | solution.py:33
  422.4 45.6 %collective-permute-start.24 = (bf16[256,2048]{1,0:T(8,128)(2,1)S(1)}, bf16[256,2048]{1,0:T(8,128)(2,1)S(1)}, u32[]{:S(2)}, u32[]{:S(2)}) collective-permute-start(bf16[256,2048]{1,0:T(8,128)(2,1)S(1)} %get-tuple-element.255), channel_id=1, source_target_pairs={{0,6},{2,4},{4,2},{6,0},{1,7},{3,5},{5,3},{7,1},{8,14},{10,12},{12... | collective-permute-start | bytes 3145736 | tf_op jit(solution)/shard_map/ppermute | solution.py:33
  423.7 73.8 %collective-permute-start.32 = (bf16[512,1024]{1,0:T(8,128)(2,1)}, bf16[512,1024]{1,0:T(8,128)(2,1)}, u32[]{:S(2)}, u32[]{:S(2)}) collective-permute-start(bf16[512,1024]{1,0:T(8,128)(2,1)} %add_convert_fusion.3), channel_id=1, source_target_pairs={{8,0},{16,8},{24,16},{9,1},{17,9},{25,17},{10,2},{18,10},{26,18},{... | collective-permute-start | bytes 3145736 | tf_op jit(solution)/shard_map/ppermute | solution.py:71
  470.2 12.7 %collective-permute-start.26 = (bf16[128,2048]{1,0:T(8,128)(2,1)S(1)}, bf16[128,2048]{1,0:T(8,128)(2,1)S(1)}, u32[]{:S(2)}, u32[]{:S(2)}) collective-permute-start(bf16[128,2048]{1,0:T(8,128)(2,1)S(1)} %get-tuple-element.343), channel_id=1, source_target_pairs={{0,4},{2,6},{4,0},{6,2},{1,5},{3,7},{5,1},{7,3},{8,12},{10,14},{12... | collective-permute-start | bytes 1572872 | tf_op jit(solution)/shard_map/ppermute | solution.py:33
  471.9 11.4 %collective-permute-start.27 = (bf16[128,2048]{1,0:T(8,128)(2,1)S(1)}, bf16[128,2048]{1,0:T(8,128)(2,1)S(1)}, u32[]{:S(2)}, u32[]{:S(2)}) collective-permute-start(bf16[128,2048]{1,0:T(8,128)(2,1)S(1)} %get-tuple-element.342), channel_id=1, source_target_pairs={{0,2},{2,0},{4,6},{6,4},{1,3},{3,1},{5,7},{7,5},{8,10},{10,8},{12,... | collective-permute-start | bytes 1572872 | tf_op jit(solution)/shard_map/ppermute | solution.py:33
  485.8 23.0 %collective-permute-start.29 = (bf16[256,2048]{1,0:T(8,128)(2,1)}, bf16[256,2048]{1,0:T(8,128)(2,1)S(1)}, u32[]{:S(2)}, u32[]{:S(2)}) collective-permute-start(bf16[256,2048]{1,0:T(8,128)(2,1)} %pad_maximum_fusion.3), channel_id=1, source_target_pairs={{0,2},{2,0},{4,6},{6,4},{1,3},{3,1},{5,7},{7,5},{8,10},{10,8},{12,... | collective-permute-start | bytes 3145736 | tf_op jit(solution)/shard_map/ppermute | solution.py:33
  487.2 23.0 %collective-permute-start.30 = (bf16[256,2048]{1,0:T(8,128)(2,1)}, bf16[256,2048]{1,0:T(8,128)(2,1)}, u32[]{:S(2)}, u32[]{:S(2)}) collective-permute-start(bf16[256,2048]{1,0:T(8,128)(2,1)} %pad_maximum_fusion.4), channel_id=1, source_target_pairs={{0,4},{2,6},{4,0},{6,2},{1,5},{3,7},{5,1},{7,3},{8,12},{10,14},{12... | collective-permute-start | bytes 3145736 | tf_op jit(solution)/shard_map/ppermute | solution.py:33
  488.7 64.9 %collective-permute-start.28 = (bf16[256,2048]{1,0:T(8,128)(2,1)}, bf16[256,2048]{1,0:T(8,128)(2,1)}, u32[]{:S(2)}, u32[]{:S(2)}) collective-permute-start(bf16[256,2048]{1,0:T(8,128)(2,1)} %fusion.8), channel_id=1, source_target_pairs={{0,1},{1,0},{2,3},{3,2},{4,5},{5,4},{6,7},{7,6},{8,9},{9,8},{10,11... | collective-permute-start | bytes 3145736 | tf_op jit(solution)/shard_map/ppermute | solution.py:33
  517.3 14.9 %collective-permute-start.33 = (bf16[128,2048]{1,0:T(8,128)(2,1)S(1)}, bf16[128,2048]{1,0:T(8,128)(2,1)S(1)}, u32[]{:S(2)}, u32[]{:S(2)}) collective-permute-start(bf16[128,2048]{1,0:T(8,128)(2,1)S(1)} %get-tuple-element.326), channel_id=1, source_target_pairs={{0,2},{2,0},{4,6},{6,4},{1,3},{3,1},{5,7},{7,5},{8,10},{10,8},{12,... | collective-permute-start | bytes 1572872 | tf_op jit(solution)/shard_map/ppermute | solution.py:33
  518.5 23.2 %collective-permute-start.34 = (bf16[128,2048]{1,0:T(8,128)(2,1)S(1)}, bf16[128,2048]{1,0:T(8,128)(2,1)S(1)}, u32[]{:S(2)}, u32[]{:S(2)}) collective-permute-start(bf16[128,2048]{1,0:T(8,128)(2,1)S(1)} %get-tuple-element.325), channel_id=1, source_target_pairs={{0,4},{2,6},{4,0},{6,2},{1,5},{3,7},{5,1},{7,3},{8,12},{10,14},{12... | collective-permute-start | bytes 1572872 | tf_op jit(solution)/shard_map/ppermute | solution.py:33
  520.0 21.7 %collective-permute-start.35 = (bf16[128,2048]{1,0:T(8,128)(2,1)S(1)}, bf16[128,2048]{1,0:T(8,128)(2,1)S(1)}, u32[]{:S(2)}, u32[]{:S(2)}) collective-permute-start(bf16[128,2048]{1,0:T(8,128)(2,1)S(1)} %get-tuple-element.324), channel_id=1, source_target_pairs={{0,6},{2,4},{4,2},{6,0},{1,7},{3,5},{5,3},{7,1},{8,14},{10,12},{12... | collective-permute-start | bytes 1572872 | tf_op jit(solution)/shard_map/ppermute | solution.py:33
  541.7 32.1 %collective-permute-start.36 = (f32[256,2048]{1,0:T(8,128)}, f32[256,2048]{1,0:T(8,128)}, u32[]{:S(2)}, u32[]{:S(2)}) collective-permute-start(f32[256,2048]{1,0:T(8,128)} %convert_add_fusion.1), channel_id=1, source_target_pairs={{0,1},{1,0},{2,3},{3,2},{4,5},{5,4},{6,7},{7,6},{8,9},{9,8},{10,11... | collective-permute-start | bytes 6291464 | tf_op jit(solution)/shard_map/ppermute | solution.py:33
  546.5 4.2 collective-permute-start.38
  550.8 5.1 collective-permute-start.39
  555.9 4.9 collective-permute-start.40
  557.2 15.1 %collective-permute-start.42 = (bf16[128,1024]{1,0:T(8,128)(2,1)S(1)}, bf16[128,1024]{1,0:T(8,128)(2,1)S(1)}, u32[]{:S(2)}, u32[]{:S(2)}) collective-permute-start(bf16[128,1024]{1,0:T(8,128)(2,1)S(1)} %get-tuple-element.340), channel_id=1, source_target_pairs={{0,2},{2,0},{4,6},{6,4},{1,3},{3,1},{5,7},{7,5},{8,10},{10,8},{12,... | collective-permute-start | bytes 786440 | tf_op jit(solution)/shard_map/ppermute | solution.py:33
  558.1 14.2 %collective-permute-start.43 = (bf16[128,1024]{1,0:T(8,128)(2,1)S(1)}, bf16[128,1024]{1,0:T(8,128)(2,1)S(1)}, u32[]{:S(2)}, u32[]{:S(2)}) collective-permute-start(bf16[128,1024]{1,0:T(8,128)(2,1)S(1)} %get-tuple-element.339), channel_id=1, source_target_pairs={{0,4},{2,6},{4,0},{6,2},{1,5},{3,7},{5,1},{7,3},{8,12},{10,14},{12... | collective-permute-start | bytes 786440 | tf_op jit(solution)/shard_map/ppermute | solution.py:33
  559.6 12.7 %collective-permute-start.44 = (bf16[128,1024]{1,0:T(8,128)(2,1)S(1)}, bf16[128,1024]{1,0:T(8,128)(2,1)S(1)}, u32[]{:S(2)}, u32[]{:S(2)}) collective-permute-start(bf16[128,1024]{1,0:T(8,128)(2,1)S(1)} %get-tuple-element.338), channel_id=1, source_target_pairs={{0,6},{2,4},{4,2},{6,0},{1,7},{3,5},{5,3},{7,1},{8,14},{10,12},{12... | collective-permute-start | bytes 786440 | tf_op jit(solution)/shard_map/ppermute | solution.py:33
  560.8 9.7 %collective-permute-start.41 = (f32[13312]{0:T(1024)S(1)}, f32[13312]{0:T(1024)S(1)}, u32[]{:S(2)}, u32[]{:S(2)}) collective-permute-start(f32[13312]{0:T(1024)S(1)} %add.329), channel_id=1, source_target_pairs={{0,4},{2,6},{4,0},{6,2},{1,5},{3,7},{5,1},{7,3},{8,12},{10,14},{12... | collective-permute-start | bytes 159752 | tf_op jit(solution)/shard_map/ppermute | solution.py:33
  (52 other events, 650.3 us)
Sparse Core Ops, SparseCore 0:
  15.3 68.7 all-gather.2
  200.7 79.4 all-gather.4
  282.7 118.1 reduce-scatter.2
  410.4 100.1 reduce-scatter.4
